TPU v7x, 32 devices: a whole 2x2x4 slice. The times are simulated.
32 devices in a mesh: groups: 2 (over y), tensor: 4 (over z), dp: 4 (over x, core).
Axes of the slice: x: 2, y: 2, z: 4, core: 2. Of those that a mesh axis runs over, the one named last changes fastest.
Arguments:
- layer_input: bfloat16 [4096, 4096], P(('groups', 'dp'), 'tensor'), parts along dimension 0, may hold values from -6 to 6
- gate_act: bfloat16 [4096, 14336], P(('groups', 'dp'), 'tensor'), parts along dimension 0, may hold values from -6 to 6
- up_act: bfloat16 [4096, 14336], P(('groups', 'dp'), 'tensor'), parts along dimension 0, may hold values from -6 to 6
- out_grad: bfloat16 [4096, 4096], P(('groups', 'dp'), 'tensor'), parts along dimension 0, may hold values from -6 to 6
- w_gate: bfloat16 [4096, 14336], P('dp', 'tensor'), may hold values from -0.09375 to 0.09375
- w_up: bfloat16 [4096, 14336], P('dp', 'tensor'), may hold values from -0.09375 to 0.09375
- w_down: bfloat16 [14336, 4096], P('tensor'), may hold values from -0.046875 to 0.046875
- proj_x: bfloat16 [4096, 64], P('tensor'), may hold values from -0.09375 to 0.09375
- proj_u: bfloat16 [14336, 64], P('tensor'), may hold values from -0.046875 to 0.046875
- proj_h: bfloat16 [14336, 64], P('tensor'), may hold values from -0.046875 to 0.046875
- proj_g: bfloat16 [4096, 64], P('tensor'), may hold values from -0.09375 to 0.09375
- doc_lengths: int32 [8, 8], P(('groups', 'dp')), parts along dimension 0, may hold values from 1 to 256, 512 in all within a row
Outputs:
- input_grad: bfloat16 [4096, 4096], P(('groups', 'dp'), 'tensor'), parts along dimension 0
- doc_logs: float32 [64, 2, 4096], P(('groups', 'dp'), None, 'tensor'), parts along dimension 0
There are 2 independent parts, one for each index of `groups`. A program takes and returns all parts, laid end to end along the dimension named above; an argument that names none is the same for every part. Nothing has to cross between parts.
Inputs may be any that keep to these rules, and one draw needn't show every extreme that they name: `doc_lengths`: each row sums to 512, and its largest entry is 256.
All inputs are finite; a program needn't handle non-finite values.
Results may differ from a plain program's by a relative error of at most 0.0059.
Values may be sent and summed in bfloat16 or wider, within the bound.
No kernel may reach another device: no remote copies, remote signals or barrier semaphores. Data moves between devices by JAX's collectives and lax.ppermute only.
A program may use at most 256 MiB of HBM per device.

v0:
```python
import jax
import jax.numpy as jnp
from jax import lax
from jax.sharding import PartitionSpec as P


def pack_table(doc_lengths, count):
    lengths = doc_lengths[0]
    ends = jnp.cumsum(lengths)
    starts = ends - lengths
    position = jnp.arange(count, dtype=jnp.int32)[:, None]
    inside = (position >= starts[None, :]) & (position < ends[None, :])
    return inside.astype(jnp.bfloat16)


def doc_outer(member, grad_rows, inputs):
    count = member.shape[0]
    weighted = (member[:, :, None] * grad_rows[:, None, :]).reshape(count, -1)
    table = lax.dot_general(
        weighted, inputs, (((0,), (0,)), ((), ())), preferred_element_type=jnp.float32
    )
    return table.reshape(member.shape[1], grad_rows.shape[1] * inputs.shape[1])


def contract_right(left, right):
    return lax.dot_general(
        left, right, (((1,), (1,)), ((), ())), preferred_element_type=jnp.float32
    )


def per_device(
    layer_input,
    gate_act,
    up_act,
    out_grad,
    w_gate,
    w_up,
    w_down,
    proj_x,
    proj_u,
    proj_h,
    proj_g,
    doc_lengths,
):
    full_grad = lax.all_gather(out_grad, "tensor", axis=1, tiled=True)
    gate_wide = gate_act.astype(jnp.float32)
    up_wide = up_act.astype(jnp.float32)
    sigma = jax.nn.sigmoid(gate_wide)
    swish = gate_wide * sigma
    hidden = (swish * up_wide).astype(jnp.bfloat16)
    hidden_grad = contract_right(full_grad, w_down)
    up_grad = (hidden_grad * swish).astype(jnp.bfloat16)
    gate_grad = (hidden_grad * up_wide * sigma * (1.0 + gate_wide * (1.0 - sigma))).astype(
        jnp.bfloat16
    )
    pieces = lax.all_gather((w_gate, w_up), "dp", axis=0, tiled=True)
    partial_grad = contract_right(gate_grad, pieces[0]) + contract_right(up_grad, pieces[1])
    input_grad = lax.psum_scatter(partial_grad, "tensor", scatter_dimension=1, tiled=True).astype(
        jnp.bfloat16
    )
    in_up_part = jnp.dot(layer_input, proj_x, preferred_element_type=jnp.float32)
    up_out_part = jnp.dot(up_grad, proj_u, preferred_element_type=jnp.float32)
    in_down_part = jnp.dot(hidden, proj_h, preferred_element_type=jnp.float32)
    out_down_part = jnp.dot(out_grad, proj_g, preferred_element_type=jnp.float32)
    token_count = layer_input.shape[0]
    member_all = pack_table(doc_lengths, token_count)
    in_up, up_out, in_down, out_down = lax.psum(
        (in_up_part, up_out_part, in_down_part, out_down_part), "tensor"
    )
    in_up = in_up.astype(jnp.bfloat16)
    up_out = up_out.astype(jnp.bfloat16)
    in_down = in_down.astype(jnp.bfloat16)
    out_down = out_down.astype(jnp.bfloat16)
    share = up_out.shape[1] // lax.axis_size("tensor")
    first = lax.axis_index("tensor") * share
    up_log = doc_outer(member_all, lax.dynamic_slice_in_dim(up_out, first, share, 1), in_up)
    down_log = doc_outer(member_all, lax.dynamic_slice_in_dim(out_down, first, share, 1), in_down)
    doc_logs = jnp.stack([up_log, down_log], axis=1)
    return (input_grad, doc_logs)


def solution(mesh):
    placed = (
        P(("groups", "dp"), "tensor"),
        P(("groups", "dp"), "tensor"),
        P(("groups", "dp"), "tensor"),
        P(("groups", "dp"), "tensor"),
        P("dp", "tensor"),
        P("dp", "tensor"),
        P("tensor", None),
        P("tensor", None),
        P("tensor", None),
        P("tensor", None),
        P("tensor", None),
        P(("groups", "dp"), None),
    )
    return jax.shard_map(
        per_device,
        mesh=mesh,
        in_specs=placed,
        out_specs=(P(("groups", "dp"), "tensor"), P(("groups", "dp"), None, "tensor")),
        check_vma=False,
    )
```

profile of v0, /device:TPU:3, one launch (start us, length us, event | category | flops | bytes accessed | tf_op | source)
XLA Modules:
  0.0 653.2 jit_solution(10867425171072713748)
XLA Ops:
  7.2 0.7 all-gather.4.cloned.1.call-update
  8.0 0.7 all-gather.6.cloned.1.call-update
  8.7 0.7 all-gather.8.cloned.1.call-update
  9.4 82.2 %all-gather.4.cloned.1.call-done = bf16[512,4096]{1,0:T(8,128)(2,1)} async-done(((bf16[512,1024]{1,0:T(8,128)(2,1)}), bf16[512,4096]{1,0:T(8,128)(2,1)}) %all-gather.4.cloned.1.call-update) | async-done | bytes 4194320 | tf_op jit(solution)/shard_map/all_gather | solution.py:45
  91.6 25.8 %multiply_convert_fusion = (bf16[512,3584]{1,0:T(8,128)(2,1)}, f32[512,3584]{1,0:T(8,128)}) fusion(bf16[512,3584]{1,0:T(8,128)(2,1)} %param.13, bf16[512,4096]{1,0:T(8,128)(2,1)} %all-gather.4.cloned.1.call-done, bf16[3584,4096]{1,0:T(8,128)(2,1)} %param.18), kind=kOutput, calls=%fused_computation.13 | convolution fusion | flops 15045230592 | bytes 48234496 | tf_op jit(solution)/shard_map/dot_general | solution.py:26
  117.5 151.6 %all-gather.6.cloned.1.call-done = bf16[4096,3584]{1,0:T(8,128)(2,1)} async-done(((bf16[1024,3584]{1,0:T(8,128)(2,1)}), bf16[4096,3584]{1,0:T(8,128)(2,1)}) %all-gather.6.cloned.1.call-update) | async-done | bytes 29360144 | tf_op jit(solution)/shard_map/all_gather | solution.py:56
  269.0 30.2 %fusion.10 = f32[512,4096]{1,0:T(8,128)} fusion(bf16[4096,3584]{1,0:T(8,128)(2,1)} %all-gather.6.cloned.1.call-done, f32[512,3584]{1,0:T(8,128)} %get-tuple-element.11, bf16[512,3584]{1,0:T(8,128)(2,1)} %param.14, bf16[512,3584]{1,0:T(8,128)(2,1)} %param.13), kind=kOutput, calls=%fused_computation.16 | convolution fusion | flops 15054405632 | bytes 52428800 | tf_op jit(solution)/shard_map/dot_general | solution.py:26
  299.2 149.5 %all-gather.8.cloned.1.call-done = bf16[4096,3584]{1,0:T(8,128)(2,1)} async-done(((bf16[1024,3584]{1,0:T(8,128)(2,1)}), bf16[4096,3584]{1,0:T(8,128)(2,1)}) %all-gather.8.cloned.1.call-update) | async-done | bytes 29360144 | tf_op jit(solution)/shard_map/all_gather | solution.py:56
  448.6 25.0 %convolution_add_fusion = f32[512,4096]{1,0:T(8,128)} fusion(f32[512,4096]{1,0:T(8,128)} %fusion.10, bf16[512,3584]{1,0:T(8,128)(2,1)} %get-tuple-element.10, bf16[4096,3584]{1,0:T(8,128)(2,1)} %all-gather.8.cloned.1.call-done), kind=kOutput, calls=%fused_computation.14 | convolution fusion | flops 15034482688 | bytes 49807360 | tf_op jit(solution)/shard_map/dot_general | solution.py:26
  473.6 1.2 copy-done.1
  474.8 0.4 fusion.24
  475.3 4.5 fusion.8
  479.8 0.4 fusion.23
  480.3 0.2 reduce-window.4
  480.5 0.1 fusion.18
  480.5 3.9 fusion.22
  484.4 63.5 %all-reduce.2 = (bf16[512,64]{0,1:T(8,128)(2,1)S(1)}, bf16[512,64]{1,0:T(8,128)(2,1)S(1)}, bf16[512,64]{0,1:T(8,128)(2,1)S(1)}, bf16[512,64]{1,0:T(8,128)(2,1)S(1)}) all-reduce(f32[512,64]{0,1:T(8,128)S(1)} %fusion.24, f32[512,64]{1,0:T(8,128)S(1)} %fusion.8, ...), channel_id=1, replica_groups=mesh['groups'=2,'tensor'=4,'dp'=4] {'tensor'}, use_global_device_ids=true, to_apply=%region_4.5 | all-reduce | flops 131072 | bytes 786432 | tf_op jit(solution)/shard_map/psum | solution.py:67
  547.9 0.2 fusion.25
  548.1 0.1 stack_reshape.7
  548.2 0.2 fusion.26
  548.4 0.1 stack_reshape.6
  548.5 0.7 copy.18
  549.2 94.8 %reduce-scatter.2.cloned.1.call-done = f32[512,1024]{1,0:T(8,128)} async-done(((f32[512,4096]{1,0:T(8,128)}), f32[512,1024]{1,0:T(8,128)}) %reduce-scatter.2.cloned.1.call-update) | async-done | bytes 2097168 | tf_op jit(solution)/shard_map/reduce_scatter | solution.py:58
  643.9 2.7 convert_element_type.41
  (22 shorter events, 0.3 us)
Async XLA Ops:
  7.2 472.7 %copy-start = (bf16[512,1024]{1,0:T(8,128)(2,1)S(1)}, bf16[512,1024]{1,0:T(8,128)(2,1)}, u32[]{:S(2)}) copy-start(bf16[512,1024]{1,0:T(8,128)(2,1)} %param.12) | copy-start | bytes 3145732
  7.2 84.4 %all-gather.4.cloned.1.call-start = ((), (), s32[]{:S(2)}) async-start(), calls=%async_computation.1 | async-start | bytes 5242880 | tf_op jit(solution)/shard_map/all_gather | solution.py:45
  7.9 261.1 %all-gather.6.cloned.1.call-start = ((), (), s32[]{:S(2)}) async-start(), calls=%async_computation.2 | async-start | bytes 36700160 | tf_op jit(solution)/shard_map/all_gather | solution.py:56
  8.7 440.0 %all-gather.8.cloned.1.call-start = ((), (), s32[]{:S(2)}) async-start(), calls=%async_computation.3 | async-start | bytes 36700160 | tf_op jit(solution)/shard_map/all_gather | solution.py:56
  9.4 634.5 %reduce-scatter.2.cloned.1.call-start = ((), (), s32[]{:S(2)}) async-start(), calls=%async_computation.4 | async-start | bytes 10485760 | tf_op jit(solution)/shard_map/reduce_scatter | solution.py:58
  473.6 1.2 copy-start.1
  473.6 1.2 copy-start.3
  473.6 1.7 copy-start.5
  475.3 4.5 copy-start.4
  475.3 5.0 copy-start.6
  475.3 5.2 copy-start.2
Sparse Core Ops, SparseCore 0:
  9.6 81.9 all-gather.3
  93.2 175.7 all-gather.5
  270.6 177.9 all-gather.7
  473.8 170.1 reduce-scatter.1
where the time goes:
time: 655 us; the launch traced here: 653 us
  waiting for transfers between devices  480 us (73%)
  matrix products  90.5 us (14%)
  blocking collectives  63.5 us (10%)
  between operations  13.9 us (2%)
    all_gather x2, waiting for transfers between devices, per_device(): pieces = lax.all_gather((w_gate, w_up), 'dp', axis=0, tiled=True)  301 us
    reduce_scatter x1, waiting for transfers between devices, per_device(): lax.psum_scatter(partial_grad, 'tensor', scatter_dimension=1, tiled=True)  94.8 us
    all_gather x1, waiting for transfers between devices, per_device(): full_grad = lax.all_gather(out_grad, 'tensor', axis=1, tiled=True)  82.2 us
    dot_general x3, matrix products, contract_right(): lax.dot_general(left, right, (((1,), (1,)), ((), ())), preferred_element_...  81 us
    psum x1, blocking collectives, per_device(): lax.psum((in_up_part, up_out_part, in_down_part, out_down_part), 'tensor')  63.5 us
  transfers between devices with their start and end apart: 4, of which 4 were waited for; matrix products, arithmetic and copies ran while one was open for 10% of the time, Pallas kernels for 0%

commit v1 on v0

v1 whole, which is shorter than its diff:
```python
import jax
import jax.numpy as jnp
from jax import lax
from jax.sharding import PartitionSpec as P

CORES = 2
CHUNKS = 4


def contract_right(left, right):
    return lax.dot_general(
        left, right, (((1,), (1,)), ((), ())), preferred_element_type=jnp.float32
    )


def project(proj, rows):
    return lax.dot_general(
        proj, rows, (((0,), (1,)), ((), ())), preferred_element_type=jnp.float32
    )


def pack_table(doc_lengths, count):
    lengths = doc_lengths[0]
    ends = jnp.cumsum(lengths)
    starts = ends - lengths
    position = jnp.arange(count, dtype=jnp.int32)[None, :]
    inside = (position >= starts[:, None]) & (position < ends[:, None])
    return inside.astype(jnp.bfloat16)


def doc_outer(member, grad_rows, inputs):
    count = member.shape[1]
    weighted = (member[:, None, :] * grad_rows[None, :, :]).reshape(-1, count)
    table = contract_right(weighted, inputs)
    return table.reshape(member.shape[0], grad_rows.shape[0] * inputs.shape[0])


def swap_cores(value):
    size = lax.axis_size("dp")
    return lax.ppermute(value, "dp", [(i, i ^ 1) for i in range(size)])


def from_chip(value, shift):
    size = lax.axis_size("dp")
    step = shift * CORES
    return lax.ppermute(value, "dp", [((i + step) % size, i) for i in range(size)])


def from_group(value, shift):
    size = lax.axis_size("groups")
    return lax.ppermute(value, "groups", [((i + shift) % size, i) for i in range(size)])


def to_rank(value, shift):
    size = lax.axis_size("tensor")
    return lax.ppermute(value, "tensor", [(i, (i + shift) % size) for i in range(size)])


def per_device(
    layer_input,
    gate_act,
    up_act,
    out_grad,
    w_gate,
    w_up,
    w_down,
    proj_x,
    proj_u,
    proj_h,
    proj_g,
    doc_lengths,
):
    groups, ranks = lax.axis_size("groups"), lax.axis_size("tensor")
    blocks = lax.axis_size("dp")
    chips = blocks // CORES
    group, rank = lax.axis_index("groups"), lax.axis_index("tensor")
    place = lax.axis_index("dp")
    chip, core = place // CORES, place % CORES
    rows = w_gate.shape[0]
    part = rows // groups
    piece = part // CHUNKS
    units = blocks * groups
    per_rank = units // ranks

    def share(k):
        first = group * part + k * piece
        return jnp.concatenate(
            [
                lax.dynamic_slice_in_dim(w_gate, first, piece, 0),
                lax.dynamic_slice_in_dim(w_up, first, piece, 0),
            ],
            axis=1,
        )

    partner_gate, partner_up = swap_cores(w_gate), swap_cores(w_up)
    fetched = {}
    for k in range(CHUNKS):
        mine = share(k)
        for s in range(1, chips):
            first_hand = from_chip(mine, s)
            for r in range(groups):
                got = first_hand if r == 0 else from_group(first_hand, r)
                fetched[k, s, 0, r] = got
                fetched[k, s, 1, r] = swap_cores(got)

    full_grad = lax.all_gather(out_grad, "tensor", axis=1, tiled=True)
    gate_wide = gate_act.astype(jnp.float32)
    up_wide = up_act.astype(jnp.float32)
    sigma = jax.nn.sigmoid(gate_wide)
    swish = gate_wide * sigma
    hidden = (swish * up_wide).astype(jnp.bfloat16)
    hidden_grad = contract_right(full_grad, w_down)
    up_grad = (hidden_grad * swish).astype(jnp.bfloat16)
    gate_grad = (hidden_grad * up_wide * sigma * (1.0 + gate_wide * (1.0 - sigma))).astype(
        jnp.bfloat16
    )
    grads = jnp.concatenate([gate_grad, up_grad], axis=1)

    in_up_part = project(proj_x, layer_input)
    up_out_part = project(proj_u, up_grad)
    in_down_part = project(proj_h, hidden)
    out_down_part = project(proj_g, out_grad)
    slot = up_out_part.shape[0] // ranks

    def factors_for(other):
        return jnp.concatenate(
            [
                in_up_part,
                in_down_part,
                lax.dynamic_slice_in_dim(out_down_part, other * slot, slot, 0),
                lax.dynamic_slice_in_dim(up_out_part, other * slot, slot, 0),
            ],
            axis=0,
        )

    factors = factors_for(rank)
    for t in range(1, ranks):
        factors = factors + to_rank(factors_for((rank + t) % ranks), t)
    factors = factors.astype(jnp.bfloat16)
    width = in_up_part.shape[0]
    in_up, in_down = factors[:width], factors[width : 2 * width]
    out_down, up_out = factors[2 * width : 2 * width + slot], factors[2 * width + slot :]
    member = pack_table(doc_lengths, layer_input.shape[0])
    doc_logs = jnp.stack(
        [doc_outer(member, up_out, in_up), doc_outer(member, out_down, in_down)], axis=1
    )

    def by_unit(table):
        table = table.astype(jnp.bfloat16).reshape(table.shape[0], groups, CHUNKS, piece)
        return jnp.roll(table, -group, axis=1)

    near = [
        by_unit(contract_right(gate_grad, w_gate) + contract_right(up_grad, w_up)),
        by_unit(contract_right(gate_grad, partner_gate) + contract_right(up_grad, partner_up)),
    ]

    def position(unit):
        block, at = unit // groups, unit % groups
        away = (block // CORES - chip) % chips
        return (away * CORES + (block % CORES) ^ core) * groups + (at - group) % groups

    results = []
    for k in range(CHUNKS):
        terms = []
        for s in range(chips):
            for c in range(CORES):
                for r in range(groups):
                    if s == 0:
                        terms.append(near[c][:, r, k])
                    else:
                        terms.append(
                            contract_right(grads, fetched[k, s, c, r]).astype(jnp.bfloat16)
                        )
        terms = jnp.stack(terms)

        def terms_for(other):
            return jnp.stack(
                [
                    lax.dynamic_index_in_dim(
                        terms, position(other * per_rank + j), 0, keepdims=False
                    )
                    for j in range(per_rank)
                ]
            )

        total = terms_for(rank).astype(jnp.float32)
        for t in range(1, ranks):
            total = total + to_rank(terms_for((rank + t) % ranks), t).astype(jnp.float32)
        results.append(total.astype(jnp.bfloat16))
    input_grad = jnp.stack(results).transpose(2, 1, 0, 3).reshape(layer_input.shape[0], -1)
    return (input_grad, doc_logs)


def solution(mesh):
    placed = (
        P(("groups", "dp"), "tensor"),
        P(("groups", "dp"), "tensor"),
        P(("groups", "dp"), "tensor"),
        P(("groups", "dp"), "tensor"),
        P("dp", "tensor"),
        P("dp", "tensor"),
        P("tensor", None),
        P("tensor", None),
        P("tensor", None),
        P("tensor", None),
        P("tensor", None),
        P(("groups", "dp"), None),
    )
    return jax.shard_map(
        per_device,
        mesh=mesh,
        in_specs=placed,
        out_specs=(P(("groups", "dp"), "tensor"), P(("groups", "dp"), None, "tensor")),
        check_vma=False,
    )
```

time: 655 us -> 443 us (0.68)
  waiting for transfers between devices: 480 us -> 219 us
  blocking collectives: 63.5 us -> 0 us
  starting transfers between devices: 0.15 us -> 57.5 us
  matrix products: 90.5 us -> 121 us
  local copies, waits for them, and re-layouts: 2.08 us -> 17 us
  other arithmetic: 3.02 us -> 9.85 us
    all_gather x2 -> x0, waiting for transfers between devices: 301 us -> none  [per_device(): pieces = lax.all_gather((w_gate, w_up), 'dp', axis=0, tiled=True)]
    ppermute x0 -> x33, waiting for transfers between devices: none -> 155 us  [the longest x15 68.7 us: to_rank(): lax.ppermute(value, 'tensor', [(i, (i + shift) % size) for i in range(siz...]
    reduce_scatter x1 -> x0, waiting for transfers between devices: 94.8 us -> none  [per_device(): lax.psum_scatter(partial_grad, 'tensor', scatter_dimension=1, tiled=True)]
    psum x1 -> x0, blocking collectives: 63.5 us -> none  [per_device(): lax.psum((in_up_part, up_out_part, in_down_part, out_down_part), 'tensor')]
    ppermute x0 -> x33, starting transfers between devices: none -> 57.4 us  [the longest x15 29.7 us: to_rank(): lax.ppermute(value, 'tensor', [(i, (i + shift) % size) for i in range(siz...]
    dot_general x3 -> x23, matrix products: 81 us -> 114 us  [contract_right(): lax.dot_general(left, right, (((1,), (1,)), ((), ())), preferred_element_...]
    all_gather x1, waiting for transfers between devices: 82.2 us -> 63.4 us  [per_device(): full_grad = lax.all_gather(out_grad, 'tensor', axis=1, tiled=True)]
    concatenate x0 -> x7, other arithmetic: none -> 8.42 us  [the longest x4 7.54 us: share(): jnp.concatenate([lax.dynamic_slice_in_dim(w_gate, first, piece, 0), lax.d...]
  transfers between devices with their start and end apart: 4 -> 34, of which waited for: 4 -> 11; matrix products, arithmetic and copies ran while one was open for 10% -> 33% of each run, Pallas kernels for 0% -> 0%
where the time goes in v1:
time: 443 us; the launch traced here: 439 us
  waiting for transfers between devices  219 us (49%)
  matrix products  121 us (27%)
  starting transfers between devices  57.5 us (13%)
  local copies, waits for them, and re-layouts  17 us (4%)
  between operations  14.8 us (3%)
  other arithmetic  9.85 us (2%)
    dot_general x23, matrix products, contract_right(): lax.dot_general(left, right, (((1,), (1,)), ((), ())), preferred_element_...  114 us
    ppermute x15, waiting for transfers between devices, to_rank(): lax.ppermute(value, 'tensor', [(i, (i + shift) % size) for i in range(siz...  68.7 us
    all_gather x1, waiting for transfers between devices, per_device(): full_grad = lax.all_gather(out_grad, 'tensor', axis=1, tiled=True)  63.4 us
    ppermute x4, waiting for transfers between devices, from_group(): lax.ppermute(value, 'groups', [((i + shift) % size, i) for i in range(siz...  50 us
    ppermute x4, waiting for transfers between devices, from_chip(): lax.ppermute(value, 'dp', [((i + step) % size, i) for i in range(size)])  36.4 us
    ppermute x15, starting transfers between devices, to_rank(): lax.ppermute(value, 'tensor', [(i, (i + shift) % size) for i in range(siz...  29.7 us
    ppermute x10, starting transfers between devices, swap_cores(): return lax.ppermute(value, 'dp', [(i, i ^ 1) for i in range(size)])  22.1 us
  transfers between devices with their start and end apart: 34, of which 11 were waited for; matrix products, arithmetic and copies ran while one was open for 33% of the time, Pallas kernels for 0%

profile of v1, /device:TPU:3, one launch (start us, length us, event | category | flops | bytes accessed | tf_op | source)
XLA Modules:
  0.0 439.1 jit_solution(5194055320937326638)
XLA Ops:
  28.2 63.4 %all-gather.2.cloned.1.call-done = bf16[512,4096]{1,0:T(8,128)(2,1)} async-done(((bf16[512,1024]{1,0:T(8,128)(2,1)}), bf16[512,4096]{1,0:T(8,128)(2,1)}) %all-gather.2.cloned.1.call-update) | async-done | bytes 4194320 | tf_op jit(solution)/shard_map/all_gather | solution.py:106
  91.6 26.6 %multiply_convert_fusion = (bf16[512,3584]{1,0:T(8,128)(2,1)}, bf16[512,3584]{1,0:T(8,128)(2,1)}) fusion(bf16[512,3584]{1,0:T(8,128)(2,1)} %param.15, bf16[512,3584]{1,0:T(8,128)(2,1)} %param.16, bf16[512,4096]{1,0:T(8,128)(2,1)} %all-gather.2.cloned.1.call-done, bf16[3584,4096]{1,0:T(8,128)(2,1)} %param.20), kind=kOutput, calls=%fused_computation.14 | convolution fusion | flops 15059910656 | bytes 48234496 | tf_op jit(solution)/shard_map/dot_general | solution.py:11
  118.2 7.5 %fusion.78 = f32[512,1024]{1,0:T(8,128)S(1)} fusion(bf16[512,3584]{1,0:T(8,128)(2,1)} %get-tuple-element.6, bf16[1024,3584]{1,0:T(8,128)(2,1)} %param.18), kind=kOutput, calls=%fused_computation.200 | convolution fusion | flops 3758096384 | bytes 13107200 | tf_op jit(solution)/shard_map/dot_general | solution.py:11
  125.8 7.1 %add_convert_fusion.1 = bf16[512,1024]{1,0:T(8,128)(2,1)S(1)} fusion(f32[512,1024]{1,0:T(8,128)S(1)} %fusion.78, bf16[512,3584]{1,0:T(8,128)(2,1)S(1)} %copy-done.3, bf16[1024,3584]{1,0:T(8,128)(2,1)} %param.19), kind=kOutput, calls=%fused_computation.21 | convolution fusion | flops 3759144960 | bytes 14155776 | tf_op jit(solution)/shard_map/dot_general | solution.py:11
  141.0 5.0 %collective-permute-done.32 = f32[160,512]{1,0:T(8,128)S(1)} collective-permute-done((f32[160,512]{1,0:T(8,128)S(1)}, f32[160,512]{1,0:T(8,128)S(1)}, u32[]{:S(2)}, u32[]{:S(2)}) %collective-permute-start.32) | collective-permute-done | bytes 327712 | tf_op jit(solution)/shard_map/ppermute | solution.py:56
  146.3 19.7 %collective-permute-done.31 = f32[160,512]{1,0:T(8,128)S(1)} collective-permute-done((f32[160,512]{1,0:T(8,128)S(1)}, f32[160,512]{1,0:T(8,128)S(1)}, u32[]{:S(2)}, u32[]{:S(2)}) %collective-permute-start.31) | collective-permute-done | bytes 327712 | tf_op jit(solution)/shard_map/ppermute | solution.py:56
  170.0 7.6 %fusion.79 = f32[512,1024]{1,0:T(8,128)S(1)} fusion(bf16[512,3584]{1,0:T(8,128)(2,1)} %get-tuple-element.5, bf16[1024,3584]{1,0:T(8,128)(2,1)} %collective-permute-done.1), kind=kOutput, calls=%fused_computation.201 | convolution fusion | flops 3758096384 | bytes 13107200 | tf_op jit(solution)/shard_map/dot_general | solution.py:11
  177.6 8.3 %collective-permute-done.16 = bf16[128,7168]{1,0:T(8,128)(2,1)} collective-permute-done((bf16[128,7168]{1,0:T(8,128)(2,1)}, bf16[128,7168]{1,0:T(8,128)(2,1)}, u32[]{:S(2)}, u32[]{:S(2)}) %collective-permute-start.16) | collective-permute-done | bytes 1835040 | tf_op jit(solution)/shard_map/ppermute | solution.py:46
  185.9 5.3 %collective-permute-start.25 = (bf16[128,7168]{1,0:T(8,128)(2,1)}, bf16[128,7168]{1,0:T(8,128)(2,1)}, u32[]{:S(2)}, u32[]{:S(2)}) collective-permute-start(bf16[128,7168]{1,0:T(8,128)(2,1)} %collective-permute-done.23), channel_id=1, source_target_pairs={{0,1},{1,0},{2,3},{3,2},{4,5},{5,4},{6,7},{7,6},{8,9},{9,8},{10,11... | collective-permute-start | bytes 5505032 | tf_op jit(solution)/shard_map/ppermute | solution.py:40
  191.2 15.4 %collective-permute-done.24 = bf16[128,7168]{1,0:T(8,128)(2,1)} collective-permute-done((bf16[128,7168]{1,0:T(8,128)(2,1)}, bf16[128,7168]{1,0:T(8,128)(2,1)}, u32[]{:S(2)}, u32[]{:S(2)}) %collective-permute-start.24) | collective-permute-done | bytes 1835040 | tf_op jit(solution)/shard_map/ppermute | solution.py:51
  210.5 7.1 %add_convert_fusion = bf16[512,1024]{1,0:T(8,128)(2,1)S(1)} fusion(f32[512,1024]{1,0:T(8,128)S(1)} %fusion.79, bf16[512,3584]{1,0:T(8,128)(2,1)S(1)} %copy-done.19, bf16[1024,3584]{1,0:T(8,128)(2,1)} %collective-permute-done), kind=kOutput, calls=%fused_computation.20 | convolution fusion | flops 3759144960 | bytes 14155776 | tf_op jit(solution)/shard_map/dot_general | solution.py:11
  220.8 5.9 %fusion.35 = bf16[8,512,128]{1,2,0:T(8,128)(2,1)} fusion(bf16[8,512,128]{1,2,0:T(8,128)(2,1)} %fusion.54, bf16[128,7168]{1,0:T(8,128)(2,1)} %collective-permute-done.23, bf16[512,3584]{1,0:T(8,128)(2,1)S(1)} %copy-done.4, bf16[512,3584]{1,0:T(8,128)(2,1)} %get-tuple-element.6), kind=kOutput, calls=%fused_computation.67 | convolution fusion | flops 954269696 | bytes 9306112 | tf_op jit(solution)/shard_map/dot_general | solution.py:11
  226.7 4.6 %fusion.37 = bf16[8,512,128]{1,2,0:T(8,128)(2,1)} fusion(bf16[8,512,128]{1,2,0:T(8,128)(2,1)} %fusion.35, bf16[128,7168]{1,0:T(8,128)(2,1)} %collective-permute-done.24, bf16[512,3584]{1,0:T(8,128)(2,1)S(1)} %copy-done.4, bf16[512,3584]{1,0:T(8,128)(2,1)S(1)} %copy-done.20), kind=kOutput, calls=%fused_computation.69 | convolution fusion | flops 954269696 | bytes 9306112 | tf_op jit(solution)/shard_map/dot_general | solution.py:11
  231.7 4.6 %fusion.39 = bf16[8,512,128]{1,2,0:T(8,128)(2,1)} fusion(bf16[8,512,128]{1,2,0:T(8,128)(2,1)} %fusion.37, bf16[128,7168]{1,0:T(8,128)(2,1)} %collective-permute-done.25, bf16[512,3584]{1,0:T(8,128)(2,1)S(1)} %copy-done.4, bf16[512,3584]{1,0:T(8,128)(2,1)S(1)} %copy-done.20), kind=kOutput, calls=%fused_computation.71 | convolution fusion | flops 954269696 | bytes 9306112 | tf_op jit(solution)/shard_map/dot_general | solution.py:11
  236.4 28.2 %collective-permute-done.2 = bf16[128,7168]{1,0:T(8,128)(2,1)} collective-permute-done((bf16[128,7168]{1,0:T(8,128)(2,1)}, bf16[128,7168]{1,0:T(8,128)(2,1)}, u32[]{:S(2)}, u32[]{:S(2)}) %collective-permute-start.2) | collective-permute-done | bytes 1835040 | tf_op jit(solution)/shard_map/ppermute | solution.py:46
  268.9 4.6 %fusion.41 = bf16[8,512,128]{1,2,0:T(8,128)(2,1)} fusion(bf16[8,512,128]{1,2,0:T(8,128)(2,1)} %fusion.39, bf16[128,7168]{1,0:T(8,128)(2,1)} %collective-permute-done.26, bf16[512,3584]{1,0:T(8,128)(2,1)S(1)} %copy-done.4, bf16[512,3584]{1,0:T(8,128)(2,1)S(1)} %copy-done.20), kind=kOutput, calls=%fused_computation.73 | convolution fusion | flops 954269696 | bytes 9306112 | tf_op jit(solution)/shard_map/dot_general | solution.py:11
  285.1 6.4 %collective-permute-start.12 = (bf16[128,7168]{1,0:T(8,128)(2,1)S(1)}, bf16[128,7168]{1,0:T(8,128)(2,1)S(1)}, u32[]{:S(2)}, u32[]{:S(2)}) collective-permute-start(bf16[128,7168]{1,0:T(8,128)(2,1)S(1)} %collective-permute-done.10), channel_id=1, source_target_pairs={{0,1},{1,0},{2,3},{3,2},{4,5},{5,4},{6,7},{7,6},{8,9},{9,8},{10,11... | collective-permute-start | bytes 5505032 | tf_op jit(solution)/shard_map/ppermute | solution.py:40
  291.5 32.9 %collective-permute-done.3 = bf16[128,7168]{1,0:T(8,128)(2,1)S(1)} collective-permute-done((bf16[128,7168]{1,0:T(8,128)(2,1)}, bf16[128,7168]{1,0:T(8,128)(2,1)S(1)}, u32[]{:S(2)}, u32[]{:S(2)}) %collective-permute-start.3) | collective-permute-done | bytes 1835040 | tf_op jit(solution)/shard_map/ppermute | solution.py:51
  340.6 4.5 %collective-permute-start.28 = (bf16[2,512,128]{1,2,0:T(8,128)(2,1)S(1)}, bf16[2,512,128]{1,2,0:T(8,128)(2,1)S(1)}, u32[]{:S(2)}, u32[]{:S(2)}) collective-permute-start(bf16[2,512,128]{1,2,0:T(8,128)(2,1)S(1)} %pad_maximum_fusion.19), channel_id=1, source_target_pairs={{0,8},{4,12},{8,0},{12,4},{1,9},{5,13},{9,1},{13,5},{2,10},{6,14},... | collective-permute-start | bytes 786440 | tf_op jit(solution)/shard_map/ppermute | solution.py:56
  352.0 4.0 fusion.11
  369.8 6.9 %collective-permute-start.14 = (bf16[2,512,128]{1,2,0:T(8,128)(2,1)S(1)}, bf16[2,512,128]{1,2,0:T(8,128)(2,1)S(1)}, u32[]{:S(2)}, u32[]{:S(2)}) collective-permute-start(bf16[2,512,128]{1,2,0:T(8,128)(2,1)S(1)} %pad_maximum_fusion.13), channel_id=1, source_target_pairs={{0,8},{4,12},{8,0},{12,4},{1,9},{5,13},{9,1},{13,5},{2,10},{6,14},... | collective-permute-start | bytes 786440 | tf_op jit(solution)/shard_map/ppermute | solution.py:56
  380.2 16.4 %collective-permute-done.21 = bf16[2,512,128]{1,2,0:T(8,128)(2,1)S(1)} collective-permute-done((bf16[2,512,128]{1,2,0:T(8,128)(2,1)S(1)}, bf16[2,512,128]{1,2,0:T(8,128)(2,1)S(1)}, u32[]{:S(2)}, u32[]{:S(2)}) %collective-permute-start.21) | collective-permute-done | bytes 262176 | tf_op jit(solution)/shard_map/ppermute | solution.py:56
  402.7 16.4 %collective-permute-done.14 = bf16[2,512,128]{1,2,0:T(8,128)(2,1)S(1)} collective-permute-done((bf16[2,512,128]{1,2,0:T(8,128)(2,1)S(1)}, bf16[2,512,128]{1,2,0:T(8,128)(2,1)S(1)}, u32[]{:S(2)}, u32[]{:S(2)}) %collective-permute-start.14) | collective-permute-done | bytes 262176 | tf_op jit(solution)/shard_map/ppermute | solution.py:56
  419.3 11.1 %collective-permute-done.7 = bf16[2,512,128]{1,2,0:T(8,128)(2,1)S(1)} collective-permute-done((bf16[2,512,128]{1,2,0:T(8,128)(2,1)S(1)}, bf16[2,512,128]{1,2,0:T(8,128)(2,1)S(1)}, u32[]{:S(2)}, u32[]{:S(2)}) %collective-permute-start.7) | collective-permute-done | bytes 262176 | tf_op jit(solution)/shard_map/ppermute | solution.py:56
  (165 shorter events, 104.6 us)
Async XLA Ops:
  7.2 84.4 %all-gather.2.cloned.1.call-start = ((), (), s32[]{:S(2)}) async-start(), calls=%async_computation | async-start | bytes 5242880 | tf_op jit(solution)/shard_map/all_gather | solution.py:106
  7.9 160.9 %collective-permute-start.1 = (bf16[1024,3584]{1,0:T(8,128)(2,1)}, bf16[1024,3584]{1,0:T(8,128)(2,1)}, u32[]{:S(2)}, u32[]{:S(2)}) collective-permute-start(bf16[1024,3584]{1,0:T(8,128)(2,1)} %param.19), channel_id=1, source_target_pairs={{0,1},{1,0},{2,3},{3,2},{4,5},{5,4},{6,7},{7,6},{8,9},{9,8},{10,11... | collective-permute-start | bytes 22020104 | tf_op jit(solution)/shard_map/ppermute | solution.py:40
  8.7 199.1 %collective-permute-start = (bf16[1024,3584]{1,0:T(8,128)(2,1)}, bf16[1024,3584]{1,0:T(8,128)(2,1)}, u32[]{:S(2)}, u32[]{:S(2)}) collective-permute-start(bf16[1024,3584]{1,0:T(8,128)(2,1)} %param.18), channel_id=1, source_target_pairs={{0,1},{1,0},{2,3},{3,2},{4,5},{5,4},{6,7},{7,6},{8,9},{9,8},{10,11... | collective-permute-start | bytes 22020104 | tf_op jit(solution)/shard_map/ppermute | solution.py:40
  16.6 121.5 %collective-permute-start.23 = (bf16[128,7168]{1,0:T(8,128)(2,1)}, bf16[128,7168]{1,0:T(8,128)(2,1)}, u32[]{:S(2)}, u32[]{:S(2)}) collective-permute-start(bf16[128,7168]{1,0:T(8,128)(2,1)} %pad_maximum_fusion.4), channel_id=1, source_target_pairs={{2,0},{3,1},{0,2},{1,3},{6,4},{7,5},{4,6},{5,7},{10,8},{11,9},{8,1... | collective-permute-start | bytes 5505032 | tf_op jit(solution)/shard_map/ppermute | solution.py:46
  146.0 39.9 %collective-permute-start.16 = (bf16[128,7168]{1,0:T(8,128)(2,1)}, bf16[128,7168]{1,0:T(8,128)(2,1)}, u32[]{:S(2)}, u32[]{:S(2)}) collective-permute-start(bf16[128,7168]{1,0:T(8,128)(2,1)} %pad_maximum_fusion.3), channel_id=1, source_target_pairs={{2,0},{3,1},{0,2},{1,3},{6,4},{7,5},{4,6},{5,7},{10,8},{11,9},{8,1... | collective-permute-start | bytes 5505032 | tf_op jit(solution)/shard_map/ppermute | solution.py:46
  166.0 65.3 %collective-permute-start.9 = (bf16[128,7168]{1,0:T(8,128)(2,1)}, bf16[128,7168]{1,0:T(8,128)(2,1)}, u32[]{:S(2)}, u32[]{:S(2)}) collective-permute-start(bf16[128,7168]{1,0:T(8,128)(2,1)} %pad_maximum_fusion.2), channel_id=1, source_target_pairs={{2,0},{3,1},{0,2},{1,3},{6,4},{7,5},{4,6},{5,7},{10,8},{11,9},{8,1... | collective-permute-start | bytes 5505032 | tf_op jit(solution)/shard_map/ppermute | solution.py:46
  166.3 40.3 %collective-permute-start.24 = (bf16[128,7168]{1,0:T(8,128)(2,1)}, bf16[128,7168]{1,0:T(8,128)(2,1)}, u32[]{:S(2)}, u32[]{:S(2)}) collective-permute-start(bf16[128,7168]{1,0:T(8,128)(2,1)} %collective-permute-done.23), channel_id=1, source_target_pairs={{16,0},{0,16},{17,1},{1,17},{18,2},{2,18},{19,3},{3,19},{20,4},{4,... | collective-permute-start | bytes 5505032 | tf_op jit(solution)/shard_map/ppermute | solution.py:51
  168.9 95.7 %collective-permute-start.2 = (bf16[128,7168]{1,0:T(8,128)(2,1)}, bf16[128,7168]{1,0:T(8,128)(2,1)}, u32[]{:S(2)}, u32[]{:S(2)}) collective-permute-start(bf16[128,7168]{1,0:T(8,128)(2,1)} %pad_maximum_fusion.1), channel_id=1, source_target_pairs={{2,0},{3,1},{0,2},{1,3},{6,4},{7,5},{4,6},{5,7},{10,8},{11,9},{8,1... | collective-permute-start | bytes 5505032 | tf_op jit(solution)/shard_map/ppermute | solution.py:46
  185.9 45.5 %collective-permute-start.25 = (bf16[128,7168]{1,0:T(8,128)(2,1)}, bf16[128,7168]{1,0:T(8,128)(2,1)}, u32[]{:S(2)}, u32[]{:S(2)}) collective-permute-start(bf16[128,7168]{1,0:T(8,128)(2,1)} %collective-permute-done.23), channel_id=1, source_target_pairs={{0,1},{1,0},{2,3},{3,2},{4,5},{5,4},{6,7},{7,6},{8,9},{9,8},{10,11... | collective-permute-start | bytes 5505032 | tf_op jit(solution)/shard_map/ppermute | solution.py:40
  206.6 60.8 %collective-permute-start.17 = (bf16[128,7168]{1,0:T(8,128)(2,1)}, bf16[128,7168]{1,0:T(8,128)(2,1)}, u32[]{:S(2)}, u32[]{:S(2)}) collective-permute-start(bf16[128,7168]{1,0:T(8,128)(2,1)} %collective-permute-done.16), channel_id=1, source_target_pairs={{16,0},{0,16},{17,1},{1,17},{18,2},{2,18},{19,3},{3,19},{20,4},{4,... | collective-permute-start | bytes 5505032 | tf_op jit(solution)/shard_map/ppermute | solution.py:51
  207.7 60.9 %collective-permute-start.26 = (bf16[128,7168]{1,0:T(8,128)(2,1)}, bf16[128,7168]{1,0:T(8,128)(2,1)}, u32[]{:S(2)}, u32[]{:S(2)}) collective-permute-start(bf16[128,7168]{1,0:T(8,128)(2,1)} %collective-permute-done.24), channel_id=1, source_target_pairs={{0,1},{1,0},{2,3},{3,2},{4,5},{5,4},{6,7},{7,6},{8,9},{9,8},{10,11... | collective-permute-start | bytes 5505032 | tf_op jit(solution)/shard_map/ppermute | solution.py:40
  231.3 51.8 %collective-permute-start.18 = (bf16[128,7168]{1,0:T(8,128)(2,1)}, bf16[128,7168]{1,0:T(8,128)(2,1)S(1)}, u32[]{:S(2)}, u32[]{:S(2)}) collective-permute-start(bf16[128,7168]{1,0:T(8,128)(2,1)} %collective-permute-done.16), channel_id=1, source_target_pairs={{0,1},{1,0},{2,3},{3,2},{4,5},{5,4},{6,7},{7,6},{8,9},{9,8},{10,11... | collective-permute-start | bytes 5505032 | tf_op jit(solution)/shard_map/ppermute | solution.py:40
  231.4 53.8 %collective-permute-start.10 = (bf16[128,7168]{1,0:T(8,128)(2,1)}, bf16[128,7168]{1,0:T(8,128)(2,1)S(1)}, u32[]{:S(2)}, u32[]{:S(2)}) collective-permute-start(bf16[128,7168]{1,0:T(8,128)(2,1)} %collective-permute-done.9), channel_id=1, source_target_pairs={{16,0},{0,16},{17,1},{1,17},{18,2},{2,18},{19,3},{3,19},{20,4},{4,... | collective-permute-start | bytes 5505032 | tf_op jit(solution)/shard_map/ppermute | solution.py:51
  264.5 76.0 %collective-permute-start.11 = (bf16[128,7168]{1,0:T(8,128)(2,1)}, bf16[128,7168]{1,0:T(8,128)(2,1)S(1)}, u32[]{:S(2)}, u32[]{:S(2)}) collective-permute-start(bf16[128,7168]{1,0:T(8,128)(2,1)} %collective-permute-done.9), channel_id=1, source_target_pairs={{0,1},{1,0},{2,3},{3,2},{4,5},{5,4},{6,7},{7,6},{8,9},{9,8},{10,11... | collective-permute-start | bytes 5505032 | tf_op jit(solution)/shard_map/ppermute | solution.py:40
  267.4 57.1 %collective-permute-start.3 = (bf16[128,7168]{1,0:T(8,128)(2,1)}, bf16[128,7168]{1,0:T(8,128)(2,1)S(1)}, u32[]{:S(2)}, u32[]{:S(2)}) collective-permute-start(bf16[128,7168]{1,0:T(8,128)(2,1)} %collective-permute-done.2), channel_id=1, source_target_pairs={{16,0},{0,16},{17,1},{1,17},{18,2},{2,18},{19,3},{3,19},{20,4},{4,... | collective-permute-start | bytes 5505032 | tf_op jit(solution)/shard_map/ppermute | solution.py:51
  268.6 61.9 %collective-permute-start.19 = (bf16[128,7168]{1,0:T(8,128)(2,1)}, bf16[128,7168]{1,0:T(8,128)(2,1)S(1)}, u32[]{:S(2)}, u32[]{:S(2)}) collective-permute-start(bf16[128,7168]{1,0:T(8,128)(2,1)} %collective-permute-done.17), channel_id=1, source_target_pairs={{0,1},{1,0},{2,3},{3,2},{4,5},{5,4},{6,7},{7,6},{8,9},{9,8},{10,11... | collective-permute-start | bytes 5505032 | tf_op jit(solution)/shard_map/ppermute | solution.py:40
  283.2 75.5 %collective-permute-start.4 = (bf16[128,7168]{1,0:T(8,128)(2,1)}, bf16[128,7168]{1,0:T(8,128)(2,1)S(1)}, u32[]{:S(2)}, u32[]{:S(2)}) collective-permute-start(bf16[128,7168]{1,0:T(8,128)(2,1)} %collective-permute-done.2), channel_id=1, source_target_pairs={{0,1},{1,0},{2,3},{3,2},{4,5},{5,4},{6,7},{7,6},{8,9},{9,8},{10,11... | collective-permute-start | bytes 5505032 | tf_op jit(solution)/shard_map/ppermute | solution.py:40
  285.1 62.6 %collective-permute-start.12 = (bf16[128,7168]{1,0:T(8,128)(2,1)S(1)}, bf16[128,7168]{1,0:T(8,128)(2,1)S(1)}, u32[]{:S(2)}, u32[]{:S(2)}) collective-permute-start(bf16[128,7168]{1,0:T(8,128)(2,1)S(1)} %collective-permute-done.10), channel_id=1, source_target_pairs={{0,1},{1,0},{2,3},{3,2},{4,5},{5,4},{6,7},{7,6},{8,9},{9,8},{10,11... | collective-permute-start | bytes 5505032 | tf_op jit(solution)/shard_map/ppermute | solution.py:40
  324.5 38.8 %collective-permute-start.5 = (bf16[128,7168]{1,0:T(8,128)(2,1)S(1)}, bf16[128,7168]{1,0:T(8,128)(2,1)S(1)}, u32[]{:S(2)}, u32[]{:S(2)}) collective-permute-start(bf16[128,7168]{1,0:T(8,128)(2,1)S(1)} %collective-permute-done.3), channel_id=1, source_target_pairs={{0,1},{1,0},{2,3},{3,2},{4,5},{5,4},{6,7},{7,6},{8,9},{9,8},{10,11... | collective-permute-start | bytes 5505032 | tf_op jit(solution)/shard_map/ppermute | solution.py:40
  330.5 35.9 %collective-permute-start.29 = (bf16[2,512,128]{1,2,0:T(8,128)(2,1)S(1)}, bf16[2,512,128]{1,2,0:T(8,128)(2,1)S(1)}, u32[]{:S(2)}, u32[]{:S(2)}) collective-permute-start(bf16[2,512,128]{1,2,0:T(8,128)(2,1)S(1)} %pad_maximum_fusion.20), channel_id=1, source_target_pairs={{0,12},{4,0},{8,4},{12,8},{1,13},{5,1},{9,5},{13,9},{2,14},{6,2},{... | collective-permute-start | bytes 786440 | tf_op jit(solution)/shard_map/ppermute | solution.py:56
  363.3 33.3 %collective-permute-start.21 = (bf16[2,512,128]{1,2,0:T(8,128)(2,1)S(1)}, bf16[2,512,128]{1,2,0:T(8,128)(2,1)S(1)}, u32[]{:S(2)}, u32[]{:S(2)}) collective-permute-start(bf16[2,512,128]{1,2,0:T(8,128)(2,1)S(1)} %pad_maximum_fusion.16), channel_id=1, source_target_pairs={{0,8},{4,12},{8,0},{12,4},{1,9},{5,13},{9,1},{13,5},{2,10},{6,14},... | collective-permute-start | bytes 786440 | tf_op jit(solution)/shard_map/ppermute | solution.py:56
  369.8 49.4 %collective-permute-start.14 = (bf16[2,512,128]{1,2,0:T(8,128)(2,1)S(1)}, bf16[2,512,128]{1,2,0:T(8,128)(2,1)S(1)}, u32[]{:S(2)}, u32[]{:S(2)}) collective-permute-start(bf16[2,512,128]{1,2,0:T(8,128)(2,1)S(1)} %pad_maximum_fusion.13), channel_id=1, source_target_pairs={{0,8},{4,12},{8,0},{12,4},{1,9},{5,13},{9,1},{13,5},{2,10},{6,14},... | collective-permute-start | bytes 786440 | tf_op jit(solution)/shard_map/ppermute | solution.py:56
  376.7 42.4 %collective-permute-start.13 = (bf16[2,512,128]{1,2,0:T(8,128)(2,1)S(1)}, bf16[2,512,128]{1,2,0:T(8,128)(2,1)S(1)}, u32[]{:S(2)}, u32[]{:S(2)}) collective-permute-start(bf16[2,512,128]{1,2,0:T(8,128)(2,1)S(1)} %pad_maximum_fusion.12), channel_id=1, source_target_pairs={{0,4},{4,8},{8,12},{12,0},{1,5},{5,9},{9,13},{13,1},{2,6},{6,10},{... | collective-permute-start | bytes 786440 | tf_op jit(solution)/shard_map/ppermute | solution.py:56
  396.7 33.7 %collective-permute-start.7 = (bf16[2,512,128]{1,2,0:T(8,128)(2,1)S(1)}, bf16[2,512,128]{1,2,0:T(8,128)(2,1)S(1)}, u32[]{:S(2)}, u32[]{:S(2)}) collective-permute-start(bf16[2,512,128]{1,2,0:T(8,128)(2,1)S(1)} %pad_maximum_fusion.10), channel_id=1, source_target_pairs={{0,8},{4,12},{8,0},{12,4},{1,9},{5,13},{9,1},{13,5},{2,10},{6,14},... | collective-permute-start | bytes 786440 | tf_op jit(solution)/shard_map/ppermute | solution.py:56
  (31 other events, 373.4 us)
Sparse Core Ops, SparseCore 0:
  9.6 81.9 all-gather.1

commit v2 on v0

v2 whole, which is shorter than its diff:
```python
import functools

import jax
import jax.numpy as jnp
import numpy as np
from jax import lax
from jax.experimental import pallas as pl
from jax.experimental.pallas import tpu as pltpu
from jax.sharding import PartitionSpec as P

CORES = 2
CHUNKS = 8
VMEM_BYTES = 60 * 1024 * 1024
LIGHT = pl.CostEstimate(flops=1, bytes_accessed=1, transcendentals=0)
ANYWHERE = pl.BlockSpec(memory_space=pl.ANY)


def contract_right(left, right):
    return lax.dot_general(
        left, right, (((1,), (1,)), ((), ())), preferred_element_type=jnp.float32
    )


def project(proj, rows):
    return lax.dot_general(
        proj, rows, (((0,), (1,)), ((), ())), preferred_element_type=jnp.float32
    )


def pack_table(doc_lengths, count):
    lengths = doc_lengths[0]
    ends = jnp.cumsum(lengths)
    starts = ends - lengths
    position = jnp.arange(count, dtype=jnp.int32)[None, :]
    inside = (position >= starts[:, None]) & (position < ends[:, None])
    return inside.astype(jnp.bfloat16)


def doc_outer(member, grad_rows, inputs):
    count = member.shape[1]
    weighted = (member[:, None, :] * grad_rows[None, :, :]).reshape(-1, count)
    table = contract_right(weighted, inputs)
    return table.reshape(member.shape[0], grad_rows.shape[0] * inputs.shape[0])


def swap_cores(value):
    size = lax.axis_size("dp")
    return lax.ppermute(value, "dp", [(i, i ^ 1) for i in range(size)])


def from_chip(value, shift):
    size = lax.axis_size("dp")
    step = shift * CORES
    return lax.ppermute(value, "dp", [((i + step) % size, i) for i in range(size)])


def from_group(value, shift):
    size = lax.axis_size("groups")
    return lax.ppermute(value, "groups", [((i + shift) % size, i) for i in range(size)])


def widest(size, options):
    return next((w for w in options if size % w == 0), size)


def share_rows(w_gate, w_up, group, places, piece, part, carried, after):
    width = w_gate.shape[1]
    kept, waits = len(carried), len(after)

    def kernel(group_ref, gate_ref, up_ref, *refs):
        outs = refs[kept + waits + kept : kept + waits + kept + len(places)]
        sems = refs[-1] if places else None
        copies = []
        for at, k in enumerate(places):
            first = pl.multiple_of(group_ref[0] * part + k * piece, piece)
            for half, source in enumerate((gate_ref, up_ref)):
                copies.append(
                    pltpu.make_async_copy(
                        source.at[pl.ds(first, piece), :],
                        outs[at].at[:, pl.ds(half * width, width)],
                        sems.at[2 * at + half],
                    )
                )
        for copy in copies:
            copy.start()
        for copy in copies:
            copy.wait()

    results = pl.pallas_call(
        kernel,
        out_shape=[jax.ShapeDtypeStruct(a.shape, a.dtype) for a in carried]
        + [jax.ShapeDtypeStruct((piece, 2 * width), w_gate.dtype) for _ in places],
        in_specs=[pl.BlockSpec(memory_space=pltpu.SMEM)] + [ANYWHERE] * (2 + kept + waits),
        out_specs=[ANYWHERE] * (kept + len(places)),
        scratch_shapes=[pltpu.SemaphoreType.DMA((2 * len(places),))] if places else [],
        input_output_aliases={3 + i: i for i in range(kept)},
        compiler_params=pltpu.CompilerParams(vmem_limit_bytes=VMEM_BYTES),
        cost_estimate=LIGHT,
        name="share_rows",
    )(group, w_gate, w_up, *carried, *after)
    return list(results[:kept]), list(results[kept:])


def spread_ranks(value):
    ranks = lax.axis_size("tensor")
    below, above = [value], [value]
    for _ in range(1, ranks):
        below.append(lax.ppermute(below[-1], "tensor", [(i, i + 1) for i in range(ranks - 1)]))
        above.append(lax.ppermute(above[-1], "tensor", [(i + 1, i) for i in range(ranks - 1)]))
    return below, above[1:]


def hidden_grads(rank, below, above, w_down, gate_act, up_act, proj_u, after):
    ranks = len(below)
    count, features = below[0].shape
    hidden, depth = w_down.shape
    tile = widest(hidden, (512, 256, 128))
    step = min(tile, 256)
    narrow = proj_u.shape[1]

    def kernel(rank_ref, down_ref, gate_ref, up_ref, proj_ref, *refs):
        both_ref, out_ref, grad_ref, sem = refs[-4:]

        def gather(at, wait):
            block = lax.rem(rank_ref[0] + ranks - at, ranks)
            cols = pl.ds(pl.multiple_of(block * features, features), features)
            for source, valid in (
                (refs[at], rank_ref[0] >= at),
                (refs[ranks + ranks - at - 1] if at else None, rank_ref[0] < at),
            ):
                if source is not None:

                    @pl.when(valid)
                    def _():
                        copy = pltpu.make_async_copy(source, grad_ref.at[:, cols], sem.at[at])
                        copy.wait() if wait else copy.start()

        @pl.when(pl.program_id(0) == 0)
        def _():
            out_ref[...] = jnp.zeros_like(out_ref)
            for at in range(ranks):
                gather(at, False)
            for at in range(ranks):
                gather(at, True)

        for first in range(0, tile, step):
            cols = slice(first, first + step)
            wide = contract_right(grad_ref[...], down_ref[cols, :])
            gate = gate_ref[:, cols].astype(jnp.float32)
            up = up_ref[:, cols].astype(jnp.float32)
            sigma = jax.nn.sigmoid(gate)
            up_grad = (wide * (gate * sigma)).astype(jnp.bfloat16)
            slope = sigma * (1.0 + gate * (1.0 - sigma))
            both_ref[0, :, cols] = (wide * up * slope).astype(jnp.bfloat16)
            both_ref[1, :, cols] = up_grad
            out_ref[...] += jnp.dot(
                up_grad, proj_ref[cols, :], preferred_element_type=jnp.float32
            )

    return pl.pallas_call(
        kernel,
        grid=(hidden // tile,),
        out_shape=[
            jax.ShapeDtypeStruct((2, count, hidden), jnp.bfloat16),
            jax.ShapeDtypeStruct((count, narrow), jnp.float32),
        ],
        in_specs=[
            pl.BlockSpec(memory_space=pltpu.SMEM),
            pl.BlockSpec((tile, depth), lambda i: (i, 0)),
            pl.BlockSpec((count, tile), lambda i: (0, i)),
            pl.BlockSpec((count, tile), lambda i: (0, i)),
            pl.BlockSpec((tile, narrow), lambda i: (i, 0)),
        ]
        + [ANYWHERE] * (2 * ranks - 1 + len(after)),
        out_specs=[
            pl.BlockSpec((2, count, tile), lambda i: (0, 0, i)),
            pl.BlockSpec((count, narrow), lambda i: (0, 0)),
        ],
        scratch_shapes=[
            pltpu.VMEM((count, depth), jnp.bfloat16),
            pltpu.SemaphoreType.DMA((ranks,)),
        ],
        compiler_params=pltpu.CompilerParams(vmem_limit_bytes=VMEM_BYTES),
        cost_estimate=LIGHT,
        name="hidden_grads",
    )(rank, w_down, gate_act, up_act, proj_u, *below, *above, *after)


def weigh(units, grads, after):
    hidden = grads[0].shape[2]
    tile = widest(hidden, (512, 256, 128))
    steps = hidden // tile
    counts = [g.shape[1] for g in grads]
    heights = [u[0].shape[0] for u in units]
    rows, count = sum(heights), sum(counts)

    def kernel(*refs):
        weights = refs[: 2 * len(units)]
        both = refs[2 * len(units) : 2 * len(units) + len(grads)]
        out_ref, total = refs[-2:]
        at = pl.program_id(0)

        @pl.when(at == 0)
        def _():
            total[...] = jnp.zeros_like(total)

        gate = jnp.concatenate([w[...] for w in weights[0::2]], axis=0)
        up = jnp.concatenate([w[...] for w in weights[1::2]], axis=0)
        first = 0
        for ref in both:
            span = slice(first, first + ref.shape[1])
            total[:, span] += contract_right(gate, ref[0]) + contract_right(up, ref[1])
            first += ref.shape[1]

        @pl.when(at == steps - 1)
        def _():
            out_ref[...] = total[...].astype(jnp.bfloat16)

    specs, operands = [], []
    for gate, up, up_at in units:
        specs.append(pl.BlockSpec((gate.shape[0], tile), lambda i: (0, i)))
        specs.append(
            pl.BlockSpec((up.shape[0], tile), functools.partial(lambda o, i: (0, o + i), up_at // tile))
        )
        operands += [gate, up]
    for g in grads:
        specs.append(pl.BlockSpec((2, g.shape[1], tile), lambda i: (0, 0, i)))
        operands.append(g)
    return pl.pallas_call(
        kernel,
        grid=(steps,),
        out_shape=jax.ShapeDtypeStruct((rows, count), jnp.bfloat16),
        in_specs=specs + [ANYWHERE] * len(after),
        out_specs=pl.BlockSpec((rows, count), lambda i: (0, 0)),
        scratch_shapes=[pltpu.VMEM((rows, count), jnp.float32)],
        compiler_params=pltpu.CompilerParams(vmem_limit_bytes=VMEM_BYTES),
        cost_estimate=LIGHT,
        name="weigh_rows",
    )(*operands, *after)


def reduce_to(value, owner):
    groups, ranks, blocks = (lax.axis_size(a) for a in ("groups", "tensor", "dp"))
    bit = 1
    while bit < ranks:
        pairs = []
        for g in range(groups):
            for p in range(blocks):
                target = owner[g, p]
                for z in range(ranks):
                    if z % bit == target % bit and (z ^ target) & bit:
                        pairs.append(((g * ranks + z) * blocks + p, (g * ranks + (z ^ bit)) * blocks + p))
        got = lax.ppermute(value, ("groups", "tensor", "dp"), pairs)
        value = (value.astype(jnp.float32) + got.astype(jnp.float32)).astype(jnp.bfloat16)
        bit *= 2
    return value


def per_device(
    layer_input,
    gate_act,
    up_act,
    out_grad,
    w_gate,
    w_up,
    w_down,
    proj_x,
    proj_u,
    proj_h,
    proj_g,
    doc_lengths,
):
    groups, ranks = lax.axis_size("groups"), lax.axis_size("tensor")
    blocks = lax.axis_size("dp")
    chips = blocks // CORES
    group, rank = lax.axis_index("groups"), lax.axis_index("tensor")
    place = lax.axis_index("dp")
    chip, core = place // CORES, place % CORES
    rows, hidden_width = w_gate.shape
    count = layer_input.shape[0]
    features = out_grad.shape[1]
    part = rows // groups
    piece = part // CHUNKS
    split = max(1, ranks // blocks)
    group_word = jnp.full((1,), group, jnp.int32)
    rank_word = jnp.full((1,), rank, jnp.int32)

    below, above = spread_ranks(out_grad)
    gate_wide = gate_act.astype(jnp.float32)
    hidden = (gate_wide * jax.nn.sigmoid(gate_wide) * up_act.astype(jnp.float32)).astype(jnp.bfloat16)
    early_part = jnp.concatenate(
        [project(proj_x, layer_input), project(proj_h, hidden), project(proj_g, out_grad)], axis=0
    )
    early = lax.all_gather(early_part, "tensor", axis=0, tiled=False)

    _, shares = share_rows(w_gate, w_up, group_word, [0, 1], piece, part, [], [])
    fetched, arriving = {}, {}

    def fetch(k):
        for s in range(1, chips):
            arriving[k, s, 0] = from_chip(shares[k], s)

    def forward(k, after):
        names = [n for n in arriving if n[0] == k and n[2] == 0] + [
            n for n in arriving if n[0] == k - 1 and n[2] > 0
        ]
        places = [k + 2] if k + 2 < CHUNKS else []
        carried, fresh = share_rows(
            w_gate, w_up, group_word, places, piece, part, [arriving.pop(n) for n in names], after
        )
        fetched.update(zip(names, carried))
        shares.extend(fresh)
        if fresh:
            fetch(k + 2)
        for s in range(1, chips):
            for r in range(1, groups):
                arriving[k, s, r] = from_group(fetched[k, s, 0], r)

    def owner_of(s, first_of):
        table = np.zeros((groups, blocks), np.int64)
        for g in range(groups):
            for p in range(blocks):
                block = (p // CORES + s) % chips * CORES + p % CORES
                table[g, p] = (block * rows + first_of(g)) // features
        return table

    near, far = [], {}

    def far_round(names, after):
        sets = {}
        for s in range(1, chips):
            for r in range(groups):
                table = owner_of(s, lambda g: (g + r) % groups * part)
                kept = [(k, s, q) for k, q in names if q == r]
                sets.setdefault((s, table.tobytes()), (table, []))[1].extend(kept)
        outs = []
        for table, kept in sets.values():
            if kept:
                units = [(fetched[n], fetched[n], hidden_width) for n in kept]
                out = weigh(units, [mine, theirs], after)
                outs.append(out)
                total = reduce_to(out, table)
                for at, n in enumerate(kept):
                    far[n] = total[at * piece : (at + 1) * piece]
        return outs

    fetch(0)
    fetch(1)
    forward(0, [])
    forward(1, [])
    forward(2, [])
    forward(3, [])
    mine, up_out_part = hidden_grads(
        rank_word, below, above, w_down, gate_act, up_act, proj_u, [shares[5], early_part]
    )
    late = lax.all_gather(up_out_part, "tensor", axis=0, tiled=False)
    forward(4, [mine])
    theirs = swap_cores(mine)
    height = rows // split
    done = []
    for which, (both, after) in enumerate(((mine, [shares[6]]), (theirs, []))):
        for j in range(split):
            gate_rows = w_gate[j * height : (j + 1) * height]
            up_rows = w_up[j * height : (j + 1) * height]
            out = weigh([(gate_rows, up_rows, 0)], [both], after)
            done.append(out)
            near.append(reduce_to(out, owner_of(0, lambda g: j * height)))
    forward(5, done)
    outs = far_round([(k, 0) for k in range(5)] + [(k, 1) for k in range(4)], [shares[7]])
    forward(6, outs)
    outs = far_round([(5, 0), (6, 0), (4, 1), (5, 1)], [])
    forward(7, outs)

    early = early.sum(axis=0).astype(jnp.bfloat16)
    late = late.sum(axis=0).astype(jnp.bfloat16).T
    width = late.shape[0]
    slot = width // ranks
    in_up, in_down, out_down = early[:width], early[width : 2 * width], early[2 * width :]
    member = pack_table(doc_lengths, count)
    own = lambda table: lax.dynamic_slice_in_dim(table, rank * slot, slot, 0)
    doc_logs = jnp.stack(
        [doc_outer(member, own(late), in_up), doc_outer(member, own(out_down), in_down)], axis=1
    )

    far_round([(7, 0), (6, 1)], [doc_logs])
    for n in list(arriving):
        fetched[n] = arriving.pop(n)
    far_round([(7, 1)], [])

    first = rank * features
    away = (first // rows // CORES - chip) % chips
    owner = first // rows % CORES == core
    inside = first % rows
    tall = features // part

    def pick(index, options):
        value = options[0]
        for at, option in enumerate(options[1:], 1):
            value = jnp.where(index == at, option, value)
        return value

    options = [
        pick(
            inside // height,
            [jnp.concatenate([near[j], near[split + j]], axis=1) for j in range(split)],
        )
    ]
    for s in range(1, chips):
        by_shift = [
            jnp.concatenate([far[k, s, r] for k in range(CHUNKS)], axis=0) for r in range(groups)
        ]
        options.append(
            jnp.concatenate(
                [
                    pick((inside // part + j - group) % groups, by_shift)
                    for j in range(tall)
                ],
                axis=0,
            )
        )
    total = pick(away, options)
    from_partner = swap_cores(total[:, count:])
    input_grad = jnp.where(owner, total[:, :count], from_partner).T
    return (input_grad, doc_logs)


def solution(mesh):
    placed = (
        P(("groups", "dp"), "tensor"),
        P(("groups", "dp"), "tensor"),
        P(("groups", "dp"), "tensor"),
        P(("groups", "dp"), "tensor"),
        P("dp", "tensor"),
        P("dp", "tensor"),
        P("tensor", None),
        P("tensor", None),
        P("tensor", None),
        P("tensor", None),
        P("tensor", None),
        P(("groups", "dp"), None),
    )
    return jax.shard_map(
        per_device,
        mesh=mesh,
        in_specs=placed,
        out_specs=(P(("groups", "dp"), "tensor"), P(("groups", "dp"), None, "tensor")),
        check_vma=False,
    )
```

time: 655 us -> 600 us (0.916)
  waiting for transfers between devices: 480 us -> 75.6 us
  Pallas kernels: 0 us -> 346 us
  starting transfers between devices: 0.15 us -> 90.9 us
  matrix products: 90.5 us -> 9.37 us
  blocking collectives: 63.5 us -> 19.5 us
  other arithmetic: 3.02 us -> 26.4 us
  local copies, waits for them, and re-layouts: 2.08 us -> 15.6 us
    all_gather x3 -> x1, waiting for transfers between devices: 383 us -> 0.01 us  [per_device(): early = lax.all_gather(early_part, 'tensor', axis=0, tiled=False)]
    pallas_call x0 -> x16, Pallas kernels: none -> 346 us  [the longest x9 230 us: share_rows(): pl.pallas_call(kernel, out_shape=[jax.ShapeDtypeStruct(a.shape, a.dtype)...]
    reduce_scatter x1 -> x0, waiting for transfers between devices: 94.8 us -> none  [per_device(): lax.psum_scatter(partial_grad, 'tensor', scatter_dimension=1, tiled=True)]
    ppermute x0 -> x36, starting transfers between devices: none -> 90.8 us  [the longest x2 30.4 us: swap_cores(): return lax.ppermute(value, 'dp', [(i, i ^ 1) for i in range(size)])]
    dot_general x3 -> x2, matrix products: 81 us -> 1.81 us  [contract_right(): lax.dot_general(left, right, (((1,), (1,)), ((), ())), preferred_element_...]
    ppermute x0 -> x36, waiting for transfers between devices: none -> 75.6 us  [the longest x8 37.1 us: from_chip(): lax.ppermute(value, 'dp', [((i + step) % size, i) for i in range(size)])]
    psum x1 -> x0, blocking collectives: 63.5 us -> none  [per_device(): lax.psum((in_up_part, up_out_part, in_down_part, out_down_part), 'tensor')]
    all_gather x0 -> x1, blocking collectives: none -> 19.5 us  [per_device(): late = lax.all_gather(up_out_part, 'tensor', axis=0, tiled=False)]
  transfers between devices with their start and end apart: 4 -> 37, of which waited for: 4 -> 11; matrix products, arithmetic and copies ran while one was open for 10% -> 5% of each run, Pallas kernels for 0% -> 42%
where the time goes in v2:
time: 600 us; the launch traced here: 598 us
  Pallas kernels  346 us (58%)
  starting transfers between devices  90.9 us (15%)
  waiting for transfers between devices  75.6 us (13%)
  other arithmetic  26.4 us (4%)
  blocking collectives  19.5 us (3%)
  local copies, waits for them, and re-layouts  15.6 us (3%)
  between operations  14.6 us (2%)
  matrix products  9.37 us (2%)
    pallas_call x9, Pallas kernels, share_rows(): pl.pallas_call(kernel, out_shape=[jax.ShapeDtypeStruct(a.shape, a.dtype)...  230 us
    pallas_call x6, Pallas kernels, weigh(): pl.pallas_call(kernel, grid=(steps,), out_shape=jax.ShapeDtypeStruct((row...  75.3 us
    pallas_call x1, Pallas kernels, hidden_grads(): pl.pallas_call(kernel, grid=(hidden // tile,), out_shape=[jax.ShapeDtypeS...  40.7 us
    ppermute x8, waiting for transfers between devices, from_chip(): lax.ppermute(value, 'dp', [((i + step) % size, i) for i in range(size)])  37.1 us
    ppermute x8, waiting for transfers between devices, from_group(): lax.ppermute(value, 'groups', [((i + shift) % size, i) for i in range(siz...  30.7 us
    ppermute x2, starting transfers between devices, swap_cores(): return lax.ppermute(value, 'dp', [(i, i ^ 1) for i in range(size)])  30.4 us
    ppermute x12, starting transfers between devices, reduce_to(): got = lax.ppermute(value, ('groups', 'tensor', 'dp'), pairs)  29.5 us
    all_gather x1, blocking collectives, per_device(): late = lax.all_gather(up_out_part, 'tensor', axis=0, tiled=False)  19.5 us
  transfers between devices with their start and end apart: 37, of which 11 were waited for; matrix products, arithmetic and copies ran while one was open for 5% of the time, Pallas kernels for 42%

profile of v2, /device:TPU:3, one launch (start us, length us, event | category | flops | bytes accessed | tf_op | source)
XLA Modules:
  0.0 598.2 jit_solution(15151888083533000532)
XLA Ops:
  7.2 56.7 %share_rows.9 = (bf16[64,7168]{1,0:T(8,128)(2,1)}, bf16[64,7168]{1,0:T(8,128)(2,1)}) custom-call(s32[1]{0:T(128)} %bitcast.group_ref, bf16[1024,3584]{1,0:T(8,128)(2,1)} %gate_ref.19, bf16[1024,3584]{1,0:T(8,128)(2,1)} %up_ref.19), custom_call_target="tpu_custom_call" | custom-call | flops 1 | bytes 1 | tf_op jit(solution)/shard_map/share_rows/pallas_call | solution.py:89
  65.3 5.1 collective-permute-start.9
  71.8 13.7 %collective-permute-done.refs_0_ = bf16[64,7168]{1,0:T(8,128)(2,1)S(1)} collective-permute-done((bf16[64,7168]{1,0:T(8,128)(2,1)}, bf16[64,7168]{1,0:T(8,128)(2,1)S(1)}, u32[]{:S(2)}, u32[]{:S(2)}) %collective-permute-start) | collective-permute-done | bytes 917536 | tf_op jit(solution)/shard_map/ppermute | solution.py:54
  86.5 28.9 %share_rows.10 = (bf16[64,7168]{1,0:T(8,128)(2,1)}, bf16[64,7168]{1,0:T(8,128)(2,1)}) custom-call(s32[1]{0:T(128)} %bitcast.group_ref, bf16[1024,3584]{1,0:T(8,128)(2,1)} %gate_ref.19, bf16[1024,3584]{1,0:T(8,128)(2,1)} %up_ref.19, bf16[64,7168]{1,0:T(8,128)(2,1)} %copy-done.14), custom_call_target="tpu_custom_call", output_to_operand_aliasing={{0}: (3, {})} | custom-call | flops 1 | bytes 1 | tf_op jit(solution)/shard_map/share_rows/pallas_call | solution.py:89
  123.3 11.8 %collective-permute-done.2.refs_1_ = bf16[64,7168]{1,0:T(8,128)(2,1)S(1)} collective-permute-done((bf16[64,7168]{1,0:T(8,128)(2,1)}, bf16[64,7168]{1,0:T(8,128)(2,1)S(1)}, u32[]{:S(2)}, u32[]{:S(2)}) %collective-permute-start.2) | collective-permute-done | bytes 917536 | tf_op jit(solution)/shard_map/ppermute | solution.py:59
  136.0 28.9 %share_rows.11 = (bf16[64,7168]{1,0:T(8,128)(2,1)}, bf16[64,7168]{1,0:T(8,128)(2,1)}, bf16[64,7168]{1,0:T(8,128)(2,1)}) custom-call(s32[1]{0:T(128)} %bitcast.group_ref, bf16[1024,3584]{1,0:T(8,128)(2,1)} %gate_ref.19, bf16[1024,3584]{1,0:T(8,128)(2,1)} %up_ref.19, ...), custom_call_target="tpu_custom_call", output_to_operand_aliasing={{0}: (3, {}), {1}: (4, {})} | custom-call | flops 1 | bytes 1 | tf_op jit(solution)/shard_map/share_rows/pallas_call | solution.py:89
  172.2 5.0 collective-permute-start.11
  177.2 6.6 %collective-permute-done.4.refs_1_ = bf16[64,7168]{1,0:T(8,128)(2,1)S(1)} collective-permute-done((bf16[64,7168]{1,0:T(8,128)(2,1)}, bf16[64,7168]{1,0:T(8,128)(2,1)S(1)}, u32[]{:S(2)}, u32[]{:S(2)}) %collective-permute-start.4) | collective-permute-done | bytes 917536 | tf_op jit(solution)/shard_map/ppermute | solution.py:59
  184.7 28.9 %share_rows.12 = (bf16[64,7168]{1,0:T(8,128)(2,1)}, bf16[64,7168]{1,0:T(8,128)(2,1)}, bf16[64,7168]{1,0:T(8,128)(2,1)}) custom-call(s32[1]{0:T(128)} %bitcast.group_ref, bf16[1024,3584]{1,0:T(8,128)(2,1)} %gate_ref.19, bf16[1024,3584]{1,0:T(8,128)(2,1)} %up_ref.19, bf16[64,7168]{1,0:T(8,128)(2,1)} %copy-done.8, ...), custom_call_target="tpu_custom_call", output_to_operand_aliasing={{0}: (3, {}), {1}: (4, {})} | custom-call | flops 1 | bytes 1 | tf_op jit(solution)/shard_map/share_rows/pallas_call | solution.py:89
  220.3 11.2 %collective-permute-done.6.refs_1_ = bf16[64,7168]{1,0:T(8,128)(2,1)S(1)} collective-permute-done((bf16[64,7168]{1,0:T(8,128)(2,1)}, bf16[64,7168]{1,0:T(8,128)(2,1)S(1)}, u32[]{:S(2)}, u32[]{:S(2)}) %collective-permute-start.6) | collective-permute-done | bytes 917536 | tf_op jit(solution)/shard_map/ppermute | solution.py:59
  232.5 28.9 %share_rows.13 = (bf16[64,7168]{1,0:T(8,128)(2,1)}, bf16[64,7168]{1,0:T(8,128)(2,1)}, bf16[64,7168]{1,0:T(8,128)(2,1)}) custom-call(s32[1]{0:T(128)} %bitcast.group_ref, bf16[1024,3584]{1,0:T(8,128)(2,1)} %gate_ref.19, bf16[1024,3584]{1,0:T(8,128)(2,1)} %up_ref.19, bf16[64,7168]{1,0:T(8,128)(2,1)} %copy-done.10, ...), custom_call_target="tpu_custom_call", output_to_operand_aliasing={{0}: (3, {}), {1}: (4, {})} | custom-call | flops 1 | bytes 1 | tf_op jit(solution)/shard_map/share_rows/pallas_call | solution.py:89
  261.5 40.7 %hidden_grads.1 = (bf16[2,512,3584]{2,1,0:T(8,128)(2,1)}, f32[512,64]{1,0:T(8,128)}) custom-call(s32[1]{0:T(128)} %bitcast.1.rank_ref, bf16[3584,4096]{1,0:T(8,128)(2,1)} %down_ref.1, bf16[512,3584]{1,0:T(8,128)(2,1)} %gate_ref.15, bf16[512,3584]{1,0:T(8,128)(2,1)} %up_ref.15, bf16[3584,64]{1,0:T(8,128)(2,1)} %copy.39.proj_ref, bf16[512,1024]{1,0:T(8,128)(2,1)} %refs_0_.3, ...), custom_call_target="tpu_custom_call" | custom-call | flops 1 | bytes 1 | tf_op jit(solution)/shard_map/hidden_grads/pallas_call | solution.py:160
  302.2 5.2 collective-permute-start.15
  310.2 19.4 %collective-permute-done.7.refs_0_ = bf16[64,7168]{1,0:T(8,128)(2,1)S(1)} collective-permute-done((bf16[64,7168]{1,0:T(8,128)(2,1)S(1)}, bf16[64,7168]{1,0:T(8,128)(2,1)S(1)}, u32[]{:S(2)}, u32[]{:S(2)}) %collective-permute-start.7) | collective-permute-done | bytes 917536 | tf_op jit(solution)/shard_map/ppermute | solution.py:54
  331.7 28.9 %share_rows.14 = (bf16[64,7168]{1,0:T(8,128)(2,1)}, bf16[64,7168]{1,0:T(8,128)(2,1)}, bf16[64,7168]{1,0:T(8,128)(2,1)}) custom-call(s32[1]{0:T(128)} %bitcast.group_ref, bf16[1024,3584]{1,0:T(8,128)(2,1)} %gate_ref.19, bf16[1024,3584]{1,0:T(8,128)(2,1)} %up_ref.19, bf16[64,7168]{1,0:T(8,128)(2,1)} %copy-done.16, ...), custom_call_target="tpu_custom_call", output_to_operand_aliasing={{0}: (3, {}), {1}: (4, {})} | custom-call | flops 1 | bytes 1 | tf_op jit(solution)/shard_map/share_rows/pallas_call | solution.py:89
  361.9 13.9 %weigh_rows.6.refs_2_ = bf16[1024,512]{1,0:T(8,128)(2,1)} custom-call(bf16[1024,3584]{1,0:T(8,128)(2,1)} %gate_ref.19, bf16[1024,3584]{1,0:T(8,128)(2,1)} %up_ref.19, bf16[2,512,3584]{2,1,0:T(8,128)(2,1)} %get-tuple-element.37.refs_2_.refs_18_.refs_8_.refs_4_, bf16[64,7168]{1,0:T(8,128)(2,1)} %get-tuple-element.43.refs_3_), custom_call_target="tpu_custom_call" | custom-call | flops 1 | bytes 1 | tf_op jit(solution)/shard_map/weigh_rows/pallas_call | solution.py:229
  382.1 14.0 %weigh_rows.7.refs_3_ = bf16[1024,512]{1,0:T(8,128)(2,1)} custom-call(bf16[1024,3584]{1,0:T(8,128)(2,1)} %gate_ref.19, bf16[1024,3584]{1,0:T(8,128)(2,1)} %up_ref.19, bf16[2,512,3584]{2,1,0:T(8,128)(2,1)} %collective-permute-done.15.refs_2_.refs_19_.refs_9_.refs_5_.refs_3_), custom_call_target="tpu_custom_call" | custom-call | flops 1 | bytes 1 | tf_op jit(solution)/shard_map/weigh_rows/pallas_call | solution.py:229
  397.0 28.9 %share_rows.15 = (bf16[64,7168]{1,0:T(8,128)(2,1)}, bf16[64,7168]{1,0:T(8,128)(2,1)}, bf16[64,7168]{1,0:T(8,128)(2,1)}) custom-call(s32[1]{0:T(128)} %bitcast.group_ref, bf16[1024,3584]{1,0:T(8,128)(2,1)} %gate_ref.19, bf16[1024,3584]{1,0:T(8,128)(2,1)} %up_ref.19, ...), custom_call_target="tpu_custom_call", output_to_operand_aliasing={{0}: (3, {}), {1}: (4, {})} | custom-call | flops 1 | bytes 1 | tf_op jit(solution)/shard_map/share_rows/pallas_call | solution.py:89
  426.3 19.5 %all-gather = f32[2048,64]{1,0:T(8,128)} all-gather(f32[512,64]{1,0:T(8,128)S(1)} %copy-done.27), channel_id=2, replica_groups=mesh['groups'=2,'tensor'=4,'dp'=4] {'tensor'}, dimensions={0}, use_global_device_ids=true | all-gather | bytes 655360 | tf_op jit(solution)/shard_map/all_gather | solution.py:356
  450.8 15.1 %weigh_rows.8.refs_2_ = bf16[576,1024]{1,0:T(8,128)(2,1)} custom-call(bf16[64,7168]{1,0:T(8,128)(2,1)} %get-tuple-element.28.refs_0_.refs_1_, bf16[64,7168]{1,0:T(8,128)(2,1)} %get-tuple-element.28.refs_0_.refs_1_, bf16[64,7168]{1,0:T(8,128)(2,1)} %get-tuple-element.30.refs_2_.refs_3_, bf16[64,7168]{1,0:T(8,128)(2,1)} %get-tuple-element.30.refs_2_.refs_3_, ...), custom_call_target="tpu_custom_call" | custom-call | flops 1 | bytes 1 | tf_op jit(solution)/shard_map/weigh_rows/pallas_call | solution.py:229
  474.4 11.2 %weigh_rows.9.refs_2_ = bf16[256,1024]{1,0:T(8,128)(2,1)} custom-call(bf16[64,7168]{1,0:T(8,128)(2,1)} %get-tuple-element.45.refs_0_.refs_1_, bf16[64,7168]{1,0:T(8,128)(2,1)} %get-tuple-element.45.refs_0_.refs_1_, bf16[64,7168]{1,0:T(8,128)(2,1)} %get-tuple-element.46.refs_2_.refs_3_, bf16[64,7168]{1,0:T(8,128)(2,1)} %get-tuple-element.46.refs_2_.refs_3_, ...), custom_call_target="tpu_custom_call" | custom-call | flops 1 | bytes 1 | tf_op jit(solution)/shard_map/weigh_rows/pallas_call | solution.py:229
  513.9 10.8 %weigh_rows.10 = bf16[128,1024]{1,0:T(8,128)(2,1)} custom-call(bf16[64,7168]{1,0:T(8,128)(2,1)} %get-tuple-element.49.refs_0_.refs_1_, bf16[64,7168]{1,0:T(8,128)(2,1)} %get-tuple-element.49.refs_0_.refs_1_, bf16[64,7168]{1,0:T(8,128)(2,1)} %get-tuple-element.50.refs_2_.refs_3_, bf16[64,7168]{1,0:T(8,128)(2,1)} %get-tuple-element.50.refs_2_.refs_3_, ...), custom_call_target="tpu_custom_call" | custom-call | flops 1 | bytes 1 | tf_op jit(solution)/shard_map/weigh_rows/pallas_call | solution.py:229
  536.7 10.3 %weigh_rows.11 = bf16[64,1024]{1,0:T(8,128)(2,1)} custom-call(bf16[64,7168]{1,0:T(8,128)(2,1)} %copy-done.23, bf16[64,7168]{1,0:T(8,128)(2,1)} %copy-done.23, bf16[2,512,3584]{2,1,0:T(8,128)(2,1)} %get-tuple-element.37.refs_2_.refs_18_.refs_8_.refs_4_, bf16[2,512,3584]{2,1,0:T(8,128)(2,1)} %collective-permute-done.15.refs_2_.refs_19_.refs_9_.refs_5_.refs_3_), custom_call_target="tpu_custom_call" | custom-call | flops 1 | bytes 1 | tf_op jit(solution)/shard_map/weigh_rows/pallas_call | solution.py:229
  559.0 25.2 %collective-permute-start.35 = (bf16[1024,512]{1,0:T(8,128)(2,1)}, bf16[1024,512]{1,0:T(8,128)(2,1)}, u32[]{:S(2)}, u32[]{:S(2)}) collective-permute-start(bf16[1024,512]{1,0:T(8,128)(2,1)} %slice.67), channel_id=1, source_target_pairs={{0,1},{1,0},{2,3},{3,2},{4,5},{5,4},{6,7},{7,6},{8,9},{9,8},{10,11... | collective-permute-start | bytes 3145736 | tf_op jit(solution)/shard_map/ppermute | solution.py:48
  (177 shorter events, 114.6 us)
Async XLA Ops:
  7.2 372.9 %all-gather.4.cloned.1.call-start = ((), (), s32[]{:S(2)}) async-start(), calls=%async_computation | async-start | bytes 1966080 | tf_op jit(solution)/shard_map/all_gather | solution.py:294
  64.0 52.7 %collective-permute-start.12 = (bf16[512,1024]{1,0:T(8,128)(2,1)}, bf16[512,1024]{1,0:T(8,128)(2,1)}, u32[]{:S(2)}, u32[]{:S(2)}) collective-permute-start(bf16[512,1024]{1,0:T(8,128)(2,1)} %refs_0_.3), channel_id=1, source_target_pairs={{4,0},{8,4},{12,8},{5,1},{9,5},{13,9},{6,2},{10,6},{14,10},{7,3},{... | collective-permute-start | bytes 3145736 | tf_op jit(solution)/shard_map/ppermute | solution.py:109
  65.3 52.7 %collective-permute-start.9 = (bf16[512,1024]{1,0:T(8,128)(2,1)}, bf16[512,1024]{1,0:T(8,128)(2,1)}, u32[]{:S(2)}, u32[]{:S(2)}) collective-permute-start(bf16[512,1024]{1,0:T(8,128)(2,1)} %refs_0_.3), channel_id=1, source_target_pairs={{0,4},{4,8},{8,12},{1,5},{5,9},{9,13},{2,6},{6,10},{10,14},{3,7},{... | collective-permute-start | bytes 3145736 | tf_op jit(solution)/shard_map/ppermute | solution.py:108
  70.5 52.8 %collective-permute-start.1 = (bf16[64,7168]{1,0:T(8,128)(2,1)}, bf16[64,7168]{1,0:T(8,128)(2,1)}, u32[]{:S(2)}, u32[]{:S(2)}) collective-permute-start(bf16[64,7168]{1,0:T(8,128)(2,1)} %get-tuple-element.29), channel_id=1, source_target_pairs={{2,0},{3,1},{0,2},{1,3},{6,4},{7,5},{4,6},{5,7},{10,8},{11,9},{8,1... | collective-permute-start | bytes 2752520 | tf_op jit(solution)/shard_map/ppermute | solution.py:54
  116.7 54.1 %collective-permute-start.13 = (bf16[512,1024]{1,0:T(8,128)(2,1)}, bf16[512,1024]{1,0:T(8,128)(2,1)}, u32[]{:S(2)}, u32[]{:S(2)}) collective-permute-start(bf16[512,1024]{1,0:T(8,128)(2,1)} %collective-permute-done.12.refs_4_), channel_id=1, source_target_pairs={{4,0},{8,4},{12,8},{5,1},{9,5},{13,9},{6,2},{10,6},{14,10},{7,3},{... | collective-permute-start | bytes 3145736 | tf_op jit(solution)/shard_map/ppermute | solution.py:109
  118.0 54.1 %collective-permute-start.10 = (bf16[512,1024]{1,0:T(8,128)(2,1)}, bf16[512,1024]{1,0:T(8,128)(2,1)}, u32[]{:S(2)}, u32[]{:S(2)}) collective-permute-start(bf16[512,1024]{1,0:T(8,128)(2,1)} %collective-permute-done.9.refs_1_), channel_id=1, source_target_pairs={{0,4},{4,8},{8,12},{1,5},{5,9},{9,13},{2,6},{6,10},{10,14},{3,7},{... | collective-permute-start | bytes 3145736 | tf_op jit(solution)/shard_map/ppermute | solution.py:108
  123.0 54.2 %collective-permute-start.3 = (bf16[64,7168]{1,0:T(8,128)(2,1)}, bf16[64,7168]{1,0:T(8,128)(2,1)S(1)}, u32[]{:S(2)}, u32[]{:S(2)}) collective-permute-start(bf16[64,7168]{1,0:T(8,128)(2,1)} %get-tuple-element.31), channel_id=1, source_target_pairs={{2,0},{3,1},{0,2},{1,3},{6,4},{7,5},{4,6},{5,7},{10,8},{11,9},{8,1... | collective-permute-start | bytes 2752520 | tf_op jit(solution)/shard_map/ppermute | solution.py:54
  170.6 49.8 %collective-permute-start.5 = (bf16[64,7168]{1,0:T(8,128)(2,1)}, bf16[64,7168]{1,0:T(8,128)(2,1)S(1)}, u32[]{:S(2)}, u32[]{:S(2)}) collective-permute-start(bf16[64,7168]{1,0:T(8,128)(2,1)} %get-tuple-element.33), channel_id=1, source_target_pairs={{2,0},{3,1},{0,2},{1,3},{6,4},{7,5},{4,6},{5,7},{10,8},{11,9},{8,1... | collective-permute-start | bytes 2752520 | tf_op jit(solution)/shard_map/ppermute | solution.py:54
  170.9 90.5 %collective-permute-start.14 = (bf16[512,1024]{1,0:T(8,128)(2,1)}, bf16[512,1024]{1,0:T(8,128)(2,1)}, u32[]{:S(2)}, u32[]{:S(2)}) collective-permute-start(bf16[512,1024]{1,0:T(8,128)(2,1)} %collective-permute-done.13.refs_5_), channel_id=1, source_target_pairs={{4,0},{8,4},{12,8},{5,1},{9,5},{13,9},{6,2},{10,6},{14,10},{7,3},{... | collective-permute-start | bytes 3145736 | tf_op jit(solution)/shard_map/ppermute | solution.py:109
  172.2 89.2 %collective-permute-start.11 = (bf16[512,1024]{1,0:T(8,128)(2,1)}, bf16[512,1024]{1,0:T(8,128)(2,1)}, u32[]{:S(2)}, u32[]{:S(2)}) collective-permute-start(bf16[512,1024]{1,0:T(8,128)(2,1)} %collective-permute-done.10.refs_2_), channel_id=1, source_target_pairs={{0,4},{4,8},{8,12},{1,5},{5,9},{9,13},{2,6},{6,10},{10,14},{3,7},{... | collective-permute-start | bytes 3145736 | tf_op jit(solution)/shard_map/ppermute | solution.py:108
  302.2 79.9 %collective-permute-start.15 = (bf16[2,512,3584]{2,1,0:T(8,128)(2,1)}, bf16[2,512,3584]{2,1,0:T(8,128)(2,1)}, u32[]{:S(2)}, u32[]{:S(2)}) collective-permute-start(bf16[2,512,3584]{2,1,0:T(8,128)(2,1)} %get-tuple-element.37.refs_2_.refs_18_.refs_8_.refs_4_), channel_id=1, source_target_pairs={{0,1},{1,0},{2,3},{3,2},{4,5},{5,4},{6,7},{7,6},{8,9},{9,8},{10,11... | collective-permute-start | bytes 22020104 | tf_op jit(solution)/shard_map/ppermute | solution.py:48
  309.0 87.1 %collective-permute-start.16 = (bf16[64,7168]{1,0:T(8,128)(2,1)}, bf16[64,7168]{1,0:T(8,128)(2,1)}, u32[]{:S(2)}, u32[]{:S(2)}) collective-permute-start(bf16[64,7168]{1,0:T(8,128)(2,1)} %get-tuple-element.36.refs_7_), channel_id=1, source_target_pairs={{2,0},{3,1},{0,2},{1,3},{6,4},{7,5},{4,6},{5,7},{10,8},{11,9},{8,1... | collective-permute-start | bytes 2752520 | tf_op jit(solution)/shard_map/ppermute | solution.py:54
  360.6 35.5 %collective-permute-start.17 = (bf16[64,7168]{1,0:T(8,128)(2,1)}, bf16[64,7168]{1,0:T(8,128)(2,1)S(1)}, u32[]{:S(2)}, u32[]{:S(2)}) collective-permute-start(bf16[64,7168]{1,0:T(8,128)(2,1)} %get-tuple-element.38.refs_8_.refs_9_), channel_id=1, source_target_pairs={{16,0},{0,16},{17,1},{1,17},{18,2},{2,18},{19,3},{3,19},{20,4},{4,... | collective-permute-start | bytes 2752520 | tf_op jit(solution)/shard_map/ppermute | solution.py:59
  375.9 92.5 %collective-permute-start.31 = (bf16[1024,512]{1,0:T(8,128)(2,1)}, bf16[1024,512]{1,0:T(8,128)(2,1)}, u32[]{:S(2)}, u32[]{:S(2)}) collective-permute-start(bf16[1024,512]{1,0:T(8,128)(2,1)} %weigh_rows.6.refs_2_), channel_id=1, source_target_pairs={{4,0},{12,8},{1,5},{9,13},{6,2},{14,10},{3,7},{11,15},{20,16},{28,... | collective-permute-start | bytes 3145736 | tf_op jit(solution)/shard_map/ppermute | solution.py:253
  381.7 90.8 %collective-permute-start.20 = (bf16[64,7168]{1,0:T(8,128)(2,1)}, bf16[64,7168]{1,0:T(8,128)(2,1)S(1)}, u32[]{:S(2)}, u32[]{:S(2)}) collective-permute-start(bf16[64,7168]{1,0:T(8,128)(2,1)} %get-tuple-element.43.refs_3_), channel_id=1, source_target_pairs={{2,0},{3,1},{0,2},{1,3},{6,4},{7,5},{4,6},{5,7},{10,8},{11,9},{8,1... | collective-permute-start | bytes 2752520 | tf_op jit(solution)/shard_map/ppermute | solution.py:54
  425.9 46.6 %collective-permute-start.21 = (bf16[64,7168]{1,0:T(8,128)(2,1)}, bf16[64,7168]{1,0:T(8,128)(2,1)S(1)}, u32[]{:S(2)}, u32[]{:S(2)}) collective-permute-start(bf16[64,7168]{1,0:T(8,128)(2,1)} %get-tuple-element.45.refs_0_.refs_1_), channel_id=1, source_target_pairs={{16,0},{0,16},{17,1},{1,17},{18,2},{2,18},{19,3},{3,19},{20,4},{4,... | collective-permute-start | bytes 2752520 | tf_op jit(solution)/shard_map/ppermute | solution.py:59
  447.3 44.5 %collective-permute-start.33 = (bf16[1024,512]{1,0:T(8,128)(2,1)S(1)}, bf16[1024,512]{1,0:T(8,128)(2,1)}, u32[]{:S(2)}, u32[]{:S(2)}) collective-permute-start(bf16[1024,512]{1,0:T(8,128)(2,1)S(1)} %copy-done.3), channel_id=1, source_target_pairs={{4,0},{12,8},{1,5},{9,13},{6,2},{14,10},{3,7},{11,15},{20,16},{28,... | collective-permute-start | bytes 3145736 | tf_op jit(solution)/shard_map/ppermute | solution.py:253
  466.0 34.5 %collective-permute-start.18 = (bf16[576,1024]{1,0:T(8,128)(2,1)}, bf16[576,1024]{1,0:T(8,128)(2,1)}, u32[]{:S(2)}, u32[]{:S(2)}) collective-permute-start(bf16[576,1024]{1,0:T(8,128)(2,1)} %weigh_rows.8.refs_2_), channel_id=1, source_target_pairs={{4,0},{12,8},{1,5},{9,13},{6,2},{14,10},{3,7},{11,15},{20,16},{28,... | collective-permute-start | bytes 3538952 | tf_op jit(solution)/shard_map/ppermute | solution.py:253
  470.8 33.1 %collective-permute-start.32 = (bf16[1024,512]{1,0:T(8,128)(2,1)}, bf16[1024,512]{1,0:T(8,128)(2,1)}, u32[]{:S(2)}, u32[]{:S(2)}) collective-permute-start(bf16[1024,512]{1,0:T(8,128)(2,1)} %add_convert_fusion.5), channel_id=1, source_target_pairs={{8,0},{13,5},{2,10},{7,15},{24,16},{29,21},{18,26},{23,31}} | collective-permute-start | bytes 3145736 | tf_op jit(solution)/shard_map/ppermute | solution.py:253
  497.6 31.9 %collective-permute-start.34 = (bf16[1024,512]{1,0:T(8,128)(2,1)}, bf16[1024,512]{1,0:T(8,128)(2,1)}, u32[]{:S(2)}, u32[]{:S(2)}) collective-permute-start(bf16[1024,512]{1,0:T(8,128)(2,1)} %add_convert_fusion.3), channel_id=1, source_target_pairs={{8,0},{13,5},{2,10},{7,15},{24,16},{29,21},{18,26},{23,31}} | collective-permute-start | bytes 3145736 | tf_op jit(solution)/shard_map/ppermute | solution.py:253
  500.5 28.7 %collective-permute-start.23 = (bf16[256,1024]{1,0:T(8,128)(2,1)S(1)}, bf16[256,1024]{1,0:T(8,128)(2,1)S(1)}, u32[]{:S(2)}, u32[]{:S(2)}) collective-permute-start(bf16[256,1024]{1,0:T(8,128)(2,1)S(1)} %add_convert_fusion.7), channel_id=1, source_target_pairs={{0,8},{5,13},{10,2},{15,7},{16,24},{21,29},{26,18},{31,23}} | collective-permute-start | bytes 1572872 | tf_op jit(solution)/shard_map/ppermute | solution.py:253
  504.0 29.6 %collective-permute-start.19 = (bf16[576,1024]{1,0:T(8,128)(2,1)}, bf16[576,1024]{1,0:T(8,128)(2,1)}, u32[]{:S(2)}, u32[]{:S(2)}) collective-permute-start(bf16[576,1024]{1,0:T(8,128)(2,1)} %add_convert_fusion.1), channel_id=1, source_target_pairs={{0,8},{5,13},{10,2},{15,7},{16,24},{21,29},{26,18},{31,23}} | collective-permute-start | bytes 3538952 | tf_op jit(solution)/shard_map/ppermute | solution.py:253
  513.5 22.2 %collective-permute-start.28 = (bf16[64,7168]{1,0:T(8,128)(2,1)}, bf16[64,7168]{1,0:T(8,128)(2,1)S(1)}, u32[]{:S(2)}, u32[]{:S(2)}) collective-permute-start(bf16[64,7168]{1,0:T(8,128)(2,1)} %get-tuple-element.49.refs_0_.refs_1_), channel_id=1, source_target_pairs={{16,0},{0,16},{17,1},{1,17},{18,2},{2,18},{19,3},{3,19},{20,4},{4,... | collective-permute-start | bytes 2752520 | tf_op jit(solution)/shard_map/ppermute | solution.py:59
  559.0 27.8 %collective-permute-start.35 = (bf16[1024,512]{1,0:T(8,128)(2,1)}, bf16[1024,512]{1,0:T(8,128)(2,1)}, u32[]{:S(2)}, u32[]{:S(2)}) collective-permute-start(bf16[1024,512]{1,0:T(8,128)(2,1)} %slice.67), channel_id=1, source_target_pairs={{0,1},{1,0},{2,3},{3,2},{4,5},{5,4},{6,7},{7,6},{8,9},{9,8},{10,11... | collective-permute-start | bytes 3145736 | tf_op jit(solution)/shard_map/ppermute | solution.py:48
  (48 other events, 905.1 us)
Sparse Core Ops, SparseCore 0:
  307.5 37.6 all-gather.3

commit v3 on v2

--- a/solution.py
+++ b/solution.py
@@ -63,41 +63,38 @@
     return next((w for w in options if size % w == 0), size)
 
 
-def share_rows(w_gate, w_up, group, places, piece, part, carried, after):
-    width = w_gate.shape[1]
-    kept, waits = len(carried), len(after)
-
-    def kernel(group_ref, gate_ref, up_ref, *refs):
-        outs = refs[kept + waits + kept : kept + waits + kept + len(places)]
-        sems = refs[-1] if places else None
-        copies = []
-        for at, k in enumerate(places):
-            first = pl.multiple_of(group_ref[0] * part + k * piece, piece)
-            for half, source in enumerate((gate_ref, up_ref)):
-                copies.append(
-                    pltpu.make_async_copy(
-                        source.at[pl.ds(first, piece), :],
-                        outs[at].at[:, pl.ds(half * width, width)],
-                        sems.at[2 * at + half],
-                    )
-                )
-        for copy in copies:
-            copy.start()
-        for copy in copies:
-            copy.wait()
-
+def share_rows(w_gate, w_up, group, places, piece, carried, after):
+    rows, width = w_gate.shape
+    tile = widest(width, (1792, 896, 128))
+    kept, waits, fresh = len(carried), len(after), len(places)
+    per_group = rows // lax.axis_size("groups") // piece
+
+    def kernel(group_ref, *refs):
+        outs = refs[len(refs) - fresh :]
+        for at in range(fresh):
+            outs[at][0] = refs[2 * at][...]
+            outs[at][1] = refs[2 * at + 1][...]
+
+    specs = []
+    for k in places:
+        at_chunk = functools.partial(lambda k, i, g: (g[0] * per_group + k, i), k)
+        specs += [pl.BlockSpec((piece, tile), at_chunk)] * 2
     results = pl.pallas_call(
         kernel,
+        grid_spec=pltpu.PrefetchScalarGridSpec(
+            num_scalar_prefetch=1,
+            grid=(width // tile if places else 1,),
+            in_specs=specs + [ANYWHERE] * (kept + waits),
+            out_specs=[ANYWHERE] * kept
+            + [pl.BlockSpec((2, piece, tile), lambda i, g: (0, 0, i))] * fresh,
+        ),
         out_shape=[jax.ShapeDtypeStruct(a.shape, a.dtype) for a in carried]
-        + [jax.ShapeDtypeStruct((piece, 2 * width), w_gate.dtype) for _ in places],
-        in_specs=[pl.BlockSpec(memory_space=pltpu.SMEM)] + [ANYWHERE] * (2 + kept + waits),
-        out_specs=[ANYWHERE] * (kept + len(places)),
-        scratch_shapes=[pltpu.SemaphoreType.DMA((2 * len(places),))] if places else [],
-        input_output_aliases={3 + i: i for i in range(kept)},
+        + [jax.ShapeDtypeStruct((2, piece, width), w_gate.dtype) for _ in places],
+        input_output_aliases={1 + 2 * fresh + i: i for i in range(kept)},
         compiler_params=pltpu.CompilerParams(vmem_limit_bytes=VMEM_BYTES),
         cost_estimate=LIGHT,
         name="share_rows",
-    )(group, w_gate, w_up, *carried, *after)
+    )(group, *[w_gate, w_up] * fresh, *carried, *after)
     return list(results[:kept]), list(results[kept:])
 
 
@@ -110,20 +107,64 @@
     return below, above[1:]
 
 
-def hidden_grads(rank, below, above, w_down, gate_act, up_act, proj_u, after):
+def prepare(gate_act, up_act, proj_h, after):
+    count, hidden = gate_act.shape
+    narrow = proj_h.shape[0]
+    tile = widest(hidden, (512, 256, 128))
+
+    def kernel(gate_ref, up_ref, proj_ref, *refs):
+        slope_ref, down_ref = refs[-2:]
+
+        @pl.when(pl.program_id(0) == 0)
+        def _():
+            down_ref[...] = jnp.zeros_like(down_ref)
+
+        gate = gate_ref[...].astype(jnp.float32).T
+        up = up_ref[...].astype(jnp.float32).T
+        sigma = jax.nn.sigmoid(gate)
+        swish = gate * sigma
+        slope_ref[0] = up * sigma * (1.0 + gate * (1.0 - sigma))
+        slope_ref[1] = swish
+        down_ref[...] += jnp.dot(
+            proj_ref[...], (swish * up).astype(jnp.bfloat16), preferred_element_type=jnp.float32
+        )
+
+    return pl.pallas_call(
+        kernel,
+        grid=(hidden // tile,),
+        out_shape=[
+            jax.ShapeDtypeStruct((2, hidden, count), jnp.float32),
+            jax.ShapeDtypeStruct((narrow, count), jnp.float32),
+        ],
+        in_specs=[
+            pl.BlockSpec((count, tile), lambda i: (0, i)),
+            pl.BlockSpec((count, tile), lambda i: (0, i)),
+            pl.BlockSpec((narrow, tile), lambda i: (0, i)),
+        ]
+        + [ANYWHERE] * len(after),
+        out_specs=[
+            pl.BlockSpec((2, tile, count), lambda i: (0, i, 0)),
+            pl.BlockSpec((narrow, count), lambda i: (0, 0)),
+        ],
+        compiler_params=pltpu.CompilerParams(vmem_limit_bytes=VMEM_BYTES),
+        cost_estimate=LIGHT,
+        name="prepare",
+    )(gate_act, up_act, proj_h, *after)
+
+
+def hidden_grads(rank, below, above, w_down, slopes, proj_u, after):
     ranks = len(below)
-    count, features = below[0].shape
+    features, count = below[0].shape
     hidden, depth = w_down.shape
     tile = widest(hidden, (512, 256, 128))
-    step = min(tile, 256)
-    narrow = proj_u.shape[1]
-
-    def kernel(rank_ref, down_ref, gate_ref, up_ref, proj_ref, *refs):
+    narrow = proj_u.shape[0]
+
+    def kernel(rank_ref, down_ref, slope_ref, proj_ref, *refs):
         both_ref, out_ref, grad_ref, sem = refs[-4:]
 
         def gather(at, wait):
             block = lax.rem(rank_ref[0] + ranks - at, ranks)
-            cols = pl.ds(pl.multiple_of(block * features, features), features)
+            span = pl.ds(pl.multiple_of(block * features, features), features)
             for source, valid in (
                 (refs[at], rank_ref[0] >= at),
                 (refs[ranks + ranks - at - 1] if at else None, rank_ref[0] < at),
@@ -132,7 +173,7 @@
 
                     @pl.when(valid)
                     def _():
-                        copy = pltpu.make_async_copy(source, grad_ref.at[:, cols], sem.at[at])
+                        copy = pltpu.make_async_copy(source, grad_ref.at[span, :], sem.at[at])
                         copy.wait() if wait else copy.start()
 
         @pl.when(pl.program_id(0) == 0)
@@ -143,60 +184,50 @@
             for at in range(ranks):
                 gather(at, True)
 
-        for first in range(0, tile, step):
-            cols = slice(first, first + step)
-            wide = contract_right(grad_ref[...], down_ref[cols, :])
-            gate = gate_ref[:, cols].astype(jnp.float32)
-            up = up_ref[:, cols].astype(jnp.float32)
-            sigma = jax.nn.sigmoid(gate)
-            up_grad = (wide * (gate * sigma)).astype(jnp.bfloat16)
-            slope = sigma * (1.0 + gate * (1.0 - sigma))
-            both_ref[0, :, cols] = (wide * up * slope).astype(jnp.bfloat16)
-            both_ref[1, :, cols] = up_grad
-            out_ref[...] += jnp.dot(
-                up_grad, proj_ref[cols, :], preferred_element_type=jnp.float32
-            )
+        wide = jnp.dot(down_ref[...], grad_ref[...], preferred_element_type=jnp.float32)
+        both_ref[0] = (wide * slope_ref[0]).astype(jnp.bfloat16)
+        up_grad = (wide * slope_ref[1]).astype(jnp.bfloat16)
+        both_ref[1] = up_grad
+        out_ref[...] += jnp.dot(proj_ref[...], up_grad, preferred_element_type=jnp.float32)
 
     return pl.pallas_call(
         kernel,
         grid=(hidden // tile,),
         out_shape=[
-            jax.ShapeDtypeStruct((2, count, hidden), jnp.bfloat16),
-            jax.ShapeDtypeStruct((count, narrow), jnp.float32),
+            jax.ShapeDtypeStruct((2, hidden, count), jnp.bfloat16),
+            jax.ShapeDtypeStruct((narrow, count), jnp.float32),
         ],
         in_specs=[
             pl.BlockSpec(memory_space=pltpu.SMEM),
             pl.BlockSpec((tile, depth), lambda i: (i, 0)),
-            pl.BlockSpec((count, tile), lambda i: (0, i)),
-            pl.BlockSpec((count, tile), lambda i: (0, i)),
-            pl.BlockSpec((tile, narrow), lambda i: (i, 0)),
+            pl.BlockSpec((2, tile, count), lambda i: (0, i, 0)),
+            pl.BlockSpec((narrow, tile), lambda i: (0, i)),
         ]
         + [ANYWHERE] * (2 * ranks - 1 + len(after)),
         out_specs=[
-            pl.BlockSpec((2, count, tile), lambda i: (0, 0, i)),
-            pl.BlockSpec((count, narrow), lambda i: (0, 0)),
+            pl.BlockSpec((2, tile, count), lambda i: (0, i, 0)),
+            pl.BlockSpec((narrow, count), lambda i: (0, 0)),
         ],
         scratch_shapes=[
-            pltpu.VMEM((count, depth), jnp.bfloat16),
+            pltpu.VMEM((depth, count), jnp.bfloat16),
             pltpu.SemaphoreType.DMA((ranks,)),
         ],
         compiler_params=pltpu.CompilerParams(vmem_limit_bytes=VMEM_BYTES),
         cost_estimate=LIGHT,
         name="hidden_grads",
-    )(rank, w_down, gate_act, up_act, proj_u, *below, *above, *after)
+    )(rank, w_down, slopes, proj_u, *below, *above, *after)
 
 
 def weigh(units, grads, after):
-    hidden = grads[0].shape[2]
+    hidden = grads[0].shape[1]
     tile = widest(hidden, (512, 256, 128))
     steps = hidden // tile
-    counts = [g.shape[1] for g in grads]
-    heights = [u[0].shape[0] for u in units]
-    rows, count = sum(heights), sum(counts)
+    counts = [g.shape[2] for g in grads]
+    rows, count = sum(u[0].shape[-2] for u in units), sum(counts)
+    flat = [w for u in units for w in u]
 
     def kernel(*refs):
-        weights = refs[: 2 * len(units)]
-        both = refs[2 * len(units) : 2 * len(units) + len(grads)]
+        weights, both = refs[: len(flat)], refs[len(flat) : len(flat) + len(grads)]
         out_ref, total = refs[-2:]
         at = pl.program_id(0)
 
@@ -204,28 +235,31 @@
         def _():
             total[...] = jnp.zeros_like(total)
 
-        gate = jnp.concatenate([w[...] for w in weights[0::2]], axis=0)
-        up = jnp.concatenate([w[...] for w in weights[1::2]], axis=0)
+        if len(units[0]) == 2:
+            gate, up = weights[0][...], weights[1][...]
+        else:
+            gate = jnp.concatenate([w[0] for w in weights], axis=0)
+            up = jnp.concatenate([w[1] for w in weights], axis=0)
         first = 0
         for ref in both:
-            span = slice(first, first + ref.shape[1])
-            total[:, span] += contract_right(gate, ref[0]) + contract_right(up, ref[1])
-            first += ref.shape[1]
+            span = slice(first, first + ref.shape[2])
+            total[:, span] += jnp.dot(
+                gate, ref[0], preferred_element_type=jnp.float32
+            ) + jnp.dot(up, ref[1], preferred_element_type=jnp.float32)
+            first += ref.shape[2]
 
         @pl.when(at == steps - 1)
         def _():
             out_ref[...] = total[...].astype(jnp.bfloat16)
 
-    specs, operands = [], []
-    for gate, up, up_at in units:
-        specs.append(pl.BlockSpec((gate.shape[0], tile), lambda i: (0, i)))
-        specs.append(
-            pl.BlockSpec((up.shape[0], tile), functools.partial(lambda o, i: (0, o + i), up_at // tile))
-        )
-        operands += [gate, up]
+    specs = []
+    for w in flat:
+        if w.ndim == 2:
+            specs.append(pl.BlockSpec((w.shape[0], tile), lambda i: (0, i)))
+        else:
+            specs.append(pl.BlockSpec((2, w.shape[1], tile), lambda i: (0, 0, i)))
     for g in grads:
-        specs.append(pl.BlockSpec((2, g.shape[1], tile), lambda i: (0, 0, i)))
-        operands.append(g)
+        specs.append(pl.BlockSpec((2, tile, g.shape[2]), lambda i: (0, i, 0)))
     return pl.pallas_call(
         kernel,
         grid=(steps,),
@@ -236,7 +270,22 @@
         compiler_params=pltpu.CompilerParams(vmem_limit_bytes=VMEM_BYTES),
         cost_estimate=LIGHT,
         name="weigh_rows",
-    )(*operands, *after)
+    )(*flat, *grads, *after)
+
+
+def scatter_ranks(value):
+    ranks, rank = lax.axis_size("tensor"), lax.axis_index("tensor")
+    bit = ranks // 2
+    while bit:
+        half = value.shape[0] // 2
+        high = rank & bit != 0
+        low_rows, high_rows = value[:half], value[half:]
+        got = lax.ppermute(
+            jnp.where(high, low_rows, high_rows), "tensor", [(i, i ^ bit) for i in range(ranks)]
+        )
+        value = jnp.where(high, high_rows, low_rows) + got
+        bit //= 2
+    return value
 
 
 def reduce_to(value, owner):
@@ -276,7 +325,7 @@
     group, rank = lax.axis_index("groups"), lax.axis_index("tensor")
     place = lax.axis_index("dp")
     chip, core = place // CORES, place % CORES
-    rows, hidden_width = w_gate.shape
+    rows = w_gate.shape[0]
     count = layer_input.shape[0]
     features = out_grad.shape[1]
     part = rows // groups
@@ -285,28 +334,27 @@
     group_word = jnp.full((1,), group, jnp.int32)
     rank_word = jnp.full((1,), rank, jnp.int32)
 
-    below, above = spread_ranks(out_grad)
-    gate_wide = gate_act.astype(jnp.float32)
-    hidden = (gate_wide * jax.nn.sigmoid(gate_wide) * up_act.astype(jnp.float32)).astype(jnp.bfloat16)
+    below, above = spread_ranks(out_grad.T)
+    _, shares = share_rows(w_gate, w_up, group_word, [0, 1], piece, [], [])
+    slopes, in_down_part = prepare(gate_act, up_act, proj_h.T, [shares[0]])
     early_part = jnp.concatenate(
-        [project(proj_x, layer_input), project(proj_h, hidden), project(proj_g, out_grad)], axis=0
+        [project(proj_x, layer_input), in_down_part, project(proj_g, out_grad)], axis=0
     )
     early = lax.all_gather(early_part, "tensor", axis=0, tiled=False)
 
-    _, shares = share_rows(w_gate, w_up, group_word, [0, 1], piece, part, [], [])
     fetched, arriving = {}, {}
 
     def fetch(k):
         for s in range(1, chips):
             arriving[k, s, 0] = from_chip(shares[k], s)
 
-    def forward(k, after):
+    def forward(k, after, held=()):
         names = [n for n in arriving if n[0] == k and n[2] == 0] + [
             n for n in arriving if n[0] == k - 1 and n[2] > 0
         ]
         places = [k + 2] if k + 2 < CHUNKS else []
         carried, fresh = share_rows(
-            w_gate, w_up, group_word, places, piece, part, [arriving.pop(n) for n in names], after
+            w_gate, w_up, group_word, places, piece, [arriving.pop(n) for n in names] + list(held), after
         )
         fetched.update(zip(names, carried))
         shares.extend(fresh)
@@ -315,6 +363,7 @@
         for s in range(1, chips):
             for r in range(1, groups):
                 arriving[k, s, r] = from_group(fetched[k, s, 0], r)
+        return carried[len(names) :]
 
     def owner_of(s, first_of):
         table = np.zeros((groups, blocks), np.int64)
@@ -336,7 +385,7 @@
         outs = []
         for table, kept in sets.values():
             if kept:
-                units = [(fetched[n], fetched[n], hidden_width) for n in kept]
+                units = [(fetched[n],) for n in kept]
                 out = weigh(units, [mine, theirs], after)
                 outs.append(out)
                 total = reduce_to(out, table)
@@ -346,14 +395,14 @@
 
     fetch(0)
     fetch(1)
-    forward(0, [])
-    forward(1, [])
+    forward(0, [slopes])
+    forward(1, [early_part])
     forward(2, [])
     forward(3, [])
     mine, up_out_part = hidden_grads(
-        rank_word, below, above, w_down, gate_act, up_act, proj_u, [shares[5], early_part]
-    )
-    late = lax.all_gather(up_out_part, "tensor", axis=0, tiled=False)
+        rank_word, below, above, w_down, slopes, proj_u.T, [shares[5]]
+    )
+    up_out = scatter_ranks(up_out_part).astype(jnp.bfloat16)
     forward(4, [mine])
     theirs = swap_cores(mine)
     height = rows // split
@@ -362,24 +411,22 @@
         for j in range(split):
             gate_rows = w_gate[j * height : (j + 1) * height]
             up_rows = w_up[j * height : (j + 1) * height]
-            out = weigh([(gate_rows, up_rows, 0)], [both], after)
+            out = weigh([(gate_rows, up_rows)], [both], after)
             done.append(out)
             near.append(reduce_to(out, owner_of(0, lambda g: j * height)))
     forward(5, done)
     outs = far_round([(k, 0) for k in range(5)] + [(k, 1) for k in range(4)], [shares[7]])
-    forward(6, outs)
+    (early,) = forward(6, outs, [early])
     outs = far_round([(5, 0), (6, 0), (4, 1), (5, 1)], [])
     forward(7, outs)
 
     early = early.sum(axis=0).astype(jnp.bfloat16)
-    late = late.sum(axis=0).astype(jnp.bfloat16).T
-    width = late.shape[0]
-    slot = width // ranks
+    width, slot = up_out_part.shape[0], up_out.shape[0]
     in_up, in_down, out_down = early[:width], early[width : 2 * width], early[2 * width :]
     member = pack_table(doc_lengths, count)
-    own = lambda table: lax.dynamic_slice_in_dim(table, rank * slot, slot, 0)
+    out_down = lax.dynamic_slice_in_dim(out_down, rank * slot, slot, 0)
     doc_logs = jnp.stack(
-        [doc_outer(member, own(late), in_up), doc_outer(member, own(out_down), in_down)], axis=1
+        [doc_outer(member, up_out, in_up), doc_outer(member, out_down, in_down)], axis=1
     )
 
     far_round([(7, 0), (6, 1)], [doc_logs])

time: 600 us -> 375 us (0.62)
  Pallas kernels: 346 us -> 127 us
  starting transfers between devices: 90.9 us -> 121 us
  blocking collectives: 19.5 us -> 0 us
  matrix products: 9.37 us -> 1.21 us
  local copies, waits for them, and re-layouts: 15.6 us -> 9.04 us
    pallas_call x9 -> x10, Pallas kernels: 230 us -> 27.7 us  [the longest x9 15.7 us: share_rows(): pl.pallas_call(kernel, grid_spec=pltpu.PrefetchScalarGridSpec(num_scalar_...]
    ppermute x8, waiting for transfers between devices: 30.7 us -> 10.3 us  [from_group(): lax.ppermute(value, 'groups', [((i + shift) % size, i) for i in range(siz...]
    ppermute x0 -> x2, starting transfers between devices: none -> 19.6 us  [scatter_ranks(): lax.ppermute(jnp.where(high, low_rows, high_rows), 'tensor', [(i, i ^ bit...]
    all_gather x1 -> x0, blocking collectives: 19.5 us -> none  [per_device(): late = lax.all_gather(up_out_part, 'tensor', axis=0, tiled=False)]
    pallas_call x1, Pallas kernels: 40.7 us -> 26.9 us  [hidden_grads(): pl.pallas_call(kernel, grid=(hidden // tile,), out_shape=[jax.ShapeDtypeS...]
    ppermute x12, waiting for transfers between devices: 5.11 us -> 17.7 us  [reduce_to(): got = lax.ppermute(value, ('groups', 'tensor', 'dp'), pairs)]
    ppermute x8, starting transfers between devices: 5.1 us -> 14.3 us  [from_chip(): lax.ppermute(value, 'dp', [((i + step) % size, i) for i in range(size)])]
    dot_general x3 -> x2, matrix products: 7.56 us -> 0.88 us  [project(): lax.dot_general(proj, rows, (((0,), (1,)), ((), ())), preferred_element_t...]
  transfers between devices with their start and end apart: 37 -> 39, of which waited for: 11 -> 16; matrix products, arithmetic and copies ran while one was open for 5% -> 5% of each run, Pallas kernels for 42% -> 26%
where the time goes in v3:
time: 375 us; the launch traced here: 373 us
  Pallas kernels  127 us (34%)
  starting transfers between devices  121 us (32%)
  waiting for transfers between devices  78.5 us (21%)
  other arithmetic  21.8 us (6%)
  between operations  14.6 us (4%)
  local copies, waits for them, and re-layouts  9.04 us (2%)
    pallas_call x6, Pallas kernels, weigh(): pl.pallas_call(kernel, grid=(steps,), out_shape=jax.ShapeDtypeStruct((row...  72.5 us
    ppermute x8, waiting for transfers between devices, from_chip(): lax.ppermute(value, 'dp', [((i + step) % size, i) for i in range(size)])  43.6 us
    ppermute x2, starting transfers between devices, swap_cores(): return lax.ppermute(value, 'dp', [(i, i ^ 1) for i in range(size)])  36.1 us
    pallas_call x1, Pallas kernels, hidden_grads(): pl.pallas_call(kernel, grid=(hidden // tile,), out_shape=[jax.ShapeDtypeS...  26.9 us
    ppermute x12, starting transfers between devices, reduce_to(): got = lax.ppermute(value, ('groups', 'tensor', 'dp'), pairs)  25.2 us
    ppermute x2, starting transfers between devices, scatter_ranks(): lax.ppermute(jnp.where(high, low_rows, high_rows), 'tensor', [(i, i ^ bit...  19.6 us
    ppermute x12, waiting for transfers between devices, reduce_to(): got = lax.ppermute(value, ('groups', 'tensor', 'dp'), pairs)  17.7 us
    pallas_call x9, Pallas kernels, share_rows(): pl.pallas_call(kernel, grid_spec=pltpu.PrefetchScalarGridSpec(num_scalar_...  15.7 us
  transfers between devices with their start and end apart: 39, of which 16 were waited for; matrix products, arithmetic and copies ran while one was open for 5% of the time, Pallas kernels for 26%

profile of v3, /device:TPU:3, one launch (start us, length us, event | category | flops | bytes accessed | tf_op | source)
XLA Modules:
  0.0 373.2 jit_solution(8768028355345316264)
XLA Ops:
  10.6 4.4 %collective-permute-start.9 = (bf16[1024,512]{1,0:T(8,128)(2,1)S(1)}, bf16[1024,512]{1,0:T(8,128)(2,1)}, u32[]{:S(2)}, u32[]{:S(2)}) collective-permute-start(bf16[1024,512]{1,0:T(8,128)(2,1)S(1)} %bitcast.22), channel_id=1, source_target_pairs={{0,4},{4,8},{8,12},{1,5},{5,9},{9,13},{2,6},{6,10},{10,14},{3,7},{... | collective-permute-start | bytes 3145736 | tf_op jit(solution)/shard_map/ppermute | solution.py:105
  17.6 12.0 %prepare.1 = (f32[2,3584,512]{2,1,0:T(8,128)}, f32[64,512]{1,0:T(8,128)}) custom-call(bf16[512,3584]{1,0:T(8,128)(2,1)} %gate_ref.1, bf16[512,3584]{1,0:T(8,128)(2,1)} %up_ref.1, bf16[64,3584]{1,0:T(8,128)(2,1)} %bitcast.28, bf16[2,64,3584]{2,1,0:T(8,128)(2,1)} %get-tuple-element.30.refs_0_), custom_call_target="tpu_custom_call" | custom-call | flops 1 | bytes 1 | tf_op jit(solution)/shard_map/prepare/pallas_call | solution.py:132
  35.6 5.3 %collective-permute-start.10 = (bf16[1024,512]{1,0:T(8,128)(2,1)}, bf16[1024,512]{1,0:T(8,128)(2,1)}, u32[]{:S(2)}, u32[]{:S(2)}) collective-permute-start(bf16[1024,512]{1,0:T(8,128)(2,1)} %collective-permute-done.9.refs_1_), channel_id=1, source_target_pairs={{0,4},{4,8},{8,12},{1,5},{5,9},{9,13},{2,6},{6,10},{10,14},{3,7},{... | collective-permute-start | bytes 3145736 | tf_op jit(solution)/shard_map/ppermute | solution.py:105
  44.6 6.6 %collective-permute-done.1.refs_2_ = bf16[2,64,3584]{2,1,0:T(8,128)(2,1)} collective-permute-done((bf16[2,64,3584]{2,1,0:T(8,128)(2,1)}, bf16[2,64,3584]{2,1,0:T(8,128)(2,1)}, u32[]{:S(2)}, u32[]{:S(2)}) %collective-permute-start.1) | collective-permute-done | bytes 917536 | tf_op jit(solution)/shard_map/ppermute | solution.py:54
  56.6 4.0 %collective-permute-done.10.refs_2_ = bf16[1024,512]{1,0:T(8,128)(2,1)} collective-permute-done((bf16[1024,512]{1,0:T(8,128)(2,1)}, bf16[1024,512]{1,0:T(8,128)(2,1)}, u32[]{:S(2)}, u32[]{:S(2)}) %collective-permute-start.10) | collective-permute-done | bytes 1048608 | tf_op jit(solution)/shard_map/ppermute | solution.py:105
  60.6 5.1 %collective-permute-start.11 = (bf16[1024,512]{1,0:T(8,128)(2,1)}, bf16[1024,512]{1,0:T(8,128)(2,1)}, u32[]{:S(2)}, u32[]{:S(2)}) collective-permute-start(bf16[1024,512]{1,0:T(8,128)(2,1)} %collective-permute-done.10.refs_2_), channel_id=1, source_target_pairs={{0,4},{4,8},{8,12},{1,5},{5,9},{9,13},{2,6},{6,10},{10,14},{3,7},{... | collective-permute-start | bytes 3145736 | tf_op jit(solution)/shard_map/ppermute | solution.py:105
  78.1 12.0 %collective-permute-done.5.refs_2_ = bf16[2,64,3584]{2,1,0:T(8,128)(2,1)S(1)} collective-permute-done((bf16[2,64,3584]{2,1,0:T(8,128)(2,1)}, bf16[2,64,3584]{2,1,0:T(8,128)(2,1)S(1)}, u32[]{:S(2)}, u32[]{:S(2)}) %collective-permute-start.5) | collective-permute-done | bytes 917536 | tf_op jit(solution)/shard_map/ppermute | solution.py:54
  90.1 4.3 %collective-permute-done.6.refs_3_ = bf16[2,64,3584]{2,1,0:T(8,128)(2,1)S(1)} collective-permute-done((bf16[2,64,3584]{2,1,0:T(8,128)(2,1)}, bf16[2,64,3584]{2,1,0:T(8,128)(2,1)S(1)}, u32[]{:S(2)}, u32[]{:S(2)}) %collective-permute-start.6) | collective-permute-done | bytes 917536 | tf_op jit(solution)/shard_map/ppermute | solution.py:59
  97.5 26.9 %hidden_grads.1 = (bf16[2,3584,512]{2,1,0:T(8,128)(2,1)}, f32[64,512]{1,0:T(8,128)}) custom-call(s32[1]{0:T(128)} %bitcast.2.rank_ref, bf16[3584,4096]{1,0:T(8,128)(2,1)} %down_ref.1, f32[2,3584,512]{2,1,0:T(8,128)} %get-tuple-element.31.refs_3_.slope_ref, bf16[64,3584]{1,0:T(8,128)(2,1)} %bitcast.27, bf16[1024,512]{1,0:T(8,128)(2,1)} %bitcast.24, ...), custom_call_target="tpu_custom_call" | custom-call | flops 1 | bytes 1 | tf_op jit(solution)/shard_map/hidden_grads/pallas_call | solution.py:193
  124.5 5.5 %collective-permute-start.15 = (bf16[2,3584,512]{2,1,0:T(8,128)(2,1)}, bf16[2,3584,512]{2,1,0:T(8,128)(2,1)}, u32[]{:S(2)}, u32[]{:S(2)}) collective-permute-start(bf16[2,3584,512]{2,1,0:T(8,128)(2,1)} %get-tuple-element.42.refs_4_.refs_2_.refs_9_.refs_1_), channel_id=1, source_target_pairs={{0,1},{1,0},{2,3},{3,2},{4,5},{5,4},{6,7},{7,6},{8,9},{9,8},{10,11... | collective-permute-start | bytes 22020104 | tf_op jit(solution)/shard_map/ppermute | solution.py:48
  131.5 20.5 %collective-permute-done.7.refs_2_ = bf16[2,64,3584]{2,1,0:T(8,128)(2,1)} collective-permute-done((bf16[2,64,3584]{2,1,0:T(8,128)(2,1)S(1)}, bf16[2,64,3584]{2,1,0:T(8,128)(2,1)}, u32[]{:S(2)}, u32[]{:S(2)}) %collective-permute-start.7) | collective-permute-done | bytes 917536 | tf_op jit(solution)/shard_map/ppermute | solution.py:54
  156.2 13.9 %weigh_rows.6.refs_4_ = bf16[1024,512]{1,0:T(8,128)(2,1)} custom-call(bf16[1024,3584]{1,0:T(8,128)(2,1)} %refs_0_.17, bf16[1024,3584]{1,0:T(8,128)(2,1)} %refs_1_.17, bf16[2,3584,512]{2,1,0:T(8,128)(2,1)} %get-tuple-element.42.refs_4_.refs_2_.refs_9_.refs_1_, bf16[2,64,3584]{2,1,0:T(8,128)(2,1)} %get-tuple-element.48.refs_3_), custom_call_target="tpu_custom_call" | custom-call | flops 1 | bytes 1 | tf_op jit(solution)/shard_map/weigh_rows/pallas_call | solution.py:263
  177.3 13.6 %collective-permute-done.33 = bf16[1024,512]{1,0:T(8,128)(2,1)S(1)} collective-permute-done((bf16[1024,512]{1,0:T(8,128)(2,1)}, bf16[1024,512]{1,0:T(8,128)(2,1)S(1)}, u32[]{:S(2)}, u32[]{:S(2)}) %collective-permute-start.33) | collective-permute-done | bytes 1048608 | tf_op jit(solution)/shard_map/ppermute | solution.py:302
  194.1 3.1 collective-permute-start.20
  197.2 13.9 %weigh_rows.7.refs_5_ = bf16[1024,512]{1,0:T(8,128)(2,1)} custom-call(bf16[1024,3584]{1,0:T(8,128)(2,1)} %refs_0_.17, bf16[1024,3584]{1,0:T(8,128)(2,1)} %refs_1_.17, bf16[2,3584,512]{2,1,0:T(8,128)(2,1)} %collective-permute-done.15.refs_2_.refs_10_.refs_5_.refs_3_), custom_call_target="tpu_custom_call" | custom-call | flops 1 | bytes 1 | tf_op jit(solution)/shard_map/weigh_rows/pallas_call | solution.py:263
  214.1 17.2 %collective-permute-start.27 = (f32[16,512]{1,0:T(8,128)S(1)}, f32[16,512]{1,0:T(8,128)S(1)}, u32[]{:S(2)}, u32[]{:S(2)}) collective-permute-start(f32[16,512]{1,0:T(8,128)S(1)} %slice_select_fusion.2), channel_id=1, source_target_pairs={{0,4},{4,0},{8,12},{12,8},{1,5},{5,1},{9,13},{13,9},{2,6},{6,2},{1... | collective-permute-start | bytes 98312 | tf_op jit(solution)/shard_map/ppermute | solution.py:283
  234.9 14.8 %weigh_rows.8.refs_3_ = bf16[576,1024]{1,0:T(8,128)(2,1)} custom-call(bf16[2,64,3584]{2,1,0:T(8,128)(2,1)} %get-tuple-element.32.refs_0_, bf16[2,64,3584]{2,1,0:T(8,128)(2,1)} %get-tuple-element.35.refs_1_, bf16[2,64,3584]{2,1,0:T(8,128)(2,1)} %get-tuple-element.37.refs_2_, bf16[2,64,3584]{2,1,0:T(8,128)(2,1)} %get-tuple-element.39.refs_3_, ...), custom_call_target="tpu_custom_call" | custom-call | flops 1 | bytes 1 | tf_op jit(solution)/shard_map/weigh_rows/pallas_call | solution.py:263
  254.7 4.9 %collective-permute-start.24 = (bf16[2,64,3584]{2,1,0:T(8,128)(2,1)}, bf16[2,64,3584]{2,1,0:T(8,128)(2,1)}, u32[]{:S(2)}, u32[]{:S(2)}) collective-permute-start(bf16[2,64,3584]{2,1,0:T(8,128)(2,1)} %get-tuple-element.49.refs_11_), channel_id=1, source_target_pairs={{2,0},{3,1},{0,2},{1,3},{6,4},{7,5},{4,6},{5,7},{10,8},{11,9},{8,1... | collective-permute-start | bytes 2752520 | tf_op jit(solution)/shard_map/ppermute | solution.py:54
  261.9 11.0 %weigh_rows.9.refs_2_ = bf16[256,1024]{1,0:T(8,128)(2,1)} custom-call(bf16[2,64,3584]{2,1,0:T(8,128)(2,1)} %get-tuple-element.50.refs_0_, bf16[2,64,3584]{2,1,0:T(8,128)(2,1)} %get-tuple-element.51.refs_1_, bf16[2,64,3584]{2,1,0:T(8,128)(2,1)} %get-tuple-element.52.refs_2_, bf16[2,64,3584]{2,1,0:T(8,128)(2,1)} %get-tuple-element.53.refs_3_, ...), custom_call_target="tpu_custom_call" | custom-call | flops 1 | bytes 1 | tf_op jit(solution)/shard_map/weigh_rows/pallas_call | solution.py:263
  287.1 9.4 %weigh_rows.10 = bf16[128,1024]{1,0:T(8,128)(2,1)} custom-call(bf16[2,64,3584]{2,1,0:T(8,128)(2,1)} %get-tuple-element.54.refs_0_, bf16[2,64,3584]{2,1,0:T(8,128)(2,1)} %get-tuple-element.55.refs_1_, bf16[2,3584,512]{2,1,0:T(8,128)(2,1)} %get-tuple-element.42.refs_4_.refs_2_.refs_9_.refs_1_, ...), custom_call_target="tpu_custom_call" | custom-call | flops 1 | bytes 1 | tf_op jit(solution)/shard_map/weigh_rows/pallas_call | solution.py:263
  296.5 3.8 %collective-permute-start.28 = (bf16[128,1024]{1,0:T(8,128)(2,1)}, bf16[128,1024]{1,0:T(8,128)(2,1)S(1)}, u32[]{:S(2)}, u32[]{:S(2)}) collective-permute-start(bf16[128,1024]{1,0:T(8,128)(2,1)} %weigh_rows.10), channel_id=1, source_target_pairs={{4,0},{12,8},{1,5},{9,13},{6,2},{14,10},{3,7},{11,15},{20,16},{28,... | collective-permute-start | bytes 786440 | tf_op jit(solution)/shard_map/ppermute | solution.py:302
  307.2 9.6 %weigh_rows.11 = bf16[64,1024]{1,0:T(8,128)(2,1)} custom-call(bf16[2,64,3584]{2,1,0:T(8,128)(2,1)} %collective-permute-done.30.refs_0_, bf16[2,3584,512]{2,1,0:T(8,128)(2,1)} %get-tuple-element.42.refs_4_.refs_2_.refs_9_.refs_1_, bf16[2,3584,512]{2,1,0:T(8,128)(2,1)} %collective-permute-done.15.refs_2_.refs_10_.refs_5_.refs_3_), custom_call_target="tpu_custom_call" | custom-call | flops 1 | bytes 1 | tf_op jit(solution)/shard_map/weigh_rows/pallas_call | solution.py:263
  316.8 4.4 %collective-permute-start.31 = (bf16[64,1024]{1,0:T(8,128)(2,1)}, bf16[64,1024]{1,0:T(8,128)(2,1)S(1)}, u32[]{:S(2)}, u32[]{:S(2)}) collective-permute-start(bf16[64,1024]{1,0:T(8,128)(2,1)} %weigh_rows.11), channel_id=1, source_target_pairs={{4,0},{12,8},{1,5},{9,13},{6,2},{14,10},{3,7},{11,15},{20,16},{28,... | collective-permute-start | bytes 393224 | tf_op jit(solution)/shard_map/ppermute | solution.py:302
  328.6 30.6 %collective-permute-start.37 = (bf16[1024,512]{1,0:T(8,128)(2,1)}, bf16[1024,512]{1,0:T(8,128)(2,1)}, u32[]{:S(2)}, u32[]{:S(2)}) collective-permute-start(bf16[1024,512]{1,0:T(8,128)(2,1)} %slice.85), channel_id=1, source_target_pairs={{0,1},{1,0},{2,3},{3,2},{4,5},{5,4},{6,7},{7,6},{8,9},{9,8},{10,11... | collective-permute-start | bytes 3145736 | tf_op jit(solution)/shard_map/ppermute | solution.py:48
  (167 shorter events, 101.9 us)
Async XLA Ops:
  7.2 252.5 %all-gather.3.cloned.1.call-start = ((), (), s32[]{:S(2)}) async-start(), calls=%async_computation | async-start | bytes 1966080 | tf_op jit(solution)/shard_map/all_gather | solution.py:343
  10.6 24.9 %collective-permute-start.9 = (bf16[1024,512]{1,0:T(8,128)(2,1)S(1)}, bf16[1024,512]{1,0:T(8,128)(2,1)}, u32[]{:S(2)}, u32[]{:S(2)}) collective-permute-start(bf16[1024,512]{1,0:T(8,128)(2,1)S(1)} %bitcast.22), channel_id=1, source_target_pairs={{0,4},{4,8},{8,12},{1,5},{5,9},{9,13},{2,6},{6,10},{10,14},{3,7},{... | collective-permute-start | bytes 3145736 | tf_op jit(solution)/shard_map/ppermute | solution.py:105
  15.1 25.8 %collective-permute-start.12 = (bf16[1024,512]{1,0:T(8,128)(2,1)S(1)}, bf16[1024,512]{1,0:T(8,128)(2,1)}, u32[]{:S(2)}, u32[]{:S(2)}) collective-permute-start(bf16[1024,512]{1,0:T(8,128)(2,1)S(1)} %bitcast.23), channel_id=1, source_target_pairs={{4,0},{8,4},{12,8},{5,1},{9,5},{13,9},{6,2},{10,6},{14,10},{7,3},{... | collective-permute-start | bytes 3145736 | tf_op jit(solution)/shard_map/ppermute | solution.py:106
  16.4 34.9 %collective-permute-start.1 = (bf16[2,64,3584]{2,1,0:T(8,128)(2,1)}, bf16[2,64,3584]{2,1,0:T(8,128)(2,1)}, u32[]{:S(2)}, u32[]{:S(2)}) collective-permute-start(bf16[2,64,3584]{2,1,0:T(8,128)(2,1)} %get-tuple-element.33), channel_id=1, source_target_pairs={{2,0},{3,1},{0,2},{1,3},{6,4},{7,5},{4,6},{5,7},{10,8},{11,9},{8,1... | collective-permute-start | bytes 2752520 | tf_op jit(solution)/shard_map/ppermute | solution.py:54
  35.6 25.1 %collective-permute-start.10 = (bf16[1024,512]{1,0:T(8,128)(2,1)}, bf16[1024,512]{1,0:T(8,128)(2,1)}, u32[]{:S(2)}, u32[]{:S(2)}) collective-permute-start(bf16[1024,512]{1,0:T(8,128)(2,1)} %collective-permute-done.9.refs_1_), channel_id=1, source_target_pairs={{0,4},{4,8},{8,12},{1,5},{5,9},{9,13},{2,6},{6,10},{10,14},{3,7},{... | collective-permute-start | bytes 3145736 | tf_op jit(solution)/shard_map/ppermute | solution.py:105
  40.8 24.9 %collective-permute-start.13 = (bf16[1024,512]{1,0:T(8,128)(2,1)}, bf16[1024,512]{1,0:T(8,128)(2,1)}, u32[]{:S(2)}, u32[]{:S(2)}) collective-permute-start(bf16[1024,512]{1,0:T(8,128)(2,1)} %collective-permute-done.12.refs_4_), channel_id=1, source_target_pairs={{4,0},{8,4},{12,8},{5,1},{9,5},{13,9},{6,2},{10,6},{14,10},{7,3},{... | collective-permute-start | bytes 3145736 | tf_op jit(solution)/shard_map/ppermute | solution.py:106
  43.4 27.4 %collective-permute-start.3 = (bf16[2,64,3584]{2,1,0:T(8,128)(2,1)}, bf16[2,64,3584]{2,1,0:T(8,128)(2,1)S(1)}, u32[]{:S(2)}, u32[]{:S(2)}) collective-permute-start(bf16[2,64,3584]{2,1,0:T(8,128)(2,1)} %get-tuple-element.36), channel_id=1, source_target_pairs={{2,0},{3,1},{0,2},{1,3},{6,4},{7,5},{4,6},{5,7},{10,8},{11,9},{8,1... | collective-permute-start | bytes 2752520 | tf_op jit(solution)/shard_map/ppermute | solution.py:54
  60.6 36.9 %collective-permute-start.11 = (bf16[1024,512]{1,0:T(8,128)(2,1)}, bf16[1024,512]{1,0:T(8,128)(2,1)}, u32[]{:S(2)}, u32[]{:S(2)}) collective-permute-start(bf16[1024,512]{1,0:T(8,128)(2,1)} %collective-permute-done.10.refs_2_), channel_id=1, source_target_pairs={{0,4},{4,8},{8,12},{1,5},{5,9},{9,13},{2,6},{6,10},{10,14},{3,7},{... | collective-permute-start | bytes 3145736 | tf_op jit(solution)/shard_map/ppermute | solution.py:105
  65.7 31.8 %collective-permute-start.14 = (bf16[1024,512]{1,0:T(8,128)(2,1)}, bf16[1024,512]{1,0:T(8,128)(2,1)}, u32[]{:S(2)}, u32[]{:S(2)}) collective-permute-start(bf16[1024,512]{1,0:T(8,128)(2,1)} %collective-permute-done.13.refs_5_), channel_id=1, source_target_pairs={{4,0},{8,4},{12,8},{5,1},{9,5},{13,9},{6,2},{10,6},{14,10},{7,3},{... | collective-permute-start | bytes 3145736 | tf_op jit(solution)/shard_map/ppermute | solution.py:106
  67.0 23.1 %collective-permute-start.5 = (bf16[2,64,3584]{2,1,0:T(8,128)(2,1)}, bf16[2,64,3584]{2,1,0:T(8,128)(2,1)S(1)}, u32[]{:S(2)}, u32[]{:S(2)}) collective-permute-start(bf16[2,64,3584]{2,1,0:T(8,128)(2,1)} %get-tuple-element.38), channel_id=1, source_target_pairs={{2,0},{3,1},{0,2},{1,3},{6,4},{7,5},{4,6},{5,7},{10,8},{11,9},{8,1... | collective-permute-start | bytes 2752520 | tf_op jit(solution)/shard_map/ppermute | solution.py:54
  124.5 72.7 %collective-permute-start.15 = (bf16[2,3584,512]{2,1,0:T(8,128)(2,1)}, bf16[2,3584,512]{2,1,0:T(8,128)(2,1)}, u32[]{:S(2)}, u32[]{:S(2)}) collective-permute-start(bf16[2,3584,512]{2,1,0:T(8,128)(2,1)} %get-tuple-element.42.refs_4_.refs_2_.refs_9_.refs_1_), channel_id=1, source_target_pairs={{0,1},{1,0},{2,3},{3,2},{4,5},{5,4},{6,7},{7,6},{8,9},{9,8},{10,11... | collective-permute-start | bytes 22020104 | tf_op jit(solution)/shard_map/ppermute | solution.py:48
  130.0 22.0 %collective-permute-start.7 = (bf16[2,64,3584]{2,1,0:T(8,128)(2,1)S(1)}, bf16[2,64,3584]{2,1,0:T(8,128)(2,1)}, u32[]{:S(2)}, u32[]{:S(2)}) collective-permute-start(bf16[2,64,3584]{2,1,0:T(8,128)(2,1)S(1)} %copy-done.24), channel_id=1, source_target_pairs={{2,0},{3,1},{0,2},{1,3},{6,4},{7,5},{4,6},{5,7},{10,8},{11,9},{8,1... | collective-permute-start | bytes 2752520 | tf_op jit(solution)/shard_map/ppermute | solution.py:54
  131.5 21.6 %collective-permute-start.8 = (bf16[2,64,3584]{2,1,0:T(8,128)(2,1)S(1)}, bf16[2,64,3584]{2,1,0:T(8,128)(2,1)S(1)}, u32[]{:S(2)}, u32[]{:S(2)}) collective-permute-start(bf16[2,64,3584]{2,1,0:T(8,128)(2,1)S(1)} %copy-done.14), channel_id=1, source_target_pairs={{16,0},{0,16},{17,1},{1,17},{18,2},{2,18},{19,3},{3,19},{20,4},{4,... | collective-permute-start | bytes 2752520 | tf_op jit(solution)/shard_map/ppermute | solution.py:59
  172.6 38.5 %collective-permute-start.16 = (bf16[2,64,3584]{2,1,0:T(8,128)(2,1)}, bf16[2,64,3584]{2,1,0:T(8,128)(2,1)}, u32[]{:S(2)}, u32[]{:S(2)}) collective-permute-start(bf16[2,64,3584]{2,1,0:T(8,128)(2,1)} %get-tuple-element.41.refs_7_), channel_id=1, source_target_pairs={{2,0},{3,1},{0,2},{1,3},{6,4},{7,5},{4,6},{5,7},{10,8},{11,9},{8,1... | collective-permute-start | bytes 2752520 | tf_op jit(solution)/shard_map/ppermute | solution.py:54
  173.6 37.4 %collective-permute-start.17 = (bf16[2,64,3584]{2,1,0:T(8,128)(2,1)}, bf16[2,64,3584]{2,1,0:T(8,128)(2,1)}, u32[]{:S(2)}, u32[]{:S(2)}) collective-permute-start(bf16[2,64,3584]{2,1,0:T(8,128)(2,1)} %get-tuple-element.43.refs_4_), channel_id=1, source_target_pairs={{16,0},{0,16},{17,1},{1,17},{18,2},{2,18},{19,3},{3,19},{20,4},{4,... | collective-permute-start | bytes 2752520 | tf_op jit(solution)/shard_map/ppermute | solution.py:59
  192.4 59.8 %collective-permute-start.34 = (bf16[1024,512]{1,0:T(8,128)(2,1)S(1)}, bf16[1024,512]{1,0:T(8,128)(2,1)}, u32[]{:S(2)}, u32[]{:S(2)}) collective-permute-start(bf16[1024,512]{1,0:T(8,128)(2,1)S(1)} %add_convert_fusion.5), channel_id=1, source_target_pairs={{8,0},{13,5},{2,10},{7,15},{24,16},{29,21},{18,26},{23,31}} | collective-permute-start | bytes 3145736 | tf_op jit(solution)/shard_map/ppermute | solution.py:302
  194.1 65.6 %collective-permute-start.20 = (bf16[2,64,3584]{2,1,0:T(8,128)(2,1)}, bf16[2,64,3584]{2,1,0:T(8,128)(2,1)S(1)}, u32[]{:S(2)}, u32[]{:S(2)}) collective-permute-start(bf16[2,64,3584]{2,1,0:T(8,128)(2,1)} %get-tuple-element.48.refs_3_), channel_id=1, source_target_pairs={{2,0},{3,1},{0,2},{1,3},{6,4},{7,5},{4,6},{5,7},{10,8},{11,9},{8,1... | collective-permute-start | bytes 2752520 | tf_op jit(solution)/shard_map/ppermute | solution.py:54
  213.2 46.4 %collective-permute-start.21 = (bf16[2,64,3584]{2,1,0:T(8,128)(2,1)}, bf16[2,64,3584]{2,1,0:T(8,128)(2,1)}, u32[]{:S(2)}, u32[]{:S(2)}) collective-permute-start(bf16[2,64,3584]{2,1,0:T(8,128)(2,1)} %get-tuple-element.50.refs_0_), channel_id=1, source_target_pairs={{16,0},{0,16},{17,1},{1,17},{18,2},{2,18},{19,3},{3,19},{20,4},{4,... | collective-permute-start | bytes 2752520 | tf_op jit(solution)/shard_map/ppermute | solution.py:59
  232.0 42.7 %collective-permute-start.35 = (bf16[1024,512]{1,0:T(8,128)(2,1)S(1)}, bf16[1024,512]{1,0:T(8,128)(2,1)}, u32[]{:S(2)}, u32[]{:S(2)}) collective-permute-start(bf16[1024,512]{1,0:T(8,128)(2,1)S(1)} %copy-done.3), channel_id=1, source_target_pairs={{4,0},{12,8},{1,5},{9,13},{6,2},{14,10},{3,7},{11,15},{20,16},{28,... | collective-permute-start | bytes 3145736 | tf_op jit(solution)/shard_map/ppermute | solution.py:302
  249.7 32.8 %collective-permute-start.18 = (bf16[576,1024]{1,0:T(8,128)(2,1)}, bf16[576,1024]{1,0:T(8,128)(2,1)}, u32[]{:S(2)}, u32[]{:S(2)}) collective-permute-start(bf16[576,1024]{1,0:T(8,128)(2,1)} %weigh_rows.8.refs_3_), channel_id=1, source_target_pairs={{4,0},{12,8},{1,5},{9,13},{6,2},{14,10},{3,7},{11,15},{20,16},{28,... | collective-permute-start | bytes 3538952 | tf_op jit(solution)/shard_map/ppermute | solution.py:302
  254.7 32.4 %collective-permute-start.24 = (bf16[2,64,3584]{2,1,0:T(8,128)(2,1)}, bf16[2,64,3584]{2,1,0:T(8,128)(2,1)}, u32[]{:S(2)}, u32[]{:S(2)}) collective-permute-start(bf16[2,64,3584]{2,1,0:T(8,128)(2,1)} %get-tuple-element.49.refs_11_), channel_id=1, source_target_pairs={{2,0},{3,1},{0,2},{1,3},{6,4},{7,5},{4,6},{5,7},{10,8},{11,9},{8,1... | collective-permute-start | bytes 2752520 | tf_op jit(solution)/shard_map/ppermute | solution.py:54
  260.6 26.5 %collective-permute-start.25 = (bf16[2,64,3584]{2,1,0:T(8,128)(2,1)}, bf16[2,64,3584]{2,1,0:T(8,128)(2,1)}, u32[]{:S(2)}, u32[]{:S(2)}) collective-permute-start(bf16[2,64,3584]{2,1,0:T(8,128)(2,1)} %get-tuple-element.51.refs_1_), channel_id=1, source_target_pairs={{16,0},{0,16},{17,1},{1,17},{18,2},{2,18},{19,3},{3,19},{20,4},{4,... | collective-permute-start | bytes 2752520 | tf_op jit(solution)/shard_map/ppermute | solution.py:59
  277.3 23.4 %collective-permute-start.36 = (bf16[1024,512]{1,0:T(8,128)(2,1)}, bf16[1024,512]{1,0:T(8,128)(2,1)}, u32[]{:S(2)}, u32[]{:S(2)}) collective-permute-start(bf16[1024,512]{1,0:T(8,128)(2,1)} %add_convert_fusion.3), channel_id=1, source_target_pairs={{8,0},{13,5},{2,10},{7,15},{24,16},{29,21},{18,26},{23,31}} | collective-permute-start | bytes 3145736 | tf_op jit(solution)/shard_map/ppermute | solution.py:302
  328.6 33.2 %collective-permute-start.37 = (bf16[1024,512]{1,0:T(8,128)(2,1)}, bf16[1024,512]{1,0:T(8,128)(2,1)}, u32[]{:S(2)}, u32[]{:S(2)}) collective-permute-start(bf16[1024,512]{1,0:T(8,128)(2,1)} %slice.85), channel_id=1, source_target_pairs={{0,1},{1,0},{2,3},{3,2},{4,5},{5,4},{6,7},{7,6},{8,9},{9,8},{10,11... | collective-permute-start | bytes 3145736 | tf_op jit(solution)/shard_map/ppermute | solution.py:48
  (43 other events, 521.6 us)
Sparse Core Ops, SparseCore 0:
  172.5 42.1 all-gather.2

commit v4 on v3

v4 whole, which is shorter than its diff:
```python
import functools

import jax
import jax.numpy as jnp
import numpy as np
from jax import lax
from jax.experimental import pallas as pl
from jax.experimental.pallas import tpu as pltpu
from jax.sharding import PartitionSpec as P

CORES = 2
CHUNKS = 8
VMEM_BYTES = 60 * 1024 * 1024
FLOPS_PER_US = 270_000_000
ANYWHERE = pl.BlockSpec(memory_space=pl.ANY)


def contract_right(left, right):
    return lax.dot_general(
        left, right, (((1,), (1,)), ((), ())), preferred_element_type=jnp.float32
    )


def project(proj, rows):
    return lax.dot_general(
        proj, rows, (((0,), (1,)), ((), ())), preferred_element_type=jnp.float32
    )


def pack_table(doc_lengths, count):
    lengths = doc_lengths[0]
    ends = jnp.cumsum(lengths)
    starts = ends - lengths
    position = jnp.arange(count, dtype=jnp.int32)[None, :]
    inside = (position >= starts[:, None]) & (position < ends[:, None])
    return inside.astype(jnp.bfloat16)


def doc_outer(member, grad_rows, inputs):
    count = member.shape[1]
    weighted = (member[:, None, :] * grad_rows[None, :, :]).reshape(-1, count)
    table = contract_right(weighted, inputs)
    return table.reshape(member.shape[0], grad_rows.shape[0] * inputs.shape[0])


def swap_cores(value):
    size = lax.axis_size("dp")
    return lax.ppermute(value, "dp", [(i, i ^ 1) for i in range(size)])


def from_chip(value, shift):
    size = lax.axis_size("dp")
    step = shift * CORES
    return lax.ppermute(value, "dp", [((i + step) % size, i) for i in range(size)])


def from_group(value, shift):
    size = lax.axis_size("groups")
    return lax.ppermute(value, "groups", [((i + shift) % size, i) for i in range(size)])


def cost(us):
    return pl.CostEstimate(flops=int(us * FLOPS_PER_US) + 1, bytes_accessed=1, transcendentals=0)


def widest(size, options):
    return next((w for w in options if size % w == 0), size)


def share_rows(w_gate, w_up, group, places, piece, carried, after):
    rows, width = w_gate.shape
    tile = widest(width, (1792, 896, 128))
    kept, waits, fresh = len(carried), len(after), len(places)
    per_group = rows // lax.axis_size("groups") // piece

    def kernel(group_ref, *refs):
        outs = refs[len(refs) - fresh :] if fresh else []
        for at, out in enumerate(outs):
            out[0] = refs[2 * at][...]
            out[1] = refs[2 * at + 1][...]
        if not fresh:
            refs[-1][...] = jnp.zeros_like(refs[-1])

    specs = []
    for k in places:
        at_chunk = functools.partial(lambda k, i, g: (g[0] * per_group + k, i), k)
        specs += [pl.BlockSpec((piece, tile), at_chunk)] * 2
    results = pl.pallas_call(
        kernel,
        grid_spec=pltpu.PrefetchScalarGridSpec(
            num_scalar_prefetch=1,
            grid=(width // tile if places else 1,),
            in_specs=specs + [ANYWHERE] * (kept + waits),
            out_specs=[ANYWHERE] * kept
            + [pl.BlockSpec((2, piece, tile), lambda i, g: (0, 0, i))] * fresh
            + [pl.BlockSpec((8, 128), lambda i, g: (0, 0))] * (not fresh),
        ),
        out_shape=[jax.ShapeDtypeStruct(a.shape, a.dtype) for a in carried]
        + [jax.ShapeDtypeStruct((2, piece, width), w_gate.dtype) for _ in places]
        + [jax.ShapeDtypeStruct((8, 128), jnp.float32)] * (not fresh),
        input_output_aliases={1 + 2 * fresh + i: i for i in range(kept)},
        compiler_params=pltpu.CompilerParams(vmem_limit_bytes=VMEM_BYTES),
        cost_estimate=cost(2),
        name="share_rows",
    )(group, *[w_gate, w_up] * fresh, *carried, *after)
    return list(results[:kept]), list(results[kept:])


def spread_ranks(value):
    ranks = lax.axis_size("tensor")
    below, above = [value], [value]
    for _ in range(1, ranks):
        below.append(lax.ppermute(below[-1], "tensor", [(i, i + 1) for i in range(ranks - 1)]))
        above.append(lax.ppermute(above[-1], "tensor", [(i + 1, i) for i in range(ranks - 1)]))
    return below, above[1:]


def prepare(gate_act, up_act, proj_h, after):
    count, hidden = gate_act.shape
    narrow = proj_h.shape[0]
    tile = widest(hidden, (512, 256, 128))

    def kernel(gate_ref, up_ref, proj_ref, *refs):
        slope_ref, down_ref = refs[-2:]

        @pl.when(pl.program_id(0) == 0)
        def _():
            down_ref[...] = jnp.zeros_like(down_ref)

        gate = gate_ref[...].astype(jnp.float32).T
        up = up_ref[...].astype(jnp.float32).T
        sigma = jax.nn.sigmoid(gate)
        swish = gate * sigma
        slope_ref[0] = up * sigma * (1.0 + gate * (1.0 - sigma))
        slope_ref[1] = swish
        down_ref[...] += jnp.dot(
            proj_ref[...], (swish * up).astype(jnp.bfloat16), preferred_element_type=jnp.float32
        )

    return pl.pallas_call(
        kernel,
        grid=(hidden // tile,),
        out_shape=[
            jax.ShapeDtypeStruct((2, hidden, count), jnp.float32),
            jax.ShapeDtypeStruct((narrow, count), jnp.float32),
        ],
        in_specs=[
            pl.BlockSpec((count, tile), lambda i: (0, i)),
            pl.BlockSpec((count, tile), lambda i: (0, i)),
            pl.BlockSpec((narrow, tile), lambda i: (0, i)),
        ]
        + [ANYWHERE] * len(after),
        out_specs=[
            pl.BlockSpec((2, tile, count), lambda i: (0, i, 0)),
            pl.BlockSpec((narrow, count), lambda i: (0, 0)),
        ],
        compiler_params=pltpu.CompilerParams(vmem_limit_bytes=VMEM_BYTES),
        cost_estimate=cost(12),
        name="prepare",
    )(gate_act, up_act, proj_h, *after)


def hidden_part(rank, below, above, w_down, first, so_far, slopes, proj_u, after):
    ranks = lax.axis_size("tensor")
    features, count = (below or above)[0].shape
    hidden = w_down.shape[0]
    far = first + len(above) - 1
    own = len(below) - len(above)
    places = own + min(2 * len(above), ranks - first)
    width = widest(features, (512, 256, 128))
    subs = features // width
    tile = widest(hidden, (512, 256, 128))
    finish = slopes is not None
    steps = places * subs
    total_steps = steps + (hidden // tile if finish else 0)

    def counts(z):
        span = far - first + 1
        under = jnp.clip(z - first + 1, 0, span)
        over = jnp.clip(ranks - z - first, 0, span)
        return under, over

    def column(i, rank_ref):
        z = rank_ref[0]
        under, over = counts(z)
        at = jnp.clip(i // subs, 0, jnp.maximum(own + under + over - 1, 0))
        block = jnp.where(at < own + under, z - first - (at - own), z + first + at - own - under)
        if own:
            block = jnp.where(at == 0, z, block)
        block = jnp.clip(block, 0, ranks - 1)
        sub = jnp.where(i // subs > at, subs - 1, lax.rem(i, subs))
        return (0, block * subs + sub)

    def kernel(rank_ref, down_ref, *refs):
        z = rank_ref[0]
        under, over = counts(z)
        sources = refs[: len(below) + len(above)]
        grad_ref, total, sem = refs[-3:]
        i = pl.program_id(0)

        def gather(wait):
            pieces = [(sources[at], True, at) for at in range(own)]
            for t in range(len(above)):
                pieces.append((sources[own + t], t < under, own + t))
                pieces.append((sources[len(below) + t], t < over, own + under + t))
            for at, (source, valid, place) in enumerate(pieces):

                @pl.when(valid)
                def _():
                    rows = pl.ds(pl.multiple_of(place * features, features), features)
                    copy = pltpu.make_async_copy(source, grad_ref.at[rows, :], sem.at[at])
                    copy.wait() if wait else copy.start()

        rest = refs[len(below) + len(above) :]

        @pl.when(i == 0)
        def _():
            gather(False)
            if so_far is not None:
                load = pltpu.make_async_copy(rest[0], total, sem.at[len(sources)])
                load.start()
                load.wait()
            else:
                total[...] = jnp.zeros_like(total)
            gather(True)

        @pl.when((i < steps) & (i // subs < own + under + over))
        def _():
            rows = pl.ds(pl.multiple_of(i * width, width), width)
            total[...] += jnp.dot(
                down_ref[...], grad_ref[rows, :], preferred_element_type=jnp.float32
            )

        if not finish:
            out = refs[-4]

            @pl.when(i == total_steps - 1)
            def _():
                store = pltpu.make_async_copy(total, out, sem.at[len(sources)])
                store.start()
                store.wait()

        else:
            slope_ref, proj_ref = rest[1:3]
            both_ref, out_ref = refs[-5:-3]

            @pl.when(i == 0)
            def _():
                out_ref[...] = jnp.zeros_like(out_ref)

            @pl.when(i >= steps)
            def _():
                rows = pl.ds(pl.multiple_of((i - steps) * tile, tile), tile)
                wide = total[rows, :]
                both_ref[0] = (wide * slope_ref[0]).astype(jnp.bfloat16)
                up_grad = (wide * slope_ref[1]).astype(jnp.bfloat16)
                both_ref[1] = up_grad
                out_ref[...] += jnp.dot(proj_ref[...], up_grad, preferred_element_type=jnp.float32)

    operands = [w_down, *below, *above]
    specs = [pl.BlockSpec((hidden, width), column)] + [ANYWHERE] * (len(below) + len(above))
    if so_far is not None:
        operands.append(so_far)
        specs.append(ANYWHERE)
    if finish:
        narrow = proj_u.shape[0]
        row = lambda i: jnp.maximum(i - steps, 0)
        operands += [slopes, proj_u]
        specs += [
            pl.BlockSpec((2, tile, count), lambda i, r: (0, row(i), 0)),
            pl.BlockSpec((narrow, tile), lambda i, r: (0, row(i))),
        ]
        out_shape = [
            jax.ShapeDtypeStruct((2, hidden, count), jnp.bfloat16),
            jax.ShapeDtypeStruct((narrow, count), jnp.float32),
        ]
        out_specs = [
            pl.BlockSpec((2, tile, count), lambda i, r: (0, row(i), 0)),
            pl.BlockSpec((narrow, count), lambda i, r: (0, 0)),
        ]
    else:
        out_shape = jax.ShapeDtypeStruct((hidden, count), jnp.float32)
        out_specs = ANYWHERE
    return pl.pallas_call(
        kernel,
        grid_spec=pltpu.PrefetchScalarGridSpec(
            num_scalar_prefetch=1,
            grid=(total_steps,),
            in_specs=specs + [ANYWHERE] * len(after),
            out_specs=out_specs,
            scratch_shapes=[
                pltpu.VMEM((places * features, count), jnp.bfloat16),
                pltpu.VMEM((hidden, count), jnp.float32),
                pltpu.SemaphoreType.DMA((len(below) + len(above) + 1,)),
            ],
        ),
        out_shape=out_shape,
        compiler_params=pltpu.CompilerParams(vmem_limit_bytes=VMEM_BYTES),
        cost_estimate=cost(15 if finish else 12),
        name="hidden_part",
    )(rank, *operands, *after)


def weigh(routes, grads, after, price):
    hidden = grads[0].shape[1]
    tile = widest(hidden, (512, 256, 128))
    steps = hidden // tile
    heights = [sum(u[0].shape[-2] for u in units) for units in routes]
    rows, count = sum(heights), sum(g.shape[2] for g in grads)
    units = [u for route in routes for u in route]
    flat = [w for u in units for w in u]

    def kernel(*refs):
        weights, both = list(refs[: len(flat)]), refs[len(flat) : len(flat) + len(grads)]
        outs, total = refs[-1 - len(routes) : -1], refs[-1]
        at = pl.program_id(0)

        @pl.when(at == 0)
        def _():
            total[...] = jnp.zeros_like(total)

        gates, ups = [], []
        for u in units:
            mine, weights = weights[: len(u)], weights[len(u) :]
            gates.append(mine[0][...] if len(u) == 2 else mine[0][0])
            ups.append(mine[1][...] if len(u) == 2 else mine[0][1])
        gate, up = jnp.concatenate(gates, axis=0), jnp.concatenate(ups, axis=0)
        first = 0
        for ref in both:
            span = slice(first, first + ref.shape[2])
            total[:, span] += jnp.dot(
                gate, ref[0], preferred_element_type=jnp.float32
            ) + jnp.dot(up, ref[1], preferred_element_type=jnp.float32)
            first += ref.shape[2]

        @pl.when(at == steps - 1)
        def _():
            top = 0
            for out, height in zip(outs, heights):
                out[...] = total[top : top + height].astype(jnp.bfloat16)
                top += height

    specs = []
    for w in flat:
        if w.ndim == 2:
            specs.append(pl.BlockSpec((w.shape[0], tile), lambda i: (0, i)))
        else:
            specs.append(pl.BlockSpec((2, w.shape[1], tile), lambda i: (0, 0, i)))
    for g in grads:
        specs.append(pl.BlockSpec((2, tile, g.shape[2]), lambda i: (0, i, 0)))
    return pl.pallas_call(
        kernel,
        grid=(steps,),
        out_shape=[jax.ShapeDtypeStruct((h, count), jnp.bfloat16) for h in heights],
        in_specs=specs + [ANYWHERE] * len(after),
        out_specs=[pl.BlockSpec((h, count), lambda i: (0, 0)) for h in heights],
        scratch_shapes=[pltpu.VMEM((rows, count), jnp.float32)],
        compiler_params=pltpu.CompilerParams(vmem_limit_bytes=VMEM_BYTES),
        cost_estimate=cost(price),
        name="weigh_rows",
    )(*flat, *grads, *after)


def add(values, others, heights, after):
    pairs = len(values)
    flat = [h for hs in heights for h in hs]

    def kernel(*refs):
        outs = list(refs[len(refs) - len(flat) :])
        for at in range(pairs):
            top = 0
            for height in heights[at]:
                rows = slice(top, top + height)
                outs.pop(0)[...] = (
                    refs[at][rows].astype(jnp.float32) + refs[pairs + at][rows].astype(jnp.float32)
                ).astype(jnp.bfloat16)
                top += height

    count = values[0].shape[1]
    width = widest(count, (128,))
    specs = [pl.BlockSpec((v.shape[0], width), lambda i: (0, i)) for v in values]
    return pl.pallas_call(
        kernel,
        grid=(count // width,),
        out_shape=[jax.ShapeDtypeStruct((h, count), jnp.bfloat16) for h in flat],
        in_specs=specs + specs + [ANYWHERE] * len(after),
        out_specs=[pl.BlockSpec((h, width), lambda i: (0, i)) for h in flat],
        compiler_params=pltpu.CompilerParams(vmem_limit_bytes=VMEM_BYTES),
        cost_estimate=cost(2),
        name="add_terms",
    )(*values, *others, *after)


def exchange(value, bit):
    ranks = lax.axis_size("tensor")
    return lax.ppermute(value, "tensor", [(i, i ^ bit) for i in range(ranks)])


def halve(value, bit):
    half = value.shape[0] // 2
    high = lax.axis_index("tensor") & bit != 0
    low_rows, high_rows = value[:half], value[half:]
    got = exchange(jnp.where(high, low_rows, high_rows), bit)
    return jnp.where(high, high_rows, low_rows) + got


def toward(value, owner, bit):
    groups, ranks, blocks = (lax.axis_size(a) for a in ("groups", "tensor", "dp"))
    pairs = []
    for g in range(groups):
        for p in range(blocks):
            target = owner[g, p]
            for z in range(ranks):
                if z % bit == target % bit and (z ^ target) & bit:
                    pairs.append(((g * ranks + z) * blocks + p, (g * ranks + (z ^ bit)) * blocks + p))
    return lax.ppermute(value, ("groups", "tensor", "dp"), pairs)


def later_steps(value, owner):
    bit = 2
    got = None
    while bit < lax.axis_size("tensor"):
        if got is not None:
            (value,) = add([value], [got], [[value.shape[0]]], [])
        got = toward(value, owner, bit)
        bit *= 2
    return value, got


def per_device(
    layer_input,
    gate_act,
    up_act,
    out_grad,
    w_gate,
    w_up,
    w_down,
    proj_x,
    proj_u,
    proj_h,
    proj_g,
    doc_lengths,
):
    groups, ranks = lax.axis_size("groups"), lax.axis_size("tensor")
    blocks = lax.axis_size("dp")
    chips = blocks // CORES
    group, rank = lax.axis_index("groups"), lax.axis_index("tensor")
    place = lax.axis_index("dp")
    chip, core = place // CORES, place % CORES
    rows = w_gate.shape[0]
    count = layer_input.shape[0]
    features = out_grad.shape[1]
    part = rows // groups
    piece = part // CHUNKS
    split = max(1, ranks // blocks)
    group_word = jnp.full((1,), group, jnp.int32)
    rank_word = jnp.full((1,), rank, jnp.int32)

    below, above = spread_ranks(out_grad.T)
    _, shares = share_rows(w_gate, w_up, group_word, [0, 1], piece, [], [])
    slopes, in_down_part = prepare(gate_act, up_act, proj_h.T, [shares[0]])
    early_part = jnp.concatenate([project(proj_x, layer_input), in_down_part], axis=0)
    out_down_part = project(proj_g, out_grad)
    fetched, ticks = {}, []

    def fetch(k):
        for s in range(1, chips):
            fetched[k, s, 0] = from_chip(shares[k], s)
            for r in range(1, groups):
                fetched[k, s, r] = from_group(fetched[k, s, 0], r)

    def forward(k, after, held=()):
        waits = [fetched[n] for n in fetched if n[0] == k and n[2] == 0]
        waits += [fetched[n] for n in fetched if n[0] == k - 1 and n[2] > 0]
        waits = [w for w in waits if not any(w is h for h in held)]
        places = [k + 2] if k + 2 < CHUNKS else []
        carried, fresh = share_rows(
            w_gate, w_up, group_word, places, piece, list(held), waits + list(after)
        )
        ticks.append(fresh[0])
        if places:
            shares.extend(fresh)
            fetch(k + 2)
        return carried

    def owner_of(s, first_of):
        table = np.zeros((groups, blocks), np.int64)
        for g in range(groups):
            for p in range(blocks):
                block = (p // CORES + s) % chips * CORES + p % CORES
                table[g, p] = (block * rows + first_of(g)) // features
        return table

    far_routes = []
    for s in range(1, chips):
        for r in range(groups):
            table = owner_of(s, lambda g: (g + r) % groups * part)
            for route in far_routes:
                if route[0] == s and (route[1] == table).all():
                    route[2].append(r)
                    break
            else:
                far_routes.append((s, table, [r]))
    height = rows // split
    near_tables = [owner_of(0, lambda g: j * height) for j in range(split)]
    near_routes = [
        [(w_gate[j * height : (j + 1) * height], w_up[j * height : (j + 1) * height])]
        for j in range(split)
    ]

    def terms(names, grads, after, price, near=False):
        routes = list(zip(near_tables, near_routes, [None] * split)) if near else []
        for s, table, shifts in far_routes:
            units = [(k, s, q) for k, q in names if q in shifts]
            if units:
                routes.append((table, [(fetched[n],) for n in units], units))
        bundles = {}
        for route in routes:
            bundles.setdefault((route[0] % 2).tobytes(), []).append(route)
        bundles = list(bundles.values())
        outs = list(weigh([[u for _, units, _ in b for u in units] for b in bundles], grads, after, price))
        got = [toward(out, b[0][0], 1) for out, b in zip(outs, bundles)]
        return outs, got, bundles

    def carry_on(work, after):
        outs, got, bundles = work
        heights = [[sum(u[0].shape[-2] for u in units) for _, units, _ in b] for b in bundles]
        sums = list(add(outs, got, heights, after))
        ends, at = [], 0
        for b in bundles:
            for table, _, names in b:
                ends.append((names, *later_steps(sums[at], table)))
                at += 1
        return sums, ends

    fetch(0)
    fetch(1)
    forward(0, [slopes])
    forward(1, [early_part, out_down_part])
    forward(2, [])
    so_far = hidden_part(
        rank_word, below[:2], above[:1], w_down, 1, None, None, None, [ticks[2]]
    )
    forward(3, [so_far])
    mine, up_out_part = hidden_part(
        rank_word, below[2:], above[1:], w_down, 2, so_far, slopes, proj_u.T, [ticks[3]]
    )
    bits = [1 << i for i in range(ranks.bit_length() - 1)]
    early = early_part + exchange(early_part, bits[0])
    (mine,) = forward(4, [early], [mine])
    theirs = swap_cores(mine)
    for bit in bits[1:]:
        early = early + exchange(early, bit)
    first_names = [(k, 0) for k in range(5)] + [(k, 1) for k in range(4)]
    first_mine = terms(first_names, [mine], [ticks[4]], 30, near=True)
    (up_out_part,) = forward(5, first_mine[0] + [early], [up_out_part])
    first_theirs = terms(first_names, [theirs], [ticks[5]], 30, near=True)
    sums_mine, end_mine = carry_on(first_mine, first_theirs[0])
    out_parts = jnp.stack([up_out_part, out_down_part]).reshape(2, ranks, -1, count)
    out_parts = halve(out_parts.transpose(1, 0, 2, 3), bits[-1])
    forward(6, sums_mine + [out_parts])
    second_names = [(5, 0), (6, 0), (4, 1), (5, 1)]
    second = terms(second_names, [mine, theirs], [ticks[6]], 18)
    sums_theirs, end_theirs = carry_on(first_theirs, second[0])
    for bit in bits[-2::-1]:
        out_parts = halve(out_parts, bit)
    last_arrived = [(CHUNKS - 1, s, 0) for s in range(1, chips)]
    held = forward(7, sums_theirs + [out_parts], [fetched[n] for n in last_arrived])
    for n, value in zip(last_arrived, held):
        fetched[n] = value
        for r in range(1, groups):
            fetched[n[0], n[1], r] = from_group(value, r)
    third_names = [(7, 0), (6, 1)]
    received = [got for _, _, got in end_mine if got is not None]
    third = terms(third_names, [mine, theirs], [ticks[7]] + received, 0)
    sums_second, end_second = carry_on(second, third[0])

    early = early.astype(jnp.bfloat16)
    width = in_down_part.shape[0]
    in_up, in_down = early[:width], early[width:]
    out_parts = out_parts.astype(jnp.bfloat16)
    up_out, out_down = out_parts[0, 0], out_parts[0, 1]
    member = pack_table(doc_lengths, count)
    doc_logs = jnp.stack(
        [doc_outer(member, up_out, in_up), doc_outer(member, out_down, in_down)], axis=1
    )

    def settle(v, got):
        if got is None:
            return v
        return (v.astype(jnp.float32) + got.astype(jnp.float32)).astype(jnp.bfloat16)

    def pick(index, options):
        value = options[0]
        for at, option in enumerate(options[1:], 1):
            value = jnp.where(index == at, option, value)
        return value

    first = rank * features
    away = (first // rows // CORES - chip) % chips
    owner = first // rows % CORES == core
    inside = first % rows
    tall = features // part
    shifts = [(inside // part + j - group) % groups for j in range(tall)]

    def in_order(near, far):
        options = [pick(inside // height, near)]
        for s in range(1, chips):
            by_shift = [
                jnp.concatenate([far[k, s, r] for k in range(CHUNKS)], axis=0)
                for r in range(groups)
            ]
            options.append(jnp.concatenate([pick(shift, by_shift) for shift in shifts], axis=0))
        return pick(away, options)

    near_half, far_half = [[], []], [{}, {}]
    for at, end in enumerate((end_mine, end_theirs)):
        for names, *pair in end:
            value = settle(*pair)
            if names is None:
                near_half[at].append(value)
            else:
                far_half[at].update(
                    (n, value[i * piece : (i + 1) * piece]) for i, n in enumerate(names)
                )

    sums_third, end_third = carry_on(third, [doc_logs])
    last_names = [(CHUNKS - 1, r) for r in range(1, groups)]
    received = [got for _, _, got in end_theirs if got is not None]
    last = terms(last_names, [mine, theirs], sums_third + received, 10)
    for names, *pair in end_second + end_third:
        value = settle(*pair)
        for i, n in enumerate(names):
            both = value[i * piece : (i + 1) * piece]
            far_half[0][n], far_half[1][n] = both[:, :count], both[:, count:]
    for s in range(1, chips):
        for _, r in last_names:
            for half in far_half:
                half[CHUNKS - 1, s, r] = jnp.zeros((piece, count), jnp.bfloat16)
    total_mine, total_theirs = (in_order(n, f) for n, f in zip(near_half, far_half))
    from_partner = swap_cores(total_theirs)
    _, end_last = carry_on(last, [])
    total = jnp.where(owner, total_mine, from_partner)

    tail = {}
    for names, *pair in end_last:
        value = settle(*pair)
        tail.update((n, value[i * piece : (i + 1) * piece]) for i, n in enumerate(names))
    pieces = jnp.concatenate(
        [
            pick(away - 1, [tail[k, s, r] for s in range(1, chips)])
            for k, r in last_names
        ],
        axis=0,
    )
    pieces = jnp.where(owner, pieces[:, :count], swap_cores(pieces[:, count:]))
    pieces = jnp.where(away > 0, pieces, jnp.zeros_like(pieces))
    parts = []
    for j, shift in enumerate(shifts):
        end = (j + 1) * part
        extra = jnp.zeros((piece, count), jnp.bfloat16)
        for at, (_, r) in enumerate(last_names):
            extra = jnp.where(shift == r, pieces[at * piece : (at + 1) * piece], extra)
        parts += [total[j * part : end - piece], total[end - piece : end] + extra]
    input_grad = jnp.concatenate(parts, axis=0).T
    return (input_grad, doc_logs)


def solution(mesh):
    placed = (
        P(("groups", "dp"), "tensor"),
        P(("groups", "dp"), "tensor"),
        P(("groups", "dp"), "tensor"),
        P(("groups", "dp"), "tensor"),
        P("dp", "tensor"),
        P("dp", "tensor"),
        P("tensor", None),
        P("tensor", None),
        P("tensor", None),
        P("tensor", None),
        P("tensor", None),
        P(("groups", "dp"), None),
    )
    return jax.shard_map(
        per_device,
        mesh=mesh,
        in_specs=placed,
        out_specs=(P(("groups", "dp"), "tensor"), P(("groups", "dp"), None, "tensor")),
        check_vma=False,
    )
```

time: 375 us -> 353 us (0.941)
  Pallas kernels: 127 us -> 157 us
  starting transfers between devices: 121 us -> 96.6 us
  between operations: 14.6 us -> 1.3 us
  other arithmetic: 21.8 us -> 12.1 us
  waiting for transfers between devices: 78.5 us -> 69.8 us
    ppermute x14 -> x16, waiting for transfers between devices: 17.8 us -> 48.4 us  [the longest x4 48 us: exchange(): return lax.ppermute(value, 'tensor', [(i, i ^ bit) for i in range(ranks)])]
    ppermute x8, waiting for transfers between devices: 43.6 us -> 13.2 us  [from_chip(): lax.ppermute(value, 'dp', [((i + step) % size, i) for i in range(size)])]
    pallas_call x7 -> x12, Pallas kernels: 99.4 us -> 128 us  [the longest x5 65.7 us: weigh(): pl.pallas_call(kernel, grid=(steps,), out_shape=[jax.ShapeDtypeStruct((h,...]
    ppermute x14 -> x16, starting transfers between devices: 44.8 us -> 31.1 us  [the longest x12 25.2 us: toward(): return lax.ppermute(value, ('groups', 'tensor', 'dp'), pairs)]
    convert_element_type x13 -> x7, other arithmetic: 15.5 us -> 4.09 us  [the longest x5 2.7 us: settle(): (v.astype(jnp.float32) + got.astype(jnp.float32)).astype(jnp.bfloat16)]
    ppermute x8, waiting for transfers between devices: 10.3 us -> 0.02 us  [from_group(): lax.ppermute(value, 'groups', [((i + shift) % size, i) for i in range(siz...]
    ppermute x8, starting transfers between devices: 14.3 us -> 6.63 us  [from_chip(): lax.ppermute(value, 'dp', [((i + step) % size, i) for i in range(size)])]
    unnamed x54 -> x68, local copies, waits for them, and re-layouts: 7.68 us -> 8.4 us
  transfers between devices with their start and end apart: 39 -> 41, of which waited for: 16 -> 8; matrix products, arithmetic and copies ran while one was open for 5% -> 5% of each run, Pallas kernels for 26% -> 42%
where the time goes in v4:
time: 353 us; the launch traced here: 350 us
  Pallas kernels  157 us (44%)
  starting transfers between devices  96.6 us (27%)
  waiting for transfers between devices  69.8 us (20%)
  other arithmetic  12.1 us (3%)
  local copies, waits for them, and re-layouts  10.2 us (3%)
  matrix products  3.67 us (1%)
    pallas_call x5, Pallas kernels, weigh(): pl.pallas_call(kernel, grid=(steps,), out_shape=[jax.ShapeDtypeStruct((h,...  65.7 us
    ppermute x4, waiting for transfers between devices, exchange(): return lax.ppermute(value, 'tensor', [(i, i ^ bit) for i in range(ranks)])  48 us
    pallas_call x2, Pallas kernels, hidden_part(): pl.pallas_call(kernel, grid_spec=pltpu.PrefetchScalarGridSpec(num_scalar_...  40.5 us
    ppermute x3, starting transfers between devices, swap_cores(): return lax.ppermute(value, 'dp', [(i, i ^ 1) for i in range(size)])  36.1 us
    ppermute x12, starting transfers between devices, toward(): return lax.ppermute(value, ('groups', 'tensor', 'dp'), pairs)  25.2 us
    pallas_call x5, Pallas kernels, add(): pl.pallas_call(kernel, grid=(count // width,), out_shape=[jax.ShapeDtypeS...  21.8 us
    pallas_call x9, Pallas kernels, share_rows(): pl.pallas_call(kernel, grid_spec=pltpu.PrefetchScalarGridSpec(num_scalar_...  16.9 us
    ppermute x8, waiting for transfers between devices, from_chip(): lax.ppermute(value, 'dp', [((i + step) % size, i) for i in range(size)])  13.2 us
  transfers between devices with their start and end apart: 41, of which 8 were waited for; matrix products, arithmetic and copies ran while one was open for 5% of the time, Pallas kernels for 42%

profile of v4, /device:TPU:3, one launch (start us, length us, event | category | flops | bytes accessed | tf_op | source)
XLA Modules:
  0.0 350.5 jit_solution(1402250765121078955)
XLA Ops:
  4.8 4.4 %collective-permute-start.9 = (bf16[1024,512]{1,0:T(8,128)(2,1)}, bf16[1024,512]{1,0:T(8,128)(2,1)}, u32[]{:S(2)}, u32[]{:S(2)}) collective-permute-start(bf16[1024,512]{1,0:T(8,128)(2,1)} %bitcast.3.refs_0_), channel_id=1, source_target_pairs={{0,4},{4,8},{8,12},{1,5},{5,9},{9,13},{2,6},{6,10},{10,14},{3,7},{... | collective-permute-start | bytes 3145736 | tf_op jit(solution)/shard_map/ppermute | solution.py:113
  11.8 13.2 %collective-permute-done.refs_2_ = bf16[2,64,3584]{2,1,0:T(8,128)(2,1)S(1)} collective-permute-done((bf16[2,64,3584]{2,1,0:T(8,128)(2,1)}, bf16[2,64,3584]{2,1,0:T(8,128)(2,1)S(1)}, u32[]{:S(2)}, u32[]{:S(2)}) %collective-permute-start) | collective-permute-done | bytes 917536 | tf_op jit(solution)/shard_map/ppermute | solution.py:54
  26.3 12.1 %prepare.1 = (f32[2,3584,512]{2,1,0:T(8,128)}, f32[64,512]{1,0:T(8,128)}) custom-call(bf16[512,3584]{1,0:T(8,128)(2,1)} %gate_ref.1, bf16[512,3584]{1,0:T(8,128)(2,1)} %up_ref.1, bf16[64,3584]{1,0:T(8,128)(2,1)} %bitcast.34, bf16[2,64,3584]{2,1,0:T(8,128)(2,1)} %get-tuple-element.18.refs_0_), custom_call_target="tpu_custom_call" | custom-call | flops 3240000000 | bytes 1 | tf_op jit(solution)/shard_map/prepare/pallas_call | solution.py:140
  38.3 4.2 %collective-permute-start.10 = (bf16[1024,512]{1,0:T(8,128)(2,1)}, bf16[1024,512]{1,0:T(8,128)(2,1)}, u32[]{:S(2)}, u32[]{:S(2)}) collective-permute-start(bf16[1024,512]{1,0:T(8,128)(2,1)} %collective-permute-done.9.refs_1_), channel_id=1, source_target_pairs={{0,4},{4,8},{8,12},{1,5},{5,9},{9,13},{2,6},{6,10},{10,14},{3,7},{... | collective-permute-start | bytes 3145736 | tf_op jit(solution)/shard_map/ppermute | solution.py:113
  54.0 7.4 %collective-permute-done.10.refs_0_ = bf16[1024,512]{1,0:T(8,128)(2,1)} collective-permute-done((bf16[1024,512]{1,0:T(8,128)(2,1)}, bf16[1024,512]{1,0:T(8,128)(2,1)}, u32[]{:S(2)}, u32[]{:S(2)}) %collective-permute-start.10) | collective-permute-done | bytes 1048608 | tf_op jit(solution)/shard_map/ppermute | solution.py:113
  61.4 4.2 %collective-permute-start.11 = (bf16[1024,512]{1,0:T(8,128)(2,1)}, bf16[1024,512]{1,0:T(8,128)(2,1)S(1)}, u32[]{:S(2)}, u32[]{:S(2)}) collective-permute-start(bf16[1024,512]{1,0:T(8,128)(2,1)} %collective-permute-done.10.refs_0_), channel_id=1, source_target_pairs={{0,4},{4,8},{8,12},{1,5},{5,9},{9,13},{2,6},{6,10},{10,14},{3,7},{... | collective-permute-start | bytes 3145736 | tf_op jit(solution)/shard_map/ppermute | solution.py:113
  72.3 22.4 %collective-permute-done.15 = f32[128,512]{1,0:T(8,128)} collective-permute-done((f32[128,512]{1,0:T(8,128)}, f32[128,512]{1,0:T(8,128)}, u32[]{:S(2)}, u32[]{:S(2)}) %collective-permute-start.15) | collective-permute-done | bytes 262176 | tf_op jit(solution)/shard_map/ppermute | solution.py:396
  97.1 15.5 %hidden_part.2.refs_4_ = f32[3584,512]{1,0:T(8,128)} custom-call(s32[1]{0:T(128)} %bitcast.2.rank_ref, bf16[3584,4096]{1,0:T(8,128)(2,1)} %down_ref.3, bf16[1024,512]{1,0:T(8,128)(2,1)} %bitcast.3.refs_0_, bf16[1024,512]{1,0:T(8,128)(2,1)} %collective-permute-done.9.refs_1_, bf16[1024,512]{1,0:T(8,128)(2,1)} %collective-permute-done.12.refs_2_, ...), custom_call_target="tpu_custom_call" | custom-call | flops 3240000000 | bytes 1 | tf_op jit(solution)/shard_map/hidden_part/pallas_call | solution.py:284
  115.8 24.9 %hidden_part.3 = (bf16[2,3584,512]{2,1,0:T(8,128)(2,1)}, f32[64,512]{1,0:T(8,128)}) custom-call(s32[1]{0:T(128)} %bitcast.2.rank_ref, bf16[3584,4096]{1,0:T(8,128)(2,1)} %down_ref.3, bf16[1024,512]{1,0:T(8,128)(2,1)} %collective-permute-done.10.refs_0_, bf16[1024,512]{1,0:T(8,128)(2,1)} %copy-done.23, bf16[1024,512]{1,0:T(8,128)(2,1)} %collective-permute-done.13.refs_2_, ...), custom_call_target="tpu_custom_call" | custom-call | flops 4050000128 | bytes 1 | tf_op jit(solution)/shard_map/hidden_part/pallas_call | solution.py:284
  143.9 5.4 %collective-permute-start.17 = (bf16[2,3584,512]{2,1,0:T(8,128)(2,1)}, bf16[2,3584,512]{2,1,0:T(8,128)(2,1)}, u32[]{:S(2)}, u32[]{:S(2)}) collective-permute-start(bf16[2,3584,512]{2,1,0:T(8,128)(2,1)} %get-tuple-element.23.refs_11_.refs_4_.refs_2_.refs_1_), channel_id=1, source_target_pairs={{0,1},{1,0},{2,3},{3,2},{4,5},{5,4},{6,7},{7,6},{8,9},{9,8},{10,11... | collective-permute-start | bytes 22020104 | tf_op jit(solution)/shard_map/ppermute | solution.py:48
  153.4 9.7 %collective-permute-done.20 = f32[128,512]{1,0:T(8,128)S(1)} collective-permute-done((f32[128,512]{1,0:T(8,128)S(1)}, f32[128,512]{1,0:T(8,128)S(1)}, u32[]{:S(2)}, u32[]{:S(2)}) %collective-permute-start.20) | collective-permute-done | bytes 262176 | tf_op jit(solution)/shard_map/ppermute | solution.py:396
  163.9 18.1 %weigh_rows.5.refs_5_.refs_0_ = bf16[1600,512]{1,0:T(8,128)(2,1)} custom-call(bf16[1024,3584]{1,0:T(8,128)(2,1)} %refs_0_.17, bf16[1024,3584]{1,0:T(8,128)(2,1)} %refs_1_.17, bf16[2,64,3584]{2,1,0:T(8,128)(2,1)} %copy-done.2, bf16[2,64,3584]{2,1,0:T(8,128)(2,1)} %copy-done.3, bf16[2,64,3584]{2,1,0:T(8,128)(2,1)} %copy-done.4, ...), custom_call_target="tpu_custom_call" | custom-call | flops 8100000256 | bytes 1 | tf_op jit(solution)/shard_map/weigh_rows/pallas_call | solution.py:351
  190.7 18.2 %weigh_rows.6.refs_2_.refs_0_ = bf16[1600,512]{1,0:T(8,128)(2,1)} custom-call(bf16[1024,3584]{1,0:T(8,128)(2,1)} %refs_0_.17, bf16[1024,3584]{1,0:T(8,128)(2,1)} %refs_1_.17, bf16[2,64,3584]{2,1,0:T(8,128)(2,1)} %copy-done.2, bf16[2,64,3584]{2,1,0:T(8,128)(2,1)} %copy-done.3, bf16[2,64,3584]{2,1,0:T(8,128)(2,1)} %copy-done.4, ...), custom_call_target="tpu_custom_call" | custom-call | flops 8100000256 | bytes 1 | tf_op jit(solution)/shard_map/weigh_rows/pallas_call | solution.py:351
  213.9 15.9 %collective-permute-done.29 = f32[1,2,16,512]{3,2,1,0:T(8,128)S(1)} collective-permute-done((f32[1,2,16,512]{3,2,1,0:T(8,128)S(1)}, f32[1,2,16,512]{3,2,1,0:T(8,128)S(1)}, u32[]{:S(2)}, u32[]{:S(2)}) %collective-permute-start.29) | collective-permute-done | bytes 65568 | tf_op jit(solution)/shard_map/ppermute | solution.py:396
  239.7 10.9 %weigh_rows.7.refs_2_.refs_0_ = bf16[256,1024]{1,0:T(8,128)(2,1)} custom-call(bf16[2,64,3584]{2,1,0:T(8,128)(2,1)} %collective-permute-done.18.refs_3_.refs_0_, bf16[2,64,3584]{2,1,0:T(8,128)(2,1)} %copy-done.14, bf16[2,64,3584]{2,1,0:T(8,128)(2,1)} %copy-done.16, bf16[2,64,3584]{2,1,0:T(8,128)(2,1)} %copy-done.15, ...), custom_call_target="tpu_custom_call" | custom-call | flops 4860000256 | bytes 1 | tf_op jit(solution)/shard_map/weigh_rows/pallas_call | solution.py:351
  250.5 5.1 %collective-permute-start.25 = (bf16[256,1024]{1,0:T(8,128)(2,1)}, bf16[256,1024]{1,0:T(8,128)(2,1)S(1)}, u32[]{:S(2)}, u32[]{:S(2)}) collective-permute-start(bf16[256,1024]{1,0:T(8,128)(2,1)} %weigh_rows.7.refs_2_.refs_0_), channel_id=1, source_target_pairs={{4,0},{12,8},{1,5},{9,13},{6,2},{14,10},{3,7},{11,15},{20,16},{28,... | collective-permute-start | bytes 1572872 | tf_op jit(solution)/shard_map/ppermute | solution.py:416
  261.4 9.4 %weigh_rows.8.refs_2_.refs_0_ = bf16[128,1024]{1,0:T(8,128)(2,1)} custom-call(bf16[2,64,3584]{2,1,0:T(8,128)(2,1)} %get-tuple-element.32.refs_0_, bf16[2,64,3584]{2,1,0:T(8,128)(2,1)} %collective-permute-done.27.refs_1_, bf16[2,3584,512]{2,1,0:T(8,128)(2,1)} %get-tuple-element.23.refs_11_.refs_4_.refs_2_.refs_1_, ...), custom_call_target="tpu_custom_call" | custom-call | flops 1 | bytes 1 | tf_op jit(solution)/shard_map/weigh_rows/pallas_call | solution.py:351
  271.5 4.9 %add_terms.7 = bf16[256,1024]{1,0:T(8,128)(2,1)} custom-call(bf16[256,1024]{1,0:T(8,128)(2,1)} %weigh_rows.7.refs_2_.refs_0_, bf16[256,1024]{1,0:T(8,128)(2,1)} %copy-done.31, bf16[128,1024]{1,0:T(8,128)(2,1)} %weigh_rows.8.refs_2_.refs_0_), custom_call_target="tpu_custom_call" | custom-call | flops 540000000 | bytes 1 | tf_op jit(solution)/shard_map/add_terms/pallas_call | solution.py:382
  278.2 6.3 %collective-permute-start.32 = (bf16[128,1024]{1,0:T(8,128)(2,1)}, bf16[128,1024]{1,0:T(8,128)(2,1)}, u32[]{:S(2)}, u32[]{:S(2)}) collective-permute-start(bf16[128,1024]{1,0:T(8,128)(2,1)} %weigh_rows.8.refs_2_.refs_0_), channel_id=1, source_target_pairs={{4,0},{12,8},{1,5},{9,13},{6,2},{14,10},{3,7},{11,15},{20,16},{28,... | collective-permute-start | bytes 786440 | tf_op jit(solution)/shard_map/ppermute | solution.py:416
  287.4 4.5 %add_terms.8.refs_3_ = bf16[128,1024]{1,0:T(8,128)(2,1)} custom-call(bf16[128,1024]{1,0:T(8,128)(2,1)} %weigh_rows.8.refs_2_.refs_0_, bf16[128,1024]{1,0:T(8,128)(2,1)} %collective-permute-done.32.refs_1_, f32[8,2,1024]{2,1,0:T(2,128)} %pad_maximum_fusion.5.refs_2_), custom_call_target="tpu_custom_call" | custom-call | flops 540000000 | bytes 1 | tf_op jit(solution)/shard_map/add_terms/pallas_call | solution.py:382
  297.2 20.9 %collective-permute-start.36 = (bf16[1024,512]{1,0:T(8,128)(2,1)S(1)}, bf16[1024,512]{1,0:T(8,128)(2,1)}, u32[]{:S(2)}, u32[]{:S(2)}) collective-permute-start(bf16[1024,512]{1,0:T(8,128)(2,1)S(1)} %fusion.2), channel_id=1, source_target_pairs={{0,1},{1,0},{2,3},{3,2},{4,5},{5,4},{6,7},{7,6},{8,9},{9,8},{10,11... | collective-permute-start | bytes 3145736 | tf_op jit(solution)/shard_map/ppermute | solution.py:48
  318.2 9.2 %weigh_rows.9.refs_0_ = bf16[64,1024]{1,0:T(8,128)(2,1)} custom-call(bf16[2,64,3584]{2,1,0:T(8,128)(2,1)} %collective-permute-done.37.refs_0_, bf16[2,3584,512]{2,1,0:T(8,128)(2,1)} %get-tuple-element.23.refs_11_.refs_4_.refs_2_.refs_1_, bf16[2,3584,512]{2,1,0:T(8,128)(2,1)} %collective-permute-done.17.refs_11_.refs_5_.refs_3_.refs_2_, ...), custom_call_target="tpu_custom_call" | custom-call | flops 2700000000 | bytes 1 | tf_op jit(solution)/shard_map/weigh_rows/pallas_call | solution.py:351
  331.1 4.4 %add_terms.9 = bf16[64,1024]{1,0:T(8,128)(2,1)} custom-call(bf16[64,1024]{1,0:T(8,128)(2,1)} %weigh_rows.9.refs_0_, bf16[64,1024]{1,0:T(8,128)(2,1)} %collective-permute-done.38.refs_1_), custom_call_target="tpu_custom_call" | custom-call | flops 540000000 | bytes 1 | tf_op jit(solution)/shard_map/add_terms/pallas_call | solution.py:382
  337.4 9.7 %collective-permute-start.40 = (bf16[64,512]{1,0:T(8,128)(2,1)S(1)}, bf16[64,512]{1,0:T(8,128)(2,1)S(1)}, u32[]{:S(2)}, u32[]{:S(2)}) collective-permute-start(bf16[64,512]{1,0:T(8,128)(2,1)S(1)} %slice.171), channel_id=1, source_target_pairs={{0,1},{1,0},{2,3},{3,2},{4,5},{5,4},{6,7},{7,6},{8,9},{9,8},{10,11... | collective-permute-start | bytes 196616 | tf_op jit(solution)/shard_map/ppermute | solution.py:48
  (188 shorter events, 88.3 us)
Async XLA Ops:
  4.8 33.5 %collective-permute-start.9 = (bf16[1024,512]{1,0:T(8,128)(2,1)}, bf16[1024,512]{1,0:T(8,128)(2,1)}, u32[]{:S(2)}, u32[]{:S(2)}) collective-permute-start(bf16[1024,512]{1,0:T(8,128)(2,1)} %bitcast.3.refs_0_), channel_id=1, source_target_pairs={{0,4},{4,8},{8,12},{1,5},{5,9},{9,13},{2,6},{6,10},{10,14},{3,7},{... | collective-permute-start | bytes 3145736 | tf_op jit(solution)/shard_map/ppermute | solution.py:113
  9.2 33.3 %collective-permute-start.12 = (bf16[1024,512]{1,0:T(8,128)(2,1)}, bf16[1024,512]{1,0:T(8,128)(2,1)}, u32[]{:S(2)}, u32[]{:S(2)}) collective-permute-start(bf16[1024,512]{1,0:T(8,128)(2,1)} %bitcast.3.refs_0_), channel_id=1, source_target_pairs={{4,0},{8,4},{12,8},{5,1},{9,5},{13,9},{6,2},{10,6},{14,10},{7,3},{... | collective-permute-start | bytes 3145736 | tf_op jit(solution)/shard_map/ppermute | solution.py:114
  10.5 37.8 %collective-permute-start.1 = (bf16[2,64,3584]{2,1,0:T(8,128)(2,1)}, bf16[2,64,3584]{2,1,0:T(8,128)(2,1)S(1)}, u32[]{:S(2)}, u32[]{:S(2)}) collective-permute-start(bf16[2,64,3584]{2,1,0:T(8,128)(2,1)} %get-tuple-element.19), channel_id=1, source_target_pairs={{2,0},{3,1},{0,2},{1,3},{6,4},{7,5},{4,6},{5,7},{10,8},{11,9},{8,1... | collective-permute-start | bytes 2752520 | tf_op jit(solution)/shard_map/ppermute | solution.py:54
  25.0 25.6 %collective-permute-start.3 = (bf16[2,64,3584]{2,1,0:T(8,128)(2,1)S(1)}, bf16[2,64,3584]{2,1,0:T(8,128)(2,1)}, u32[]{:S(2)}, u32[]{:S(2)}) collective-permute-start(bf16[2,64,3584]{2,1,0:T(8,128)(2,1)S(1)} %collective-permute-done.refs_2_), channel_id=1, source_target_pairs={{16,0},{0,16},{17,1},{1,17},{18,2},{2,18},{19,3},{3,19},{20,4},{4,... | collective-permute-start | bytes 2752520 | tf_op jit(solution)/shard_map/ppermute | solution.py:59
  42.5 23.7 %collective-permute-start.13 = (bf16[1024,512]{1,0:T(8,128)(2,1)}, bf16[1024,512]{1,0:T(8,128)(2,1)}, u32[]{:S(2)}, u32[]{:S(2)}) collective-permute-start(bf16[1024,512]{1,0:T(8,128)(2,1)} %collective-permute-done.12.refs_2_), channel_id=1, source_target_pairs={{4,0},{8,4},{12,8},{5,1},{9,5},{13,9},{6,2},{10,6},{14,10},{7,3},{... | collective-permute-start | bytes 3145736 | tf_op jit(solution)/shard_map/ppermute | solution.py:114
  52.8 42.1 %collective-permute-start.4 = (bf16[2,64,3584]{2,1,0:T(8,128)(2,1)}, bf16[2,64,3584]{2,1,0:T(8,128)(2,1)S(1)}, u32[]{:S(2)}, u32[]{:S(2)}) collective-permute-start(bf16[2,64,3584]{2,1,0:T(8,128)(2,1)} %share_rows.11), channel_id=1, source_target_pairs={{2,0},{3,1},{0,2},{1,3},{6,4},{7,5},{4,6},{5,7},{10,8},{11,9},{8,1... | collective-permute-start | bytes 2752520 | tf_op jit(solution)/shard_map/ppermute | solution.py:54
  61.4 53.4 %collective-permute-start.11 = (bf16[1024,512]{1,0:T(8,128)(2,1)}, bf16[1024,512]{1,0:T(8,128)(2,1)S(1)}, u32[]{:S(2)}, u32[]{:S(2)}) collective-permute-start(bf16[1024,512]{1,0:T(8,128)(2,1)} %collective-permute-done.10.refs_0_), channel_id=1, source_target_pairs={{0,4},{4,8},{8,12},{1,5},{5,9},{9,13},{2,6},{6,10},{10,14},{3,7},{... | collective-permute-start | bytes 3145736 | tf_op jit(solution)/shard_map/ppermute | solution.py:113
  66.2 48.6 %collective-permute-start.14 = (bf16[1024,512]{1,0:T(8,128)(2,1)}, bf16[1024,512]{1,0:T(8,128)(2,1)}, u32[]{:S(2)}, u32[]{:S(2)}) collective-permute-start(bf16[1024,512]{1,0:T(8,128)(2,1)} %collective-permute-done.13.refs_2_), channel_id=1, source_target_pairs={{4,0},{8,4},{12,8},{5,1},{9,5},{13,9},{6,2},{10,6},{14,10},{7,3},{... | collective-permute-start | bytes 3145736 | tf_op jit(solution)/shard_map/ppermute | solution.py:114
  67.6 45.1 %collective-permute-start.7 = (bf16[2,64,3584]{2,1,0:T(8,128)(2,1)S(1)}, bf16[2,64,3584]{2,1,0:T(8,128)(2,1)}, u32[]{:S(2)}, u32[]{:S(2)}) collective-permute-start(bf16[2,64,3584]{2,1,0:T(8,128)(2,1)S(1)} %collective-permute-done.2.refs_2_.refs_4_), channel_id=1, source_target_pairs={{16,0},{0,16},{17,1},{1,17},{18,2},{2,18},{19,3},{3,19},{20,4},{4,... | collective-permute-start | bytes 2752520 | tf_op jit(solution)/shard_map/ppermute | solution.py:59
  68.0 26.6 %collective-permute-start.15 = (f32[128,512]{1,0:T(8,128)}, f32[128,512]{1,0:T(8,128)}, u32[]{:S(2)}, u32[]{:S(2)}) collective-permute-start(f32[128,512]{1,0:T(8,128)} %pad_maximum_fusion.4.refs_4_), channel_id=1, source_target_pairs={{0,4},{4,0},{8,12},{12,8},{1,5},{5,1},{9,13},{13,9},{2,6},{6,2},{1... | collective-permute-start | bytes 786440 | tf_op jit(solution)/shard_map/ppermute | solution.py:396
  94.6 46.1 %collective-permute-start.6 = (bf16[2,64,3584]{2,1,0:T(8,128)(2,1)}, bf16[2,64,3584]{2,1,0:T(8,128)(2,1)S(1)}, u32[]{:S(2)}, u32[]{:S(2)}) collective-permute-start(bf16[2,64,3584]{2,1,0:T(8,128)(2,1)} %share_rows.12.refs_3_), channel_id=1, source_target_pairs={{2,0},{3,1},{0,2},{1,3},{6,4},{7,5},{4,6},{5,7},{10,8},{11,9},{8,1... | collective-permute-start | bytes 2752520 | tf_op jit(solution)/shard_map/ppermute | solution.py:54
  94.9 45.9 %collective-permute-start.8 = (bf16[2,64,3584]{2,1,0:T(8,128)(2,1)S(1)}, bf16[2,64,3584]{2,1,0:T(8,128)(2,1)}, u32[]{:S(2)}, u32[]{:S(2)}) collective-permute-start(bf16[2,64,3584]{2,1,0:T(8,128)(2,1)S(1)} %collective-permute-done.4.refs_2_.refs_5_), channel_id=1, source_target_pairs={{16,0},{0,16},{17,1},{1,17},{18,2},{2,18},{19,3},{3,19},{20,4},{4,... | collective-permute-start | bytes 2752520 | tf_op jit(solution)/shard_map/ppermute | solution.py:59
  143.9 46.8 %collective-permute-start.17 = (bf16[2,3584,512]{2,1,0:T(8,128)(2,1)}, bf16[2,3584,512]{2,1,0:T(8,128)(2,1)}, u32[]{:S(2)}, u32[]{:S(2)}) collective-permute-start(bf16[2,3584,512]{2,1,0:T(8,128)(2,1)} %get-tuple-element.23.refs_11_.refs_4_.refs_2_.refs_1_), channel_id=1, source_target_pairs={{0,1},{1,0},{2,3},{3,2},{4,5},{5,4},{6,7},{7,6},{8,9},{9,8},{10,11... | collective-permute-start | bytes 22020104 | tf_op jit(solution)/shard_map/ppermute | solution.py:48
  151.2 33.3 %collective-permute-start.18 = (bf16[2,64,3584]{2,1,0:T(8,128)(2,1)S(1)}, bf16[2,64,3584]{2,1,0:T(8,128)(2,1)}, u32[]{:S(2)}, u32[]{:S(2)}) collective-permute-start(bf16[2,64,3584]{2,1,0:T(8,128)(2,1)S(1)} %copy-done.13), channel_id=1, source_target_pairs={{2,0},{3,1},{0,2},{1,3},{6,4},{7,5},{4,6},{5,7},{10,8},{11,9},{8,1... | collective-permute-start | bytes 2752520 | tf_op jit(solution)/shard_map/ppermute | solution.py:54
  152.4 32.1 %collective-permute-start.19 = (bf16[2,64,3584]{2,1,0:T(8,128)(2,1)}, bf16[2,64,3584]{2,1,0:T(8,128)(2,1)S(1)}, u32[]{:S(2)}, u32[]{:S(2)}) collective-permute-start(bf16[2,64,3584]{2,1,0:T(8,128)(2,1)} %copy-done.6), channel_id=1, source_target_pairs={{16,0},{0,16},{17,1},{1,17},{18,2},{2,18},{19,3},{3,19},{20,4},{4,... | collective-permute-start | bytes 2752520 | tf_op jit(solution)/shard_map/ppermute | solution.py:59
  181.9 50.8 %collective-permute-start.16 = (bf16[1600,512]{1,0:T(8,128)(2,1)}, bf16[1600,512]{1,0:T(8,128)(2,1)}, u32[]{:S(2)}, u32[]{:S(2)}) collective-permute-start(bf16[1600,512]{1,0:T(8,128)(2,1)} %weigh_rows.5.refs_5_.refs_0_), channel_id=1, source_target_pairs={{4,0},{12,8},{1,5},{9,13},{6,2},{14,10},{3,7},{11,15},{20,16},{28,... | collective-permute-start | bytes 4915208 | tf_op jit(solution)/shard_map/ppermute | solution.py:416
  188.5 25.1 %collective-permute-start.24 = (f32[2,2,16,512]{3,2,1,0:T(8,128)S(1)}, f32[2,2,16,512]{3,2,1,0:T(8,128)S(1)}, u32[]{:S(2)}, u32[]{:S(2)}) collective-permute-start(f32[2,2,16,512]{3,2,1,0:T(8,128)S(1)} %slice_select_fusion), channel_id=1, source_target_pairs={{0,8},{4,12},{8,0},{12,4},{1,9},{5,13},{9,1},{13,5},{2,10},{6,14},... | collective-permute-start | bytes 393224 | tf_op jit(solution)/shard_map/ppermute | solution.py:396
  208.9 41.6 %collective-permute-start.28 = (bf16[1600,512]{1,0:T(8,128)(2,1)}, bf16[1600,512]{1,0:T(8,128)(2,1)}, u32[]{:S(2)}, u32[]{:S(2)}) collective-permute-start(bf16[1600,512]{1,0:T(8,128)(2,1)} %weigh_rows.6.refs_2_.refs_0_), channel_id=1, source_target_pairs={{4,0},{12,8},{1,5},{9,13},{6,2},{14,10},{3,7},{11,15},{20,16},{28,... | collective-permute-start | bytes 4915208 | tf_op jit(solution)/shard_map/ppermute | solution.py:416
  212.6 24.9 %collective-permute-start.23 = (bf16[2,64,3584]{2,1,0:T(8,128)(2,1)}, bf16[2,64,3584]{2,1,0:T(8,128)(2,1)S(1)}, u32[]{:S(2)}, u32[]{:S(2)}) collective-permute-start(bf16[2,64,3584]{2,1,0:T(8,128)(2,1)} %collective-permute-done.18.refs_3_.refs_0_), channel_id=1, source_target_pairs={{16,0},{0,16},{17,1},{1,17},{18,2},{2,18},{19,3},{3,19},{20,4},{4,... | collective-permute-start | bytes 2752520 | tf_op jit(solution)/shard_map/ppermute | solution.py:59
  229.8 29.8 %collective-permute-start.26 = (bf16[2,64,3584]{2,1,0:T(8,128)(2,1)}, bf16[2,64,3584]{2,1,0:T(8,128)(2,1)}, u32[]{:S(2)}, u32[]{:S(2)}) collective-permute-start(bf16[2,64,3584]{2,1,0:T(8,128)(2,1)} %get-tuple-element.26.refs_12_), channel_id=1, source_target_pairs={{2,0},{3,1},{0,2},{1,3},{6,4},{7,5},{4,6},{5,7},{10,8},{11,9},{8,1... | collective-permute-start | bytes 2752520 | tf_op jit(solution)/shard_map/ppermute | solution.py:54
  231.7 28.0 %collective-permute-start.27 = (bf16[2,64,3584]{2,1,0:T(8,128)(2,1)S(1)}, bf16[2,64,3584]{2,1,0:T(8,128)(2,1)}, u32[]{:S(2)}, u32[]{:S(2)}) collective-permute-start(bf16[2,64,3584]{2,1,0:T(8,128)(2,1)S(1)} %collective-permute-done.22.refs_0_.refs_1_), channel_id=1, source_target_pairs={{16,0},{0,16},{17,1},{1,17},{18,2},{2,18},{19,3},{3,19},{20,4},{4,... | collective-permute-start | bytes 2752520 | tf_op jit(solution)/shard_map/ppermute | solution.py:59
  236.8 23.5 %collective-permute-start.30 = (bf16[1024,512]{1,0:T(8,128)(2,1)}, bf16[1024,512]{1,0:T(8,128)(2,1)S(1)}, u32[]{:S(2)}, u32[]{:S(2)}) collective-permute-start(bf16[1024,512]{1,0:T(8,128)(2,1)} %get-tuple-element.28.refs_2_), channel_id=1, source_target_pairs={{8,0},{13,5},{2,10},{7,15},{24,16},{29,21},{18,26},{23,31}} | collective-permute-start | bytes 3145736 | tf_op jit(solution)/shard_map/ppermute | solution.py:416
  285.5 32.7 %collective-permute-start.37 = (bf16[2,64,3584]{2,1,0:T(8,128)(2,1)}, bf16[2,64,3584]{2,1,0:T(8,128)(2,1)}, u32[]{:S(2)}, u32[]{:S(2)}) collective-permute-start(bf16[2,64,3584]{2,1,0:T(8,128)(2,1)} %get-tuple-element.32.refs_0_), channel_id=1, source_target_pairs={{16,0},{0,16},{17,1},{1,17},{18,2},{2,18},{19,3},{3,19},{20,4},{4,... | collective-permute-start | bytes 2752520 | tf_op jit(solution)/shard_map/ppermute | solution.py:59
  297.2 49.9 %collective-permute-start.36 = (bf16[1024,512]{1,0:T(8,128)(2,1)S(1)}, bf16[1024,512]{1,0:T(8,128)(2,1)}, u32[]{:S(2)}, u32[]{:S(2)}) collective-permute-start(bf16[1024,512]{1,0:T(8,128)(2,1)S(1)} %fusion.2), channel_id=1, source_target_pairs={{0,1},{1,0},{2,3},{3,2},{4,5},{5,4},{6,7},{7,6},{8,9},{9,8},{10,11... | collective-permute-start | bytes 3145736 | tf_op jit(solution)/shard_map/ppermute | solution.py:48
  (50 other events, 519.2 us)

commit v5 on v4

--- a/solution.py
+++ b/solution.py
@@ -160,49 +160,45 @@
     )(gate_act, up_act, proj_h, *after)
 
 
-def hidden_part(rank, below, above, w_down, first, so_far, slopes, proj_u, after):
+def hidden_part(rank, below, above, w_down, first, so_far, slopes, after):
     ranks = lax.axis_size("tensor")
     features, count = (below or above)[0].shape
     hidden = w_down.shape[0]
-    far = first + len(above) - 1
     own = len(below) - len(above)
-    places = own + min(2 * len(above), ranks - first)
-    width = widest(features, (512, 256, 128))
-    subs = features // width
-    tile = widest(hidden, (512, 256, 128))
+    span = len(above)
+    slots = own + min(2 * span, ranks - first)
     finish = slopes is not None
-    steps = places * subs
-    total_steps = steps + (hidden // tile if finish else 0)
-
-    def counts(z):
-        span = far - first + 1
+    tile = widest(hidden, (896, 512, 128) if finish else (1792, 896, 128))
+    sources = [*below, *above]
+
+    def slot_of(z, at):
+        if at < own:
+            return z, True
         under = jnp.clip(z - first + 1, 0, span)
         over = jnp.clip(ranks - z - first, 0, span)
-        return under, over
-
-    def column(i, rank_ref):
+        at -= own
+        block = jnp.where(at < under, z - first - at, z + first + at - under)
+        return block, at < under + over
+
+    def column(at, i, rank_ref):
+        block, valid = slot_of(rank_ref[0], at)
+        if valid is True:
+            return (i, block)
+        return (jnp.where(valid, i, 0), jnp.where(valid, block, 0))
+
+    def kernel(rank_ref, *refs):
         z = rank_ref[0]
-        under, over = counts(z)
-        at = jnp.clip(i // subs, 0, jnp.maximum(own + under + over - 1, 0))
-        block = jnp.where(at < own + under, z - first - (at - own), z + first + at - own - under)
-        if own:
-            block = jnp.where(at == 0, z, block)
-        block = jnp.clip(block, 0, ranks - 1)
-        sub = jnp.where(i // subs > at, subs - 1, lax.rem(i, subs))
-        return (0, block * subs + sub)
-
-    def kernel(rank_ref, down_ref, *refs):
-        z = rank_ref[0]
-        under, over = counts(z)
-        sources = refs[: len(below) + len(above)]
+        downs, arrived = refs[:slots], refs[slots : slots + len(sources)]
         grad_ref, total, sem = refs[-3:]
-        i = pl.program_id(0)
+        out = refs[-4]
 
         def gather(wait):
-            pieces = [(sources[at], True, at) for at in range(own)]
-            for t in range(len(above)):
-                pieces.append((sources[own + t], t < under, own + t))
-                pieces.append((sources[len(below) + t], t < over, own + under + t))
+            under = jnp.clip(z - first + 1, 0, span)
+            over = jnp.clip(ranks - z - first, 0, span)
+            pieces = [(arrived[at], z >= 0, at) for at in range(own)]
+            for t in range(span):
+                pieces.append((arrived[own + t], t < under, own + t))
+                pieces.append((arrived[len(below) + t], t < over, own + under + t))
             for at, (source, valid, place) in enumerate(pieces):
 
                 @pl.when(valid)
@@ -211,97 +207,73 @@
                     copy = pltpu.make_async_copy(source, grad_ref.at[rows, :], sem.at[at])
                     copy.wait() if wait else copy.start()
 
-        rest = refs[len(below) + len(above) :]
-
-        @pl.when(i == 0)
+        @pl.when(pl.program_id(0) == 0)
         def _():
             gather(False)
-            if so_far is not None:
-                load = pltpu.make_async_copy(rest[0], total, sem.at[len(sources)])
-                load.start()
-                load.wait()
+            gather(True)
+
+        rest = refs[slots + len(sources) :]
+        if so_far is not None:
+            total[...] = rest[0][...]
+        for at in range(slots):
+
+            def add_slot(at=at):
+                term = jnp.dot(
+                    downs[at][...],
+                    grad_ref[at * features : (at + 1) * features, :],
+                    preferred_element_type=jnp.float32,
+                )
+                if at == 0 and so_far is None:
+                    total[...] = term
+                else:
+                    total[...] += term
+
+            _, valid = slot_of(z, at)
+            if valid is True:
+                add_slot()
             else:
-                total[...] = jnp.zeros_like(total)
-            gather(True)
-
-        @pl.when((i < steps) & (i // subs < own + under + over))
-        def _():
-            rows = pl.ds(pl.multiple_of(i * width, width), width)
-            total[...] += jnp.dot(
-                down_ref[...], grad_ref[rows, :], preferred_element_type=jnp.float32
-            )
-
-        if not finish:
-            out = refs[-4]
-
-            @pl.when(i == total_steps - 1)
-            def _():
-                store = pltpu.make_async_copy(total, out, sem.at[len(sources)])
-                store.start()
-                store.wait()
-
+                pl.when(valid)(add_slot)
+        if finish:
+            out[0] = (total[...] * rest[1][0]).astype(jnp.bfloat16)
+            out[1] = (total[...] * rest[1][1]).astype(jnp.bfloat16)
         else:
-            slope_ref, proj_ref = rest[1:3]
-            both_ref, out_ref = refs[-5:-3]
-
-            @pl.when(i == 0)
-            def _():
-                out_ref[...] = jnp.zeros_like(out_ref)
-
-            @pl.when(i >= steps)
-            def _():
-                rows = pl.ds(pl.multiple_of((i - steps) * tile, tile), tile)
-                wide = total[rows, :]
-                both_ref[0] = (wide * slope_ref[0]).astype(jnp.bfloat16)
-                up_grad = (wide * slope_ref[1]).astype(jnp.bfloat16)
-                both_ref[1] = up_grad
-                out_ref[...] += jnp.dot(proj_ref[...], up_grad, preferred_element_type=jnp.float32)
-
-    operands = [w_down, *below, *above]
-    specs = [pl.BlockSpec((hidden, width), column)] + [ANYWHERE] * (len(below) + len(above))
+            out[...] = total[...]
+
+    operands = [w_down] * slots + sources
+    specs = [pl.BlockSpec((tile, features), functools.partial(column, at)) for at in range(slots)]
+    specs += [ANYWHERE] * len(sources)
     if so_far is not None:
         operands.append(so_far)
-        specs.append(ANYWHERE)
+        specs.append(pl.BlockSpec((tile, count), lambda i, r: (i, 0)))
     if finish:
-        narrow = proj_u.shape[0]
-        row = lambda i: jnp.maximum(i - steps, 0)
-        operands += [slopes, proj_u]
-        specs += [
-            pl.BlockSpec((2, tile, count), lambda i, r: (0, row(i), 0)),
-            pl.BlockSpec((narrow, tile), lambda i, r: (0, row(i))),
-        ]
-        out_shape = [
-            jax.ShapeDtypeStruct((2, hidden, count), jnp.bfloat16),
-            jax.ShapeDtypeStruct((narrow, count), jnp.float32),
-        ]
-        out_specs = [
-            pl.BlockSpec((2, tile, count), lambda i, r: (0, row(i), 0)),
-            pl.BlockSpec((narrow, count), lambda i, r: (0, 0)),
-        ]
+        operands.append(slopes)
+        specs.append(pl.BlockSpec((2, tile, count), lambda i, r: (0, i, 0)))
+        out_shape = jax.ShapeDtypeStruct((2, hidden, count), jnp.bfloat16)
+        out_specs = pl.BlockSpec((2, tile, count), lambda i, r: (0, i, 0))
     else:
         out_shape = jax.ShapeDtypeStruct((hidden, count), jnp.float32)
-        out_specs = ANYWHERE
+        out_specs = pl.BlockSpec((tile, count), lambda i, r: (i, 0))
     return pl.pallas_call(
         kernel,
         grid_spec=pltpu.PrefetchScalarGridSpec(
             num_scalar_prefetch=1,
-            grid=(total_steps,),
+            grid=(hidden // tile,),
             in_specs=specs + [ANYWHERE] * len(after),
             out_specs=out_specs,
             scratch_shapes=[
-                pltpu.VMEM((places * features, count), jnp.bfloat16),
-                pltpu.VMEM((hidden, count), jnp.float32),
-                pltpu.SemaphoreType.DMA((len(below) + len(above) + 1,)),
+                pltpu.VMEM((slots * features, count), jnp.bfloat16),
+                pltpu.VMEM((tile, count), jnp.float32),
+                pltpu.SemaphoreType.DMA((len(sources),)),
             ],
         ),
         out_shape=out_shape,
         compiler_params=pltpu.CompilerParams(vmem_limit_bytes=VMEM_BYTES),
-        cost_estimate=cost(15 if finish else 12),
+        cost_estimate=cost(12),
         name="hidden_part",
     )(rank, *operands, *after)
 
 
-def weigh(routes, grads, after, price):
+def weigh(routes, grads, after, price, extra=None):
     hidden = grads[0].shape[1]
     tile = widest(hidden, (512, 256, 128))
     steps = hidden // tile
@@ -309,10 +281,12 @@
     rows, count = sum(heights), sum(g.shape[2] for g in grads)
     units = [u for route in routes for u in route]
     flat = [w for u in units for w in u]
+    extras = [] if extra is None else [extra]
 
     def kernel(*refs):
         weights, both = list(refs[: len(flat)]), refs[len(flat) : len(flat) + len(grads)]
-        outs, total = refs[-1 - len(routes) : -1], refs[-1]
+        more = refs[len(flat) + len(grads) : len(flat) + len(grads) + len(extras)]
+        outs, total = refs[-1 - len(routes) - len(extras) : -1], refs[-1]
         at = pl.program_id(0)
 
         @pl.when(at == 0)
@@ -324,13 +298,16 @@
             mine, weights = weights[: len(u)], weights[len(u) :]
             gates.append(mine[0][...] if len(u) == 2 else mine[0][0])
             ups.append(mine[1][...] if len(u) == 2 else mine[0][1])
-        gate, up = jnp.concatenate(gates, axis=0), jnp.concatenate(ups, axis=0)
+        gate, up = jnp.concatenate(gates, axis=0), jnp.concatenate(ups + [m[...] for m in more], axis=0)
         first = 0
         for ref in both:
             span = slice(first, first + ref.shape[2])
-            total[:, span] += jnp.dot(
-                gate, ref[0], preferred_element_type=jnp.float32
-            ) + jnp.dot(up, ref[1], preferred_element_type=jnp.float32)
+            by_up = jnp.dot(up, ref[1], preferred_element_type=jnp.float32)
+            total[:rows, span] += (
+                jnp.dot(gate, ref[0], preferred_element_type=jnp.float32) + by_up[:rows]
+            )
+            if more:
+                total[rows:, span] += by_up[rows:]
             first += ref.shape[2]
 
         @pl.when(at == steps - 1)
@@ -339,6 +316,8 @@
             for out, height in zip(outs, heights):
                 out[...] = total[top : top + height].astype(jnp.bfloat16)
                 top += height
+            if more:
+                outs[-1][...] = total[rows:]
 
     specs = []
     for w in flat:
@@ -348,17 +327,21 @@
             specs.append(pl.BlockSpec((2, w.shape[1], tile), lambda i: (0, 0, i)))
     for g in grads:
         specs.append(pl.BlockSpec((2, tile, g.shape[2]), lambda i: (0, i, 0)))
+    shapes = [jax.ShapeDtypeStruct((h, count), jnp.bfloat16) for h in heights]
+    for e in extras:
+        specs.append(pl.BlockSpec((e.shape[0], tile), lambda i: (0, i)))
+        shapes.append(jax.ShapeDtypeStruct((e.shape[0], count), jnp.float32))
     return pl.pallas_call(
         kernel,
         grid=(steps,),
-        out_shape=[jax.ShapeDtypeStruct((h, count), jnp.bfloat16) for h in heights],
+        out_shape=shapes,
         in_specs=specs + [ANYWHERE] * len(after),
-        out_specs=[pl.BlockSpec((h, count), lambda i: (0, 0)) for h in heights],
-        scratch_shapes=[pltpu.VMEM((rows, count), jnp.float32)],
+        out_specs=[pl.BlockSpec(s.shape, lambda i: (0, 0)) for s in shapes],
+        scratch_shapes=[pltpu.VMEM((rows + sum(e.shape[0] for e in extras), count), jnp.float32)],
         compiler_params=pltpu.CompilerParams(vmem_limit_bytes=VMEM_BYTES),
         cost_estimate=cost(price),
         name="weigh_rows",
-    )(*flat, *grads, *after)
+    )(*flat, *grads, *extras, *after)
 
 
 def add(values, others, heights, after):
@@ -377,14 +360,12 @@
                 top += height
 
     count = values[0].shape[1]
-    width = widest(count, (128,))
-    specs = [pl.BlockSpec((v.shape[0], width), lambda i: (0, i)) for v in values]
+    whole = pl.BlockSpec(memory_space=pltpu.VMEM)
     return pl.pallas_call(
         kernel,
-        grid=(count // width,),
         out_shape=[jax.ShapeDtypeStruct((h, count), jnp.bfloat16) for h in flat],
-        in_specs=specs + specs + [ANYWHERE] * len(after),
-        out_specs=[pl.BlockSpec((h, width), lambda i: (0, i)) for h in flat],
+        in_specs=[whole] * (2 * pairs) + [ANYWHERE] * len(after),
+        out_specs=[whole] * len(flat),
         compiler_params=pltpu.CompilerParams(vmem_limit_bytes=VMEM_BYTES),
         cost_estimate=cost(2),
         name="add_terms",
@@ -404,7 +385,7 @@
     return jnp.where(high, high_rows, low_rows) + got
 
 
-def toward(value, owner, bit):
+def hops(owner, bit):
     groups, ranks, blocks = (lax.axis_size(a) for a in ("groups", "tensor", "dp"))
     pairs = []
     for g in range(groups):
@@ -413,18 +394,25 @@
             for z in range(ranks):
                 if z % bit == target % bit and (z ^ target) & bit:
                     pairs.append(((g * ranks + z) * blocks + p, (g * ranks + (z ^ bit)) * blocks + p))
+    return pairs
+
+
+def send(value, pairs):
     return lax.ppermute(value, ("groups", "tensor", "dp"), pairs)
 
 
-def later_steps(value, owner):
-    bit = 2
-    got = None
-    while bit < lax.axis_size("tensor"):
-        if got is not None:
-            (value,) = add([value], [got], [[value.shape[0]]], [])
-        got = toward(value, owner, bit)
-        bit *= 2
-    return value, got
+def later_steps(values, owners):
+    ranks = lax.axis_size("tensor")
+    ends = []
+    for value, owner in zip(values, owners):
+        bit, got = 2, None
+        while bit < ranks:
+            if got is not None:
+                (value,) = add([value], [got], [[value.shape[0]]], [])
+            got = send(value, hops(owner, bit))
+            bit *= 2
+        ends.append((value, got))
+    return ends
 
 
 def per_device(
@@ -508,7 +496,7 @@
         for j in range(split)
     ]
 
-    def terms(names, grads, after, price, near=False):
+    def terms(names, grads, after, price, near=False, extra=None):
         routes = list(zip(near_tables, near_routes, [None] * split)) if near else []
         for s, table, shifts in far_routes:
             units = [(k, s, q) for k, q in names if q in shifts]
@@ -518,61 +506,61 @@
         for route in routes:
             bundles.setdefault((route[0] % 2).tobytes(), []).append(route)
         bundles = list(bundles.values())
-        outs = list(weigh([[u for _, units, _ in b for u in units] for b in bundles], grads, after, price))
-        got = [toward(out, b[0][0], 1) for out, b in zip(outs, bundles)]
+        joined = [[u for _, units, _ in b for u in units] for b in bundles]
+        outs = list(weigh(joined, grads, after, price, extra))
+        got = [send(out, hops(b[0][0], 1)) for out, b in zip(outs, bundles)]
         return outs, got, bundles
 
     def carry_on(work, after):
         outs, got, bundles = work
         heights = [[sum(u[0].shape[-2] for u in units) for _, units, _ in b] for b in bundles]
         sums = list(add(outs, got, heights, after))
-        ends, at = [], 0
-        for b in bundles:
-            for table, _, names in b:
-                ends.append((names, *later_steps(sums[at], table)))
-                at += 1
-        return sums, ends
+        routes = [route for b in bundles for route in b]
+        ends = later_steps(sums, [table for table, _, _ in routes])
+        return sums, [(names, *end) for (_, _, names), end in zip(routes, ends)]
 
     fetch(0)
     fetch(1)
-    forward(0, [slopes])
-    forward(1, [early_part, out_down_part])
-    forward(2, [])
-    so_far = hidden_part(
-        rank_word, below[:2], above[:1], w_down, 1, None, None, None, [ticks[2]]
-    )
-    forward(3, [so_far])
-    mine, up_out_part = hidden_part(
-        rank_word, below[2:], above[1:], w_down, 2, so_far, slopes, proj_u.T, [ticks[3]]
-    )
+
+    def hold_arrived(k, after, held=()):
+        names = [(k, s, 0) for s in range(1, chips)]
+        values = forward(k, after, [fetched[n] for n in names] + list(held))
+        for n, value in zip(names, values):
+            fetched[n] = value
+            for r in range(1, groups):
+                fetched[k, n[1], r] = from_group(value, r)
+        return values[len(names) :]
+
     bits = [1 << i for i in range(ranks.bit_length() - 1)]
-    early = early_part + exchange(early_part, bits[0])
-    (mine,) = forward(4, [early], [mine])
+    hold_arrived(0, [slopes])
+    so_far = hidden_part(rank_word, below[:2], above[:1], w_down, 1, None, None, [ticks[0]])
+    hold_arrived(1, [so_far])
+    hold_arrived(2, [below[2], above[1], early_part, out_down_part])
+    (early,) = hold_arrived(3, below[3:] + above[2:], [early_part])
+    mine = hidden_part(rank_word, below[2:], above[1:], w_down, 2, so_far, slopes, [ticks[3]])
+    early = early + exchange(early, bits[0])
+    mine, early = hold_arrived(4, [], [mine, early])
     theirs = swap_cores(mine)
     for bit in bits[1:]:
         early = early + exchange(early, bit)
     first_names = [(k, 0) for k in range(5)] + [(k, 1) for k in range(4)]
-    first_mine = terms(first_names, [mine], [ticks[4]], 30, near=True)
-    (up_out_part,) = forward(5, first_mine[0] + [early], [up_out_part])
-    first_theirs = terms(first_names, [theirs], [ticks[5]], 30, near=True)
+    first_mine = terms(first_names, [mine], [ticks[4]], 16, near=True, extra=proj_u.T)
+    up_out_part = first_mine[0].pop()
+    (up_out_part,) = hold_arrived(5, first_mine[0] + [early], [up_out_part])
+    first_theirs = terms(first_names, [theirs], [ticks[5]], 16, near=True)
     sums_mine, end_mine = carry_on(first_mine, first_theirs[0])
     out_parts = jnp.stack([up_out_part, out_down_part]).reshape(2, ranks, -1, count)
     out_parts = halve(out_parts.transpose(1, 0, 2, 3), bits[-1])
-    forward(6, sums_mine + [out_parts])
+    (out_parts,) = hold_arrived(6, first_theirs[0], [out_parts])
     second_names = [(5, 0), (6, 0), (4, 1), (5, 1)]
-    second = terms(second_names, [mine, theirs], [ticks[6]], 18)
+    second = terms(second_names, [mine, theirs], [ticks[6]] + sums_mine, 10)
     sums_theirs, end_theirs = carry_on(first_theirs, second[0])
     for bit in bits[-2::-1]:
         out_parts = halve(out_parts, bit)
-    last_arrived = [(CHUNKS - 1, s, 0) for s in range(1, chips)]
-    held = forward(7, sums_theirs + [out_parts], [fetched[n] for n in last_arrived])
-    for n, value in zip(last_arrived, held):
-        fetched[n] = value
-        for r in range(1, groups):
-            fetched[n[0], n[1], r] = from_group(value, r)
+    hold_arrived(7, second[0] + [out_parts])
     third_names = [(7, 0), (6, 1)]
     received = [got for _, _, got in end_mine if got is not None]
-    third = terms(third_names, [mine, theirs], [ticks[7]] + received, 0)
+    third = terms(third_names, [mine, theirs], [ticks[7]] + sums_theirs + received, 4)
     sums_second, end_second = carry_on(second, third[0])
 
     early = early.astype(jnp.bfloat16)
@@ -613,10 +601,27 @@
             options.append(jnp.concatenate([pick(shift, by_shift) for shift in shifts], axis=0))
         return pick(away, options)
 
+    def settle_at_once(end, after):
+        if end[0][2] is None:
+            return [v for _, v, _ in end]
+        mine = [v for _, v, _ in end]
+        return add(mine, [got for _, _, got in end], [[v.shape[0]] for v in mine], after)
+
+    sums_third, end_third = carry_on(third, [doc_logs])
+    last_names = [(CHUNKS - 1, r) for r in range(1, groups)]
+    settled_mine = settle_at_once(end_mine, third[0])
+    received = [got for _, _, got in end_theirs if got is not None]
+    last = terms(last_names, [mine, theirs], list(settled_mine) + sums_third + received, 20)
+    sums_last, end_last = carry_on(last, [])
+    settled_theirs = settle_at_once(end_theirs, sums_last)
+    later = end_second + end_third
+    settled_later = settle_at_once(later, sums_last)
+
     near_half, far_half = [[], []], [{}, {}]
-    for at, end in enumerate((end_mine, end_theirs)):
-        for names, *pair in end:
-            value = settle(*pair)
+    for at, (end, settled) in enumerate(
+        ((end_mine, settled_mine), (end_theirs, settled_theirs))
+    ):
+        for (names, _, _), value in zip(end, settled):
             if names is None:
                 near_half[at].append(value)
             else:
@@ -624,12 +629,7 @@
                     (n, value[i * piece : (i + 1) * piece]) for i, n in enumerate(names)
                 )
 
-    sums_third, end_third = carry_on(third, [doc_logs])
-    last_names = [(CHUNKS - 1, r) for r in range(1, groups)]
-    received = [got for _, _, got in end_theirs if got is not None]
-    last = terms(last_names, [mine, theirs], sums_third + received, 10)
-    for names, *pair in end_second + end_third:
-        value = settle(*pair)
+    for (names, _, _), value in zip(later, settled_later):
         for i, n in enumerate(names):
             both = value[i * piece : (i + 1) * piece]
             far_half[0][n], far_half[1][n] = both[:, :count], both[:, count:]
@@ -639,7 +639,6 @@
                 half[CHUNKS - 1, s, r] = jnp.zeros((piece, count), jnp.bfloat16)
     total_mine, total_theirs = (in_order(n, f) for n, f in zip(near_half, far_half))
     from_partner = swap_cores(total_theirs)
-    _, end_last = carry_on(last, [])
     total = jnp.where(owner, total_mine, from_partner)
 
     tail = {}

time: 353 us -> 333 us (0.943)
  waiting for transfers between devices: 69.8 us -> 41.4 us
  local copies, waits for them, and re-layouts: 10.2 us -> 25.1 us
    ppermute x4, waiting for transfers between devices: 48 us -> 19.1 us  [exchange(): return lax.ppermute(value, 'tensor', [(i, i ^ bit) for i in range(ranks)])]
    ppermute x3, starting transfers between devices: 36.1 us -> 19.1 us  [swap_cores(): return lax.ppermute(value, 'dp', [(i, i ^ 1) for i in range(size)])]
    unnamed x68 -> x76, local copies, waits for them, and re-layouts: 8.4 us -> 17.5 us
    ppermute x3, waiting for transfers between devices: 7.45 us -> 0.45 us  [spread_ranks(): lax.ppermute(below[-1], 'tensor', [(i, i + 1) for i in range(ranks - 1)])]
    ppermute x3, starting transfers between devices: 12.8 us -> 19.2 us  [spread_ranks(): lax.ppermute(below[-1], 'tensor', [(i, i + 1) for i in range(ranks - 1)])]
    ppermute x12, starting transfers between devices: 25.2 us -> 29 us  [send(): return lax.ppermute(value, ('groups', 'tensor', 'dp'), pairs)]
    slice x4, local copies, waits for them, and re-layouts: 0.08 us -> 3.93 us  [per_device(): value[i * piece:(i + 1) * piece]]
    ppermute x8, waiting for transfers between devices: 0.02 us -> 3.78 us  [from_group(): lax.ppermute(value, 'groups', [((i + shift) % size, i) for i in range(siz...]
  transfers between devices with their start and end apart: 41 -> 41, of which waited for: 8 -> 10; matrix products, arithmetic and copies ran while one was open for 5% -> 6% of each run, Pallas kernels for 42% -> 45%
where the time goes in v5:
time: 333 us; the launch traced here: 331 us
  Pallas kernels  155 us (47%)
  starting transfers between devices  93.2 us (28%)
  waiting for transfers between devices  41.4 us (12%)
  local copies, waits for them, and re-layouts  25.1 us (8%)
  other arithmetic  11 us (3%)
  matrix products  3.99 us (1%)
    pallas_call x5, Pallas kernels, weigh(): pl.pallas_call(kernel, grid=(steps,), out_shape=shapes, in_specs=specs +...  65.9 us
    pallas_call x2, Pallas kernels, hidden_part(): pl.pallas_call(kernel, grid_spec=pltpu.PrefetchScalarGridSpec(num_scalar_...  39.3 us
    ppermute x12, starting transfers between devices, send(): return lax.ppermute(value, ('groups', 'tensor', 'dp'), pairs)  29 us
    pallas_call x8, Pallas kernels, add(): pl.pallas_call(kernel, out_shape=[jax.ShapeDtypeStruct((h, count), jnp.bf...  21.1 us
    ppermute x3, starting transfers between devices, spread_ranks(): lax.ppermute(below[-1], 'tensor', [(i, i + 1) for i in range(ranks - 1)])  19.2 us
    ppermute x4, waiting for transfers between devices, exchange(): return lax.ppermute(value, 'tensor', [(i, i ^ bit) for i in range(ranks)])  19.1 us
    ppermute x3, starting transfers between devices, swap_cores(): return lax.ppermute(value, 'dp', [(i, i ^ 1) for i in range(size)])  19.1 us
    unnamed x76, local copies, waits for them, and re-layouts  17.5 us
  transfers between devices with their start and end apart: 41, of which 10 were waited for; matrix products, arithmetic and copies ran while one was open for 6% of the time, Pallas kernels for 45%

profile of v5, /device:TPU:3, one launch (start us, length us, event | category | flops | bytes accessed | tf_op | source)
XLA Modules:
  0.0 331.0 jit_solution(5032542193867363670)
XLA Ops:
  4.8 4.5 %collective-permute-start.3 = (bf16[1024,512]{1,0:T(8,128)(2,1)}, bf16[1024,512]{1,0:T(8,128)(2,1)}, u32[]{:S(2)}, u32[]{:S(2)}) collective-permute-start(bf16[1024,512]{1,0:T(8,128)(2,1)} %bitcast.3.refs_3_), channel_id=1, source_target_pairs={{0,4},{4,8},{8,12},{1,5},{5,9},{9,13},{2,6},{6,10},{10,14},{3,7},{... | collective-permute-start | bytes 3145736 | tf_op jit(solution)/shard_map/ppermute | solution.py:113
  11.9 12.0 %prepare.1 = (f32[2,3584,512]{2,1,0:T(8,128)}, f32[64,512]{1,0:T(8,128)}) custom-call(bf16[512,3584]{1,0:T(8,128)(2,1)} %gate_ref.1, bf16[512,3584]{1,0:T(8,128)(2,1)} %up_ref.1, bf16[64,3584]{1,0:T(8,128)(2,1)} %bitcast.34, bf16[2,64,3584]{2,1,0:T(8,128)(2,1)} %get-tuple-element.39.refs_0_), custom_call_target="tpu_custom_call" | custom-call | flops 3240000000 | bytes 1 | tf_op jit(solution)/shard_map/prepare/pallas_call | solution.py:140
  30.0 4.2 %collective-permute-start.7 = (bf16[1024,512]{1,0:T(8,128)(2,1)}, bf16[1024,512]{1,0:T(8,128)(2,1)S(1)}, u32[]{:S(2)}, u32[]{:S(2)}) collective-permute-start(bf16[1024,512]{1,0:T(8,128)(2,1)} %collective-permute-done.3.refs_4_), channel_id=1, source_target_pairs={{0,4},{4,8},{8,12},{1,5},{5,9},{9,13},{2,6},{6,10},{10,14},{3,7},{... | collective-permute-start | bytes 3145736 | tf_op jit(solution)/shard_map/ppermute | solution.py:113
  36.2 17.8 %hidden_part.2.refs_4_.refs_6_ = f32[3584,512]{1,0:T(8,128)} custom-call(s32[1]{0:T(128)} %bitcast.2.rank_ref, bf16[3584,4096]{1,0:T(8,128)(2,1)} %refs_1_.17, bf16[3584,4096]{1,0:T(8,128)(2,1)} %refs_1_.17, bf16[3584,4096]{1,0:T(8,128)(2,1)} %refs_1_.17, bf16[1024,512]{1,0:T(8,128)(2,1)} %bitcast.3.refs_3_, ...), custom_call_target="tpu_custom_call" | custom-call | flops 3240000000 | bytes 1 | tf_op jit(solution)/shard_map/hidden_part/pallas_call | solution.py:256
  62.1 10.5 %collective-permute-start.11 = (bf16[1024,512]{1,0:T(8,128)(2,1)S(1)}, bf16[1024,512]{1,0:T(8,128)(2,1)}, u32[]{:S(2)}, u32[]{:S(2)}) collective-permute-start(bf16[1024,512]{1,0:T(8,128)(2,1)S(1)} %collective-permute-done.7.refs_4_.refs_2_), channel_id=1, source_target_pairs={{0,4},{4,8},{8,12},{1,5},{5,9},{9,13},{2,6},{6,10},{10,14},{3,7},{... | collective-permute-start | bytes 3145736 | tf_op jit(solution)/shard_map/ppermute | solution.py:113
  82.5 11.4 %collective-permute-done.9.refs_2_ = bf16[2,64,3584]{2,1,0:T(8,128)(2,1)} collective-permute-done((bf16[2,64,3584]{2,1,0:T(8,128)(2,1)}, bf16[2,64,3584]{2,1,0:T(8,128)(2,1)}, u32[]{:S(2)}, u32[]{:S(2)}) %collective-permute-start.9) | collective-permute-done | bytes 917536 | tf_op jit(solution)/shard_map/ppermute | solution.py:54
  103.4 7.1 %collective-permute-start.14 = (f32[128,512]{1,0:T(8,128)}, f32[128,512]{1,0:T(8,128)S(1)}, u32[]{:S(2)}, u32[]{:S(2)}) collective-permute-start(f32[128,512]{1,0:T(8,128)} %get-tuple-element.51), channel_id=1, source_target_pairs={{0,4},{4,0},{8,12},{12,8},{1,5},{5,1},{9,13},{13,9},{2,6},{6,2},{1... | collective-permute-start | bytes 786440 | tf_op jit(solution)/shard_map/ppermute | solution.py:377
  110.5 21.5 %hidden_part.3.refs_3_ = bf16[2,3584,512]{2,1,0:T(8,128)(2,1)} custom-call(s32[1]{0:T(128)} %bitcast.2.rank_ref, bf16[3584,4096]{1,0:T(8,128)(2,1)} %refs_1_.17, bf16[3584,4096]{1,0:T(8,128)(2,1)} %refs_1_.17, bf16[1024,512]{1,0:T(8,128)(2,1)} %copy-done.9, bf16[1024,512]{1,0:T(8,128)(2,1)} %collective-permute-done.11.refs_5_.refs_3_, ...), custom_call_target="tpu_custom_call" | custom-call | flops 3240000000 | bytes 1 | tf_op jit(solution)/shard_map/hidden_part/pallas_call | solution.py:256
  136.7 4.7 %collective-permute-start.17 = (bf16[2,3584,512]{2,1,0:T(8,128)(2,1)}, bf16[2,3584,512]{2,1,0:T(8,128)(2,1)}, u32[]{:S(2)}, u32[]{:S(2)}) collective-permute-start(bf16[2,3584,512]{2,1,0:T(8,128)(2,1)} %get-tuple-element.53.refs_11_.refs_4_.refs_2_.refs_1_), channel_id=1, source_target_pairs={{0,1},{1,0},{2,3},{3,2},{4,5},{5,4},{6,7},{7,6},{8,9},{9,8},{10,11... | collective-permute-start | bytes 22020104 | tf_op jit(solution)/shard_map/ppermute | solution.py:48
  143.4 18.3 %weigh_rows.5 = (bf16[1600,512]{1,0:T(8,128)(2,1)}, f32[64,512]{1,0:T(8,128)}) custom-call(bf16[1024,3584]{1,0:T(8,128)(2,1)} %refs_0_.21, bf16[1024,3584]{1,0:T(8,128)(2,1)} %refs_1_.21, bf16[2,64,3584]{2,1,0:T(8,128)(2,1)} %get-tuple-element.41.refs_2_, bf16[2,64,3584]{2,1,0:T(8,128)(2,1)} %get-tuple-element.44.refs_3_, ...), custom_call_target="tpu_custom_call" | custom-call | flops 4320000000 | bytes 1 | tf_op jit(solution)/shard_map/weigh_rows/pallas_call | solution.py:334
  161.7 4.8 %collective-permute-start.16 = (bf16[1600,512]{1,0:T(8,128)(2,1)}, bf16[1600,512]{1,0:T(8,128)(2,1)}, u32[]{:S(2)}, u32[]{:S(2)}) collective-permute-start(bf16[1600,512]{1,0:T(8,128)(2,1)} %get-tuple-element.55.refs_5_.refs_0_), channel_id=1, source_target_pairs={{4,0},{12,8},{1,5},{9,13},{6,2},{14,10},{3,7},{11,15},{20,16},{28,... | collective-permute-start | bytes 4915208 | tf_op jit(solution)/shard_map/ppermute | solution.py:401
  173.0 18.1 %weigh_rows.6.refs_2_.refs_3_.refs_0_ = bf16[1600,512]{1,0:T(8,128)(2,1)} custom-call(bf16[1024,3584]{1,0:T(8,128)(2,1)} %refs_0_.21, bf16[1024,3584]{1,0:T(8,128)(2,1)} %refs_1_.21, bf16[2,64,3584]{2,1,0:T(8,128)(2,1)} %get-tuple-element.41.refs_2_, bf16[2,64,3584]{2,1,0:T(8,128)(2,1)} %get-tuple-element.44.refs_3_, ...), custom_call_target="tpu_custom_call" | custom-call | flops 4320000000 | bytes 1 | tf_op jit(solution)/shard_map/weigh_rows/pallas_call | solution.py:334
  194.4 19.1 %collective-permute-done.25 = f32[2,2,16,512]{3,2,1,0:T(8,128)S(1)} collective-permute-done((f32[2,2,16,512]{3,2,1,0:T(8,128)S(1)}, f32[2,2,16,512]{3,2,1,0:T(8,128)S(1)}, u32[]{:S(2)}, u32[]{:S(2)}) %collective-permute-start.25) | collective-permute-done | bytes 131104 | tf_op jit(solution)/shard_map/ppermute | solution.py:377
  219.1 3.3 %add_terms.8 = (bf16[1024,512]{1,0:T(8,128)(2,1)}, bf16[576,512]{1,0:T(8,128)(2,1)}) custom-call(bf16[1600,512]{1,0:T(8,128)(2,1)} %get-tuple-element.55.refs_5_.refs_0_, bf16[1600,512]{1,0:T(8,128)(2,1)} %collective-permute-done.16.refs_1_, bf16[1600,512]{1,0:T(8,128)(2,1)} %weigh_rows.6.refs_2_.refs_3_.refs_0_), custom_call_target="tpu_custom_call" | custom-call | flops 540000000 | bytes 1 | tf_op jit(solution)/shard_map/add_terms/pallas_call | solution.py:364
  223.1 10.9 %weigh_rows.7.refs_2_.refs_0_ = bf16[256,1024]{1,0:T(8,128)(2,1)} custom-call(bf16[2,64,3584]{2,1,0:T(8,128)(2,1)} %get-tuple-element.62.refs_0_, bf16[2,64,3584]{2,1,0:T(8,128)(2,1)} %get-tuple-element.63.refs_1_, bf16[2,64,3584]{2,1,0:T(8,128)(2,1)} %copy-done.17, bf16[2,64,3584]{2,1,0:T(8,128)(2,1)} %copy-done.16, ...), custom_call_target="tpu_custom_call" | custom-call | flops 2700000000 | bytes 1 | tf_op jit(solution)/shard_map/weigh_rows/pallas_call | solution.py:334
  236.3 8.8 %collective-permute-start.30 = (bf16[256,1024]{1,0:T(8,128)(2,1)}, bf16[256,1024]{1,0:T(8,128)(2,1)}, u32[]{:S(2)}, u32[]{:S(2)}) collective-permute-start(bf16[256,1024]{1,0:T(8,128)(2,1)} %weigh_rows.7.refs_2_.refs_0_), channel_id=1, source_target_pairs={{4,0},{12,8},{1,5},{9,13},{6,2},{14,10},{3,7},{11,15},{20,16},{28,... | collective-permute-start | bytes 1572872 | tf_op jit(solution)/shard_map/ppermute | solution.py:401
  247.9 3.3 %add_terms.9 = (bf16[1024,512]{1,0:T(8,128)(2,1)}, bf16[576,512]{1,0:T(8,128)(2,1)}) custom-call(bf16[1600,512]{1,0:T(8,128)(2,1)} %weigh_rows.6.refs_2_.refs_3_.refs_0_, bf16[1600,512]{1,0:T(8,128)(2,1)} %collective-permute-done.29.refs_1_, bf16[256,1024]{1,0:T(8,128)(2,1)} %weigh_rows.7.refs_2_.refs_0_), custom_call_target="tpu_custom_call" | custom-call | flops 540000000 | bytes 1 | tf_op jit(solution)/shard_map/add_terms/pallas_call | solution.py:364
  253.9 9.4 %weigh_rows.8.refs_4_.refs_2_.refs_0_ = bf16[128,1024]{1,0:T(8,128)(2,1)} custom-call(bf16[2,64,3584]{2,1,0:T(8,128)(2,1)} %get-tuple-element.66.refs_0_, bf16[2,64,3584]{2,1,0:T(8,128)(2,1)} %copy-done.13, bf16[2,3584,512]{2,1,0:T(8,128)(2,1)} %get-tuple-element.53.refs_11_.refs_4_.refs_2_.refs_1_, ...), custom_call_target="tpu_custom_call" | custom-call | flops 1080000000 | bytes 1 | tf_op jit(solution)/shard_map/weigh_rows/pallas_call | solution.py:334
  263.3 5.4 %collective-permute-start.31 = (bf16[128,1024]{1,0:T(8,128)(2,1)}, bf16[128,1024]{1,0:T(8,128)(2,1)S(1)}, u32[]{:S(2)}, u32[]{:S(2)}) collective-permute-start(bf16[128,1024]{1,0:T(8,128)(2,1)} %weigh_rows.8.refs_4_.refs_2_.refs_0_), channel_id=1, source_target_pairs={{4,0},{12,8},{1,5},{9,13},{6,2},{14,10},{3,7},{11,15},{20,16},{28,... | collective-permute-start | bytes 786440 | tf_op jit(solution)/shard_map/ppermute | solution.py:401
  272.6 3.3 add_terms.10
  280.3 9.2 %weigh_rows.9.refs_0_ = bf16[64,1024]{1,0:T(8,128)(2,1)} custom-call(bf16[2,64,3584]{2,1,0:T(8,128)(2,1)} %collective-permute-done.34.refs_0_, bf16[2,3584,512]{2,1,0:T(8,128)(2,1)} %get-tuple-element.53.refs_11_.refs_4_.refs_2_.refs_1_, bf16[2,3584,512]{2,1,0:T(8,128)(2,1)} %collective-permute-done.17.refs_11_.refs_5_.refs_3_.refs_2_, ...), custom_call_target="tpu_custom_call" | custom-call | flops 5400000000 | bytes 1 | tf_op jit(solution)/shard_map/weigh_rows/pallas_call | solution.py:334
  296.5 3.3 add_terms.15
  310.5 5.7 %collective-permute-start.38 = (bf16[1024,512]{1,0:T(8,128)(2,1)}, bf16[1024,512]{1,0:T(8,128)(2,1)S(1)}, u32[]{:S(2)}, u32[]{:S(2)}) collective-permute-start(bf16[1024,512]{1,0:T(8,128)(2,1)} %maximum_select_fusion.1), channel_id=1, source_target_pairs={{0,1},{1,0},{2,3},{3,2},{4,5},{5,4},{6,7},{7,6},{8,9},{9,8},{10,11... | collective-permute-start | bytes 3145736 | tf_op jit(solution)/shard_map/ppermute | solution.py:48
  320.1 8.6 %collective-permute-start.40 = (bf16[64,512]{1,0:T(8,128)(2,1)S(1)}, bf16[64,512]{1,0:T(8,128)(2,1)S(1)}, u32[]{:S(2)}, u32[]{:S(2)}) collective-permute-start(bf16[64,512]{1,0:T(8,128)(2,1)S(1)} %slice.157), channel_id=1, source_target_pairs={{0,1},{1,0},{2,3},{3,2},{4,5},{5,4},{6,7},{7,6},{8,9},{9,8},{10,11... | collective-permute-start | bytes 196616 | tf_op jit(solution)/shard_map/ppermute | solution.py:48
  (195 shorter events, 104.4 us)
Async XLA Ops:
  4.8 25.2 %collective-permute-start.3 = (bf16[1024,512]{1,0:T(8,128)(2,1)}, bf16[1024,512]{1,0:T(8,128)(2,1)}, u32[]{:S(2)}, u32[]{:S(2)}) collective-permute-start(bf16[1024,512]{1,0:T(8,128)(2,1)} %bitcast.3.refs_3_), channel_id=1, source_target_pairs={{0,4},{4,8},{8,12},{1,5},{5,9},{9,13},{2,6},{6,10},{10,14},{3,7},{... | collective-permute-start | bytes 3145736 | tf_op jit(solution)/shard_map/ppermute | solution.py:113
  9.3 25.6 %collective-permute-start.4 = (bf16[1024,512]{1,0:T(8,128)(2,1)}, bf16[1024,512]{1,0:T(8,128)(2,1)}, u32[]{:S(2)}, u32[]{:S(2)}) collective-permute-start(bf16[1024,512]{1,0:T(8,128)(2,1)} %bitcast.3.refs_3_), channel_id=1, source_target_pairs={{4,0},{8,4},{12,8},{5,1},{9,5},{13,9},{6,2},{10,6},{14,10},{7,3},{... | collective-permute-start | bytes 3145736 | tf_op jit(solution)/shard_map/ppermute | solution.py:114
  10.6 43.5 %collective-permute-start.1 = (bf16[2,64,3584]{2,1,0:T(8,128)(2,1)}, bf16[2,64,3584]{2,1,0:T(8,128)(2,1)}, u32[]{:S(2)}, u32[]{:S(2)}) collective-permute-start(bf16[2,64,3584]{2,1,0:T(8,128)(2,1)} %get-tuple-element.42), channel_id=1, source_target_pairs={{2,0},{3,1},{0,2},{1,3},{6,4},{7,5},{4,6},{5,7},{10,8},{11,9},{8,1... | collective-permute-start | bytes 2752520 | tf_op jit(solution)/shard_map/ppermute | solution.py:54
  28.1 26.0 %collective-permute-start.2 = (bf16[2,64,3584]{2,1,0:T(8,128)(2,1)}, bf16[2,64,3584]{2,1,0:T(8,128)(2,1)S(1)}, u32[]{:S(2)}, u32[]{:S(2)}) collective-permute-start(bf16[2,64,3584]{2,1,0:T(8,128)(2,1)} %get-tuple-element.41.refs_2_), channel_id=1, source_target_pairs={{16,0},{0,16},{17,1},{1,17},{18,2},{2,18},{19,3},{3,19},{20,4},{4,... | collective-permute-start | bytes 2752520 | tf_op jit(solution)/shard_map/ppermute | solution.py:59
  29.3 46.6 %collective-permute-start.5 = (bf16[2,64,3584]{2,1,0:T(8,128)(2,1)}, bf16[2,64,3584]{2,1,0:T(8,128)(2,1)S(1)}, u32[]{:S(2)}, u32[]{:S(2)}) collective-permute-start(bf16[2,64,3584]{2,1,0:T(8,128)(2,1)} %get-tuple-element.43.refs_6_), channel_id=1, source_target_pairs={{2,0},{3,1},{0,2},{1,3},{6,4},{7,5},{4,6},{5,7},{10,8},{11,9},{8,1... | collective-permute-start | bytes 2752520 | tf_op jit(solution)/shard_map/ppermute | solution.py:54
  30.0 32.0 %collective-permute-start.7 = (bf16[1024,512]{1,0:T(8,128)(2,1)}, bf16[1024,512]{1,0:T(8,128)(2,1)S(1)}, u32[]{:S(2)}, u32[]{:S(2)}) collective-permute-start(bf16[1024,512]{1,0:T(8,128)(2,1)} %collective-permute-done.3.refs_4_), channel_id=1, source_target_pairs={{0,4},{4,8},{8,12},{1,5},{5,9},{9,13},{2,6},{6,10},{10,14},{3,7},{... | collective-permute-start | bytes 3145736 | tf_op jit(solution)/shard_map/ppermute | solution.py:113
  34.9 37.6 %collective-permute-start.8 = (bf16[1024,512]{1,0:T(8,128)(2,1)}, bf16[1024,512]{1,0:T(8,128)(2,1)}, u32[]{:S(2)}, u32[]{:S(2)}) collective-permute-start(bf16[1024,512]{1,0:T(8,128)(2,1)} %collective-permute-done.4.refs_5_), channel_id=1, source_target_pairs={{4,0},{8,4},{12,8},{5,1},{9,5},{13,9},{6,2},{10,6},{14,10},{7,3},{... | collective-permute-start | bytes 3145736 | tf_op jit(solution)/shard_map/ppermute | solution.py:114
  62.1 31.8 %collective-permute-start.11 = (bf16[1024,512]{1,0:T(8,128)(2,1)S(1)}, bf16[1024,512]{1,0:T(8,128)(2,1)}, u32[]{:S(2)}, u32[]{:S(2)}) collective-permute-start(bf16[1024,512]{1,0:T(8,128)(2,1)S(1)} %collective-permute-done.7.refs_4_.refs_2_), channel_id=1, source_target_pairs={{0,4},{4,8},{8,12},{1,5},{5,9},{9,13},{2,6},{6,10},{10,14},{3,7},{... | collective-permute-start | bytes 3145736 | tf_op jit(solution)/shard_map/ppermute | solution.py:113
  81.3 51.5 %collective-permute-start.13 = (bf16[2,64,3584]{2,1,0:T(8,128)(2,1)}, bf16[2,64,3584]{2,1,0:T(8,128)(2,1)S(1)}, u32[]{:S(2)}, u32[]{:S(2)}) collective-permute-start(bf16[2,64,3584]{2,1,0:T(8,128)(2,1)} %get-tuple-element.49), channel_id=1, source_target_pairs={{2,0},{3,1},{0,2},{1,3},{6,4},{7,5},{4,6},{5,7},{10,8},{11,9},{8,1... | collective-permute-start | bytes 2752520 | tf_op jit(solution)/shard_map/ppermute | solution.py:54
  102.1 30.7 %collective-permute-start.15 = (bf16[2,64,3584]{2,1,0:T(8,128)(2,1)}, bf16[2,64,3584]{2,1,0:T(8,128)(2,1)S(1)}, u32[]{:S(2)}, u32[]{:S(2)}) collective-permute-start(bf16[2,64,3584]{2,1,0:T(8,128)(2,1)} %get-tuple-element.48.refs_5_), channel_id=1, source_target_pairs={{16,0},{0,16},{17,1},{1,17},{18,2},{2,18},{19,3},{3,19},{20,4},{4,... | collective-permute-start | bytes 2752520 | tf_op jit(solution)/shard_map/ppermute | solution.py:59
  103.4 28.6 %collective-permute-start.14 = (f32[128,512]{1,0:T(8,128)}, f32[128,512]{1,0:T(8,128)S(1)}, u32[]{:S(2)}, u32[]{:S(2)}) collective-permute-start(f32[128,512]{1,0:T(8,128)} %get-tuple-element.51), channel_id=1, source_target_pairs={{0,4},{4,0},{8,12},{12,8},{1,5},{5,1},{9,13},{13,9},{2,6},{6,2},{1... | collective-permute-start | bytes 786440 | tf_op jit(solution)/shard_map/ppermute | solution.py:377
  136.7 36.3 %collective-permute-start.17 = (bf16[2,3584,512]{2,1,0:T(8,128)(2,1)}, bf16[2,3584,512]{2,1,0:T(8,128)(2,1)}, u32[]{:S(2)}, u32[]{:S(2)}) collective-permute-start(bf16[2,3584,512]{2,1,0:T(8,128)(2,1)} %get-tuple-element.53.refs_11_.refs_4_.refs_2_.refs_1_), channel_id=1, source_target_pairs={{0,1},{1,0},{2,3},{3,2},{4,5},{5,4},{6,7},{7,6},{8,9},{9,8},{10,11... | collective-permute-start | bytes 22020104 | tf_op jit(solution)/shard_map/ppermute | solution.py:48
  141.5 25.9 %collective-permute-start.18 = (bf16[2,64,3584]{2,1,0:T(8,128)(2,1)}, bf16[2,64,3584]{2,1,0:T(8,128)(2,1)S(1)}, u32[]{:S(2)}, u32[]{:S(2)}) collective-permute-start(bf16[2,64,3584]{2,1,0:T(8,128)(2,1)} %get-tuple-element.50.refs_8_), channel_id=1, source_target_pairs={{2,0},{3,1},{0,2},{1,3},{6,4},{7,5},{4,6},{5,7},{10,8},{11,9},{8,1... | collective-permute-start | bytes 2752520 | tf_op jit(solution)/shard_map/ppermute | solution.py:54
  143.1 72.3 %collective-permute-start.24 = (bf16[2,64,3584]{2,1,0:T(8,128)(2,1)}, bf16[2,64,3584]{2,1,0:T(8,128)(2,1)S(1)}, u32[]{:S(2)}, u32[]{:S(2)}) collective-permute-start(bf16[2,64,3584]{2,1,0:T(8,128)(2,1)} %get-tuple-element.54.refs_13_), channel_id=1, source_target_pairs={{2,0},{3,1},{0,2},{1,3},{6,4},{7,5},{4,6},{5,7},{10,8},{11,9},{8,1... | collective-permute-start | bytes 2752520 | tf_op jit(solution)/shard_map/ppermute | solution.py:54
  161.7 57.3 %collective-permute-start.16 = (bf16[1600,512]{1,0:T(8,128)(2,1)}, bf16[1600,512]{1,0:T(8,128)(2,1)}, u32[]{:S(2)}, u32[]{:S(2)}) collective-permute-start(bf16[1600,512]{1,0:T(8,128)(2,1)} %get-tuple-element.55.refs_5_.refs_0_), channel_id=1, source_target_pairs={{4,0},{12,8},{1,5},{9,13},{6,2},{14,10},{3,7},{11,15},{20,16},{28,... | collective-permute-start | bytes 4915208 | tf_op jit(solution)/shard_map/ppermute | solution.py:401
  170.9 44.5 %collective-permute-start.26 = (bf16[2,64,3584]{2,1,0:T(8,128)(2,1)}, bf16[2,64,3584]{2,1,0:T(8,128)(2,1)S(1)}, u32[]{:S(2)}, u32[]{:S(2)}) collective-permute-start(bf16[2,64,3584]{2,1,0:T(8,128)(2,1)} %get-tuple-element.62.refs_0_), channel_id=1, source_target_pairs={{16,0},{0,16},{17,1},{1,17},{18,2},{2,18},{19,3},{3,19},{20,4},{4,... | collective-permute-start | bytes 2752520 | tf_op jit(solution)/shard_map/ppermute | solution.py:59
  191.1 56.8 %collective-permute-start.29 = (bf16[1600,512]{1,0:T(8,128)(2,1)}, bf16[1600,512]{1,0:T(8,128)(2,1)}, u32[]{:S(2)}, u32[]{:S(2)}) collective-permute-start(bf16[1600,512]{1,0:T(8,128)(2,1)} %weigh_rows.6.refs_2_.refs_3_.refs_0_), channel_id=1, source_target_pairs={{4,0},{12,8},{1,5},{9,13},{6,2},{14,10},{3,7},{11,15},{20,16},{28,... | collective-permute-start | bytes 4915208 | tf_op jit(solution)/shard_map/ppermute | solution.py:401
  217.9 27.2 %collective-permute-start.27 = (bf16[2,64,3584]{2,1,0:T(8,128)(2,1)}, bf16[2,64,3584]{2,1,0:T(8,128)(2,1)S(1)}, u32[]{:S(2)}, u32[]{:S(2)}) collective-permute-start(bf16[2,64,3584]{2,1,0:T(8,128)(2,1)} %get-tuple-element.63.refs_1_), channel_id=1, source_target_pairs={{16,0},{0,16},{17,1},{1,17},{18,2},{2,18},{19,3},{3,19},{20,4},{4,... | collective-permute-start | bytes 2752520 | tf_op jit(solution)/shard_map/ppermute | solution.py:59
  222.4 30.5 %collective-permute-start.21 = (bf16[1024,512]{1,0:T(8,128)(2,1)}, bf16[1024,512]{1,0:T(8,128)(2,1)S(1)}, u32[]{:S(2)}, u32[]{:S(2)}) collective-permute-start(bf16[1024,512]{1,0:T(8,128)(2,1)} %get-tuple-element.59.refs_7_.refs_0_), channel_id=1, source_target_pairs={{8,0},{13,5},{2,10},{7,15},{24,16},{29,21},{18,26},{23,31}} | collective-permute-start | bytes 3145736 | tf_op jit(solution)/shard_map/ppermute | solution.py:401
  236.3 33.5 %collective-permute-start.30 = (bf16[256,1024]{1,0:T(8,128)(2,1)}, bf16[256,1024]{1,0:T(8,128)(2,1)}, u32[]{:S(2)}, u32[]{:S(2)}) collective-permute-start(bf16[256,1024]{1,0:T(8,128)(2,1)} %weigh_rows.7.refs_2_.refs_0_), channel_id=1, source_target_pairs={{4,0},{12,8},{1,5},{9,13},{6,2},{14,10},{3,7},{11,15},{20,16},{28,... | collective-permute-start | bytes 1572872 | tf_op jit(solution)/shard_map/ppermute | solution.py:401
  246.7 32.4 %collective-permute-start.34 = (bf16[2,64,3584]{2,1,0:T(8,128)(2,1)}, bf16[2,64,3584]{2,1,0:T(8,128)(2,1)}, u32[]{:S(2)}, u32[]{:S(2)}) collective-permute-start(bf16[2,64,3584]{2,1,0:T(8,128)(2,1)} %get-tuple-element.66.refs_0_), channel_id=1, source_target_pairs={{16,0},{0,16},{17,1},{1,17},{18,2},{2,18},{19,3},{3,19},{20,4},{4,... | collective-permute-start | bytes 2752520 | tf_op jit(solution)/shard_map/ppermute | solution.py:59
  251.2 27.9 %collective-permute-start.35 = (bf16[1024,512]{1,0:T(8,128)(2,1)}, bf16[1024,512]{1,0:T(8,128)(2,1)S(1)}, u32[]{:S(2)}, u32[]{:S(2)}) collective-permute-start(bf16[1024,512]{1,0:T(8,128)(2,1)} %get-tuple-element.68.refs_5_.refs_0_), channel_id=1, source_target_pairs={{8,0},{13,5},{2,10},{7,15},{24,16},{29,21},{18,26},{23,31}} | collective-permute-start | bytes 3145736 | tf_op jit(solution)/shard_map/ppermute | solution.py:401
  252.2 26.9 %collective-permute-start.36 = (bf16[576,512]{1,0:T(8,128)(2,1)}, bf16[576,512]{1,0:T(8,128)(2,1)S(1)}, u32[]{:S(2)}, u32[]{:S(2)}) collective-permute-start(bf16[576,512]{1,0:T(8,128)(2,1)} %get-tuple-element.69.refs_6_.refs_1_), channel_id=1, source_target_pairs={{0,8},{5,13},{10,2},{15,7},{16,24},{21,29},{26,18},{31,23}} | collective-permute-start | bytes 1769480 | tf_op jit(solution)/shard_map/ppermute | solution.py:401
  271.9 29.8 %collective-permute-start.32 = (bf16[256,1024]{1,0:T(8,128)(2,1)}, bf16[256,1024]{1,0:T(8,128)(2,1)S(1)}, u32[]{:S(2)}, u32[]{:S(2)}) collective-permute-start(bf16[256,1024]{1,0:T(8,128)(2,1)} %add_terms.11.refs_0_), channel_id=1, source_target_pairs={{0,8},{5,13},{10,2},{15,7},{16,24},{21,29},{26,18},{31,23}} | collective-permute-start | bytes 1572872 | tf_op jit(solution)/shard_map/ppermute | solution.py:401
  (54 other events, 531.2 us)

commit v6 on v5

--- a/solution.py
+++ b/solution.py
@@ -160,51 +160,52 @@
     )(gate_act, up_act, proj_h, *after)
 
 
-def hidden_part(rank, below, above, w_down, first, so_far, slopes, after):
+def hidden_part(rank, below, above, w_down, so_far, slopes, proj_u, after):
     ranks = lax.axis_size("tensor")
-    features, count = (below or above)[0].shape
+    features, count = below[0].shape
     hidden = w_down.shape[0]
-    own = len(below) - len(above)
-    span = len(above)
-    slots = own + min(2 * span, ranks - first)
-    finish = slopes is not None
-    tile = widest(hidden, (896, 512, 128) if finish else (1792, 896, 128))
-    sources = [*below, *above]
-
-    def slot_of(z, at):
-        if at < own:
-            return z, True
-        under = jnp.clip(z - first + 1, 0, span)
-        over = jnp.clip(ranks - z - first, 0, span)
-        at -= own
-        block = jnp.where(at < under, z - first - at, z + first + at - under)
-        return block, at < under + over
+    finish = so_far is not None
+    slots = ranks - 2 if finish else 2
+    tile = widest(hidden, (896, 512, 128))
+    sources = [(t, -1, below[t]) for t in range(2 if finish else 0, ranks if finish else 2)]
+    sources += [(t, 1, above[t - 1]) for t in range(1, ranks if finish else 2)]
+
+    def counts(z):
+        both = ((z >= 1) & (z <= ranks - 2)).astype(jnp.int32)
+        return both, jnp.maximum(z - 1, 0)
+
+    def place_of(z, t, side):
+        if not finish:
+            return (0, z >= 0) if t == 0 else (1, z >= 1 if side < 0 else z == 0)
+        both, under = counts(z)
+        if side < 0:
+            return both + t - 2, t <= z
+        if t == 1:
+            return 0, both == 1
+        return both + under + t - 2, z + t <= ranks - 1
 
     def column(at, i, rank_ref):
-        block, valid = slot_of(rank_ref[0], at)
-        if valid is True:
-            return (i, block)
-        return (jnp.where(valid, i, 0), jnp.where(valid, block, 0))
+        z = rank_ref[0]
+        if not finish:
+            return (i, z) if at == 0 else (i, jnp.where(z >= 1, z - 1, 1))
+        both, under = counts(z)
+        block = jnp.where(at < both + under, z - (at - both + 2), z + (at - both - under + 2))
+        return (i, jnp.where(at < both, z + 1, block))
 
     def kernel(rank_ref, *refs):
         z = rank_ref[0]
         downs, arrived = refs[:slots], refs[slots : slots + len(sources)]
         grad_ref, total, sem = refs[-3:]
-        out = refs[-4]
+        rest = refs[slots + len(sources) :]
 
         def gather(wait):
-            under = jnp.clip(z - first + 1, 0, span)
-            over = jnp.clip(ranks - z - first, 0, span)
-            pieces = [(arrived[at], z >= 0, at) for at in range(own)]
-            for t in range(span):
-                pieces.append((arrived[own + t], t < under, own + t))
-                pieces.append((arrived[len(below) + t], t < over, own + under + t))
-            for at, (source, valid, place) in enumerate(pieces):
+            for at, (t, side, _) in enumerate(sources):
+                place, valid = place_of(z, t, side)
 
                 @pl.when(valid)
                 def _():
                     rows = pl.ds(pl.multiple_of(place * features, features), features)
-                    copy = pltpu.make_async_copy(source, grad_ref.at[rows, :], sem.at[at])
+                    copy = pltpu.make_async_copy(arrived[at], grad_ref.at[rows, :], sem.at[at])
                     copy.wait() if wait else copy.start()
 
         @pl.when(pl.program_id(0) == 0)
@@ -212,44 +213,52 @@
             gather(False)
             gather(True)
 
-        rest = refs[slots + len(sources) :]
-        if so_far is not None:
+        if finish:
             total[...] = rest[0][...]
         for at in range(slots):
-
-            def add_slot(at=at):
-                term = jnp.dot(
-                    downs[at][...],
-                    grad_ref[at * features : (at + 1) * features, :],
-                    preferred_element_type=jnp.float32,
-                )
-                if at == 0 and so_far is None:
-                    total[...] = term
-                else:
-                    total[...] += term
-
-            _, valid = slot_of(z, at)
-            if valid is True:
-                add_slot()
-            else:
-                pl.when(valid)(add_slot)
+            term = jnp.dot(
+                downs[at][...],
+                grad_ref[at * features : (at + 1) * features, :],
+                preferred_element_type=jnp.float32,
+            )
+            total[...] = total[...] + term if at or finish else term
         if finish:
-            out[0] = (total[...] * rest[1][0]).astype(jnp.bfloat16)
-            out[1] = (total[...] * rest[1][1]).astype(jnp.bfloat16)
+            both_ref, out_ref = refs[-5:-3]
+            both_ref[0] = (total[...] * rest[1][0]).astype(jnp.bfloat16)
+            up_grad = (total[...] * rest[1][1]).astype(jnp.bfloat16)
+            both_ref[1] = up_grad
+            part = jnp.dot(rest[2][...], up_grad, preferred_element_type=jnp.float32)
+
+            @pl.when(pl.program_id(0) == 0)
+            def _():
+                out_ref[...] = part
+
+            @pl.when(pl.program_id(0) > 0)
+            def _():
+                out_ref[...] += part
+
         else:
-            out[...] = total[...]
-
-    operands = [w_down] * slots + sources
+            refs[-4][...] = total[...]
+
+    operands = [w_down] * slots + [value for _, _, value in sources]
     specs = [pl.BlockSpec((tile, features), functools.partial(column, at)) for at in range(slots)]
     specs += [ANYWHERE] * len(sources)
-    if so_far is not None:
-        operands.append(so_far)
-        specs.append(pl.BlockSpec((tile, count), lambda i, r: (i, 0)))
     if finish:
-        operands.append(slopes)
-        specs.append(pl.BlockSpec((2, tile, count), lambda i, r: (0, i, 0)))
-        out_shape = jax.ShapeDtypeStruct((2, hidden, count), jnp.bfloat16)
-        out_specs = pl.BlockSpec((2, tile, count), lambda i, r: (0, i, 0))
+        narrow = proj_u.shape[0]
+        operands += [so_far, slopes, proj_u]
+        specs += [
+            pl.BlockSpec((tile, count), lambda i, r: (i, 0)),
+            pl.BlockSpec((2, tile, count), lambda i, r: (0, i, 0)),
+            pl.BlockSpec((narrow, tile), lambda i, r: (0, i)),
+        ]
+        out_shape = [
+            jax.ShapeDtypeStruct((2, hidden, count), jnp.bfloat16),
+            jax.ShapeDtypeStruct((narrow, count), jnp.float32),
+        ]
+        out_specs = [
+            pl.BlockSpec((2, tile, count), lambda i, r: (0, i, 0)),
+            pl.BlockSpec((narrow, count), lambda i, r: (0, 0)),
+        ]
     else:
         out_shape = jax.ShapeDtypeStruct((hidden, count), jnp.float32)
         out_specs = pl.BlockSpec((tile, count), lambda i, r: (i, 0))
@@ -344,7 +353,7 @@
     )(*flat, *grads, *extras, *after)
 
 
-def add(values, others, heights, after):
+def add(values, others, heights, after, price=2):
     pairs = len(values)
     flat = [h for hs in heights for h in hs]
 
@@ -367,9 +376,119 @@
         in_specs=[whole] * (2 * pairs) + [ANYWHERE] * len(after),
         out_specs=[whole] * len(flat),
         compiler_params=pltpu.CompilerParams(vmem_limit_bytes=VMEM_BYTES),
-        cost_estimate=cost(2),
+        cost_estimate=cost(price),
         name="add_terms",
     )(*values, *others, *after)
+
+
+def assemble(words, count, features, part, near, far, chips, after):
+    groups = lax.axis_size("groups")
+    height = near[0][0][0].shape[0]
+    tall = features // part
+    arrays, index = [], {}
+
+    def at_of(value):
+        if id(value) not in index:
+            index[id(value)] = len(arrays)
+            arrays.append(value)
+        return index[id(value)]
+
+    near_at = [[[at_of(v) for v in pair] for pair in half] for half in near]
+    far_at = {
+        n: (row, [([at_of(v) for v in pair], first) for pair, first in halves])
+        for n, (row, halves) in far.items()
+    }
+    chunks = 1 + max(n[0] for n in far)
+    piece = part // CHUNKS
+
+    def kernel(words_ref, *refs):
+        outs = refs[-2:]
+        away, group, inside = words_ref[0], words_ref[1], words_ref[2]
+
+        def total(pair, rows, cols):
+            one, two = (refs[at][rows, cols].astype(jnp.float32) for at in pair)
+            return (one + two).astype(jnp.bfloat16)
+
+        for j in range(len(near[0])):
+
+            @pl.when((away == 0) & (inside == j * height))
+            def _(j=j):
+                for half in range(2):
+                    outs[half][...] = total(near_at[half][j], slice(0, height), slice(0, count))
+
+        for s in range(1, chips):
+            for g in range(groups):
+                for h in range(0, groups, tall):
+
+                    @pl.when((away == s) & (group == g) & (inside == h * part))
+                    def _(s=s, g=g, h=h):
+                        for j in range(tall):
+                            shift = (h + j - g) % groups
+                            for k in range(CHUNKS):
+                                top = j * part + k * piece
+                                for half in range(2):
+                                    if (k, s, shift) in far_at:
+                                        row, halves = far_at[k, s, shift]
+                                        pair, first = halves[half]
+                                        value = total(
+                                            pair, slice(row, row + piece), slice(first, first + count)
+                                        )
+                                    else:
+                                        value = jnp.zeros((piece, count), jnp.bfloat16)
+                                    outs[half][top : top + piece] = value
+
+    whole = pl.BlockSpec(memory_space=pltpu.VMEM)
+    return pl.pallas_call(
+        kernel,
+        out_shape=[jax.ShapeDtypeStruct((features, count), jnp.bfloat16)] * 2,
+        in_specs=[pl.BlockSpec(memory_space=pltpu.SMEM)]
+        + [whole] * len(arrays)
+        + [ANYWHERE] * len(after),
+        out_specs=[whole] * 2,
+        compiler_params=pltpu.CompilerParams(vmem_limit_bytes=VMEM_BYTES),
+        cost_estimate=cost(5),
+        name="assemble",
+    )(words, *arrays, *after)
+
+
+def finish(words, part, mine, theirs, late_mine, late_theirs, late, chips):
+    features, count = mine.shape
+    groups = lax.axis_size("groups")
+    tall = features // part
+    piece = part // CHUNKS
+
+    def kernel(words_ref, mine_ref, theirs_ref, late_mine_ref, late_theirs_ref, out_ref, rows_ref):
+        away, group, inside = words_ref[0], words_ref[1], words_ref[2]
+        for own, base, extra in ((1, mine_ref, late_mine_ref), (0, theirs_ref, late_theirs_ref)):
+
+            @pl.when(words_ref[3] == own)
+            def _(base=base, extra=extra):
+                rows_ref[...] = base[...]
+                for g in range(groups):
+                    for h in range(0, groups, tall):
+
+                        @pl.when((away > 0) & (group == g) & (inside == h * part))
+                        def _(g=g, h=h):
+                            for j in range(tall):
+                                for at, (k, r) in enumerate(late):
+                                    if (h + j - g) % groups == r:
+                                        top = j * part + k * piece
+                                        rows_ref[top : top + piece] = extra[
+                                            at * piece : (at + 1) * piece
+                                        ]
+
+        out_ref[...] = rows_ref[...].T
+
+    return pl.pallas_call(
+        kernel,
+        out_shape=jax.ShapeDtypeStruct((count, features), mine.dtype),
+        in_specs=[pl.BlockSpec(memory_space=pltpu.SMEM)] + [pl.BlockSpec(memory_space=pltpu.VMEM)] * 4,
+        out_specs=pl.BlockSpec(memory_space=pltpu.VMEM),
+        scratch_shapes=[pltpu.VMEM((features, count), mine.dtype)],
+        compiler_params=pltpu.CompilerParams(vmem_limit_bytes=VMEM_BYTES),
+        cost_estimate=cost(3),
+        name="finish",
+    )(words, mine, theirs, late_mine, late_theirs)
 
 
 def exchange(value, bit):
@@ -511,10 +630,10 @@
         got = [send(out, hops(b[0][0], 1)) for out, b in zip(outs, bundles)]
         return outs, got, bundles
 
-    def carry_on(work, after):
+    def carry_on(work, after, price=2):
         outs, got, bundles = work
         heights = [[sum(u[0].shape[-2] for u in units) for _, units, _ in b] for b in bundles]
-        sums = list(add(outs, got, heights, after))
+        sums = list(add(outs, got, heights, after, price))
         routes = [route for b in bundles for route in b]
         ends = later_steps(sums, [table for table, _, _ in routes])
         return sums, [(names, *end) for (_, _, names), end in zip(routes, ends)]
@@ -533,50 +652,83 @@
 
     bits = [1 << i for i in range(ranks.bit_length() - 1)]
     hold_arrived(0, [slopes])
-    so_far = hidden_part(rank_word, below[:2], above[:1], w_down, 1, None, None, [ticks[0]])
+    so_far = hidden_part(rank_word, below, above, w_down, None, None, None, [ticks[0]])
     hold_arrived(1, [so_far])
-    hold_arrived(2, [below[2], above[1], early_part, out_down_part])
-    (early,) = hold_arrived(3, below[3:] + above[2:], [early_part])
-    mine = hidden_part(rank_word, below[2:], above[1:], w_down, 2, so_far, slopes, [ticks[3]])
+    forward(2, [below[2], above[1], early_part, out_down_part])
+    (early,) = forward(3, below[3:] + above[2:], [early_part])
+    mine, up_out_part = hidden_part(
+        rank_word, below, above, w_down, so_far, slopes, proj_u.T, [ticks[3]]
+    )
     early = early + exchange(early, bits[0])
-    mine, early = hold_arrived(4, [], [mine, early])
+    mine, early = forward(4, [], [mine, early])
     theirs = swap_cores(mine)
-    for bit in bits[1:]:
+
+    out_parts = jnp.stack([up_out_part, out_down_part]).reshape(2, ranks, -1, count)
+    out_parts = out_parts.transpose(1, 0, 2, 3).reshape(-1, count)
+    half = out_parts.shape[0] // 2
+    high = rank & bits[-1] != 0
+    width = early.shape[0]
+    got = exchange(
+        jnp.concatenate([early, jnp.where(high, out_parts[:half], out_parts[half:])], axis=0),
+        bits[-1],
+    )
+    early = early + got[:width]
+    out_parts = jnp.where(high, out_parts[half:], out_parts[:half]) + got[width:]
+    for bit in bits[1:-1]:
         early = early + exchange(early, bit)
+
     first_names = [(k, 0) for k in range(5)] + [(k, 1) for k in range(4)]
-    first_mine = terms(first_names, [mine], [ticks[4]], 16, near=True, extra=proj_u.T)
-    up_out_part = first_mine[0].pop()
-    (up_out_part,) = hold_arrived(5, first_mine[0] + [early], [up_out_part])
+    first_mine = terms(first_names, [mine], [ticks[4]], 16, near=True)
+    (out_parts,) = forward(5, first_mine[0] + [early], [out_parts])
     first_theirs = terms(first_names, [theirs], [ticks[5]], 16, near=True)
     sums_mine, end_mine = carry_on(first_mine, first_theirs[0])
-    out_parts = jnp.stack([up_out_part, out_down_part]).reshape(2, ranks, -1, count)
-    out_parts = halve(out_parts.transpose(1, 0, 2, 3), bits[-1])
-    (out_parts,) = hold_arrived(6, first_theirs[0], [out_parts])
+    hold_arrived(6, first_theirs[0])
     second_names = [(5, 0), (6, 0), (4, 1), (5, 1)]
     second = terms(second_names, [mine, theirs], [ticks[6]] + sums_mine, 10)
     sums_theirs, end_theirs = carry_on(first_theirs, second[0])
+    (out_parts,) = hold_arrived(7, second[0], [out_parts])
+    third_names = [(7, 0), (6, 1)]
+    received = [got for _, _, got in end_mine]
+    third = terms(third_names, [mine, theirs], [ticks[7]] + sums_theirs + received, 4)
+    sums_second, end_second = carry_on(second, third[0])
+
     for bit in bits[-2::-1]:
         out_parts = halve(out_parts, bit)
-    hold_arrived(7, second[0] + [out_parts])
-    third_names = [(7, 0), (6, 1)]
-    received = [got for _, _, got in end_mine if got is not None]
-    third = terms(third_names, [mine, theirs], [ticks[7]] + sums_theirs + received, 4)
-    sums_second, end_second = carry_on(second, third[0])
-
     early = early.astype(jnp.bfloat16)
     width = in_down_part.shape[0]
     in_up, in_down = early[:width], early[width:]
     out_parts = out_parts.astype(jnp.bfloat16)
-    up_out, out_down = out_parts[0, 0], out_parts[0, 1]
+    slot = out_parts.shape[0] // 2
+    up_out, out_down = out_parts[:slot], out_parts[slot:]
     member = pack_table(doc_lengths, count)
     doc_logs = jnp.stack(
         [doc_outer(member, up_out, in_up), doc_outer(member, out_down, in_down)], axis=1
     )
 
-    def settle(v, got):
-        if got is None:
-            return v
-        return (v.astype(jnp.float32) + got.astype(jnp.float32)).astype(jnp.bfloat16)
+    sums_third, end_third = carry_on(third, [])
+    last_names = [(CHUNKS - 1, r) for r in range(1, groups)]
+    received = [got for _, _, got in end_theirs]
+    last = terms(last_names, [mine, theirs], sums_third + received, 20)
+    sums_last, end_last = carry_on(last, [], 40)
+
+    first = rank * features
+    away = (first // rows // CORES - chip) % chips
+    owner = first // rows % CORES == core
+    inside = first % rows
+    near, far = [[], []], {}
+    for (names, *m), (_, *t) in zip(end_mine, end_theirs):
+        if names is None:
+            near[0].append(m)
+            near[1].append(t)
+        else:
+            far.update((n, (i * piece, [(m, 0), (t, 0)])) for i, n in enumerate(names))
+    for names, *pair in end_second:
+        far.update((n, (i * piece, [(pair, 0), (pair, count)])) for i, n in enumerate(names))
+    words = jnp.stack([away, group, inside, owner]).astype(jnp.int32)
+    total_mine, total_theirs = assemble(
+        words, count, features, part, near, far, chips, last[0]
+    )
+    from_partner = swap_cores(total_theirs)
 
     def pick(index, options):
         value = options[0]
@@ -584,84 +736,24 @@
             value = jnp.where(index == at, option, value)
         return value
 
-    first = rank * features
-    away = (first // rows // CORES - chip) % chips
-    owner = first // rows % CORES == core
-    inside = first % rows
-    tall = features // part
-    shifts = [(inside // part + j - group) % groups for j in range(tall)]
-
-    def in_order(near, far):
-        options = [pick(inside // height, near)]
-        for s in range(1, chips):
-            by_shift = [
-                jnp.concatenate([far[k, s, r] for k in range(CHUNKS)], axis=0)
-                for r in range(groups)
-            ]
-            options.append(jnp.concatenate([pick(shift, by_shift) for shift in shifts], axis=0))
-        return pick(away, options)
-
-    def settle_at_once(end, after):
-        if end[0][2] is None:
-            return [v for _, v, _ in end]
-        mine = [v for _, v, _ in end]
-        return add(mine, [got for _, _, got in end], [[v.shape[0]] for v in mine], after)
-
-    sums_third, end_third = carry_on(third, [doc_logs])
-    last_names = [(CHUNKS - 1, r) for r in range(1, groups)]
-    settled_mine = settle_at_once(end_mine, third[0])
-    received = [got for _, _, got in end_theirs if got is not None]
-    last = terms(last_names, [mine, theirs], list(settled_mine) + sums_third + received, 20)
-    sums_last, end_last = carry_on(last, [])
-    settled_theirs = settle_at_once(end_theirs, sums_last)
-    later = end_second + end_third
-    settled_later = settle_at_once(later, sums_last)
-
-    near_half, far_half = [[], []], [{}, {}]
-    for at, (end, settled) in enumerate(
-        ((end_mine, settled_mine), (end_theirs, settled_theirs))
-    ):
-        for (names, _, _), value in zip(end, settled):
-            if names is None:
-                near_half[at].append(value)
-            else:
-                far_half[at].update(
-                    (n, value[i * piece : (i + 1) * piece]) for i, n in enumerate(names)
-                )
-
-    for (names, _, _), value in zip(later, settled_later):
-        for i, n in enumerate(names):
-            both = value[i * piece : (i + 1) * piece]
-            far_half[0][n], far_half[1][n] = both[:, :count], both[:, count:]
-    for s in range(1, chips):
-        for _, r in last_names:
-            for half in far_half:
-                half[CHUNKS - 1, s, r] = jnp.zeros((piece, count), jnp.bfloat16)
-    total_mine, total_theirs = (in_order(n, f) for n, f in zip(near_half, far_half))
-    from_partner = swap_cores(total_theirs)
-    total = jnp.where(owner, total_mine, from_partner)
-
     tail = {}
-    for names, *pair in end_last:
-        value = settle(*pair)
+    for names, value, got in end_third + end_last:
+        value = (value.astype(jnp.float32) + got.astype(jnp.float32)).astype(jnp.bfloat16)
         tail.update((n, value[i * piece : (i + 1) * piece]) for i, n in enumerate(names))
+    late = sorted({(k, r) for k, _, r in tail})
     pieces = jnp.concatenate(
-        [
-            pick(away - 1, [tail[k, s, r] for s in range(1, chips)])
-            for k, r in last_names
-        ],
-        axis=0,
-    )
-    pieces = jnp.where(owner, pieces[:, :count], swap_cores(pieces[:, count:]))
-    pieces = jnp.where(away > 0, pieces, jnp.zeros_like(pieces))
-    parts = []
-    for j, shift in enumerate(shifts):
-        end = (j + 1) * part
-        extra = jnp.zeros((piece, count), jnp.bfloat16)
-        for at, (_, r) in enumerate(last_names):
-            extra = jnp.where(shift == r, pieces[at * piece : (at + 1) * piece], extra)
-        parts += [total[j * part : end - piece], total[end - piece : end] + extra]
-    input_grad = jnp.concatenate(parts, axis=0).T
+        [pick(away - 1, [tail[k, s, r] for s in range(1, chips)]) for k, r in late], axis=0
+    )
+    input_grad = finish(
+        words,
+        part,
+        total_mine,
+        from_partner,
+        pieces[:, :count],
+        swap_cores(pieces[:, count:]),
+        late,
+        chips,
+    )
     return (input_grad, doc_logs)
 
 

time: 333 us -> 287 us (0.86)
  waiting for transfers between devices: 41.4 us -> 27.4 us
  starting transfers between devices: 93.2 us -> 79.7 us
  local copies, waits for them, and re-layouts: 25.1 us -> 16.4 us
  Pallas kernels: 155 us -> 150 us
  other arithmetic: 11 us -> 7.65 us
    ppermute x4 -> x3, waiting for transfers between devices: 19.1 us -> 0.01 us  [exchange(): return lax.ppermute(value, 'tensor', [(i, i ^ bit) for i in range(ranks)])]
    ppermute x8, waiting for transfers between devices: 3.78 us -> 19.4 us  [from_group(): lax.ppermute(value, 'groups', [((i + shift) % size, i) for i in range(siz...]
    pallas_call x8 -> x5, Pallas kernels: 21.1 us -> 12.4 us  [add(): pl.pallas_call(kernel, out_shape=[jax.ShapeDtypeStruct((h, count), jnp.bf...]
    pallas_call x0 -> x2, Pallas kernels: none -> 7.93 us  [the longest x1 4.89 us: assemble(): pl.pallas_call(kernel, out_shape=[jax.ShapeDtypeStruct((features, count),...]
    ppermute x8, waiting for transfers between devices: 12.5 us -> 5.53 us  [from_chip(): lax.ppermute(value, 'dp', [((i + step) % size, i) for i in range(size)])]
    ppermute x4 -> x3, starting transfers between devices: 7.3 us -> 2.27 us  [exchange(): return lax.ppermute(value, 'tensor', [(i, i ^ bit) for i in range(ranks)])]
    ppermute x3, starting transfers between devices: 19.2 us -> 15 us  [spread_ranks(): lax.ppermute(below[-1], 'tensor', [(i, i + 1) for i in range(ranks - 1)])]
    pallas_call x2, Pallas kernels: 39.3 us -> 35.4 us  [hidden_part(): pl.pallas_call(kernel, grid_spec=pltpu.PrefetchScalarGridSpec(num_scalar_...]
  transfers between devices with their start and end apart: 41 -> 40, of which waited for: 10 -> 8; matrix products, arithmetic and copies ran while one was open for 6% -> 5% of each run, Pallas kernels for 45% -> 50%
where the time goes in v6:
time: 287 us; the launch traced here: 285 us
  Pallas kernels  150 us (52%)
  starting transfers between devices  79.7 us (28%)
  waiting for transfers between devices  27.4 us (10%)
  local copies, waits for them, and re-layouts  16.4 us (6%)
  other arithmetic  7.65 us (3%)
  matrix products  3.08 us (1%)
    pallas_call x5, Pallas kernels, weigh(): pl.pallas_call(kernel, grid=(steps,), out_shape=shapes, in_specs=specs +...  65.8 us
    pallas_call x2, Pallas kernels, hidden_part(): pl.pallas_call(kernel, grid_spec=pltpu.PrefetchScalarGridSpec(num_scalar_...  35.4 us
    ppermute x12, starting transfers between devices, send(): return lax.ppermute(value, ('groups', 'tensor', 'dp'), pairs)  25.4 us
    ppermute x8, waiting for transfers between devices, from_group(): lax.ppermute(value, 'groups', [((i + shift) % size, i) for i in range(siz...  19.4 us
    ppermute x3, starting transfers between devices, swap_cores(): return lax.ppermute(value, 'dp', [(i, i ^ 1) for i in range(size)])  19.1 us
    pallas_call x9, Pallas kernels, share_rows(): pl.pallas_call(kernel, grid_spec=pltpu.PrefetchScalarGridSpec(num_scalar_...  16.7 us
    unnamed x64, local copies, waits for them, and re-layouts  15.5 us
    ppermute x3, starting transfers between devices, spread_ranks(): lax.ppermute(below[-1], 'tensor', [(i, i + 1) for i in range(ranks - 1)])  15 us
  transfers between devices with their start and end apart: 40, of which 8 were waited for; matrix products, arithmetic and copies ran while one was open for 5% of the time, Pallas kernels for 50%

profile of v6, /device:TPU:3, one launch (start us, length us, event | category | flops | bytes accessed | tf_op | source)
XLA Modules:
  0.0 285.5 jit_solution(15746541385165434086)
XLA Ops:
  6.1 5.1 %collective-permute-start.3 = (bf16[1024,512]{1,0:T(8,128)(2,1)}, bf16[1024,512]{1,0:T(8,128)(2,1)}, u32[]{:S(2)}, u32[]{:S(2)}) collective-permute-start(bf16[1024,512]{1,0:T(8,128)(2,1)} %bitcast.33), channel_id=1, source_target_pairs={{0,4},{4,8},{8,12},{1,5},{5,9},{9,13},{2,6},{6,10},{10,14},{3,7},{... | collective-permute-start | bytes 3145736 | tf_op jit(solution)/shard_map/ppermute | solution.py:113
  12.5 12.0 %prepare.1 = (f32[2,3584,512]{2,1,0:T(8,128)}, f32[64,512]{1,0:T(8,128)}) custom-call(bf16[512,3584]{1,0:T(8,128)(2,1)} %gate_ref.1, bf16[512,3584]{1,0:T(8,128)(2,1)} %up_ref.1, bf16[64,3584]{1,0:T(8,128)(2,1)} %bitcast.42, bf16[2,64,3584]{2,1,0:T(8,128)(2,1)} %get-tuple-element.30.refs_0_), custom_call_target="tpu_custom_call" | custom-call | flops 3240000000 | bytes 1 | tf_op jit(solution)/shard_map/prepare/pallas_call | solution.py:140
  32.4 5.0 %collective-permute-start.8 = (bf16[1024,512]{1,0:T(8,128)(2,1)}, bf16[1024,512]{1,0:T(8,128)(2,1)}, u32[]{:S(2)}, u32[]{:S(2)}) collective-permute-start(bf16[1024,512]{1,0:T(8,128)(2,1)} %collective-permute-done.3.refs_3_), channel_id=1, source_target_pairs={{0,4},{4,8},{8,12},{1,5},{5,9},{9,13},{2,6},{6,10},{10,14},{3,7},{... | collective-permute-start | bytes 3145736 | tf_op jit(solution)/shard_map/ppermute | solution.py:113
  38.4 14.3 %hidden_part.2.refs_4_.refs_7_ = f32[3584,512]{1,0:T(8,128)} custom-call(s32[1]{0:T(128)} %bitcast.5.rank_ref, bf16[3584,4096]{1,0:T(8,128)(2,1)} %refs_1_.17, bf16[3584,4096]{1,0:T(8,128)(2,1)} %refs_1_.17, bf16[1024,512]{1,0:T(8,128)(2,1)} %bitcast.34, bf16[1024,512]{1,0:T(8,128)(2,1)} %collective-permute-done.3.refs_3_, ...), custom_call_target="tpu_custom_call" | custom-call | flops 3240000000 | bytes 1 | tf_op jit(solution)/shard_map/hidden_part/pallas_call | solution.py:265
  58.6 5.0 %collective-permute-start.13 = (bf16[1024,512]{1,0:T(8,128)(2,1)}, bf16[1024,512]{1,0:T(8,128)(2,1)}, u32[]{:S(2)}, u32[]{:S(2)}) collective-permute-start(bf16[1024,512]{1,0:T(8,128)(2,1)} %collective-permute-done.8.refs_4_.refs_2_), channel_id=1, source_target_pairs={{0,4},{4,8},{8,12},{1,5},{5,9},{9,13},{2,6},{6,10},{10,14},{3,7},{... | collective-permute-start | bytes 3145736 | tf_op jit(solution)/shard_map/ppermute | solution.py:113
  68.5 6.8 %collective-permute-done.7.refs_3_.refs_8_ = bf16[2,64,3584]{2,1,0:T(8,128)(2,1)S(1)} collective-permute-done((bf16[2,64,3584]{2,1,0:T(8,128)(2,1)}, bf16[2,64,3584]{2,1,0:T(8,128)(2,1)S(1)}, u32[]{:S(2)}, u32[]{:S(2)}) %collective-permute-start.7) | collective-permute-done | bytes 917536 | tf_op jit(solution)/shard_map/ppermute | solution.py:59
  79.1 4.9 %collective-permute-done.6.refs_3_.refs_5_ = bf16[2,64,3584]{2,1,0:T(8,128)(2,1)} collective-permute-done((bf16[2,64,3584]{2,1,0:T(8,128)(2,1)}, bf16[2,64,3584]{2,1,0:T(8,128)(2,1)}, u32[]{:S(2)}, u32[]{:S(2)}) %collective-permute-start.6) | collective-permute-done | bytes 917536 | tf_op jit(solution)/shard_map/ppermute | solution.py:54
  85.2 9.6 %collective-permute-done.11.refs_4_.refs_9_ = bf16[2,64,3584]{2,1,0:T(8,128)(2,1)S(1)} collective-permute-done((bf16[2,64,3584]{2,1,0:T(8,128)(2,1)S(1)}, bf16[2,64,3584]{2,1,0:T(8,128)(2,1)S(1)}, u32[]{:S(2)}, u32[]{:S(2)}) %collective-permute-start.11) | collective-permute-done | bytes 917536 | tf_op jit(solution)/shard_map/ppermute | solution.py:59
  98.2 21.1 %hidden_part.3 = (bf16[2,3584,512]{2,1,0:T(8,128)(2,1)}, f32[64,512]{1,0:T(8,128)}) custom-call(s32[1]{0:T(128)} %bitcast.5.rank_ref, bf16[3584,4096]{1,0:T(8,128)(2,1)} %refs_1_.17, bf16[3584,4096]{1,0:T(8,128)(2,1)} %refs_1_.17, bf16[1024,512]{1,0:T(8,128)(2,1)} %collective-permute-done.8.refs_4_.refs_2_, ...), custom_call_target="tpu_custom_call" | custom-call | flops 3240000000 | bytes 1 | tf_op jit(solution)/shard_map/hidden_part/pallas_call | solution.py:265
  123.2 7.1 %collective-permute-start.17 = (bf16[2,3584,512]{2,1,0:T(8,128)(2,1)}, bf16[2,3584,512]{2,1,0:T(8,128)(2,1)}, u32[]{:S(2)}, u32[]{:S(2)}) collective-permute-start(bf16[2,3584,512]{2,1,0:T(8,128)(2,1)} %get-tuple-element.41.refs_11_.refs_4_.refs_2_.refs_1_), channel_id=1, source_target_pairs={{0,1},{1,0},{2,3},{3,2},{4,5},{5,4},{6,7},{7,6},{8,9},{9,8},{10,11... | collective-permute-start | bytes 22020104 | tf_op jit(solution)/shard_map/ppermute | solution.py:48
  135.9 18.2 %weigh_rows.5.refs_5_.refs_0_ = bf16[1600,512]{1,0:T(8,128)(2,1)} custom-call(bf16[1024,3584]{1,0:T(8,128)(2,1)} %refs_0_.21, bf16[1024,3584]{1,0:T(8,128)(2,1)} %refs_1_.21, bf16[2,64,3584]{2,1,0:T(8,128)(2,1)} %get-tuple-element.32.refs_2_, bf16[2,64,3584]{2,1,0:T(8,128)(2,1)} %get-tuple-element.35.refs_3_, bf16[2,64,3584]{2,1,0:T(8,128)(2,1)} %copy-done.3, ...), custom_call_target="tpu_custom_call" | custom-call | flops 4320000000 | bytes 1 | tf_op jit(solution)/shard_map/weigh_rows/pallas_call | solution.py:343
  154.1 4.8 %collective-permute-start.16 = (bf16[1600,512]{1,0:T(8,128)(2,1)}, bf16[1600,512]{1,0:T(8,128)(2,1)}, u32[]{:S(2)}, u32[]{:S(2)}) collective-permute-start(bf16[1600,512]{1,0:T(8,128)(2,1)} %weigh_rows.5.refs_5_.refs_0_), channel_id=1, source_target_pairs={{4,0},{12,8},{1,5},{9,13},{6,2},{14,10},{3,7},{11,15},{20,16},{28,... | collective-permute-start | bytes 4915208 | tf_op jit(solution)/shard_map/ppermute | solution.py:520
  162.6 18.1 %weigh_rows.6.refs_2_.refs_0_ = bf16[1600,512]{1,0:T(8,128)(2,1)} custom-call(bf16[1024,3584]{1,0:T(8,128)(2,1)} %refs_0_.21, bf16[1024,3584]{1,0:T(8,128)(2,1)} %refs_1_.21, bf16[2,64,3584]{2,1,0:T(8,128)(2,1)} %get-tuple-element.32.refs_2_, bf16[2,64,3584]{2,1,0:T(8,128)(2,1)} %get-tuple-element.35.refs_3_, bf16[2,64,3584]{2,1,0:T(8,128)(2,1)} %copy-done.3, ...), custom_call_target="tpu_custom_call" | custom-call | flops 4320000000 | bytes 1 | tf_op jit(solution)/shard_map/weigh_rows/pallas_call | solution.py:343
  187.4 3.4 %add_terms.5 = (bf16[1024,512]{1,0:T(8,128)(2,1)}, bf16[576,512]{1,0:T(8,128)(2,1)}) custom-call(bf16[1600,512]{1,0:T(8,128)(2,1)} %weigh_rows.5.refs_5_.refs_0_, bf16[1600,512]{1,0:T(8,128)(2,1)} %collective-permute-done.16.refs_1_, bf16[1600,512]{1,0:T(8,128)(2,1)} %weigh_rows.6.refs_2_.refs_0_), custom_call_target="tpu_custom_call" | custom-call | flops 540000000 | bytes 1 | tf_op jit(solution)/shard_map/add_terms/pallas_call | solution.py:373
  192.4 10.9 %weigh_rows.7.refs_2_.refs_3_.refs_0_ = bf16[256,1024]{1,0:T(8,128)(2,1)} custom-call(bf16[2,64,3584]{2,1,0:T(8,128)(2,1)} %copy-done.15, bf16[2,64,3584]{2,1,0:T(8,128)(2,1)} %get-tuple-element.47.refs_1_, bf16[2,64,3584]{2,1,0:T(8,128)(2,1)} %collective-permute-done.20.refs_4_.refs_2_, bf16[2,64,3584]{2,1,0:T(8,128)(2,1)} %copy-done.13, ...), custom_call_target="tpu_custom_call" | custom-call | flops 2700000000 | bytes 1 | tf_op jit(solution)/shard_map/weigh_rows/pallas_call | solution.py:343
  209.4 4.1 %collective-permute-start.28 = (bf16[256,1024]{1,0:T(8,128)(2,1)}, bf16[256,1024]{1,0:T(8,128)(2,1)}, u32[]{:S(2)}, u32[]{:S(2)}) collective-permute-start(bf16[256,1024]{1,0:T(8,128)(2,1)} %weigh_rows.7.refs_2_.refs_3_.refs_0_), channel_id=1, source_target_pairs={{4,0},{12,8},{1,5},{9,13},{6,2},{14,10},{3,7},{11,15},{20,16},{28,... | collective-permute-start | bytes 1572872 | tf_op jit(solution)/shard_map/ppermute | solution.py:520
  214.8 3.4 %add_terms.6 = (bf16[1024,512]{1,0:T(8,128)(2,1)}, bf16[576,512]{1,0:T(8,128)(2,1)}) custom-call(bf16[1600,512]{1,0:T(8,128)(2,1)} %weigh_rows.6.refs_2_.refs_0_, bf16[1600,512]{1,0:T(8,128)(2,1)} %collective-permute-done.22.refs_1_, bf16[256,1024]{1,0:T(8,128)(2,1)} %weigh_rows.7.refs_2_.refs_3_.refs_0_), custom_call_target="tpu_custom_call" | custom-call | flops 540000000 | bytes 1 | tf_op jit(solution)/shard_map/add_terms/pallas_call | solution.py:373
  221.6 9.4 %weigh_rows.8.refs_2_.refs_0_ = bf16[128,1024]{1,0:T(8,128)(2,1)} custom-call(bf16[2,64,3584]{2,1,0:T(8,128)(2,1)} %get-tuple-element.53.refs_0_, bf16[2,64,3584]{2,1,0:T(8,128)(2,1)} %copy-done.12, bf16[2,3584,512]{2,1,0:T(8,128)(2,1)} %get-tuple-element.41.refs_11_.refs_4_.refs_2_.refs_1_, ...), custom_call_target="tpu_custom_call" | custom-call | flops 1080000000 | bytes 1 | tf_op jit(solution)/shard_map/weigh_rows/pallas_call | solution.py:343
  231.0 4.6 %collective-permute-start.33 = (bf16[128,1024]{1,0:T(8,128)(2,1)}, bf16[128,1024]{1,0:T(8,128)(2,1)S(1)}, u32[]{:S(2)}, u32[]{:S(2)}) collective-permute-start(bf16[128,1024]{1,0:T(8,128)(2,1)} %weigh_rows.8.refs_2_.refs_0_), channel_id=1, source_target_pairs={{4,0},{12,8},{1,5},{9,13},{6,2},{14,10},{3,7},{11,15},{20,16},{28,... | collective-permute-start | bytes 786440 | tf_op jit(solution)/shard_map/ppermute | solution.py:520
  244.3 9.2 %weigh_rows.9.refs_10_.refs_0_ = bf16[64,1024]{1,0:T(8,128)(2,1)} custom-call(bf16[2,64,3584]{2,1,0:T(8,128)(2,1)} %collective-permute-done.32.refs_0_, bf16[2,3584,512]{2,1,0:T(8,128)(2,1)} %get-tuple-element.41.refs_11_.refs_4_.refs_2_.refs_1_, bf16[2,3584,512]{2,1,0:T(8,128)(2,1)} %collective-permute-done.17.refs_11_.refs_5_.refs_3_.refs_2_, ...), custom_call_target="tpu_custom_call" | custom-call | flops 5400000000 | bytes 1 | tf_op jit(solution)/shard_map/weigh_rows/pallas_call | solution.py:343
  253.5 4.3 %collective-permute-start.36 = (bf16[64,1024]{1,0:T(8,128)(2,1)}, bf16[64,1024]{1,0:T(8,128)(2,1)S(1)}, u32[]{:S(2)}, u32[]{:S(2)}) collective-permute-start(bf16[64,1024]{1,0:T(8,128)(2,1)} %weigh_rows.9.refs_10_.refs_0_), channel_id=1, source_target_pairs={{4,0},{12,8},{1,5},{9,13},{6,2},{14,10},{3,7},{11,15},{20,16},{28,... | collective-permute-start | bytes 393224 | tf_op jit(solution)/shard_map/ppermute | solution.py:520
  258.7 4.9 %assemble.1 = (bf16[1024,512]{1,0:T(8,128)(2,1)}, bf16[1024,512]{1,0:T(8,128)(2,1)}) custom-call(s32[4]{0:T(128)} %pad_add_fusion.words_ref, bf16[1024,512]{1,0:T(8,128)(2,1)} %get-tuple-element.46.refs_7_.refs_0_, bf16[1024,512]{1,0:T(8,128)(2,1)} %copy-done.10, bf16[1024,512]{1,0:T(8,128)(2,1)} %get-tuple-element.50.refs_5_.refs_2_, ...), custom_call_target="tpu_custom_call" | custom-call | flops 1350000000 | bytes 1 | tf_op jit(solution)/shard_map/assemble/pallas_call | solution.py:441
  268.6 11.7 %collective-permute-start.38 = (bf16[192,512]{1,0:T(8,128)(2,1)S(1)}, bf16[192,512]{1,0:T(8,128)(2,1)S(1)}, u32[]{:S(2)}, u32[]{:S(2)}) collective-permute-start(bf16[192,512]{1,0:T(8,128)(2,1)S(1)} %get-tuple-element.62), channel_id=1, source_target_pairs={{0,1},{1,0},{2,3},{3,2},{4,5},{5,4},{6,7},{7,6},{8,9},{9,8},{10,11... | collective-permute-start | bytes 589832 | tf_op jit(solution)/shard_map/ppermute | solution.py:48
  282.4 3.0 %finish.1 = bf16[512,1024]{1,0:T(8,128)(2,1)} custom-call(s32[4]{0:T(128)} %pad_add_fusion.words_ref, bf16[1024,512]{1,0:T(8,128)(2,1)} %get-tuple-element.55.mine_ref, bf16[1024,512]{1,0:T(8,128)(2,1)} %copy-done.19, bf16[192,512]{1,0:T(8,128)(2,1)} %get-tuple-element.63.late_mine_ref, bf16[192,512]{1,0:T(8,128)(2,1)} %copy-done.23), custom_call_target="tpu_custom_call" | custom-call | flops 810000000 | bytes 1 | tf_op jit(solution)/shard_map/finish/pallas_call | solution.py:482
  (171 shorter events, 83.6 us)
Async XLA Ops:
  4.8 26.3 %collective-permute-start.4 = (bf16[1024,512]{1,0:T(8,128)(2,1)}, bf16[1024,512]{1,0:T(8,128)(2,1)}, u32[]{:S(2)}, u32[]{:S(2)}) collective-permute-start(bf16[1024,512]{1,0:T(8,128)(2,1)} %bitcast.32), channel_id=1, source_target_pairs={{4,0},{8,4},{12,8},{5,1},{9,5},{13,9},{6,2},{10,6},{14,10},{7,3},{... | collective-permute-start | bytes 3145736 | tf_op jit(solution)/shard_map/ppermute | solution.py:114
  6.1 26.3 %collective-permute-start.3 = (bf16[1024,512]{1,0:T(8,128)(2,1)}, bf16[1024,512]{1,0:T(8,128)(2,1)}, u32[]{:S(2)}, u32[]{:S(2)}) collective-permute-start(bf16[1024,512]{1,0:T(8,128)(2,1)} %bitcast.33), channel_id=1, source_target_pairs={{0,4},{4,8},{8,12},{1,5},{5,9},{9,13},{2,6},{6,10},{10,14},{3,7},{... | collective-permute-start | bytes 3145736 | tf_op jit(solution)/shard_map/ppermute | solution.py:113
  11.1 41.7 %collective-permute-start.1 = (bf16[2,64,3584]{2,1,0:T(8,128)(2,1)}, bf16[2,64,3584]{2,1,0:T(8,128)(2,1)}, u32[]{:S(2)}, u32[]{:S(2)}) collective-permute-start(bf16[2,64,3584]{2,1,0:T(8,128)(2,1)} %get-tuple-element.33), channel_id=1, source_target_pairs={{2,0},{3,1},{0,2},{1,3},{6,4},{7,5},{4,6},{5,7},{10,8},{11,9},{8,1... | collective-permute-start | bytes 2752520 | tf_op jit(solution)/shard_map/ppermute | solution.py:54
  28.1 24.7 %collective-permute-start.2 = (bf16[2,64,3584]{2,1,0:T(8,128)(2,1)}, bf16[2,64,3584]{2,1,0:T(8,128)(2,1)S(1)}, u32[]{:S(2)}, u32[]{:S(2)}) collective-permute-start(bf16[2,64,3584]{2,1,0:T(8,128)(2,1)} %get-tuple-element.32.refs_2_), channel_id=1, source_target_pairs={{16,0},{0,16},{17,1},{1,17},{18,2},{2,18},{19,3},{3,19},{20,4},{4,... | collective-permute-start | bytes 2752520 | tf_op jit(solution)/shard_map/ppermute | solution.py:59
  31.1 26.2 %collective-permute-start.9 = (bf16[1024,512]{1,0:T(8,128)(2,1)}, bf16[1024,512]{1,0:T(8,128)(2,1)}, u32[]{:S(2)}, u32[]{:S(2)}) collective-permute-start(bf16[1024,512]{1,0:T(8,128)(2,1)} %collective-permute-done.4.refs_4_), channel_id=1, source_target_pairs={{4,0},{8,4},{12,8},{5,1},{9,5},{13,9},{6,2},{10,6},{14,10},{7,3},{... | collective-permute-start | bytes 3145736 | tf_op jit(solution)/shard_map/ppermute | solution.py:114
  32.4 26.2 %collective-permute-start.8 = (bf16[1024,512]{1,0:T(8,128)(2,1)}, bf16[1024,512]{1,0:T(8,128)(2,1)}, u32[]{:S(2)}, u32[]{:S(2)}) collective-permute-start(bf16[1024,512]{1,0:T(8,128)(2,1)} %collective-permute-done.3.refs_3_), channel_id=1, source_target_pairs={{0,4},{4,8},{8,12},{1,5},{5,9},{9,13},{2,6},{6,10},{10,14},{3,7},{... | collective-permute-start | bytes 3145736 | tf_op jit(solution)/shard_map/ppermute | solution.py:113
  37.4 26.8 %collective-permute-start.5 = (bf16[2,64,3584]{2,1,0:T(8,128)(2,1)}, bf16[2,64,3584]{2,1,0:T(8,128)(2,1)S(1)}, u32[]{:S(2)}, u32[]{:S(2)}) collective-permute-start(bf16[2,64,3584]{2,1,0:T(8,128)(2,1)} %get-tuple-element.34.refs_5_), channel_id=1, source_target_pairs={{2,0},{3,1},{0,2},{1,3},{6,4},{7,5},{4,6},{5,7},{10,8},{11,9},{8,1... | collective-permute-start | bytes 2752520 | tf_op jit(solution)/shard_map/ppermute | solution.py:54
  57.1 26.9 %collective-permute-start.6 = (bf16[2,64,3584]{2,1,0:T(8,128)(2,1)}, bf16[2,64,3584]{2,1,0:T(8,128)(2,1)}, u32[]{:S(2)}, u32[]{:S(2)}) collective-permute-start(bf16[2,64,3584]{2,1,0:T(8,128)(2,1)} %get-tuple-element.36), channel_id=1, source_target_pairs={{2,0},{3,1},{0,2},{1,3},{6,4},{7,5},{4,6},{5,7},{10,8},{11,9},{8,1... | collective-permute-start | bytes 2752520 | tf_op jit(solution)/shard_map/ppermute | solution.py:54
  57.3 37.5 %collective-permute-start.14 = (bf16[1024,512]{1,0:T(8,128)(2,1)}, bf16[1024,512]{1,0:T(8,128)(2,1)}, u32[]{:S(2)}, u32[]{:S(2)}) collective-permute-start(bf16[1024,512]{1,0:T(8,128)(2,1)} %collective-permute-done.9.refs_5_), channel_id=1, source_target_pairs={{4,0},{8,4},{12,8},{5,1},{9,5},{13,9},{6,2},{10,6},{14,10},{7,3},{... | collective-permute-start | bytes 3145736 | tf_op jit(solution)/shard_map/ppermute | solution.py:114
  58.6 36.2 %collective-permute-start.13 = (bf16[1024,512]{1,0:T(8,128)(2,1)}, bf16[1024,512]{1,0:T(8,128)(2,1)}, u32[]{:S(2)}, u32[]{:S(2)}) collective-permute-start(bf16[1024,512]{1,0:T(8,128)(2,1)} %collective-permute-done.8.refs_4_.refs_2_), channel_id=1, source_target_pairs={{0,4},{4,8},{8,12},{1,5},{5,9},{9,13},{2,6},{6,10},{10,14},{3,7},{... | collective-permute-start | bytes 3145736 | tf_op jit(solution)/shard_map/ppermute | solution.py:113
  64.2 30.6 %collective-permute-start.11 = (bf16[2,64,3584]{2,1,0:T(8,128)(2,1)S(1)}, bf16[2,64,3584]{2,1,0:T(8,128)(2,1)S(1)}, u32[]{:S(2)}, u32[]{:S(2)}) collective-permute-start(bf16[2,64,3584]{2,1,0:T(8,128)(2,1)S(1)} %collective-permute-done.5.refs_2_.refs_4_), channel_id=1, source_target_pairs={{16,0},{0,16},{17,1},{1,17},{18,2},{2,18},{19,3},{3,19},{20,4},{4,... | collective-permute-start | bytes 2752520 | tf_op jit(solution)/shard_map/ppermute | solution.py:59
  78.4 41.7 %collective-permute-start.10 = (bf16[2,64,3584]{2,1,0:T(8,128)(2,1)}, bf16[2,64,3584]{2,1,0:T(8,128)(2,1)S(1)}, u32[]{:S(2)}, u32[]{:S(2)}) collective-permute-start(bf16[2,64,3584]{2,1,0:T(8,128)(2,1)} %share_rows.12), channel_id=1, source_target_pairs={{2,0},{3,1},{0,2},{1,3},{6,4},{7,5},{4,6},{5,7},{10,8},{11,9},{8,1... | collective-permute-start | bytes 2752520 | tf_op jit(solution)/shard_map/ppermute | solution.py:54
  84.0 36.1 %collective-permute-start.12 = (bf16[2,64,3584]{2,1,0:T(8,128)(2,1)}, bf16[2,64,3584]{2,1,0:T(8,128)(2,1)}, u32[]{:S(2)}, u32[]{:S(2)}) collective-permute-start(bf16[2,64,3584]{2,1,0:T(8,128)(2,1)} %collective-permute-done.6.refs_3_.refs_5_), channel_id=1, source_target_pairs={{16,0},{0,16},{17,1},{1,17},{18,2},{2,18},{19,3},{3,19},{20,4},{4,... | collective-permute-start | bytes 2752520 | tf_op jit(solution)/shard_map/ppermute | solution.py:59
  123.2 39.5 %collective-permute-start.17 = (bf16[2,3584,512]{2,1,0:T(8,128)(2,1)}, bf16[2,3584,512]{2,1,0:T(8,128)(2,1)}, u32[]{:S(2)}, u32[]{:S(2)}) collective-permute-start(bf16[2,3584,512]{2,1,0:T(8,128)(2,1)} %get-tuple-element.41.refs_11_.refs_4_.refs_2_.refs_1_), channel_id=1, source_target_pairs={{0,1},{1,0},{2,3},{3,2},{4,5},{5,4},{6,7},{7,6},{8,9},{9,8},{10,11... | collective-permute-start | bytes 22020104 | tf_op jit(solution)/shard_map/ppermute | solution.py:48
  130.6 29.9 %collective-permute-start.20 = (bf16[2,64,3584]{2,1,0:T(8,128)(2,1)}, bf16[2,64,3584]{2,1,0:T(8,128)(2,1)}, u32[]{:S(2)}, u32[]{:S(2)}) collective-permute-start(bf16[2,64,3584]{2,1,0:T(8,128)(2,1)} %copy-done.7), channel_id=1, source_target_pairs={{16,0},{0,16},{17,1},{1,17},{18,2},{2,18},{19,3},{3,19},{20,4},{4,... | collective-permute-start | bytes 2752520 | tf_op jit(solution)/shard_map/ppermute | solution.py:59
  132.9 26.0 %collective-permute-start.18 = (f32[192,512]{1,0:T(8,128)S(1)}, f32[192,512]{1,0:T(8,128)S(1)}, u32[]{:S(2)}, u32[]{:S(2)}) collective-permute-start(f32[192,512]{1,0:T(8,128)S(1)} %pad_maximum_fusion), channel_id=1, source_target_pairs={{0,8},{4,12},{8,0},{12,4},{1,9},{5,13},{9,1},{13,5},{2,10},{6,14},... | collective-permute-start | bytes 1179656 | tf_op jit(solution)/shard_map/ppermute | solution.py:496
  134.7 48.7 %collective-permute-start.23 = (bf16[2,64,3584]{2,1,0:T(8,128)(2,1)}, bf16[2,64,3584]{2,1,0:T(8,128)(2,1)S(1)}, u32[]{:S(2)}, u32[]{:S(2)}) collective-permute-start(bf16[2,64,3584]{2,1,0:T(8,128)(2,1)} %get-tuple-element.42.refs_12_), channel_id=1, source_target_pairs={{2,0},{3,1},{0,2},{1,3},{6,4},{7,5},{4,6},{5,7},{10,8},{11,9},{8,1... | collective-permute-start | bytes 2752520 | tf_op jit(solution)/shard_map/ppermute | solution.py:54
  154.1 33.3 %collective-permute-start.16 = (bf16[1600,512]{1,0:T(8,128)(2,1)}, bf16[1600,512]{1,0:T(8,128)(2,1)}, u32[]{:S(2)}, u32[]{:S(2)}) collective-permute-start(bf16[1600,512]{1,0:T(8,128)(2,1)} %weigh_rows.5.refs_5_.refs_0_), channel_id=1, source_target_pairs={{4,0},{12,8},{1,5},{9,13},{6,2},{14,10},{3,7},{11,15},{20,16},{28,... | collective-permute-start | bytes 4915208 | tf_op jit(solution)/shard_map/ppermute | solution.py:520
  158.9 24.6 %collective-permute-start.24 = (bf16[2,64,3584]{2,1,0:T(8,128)(2,1)}, bf16[2,64,3584]{2,1,0:T(8,128)(2,1)S(1)}, u32[]{:S(2)}, u32[]{:S(2)}) collective-permute-start(bf16[2,64,3584]{2,1,0:T(8,128)(2,1)} %copy-done.15), channel_id=1, source_target_pairs={{16,0},{0,16},{17,1},{1,17},{18,2},{2,18},{19,3},{3,19},{20,4},{4,... | collective-permute-start | bytes 2752520 | tf_op jit(solution)/shard_map/ppermute | solution.py:59
  180.8 32.8 %collective-permute-start.22 = (bf16[1600,512]{1,0:T(8,128)(2,1)}, bf16[1600,512]{1,0:T(8,128)(2,1)}, u32[]{:S(2)}, u32[]{:S(2)}) collective-permute-start(bf16[1600,512]{1,0:T(8,128)(2,1)} %weigh_rows.6.refs_2_.refs_0_), channel_id=1, source_target_pairs={{4,0},{12,8},{1,5},{9,13},{6,2},{14,10},{3,7},{11,15},{20,16},{28,... | collective-permute-start | bytes 4915208 | tf_op jit(solution)/shard_map/ppermute | solution.py:520
  190.8 29.8 %collective-permute-start.21 = (bf16[1024,512]{1,0:T(8,128)(2,1)}, bf16[1024,512]{1,0:T(8,128)(2,1)S(1)}, u32[]{:S(2)}, u32[]{:S(2)}) collective-permute-start(bf16[1024,512]{1,0:T(8,128)(2,1)} %get-tuple-element.46.refs_7_.refs_0_), channel_id=1, source_target_pairs={{8,0},{13,5},{2,10},{7,15},{24,16},{29,21},{18,26},{23,31}} | collective-permute-start | bytes 3145736 | tf_op jit(solution)/shard_map/ppermute | solution.py:520
  191.5 28.3 %collective-permute-start.26 = (bf16[576,512]{1,0:T(8,128)(2,1)}, bf16[576,512]{1,0:T(8,128)(2,1)S(1)}, u32[]{:S(2)}, u32[]{:S(2)}) collective-permute-start(bf16[576,512]{1,0:T(8,128)(2,1)} %get-tuple-element.49.refs_8_.refs_4_), channel_id=1, source_target_pairs={{0,8},{5,13},{10,2},{15,7},{16,24},{21,29},{26,18},{31,23}} | collective-permute-start | bytes 1769480 | tf_op jit(solution)/shard_map/ppermute | solution.py:520
  209.4 26.4 %collective-permute-start.28 = (bf16[256,1024]{1,0:T(8,128)(2,1)}, bf16[256,1024]{1,0:T(8,128)(2,1)}, u32[]{:S(2)}, u32[]{:S(2)}) collective-permute-start(bf16[256,1024]{1,0:T(8,128)(2,1)} %weigh_rows.7.refs_2_.refs_3_.refs_0_), channel_id=1, source_target_pairs={{4,0},{12,8},{1,5},{9,13},{6,2},{14,10},{3,7},{11,15},{20,16},{28,... | collective-permute-start | bytes 1572872 | tf_op jit(solution)/shard_map/ppermute | solution.py:520
  213.5 28.9 %collective-permute-start.32 = (bf16[2,64,3584]{2,1,0:T(8,128)(2,1)}, bf16[2,64,3584]{2,1,0:T(8,128)(2,1)}, u32[]{:S(2)}, u32[]{:S(2)}) collective-permute-start(bf16[2,64,3584]{2,1,0:T(8,128)(2,1)} %get-tuple-element.53.refs_0_), channel_id=1, source_target_pairs={{16,0},{0,16},{17,1},{1,17},{18,2},{2,18},{19,3},{3,19},{20,4},{4,... | collective-permute-start | bytes 2752520 | tf_op jit(solution)/shard_map/ppermute | solution.py:59
  (47 other events, 528.9 us)

commit v7 on v6

--- a/solution.py
+++ b/solution.py
@@ -9,7 +9,7 @@
 from jax.sharding import PartitionSpec as P
 
 CORES = 2
-CHUNKS = 8
+CHUNKS = (2, 2, 2, 2, 3, 3, 2)
 VMEM_BYTES = 60 * 1024 * 1024
 FLOPS_PER_US = 270_000_000
 ANYWHERE = pl.BlockSpec(memory_space=pl.ANY)
@@ -59,6 +59,10 @@
     return lax.ppermute(value, "groups", [((i + shift) % size, i) for i in range(size)])
 
 
+def chunk_edges(part):
+    return [part // 16 * sum(CHUNKS[:k]) for k in range(len(CHUNKS) + 1)]
+
+
 def cost(us):
     return pl.CostEstimate(flops=int(us * FLOPS_PER_US) + 1, bytes_accessed=1, transcendentals=0)
 
@@ -67,11 +71,12 @@
     return next((w for w in options if size % w == 0), size)
 
 
-def share_rows(w_gate, w_up, group, places, piece, carried, after):
+def share_rows(w_gate, w_up, group, spans, carried, after):
     rows, width = w_gate.shape
-    tile = widest(width, (1792, 896, 128))
-    kept, waits, fresh = len(carried), len(after), len(places)
-    per_group = rows // lax.axis_size("groups") // piece
+    part = rows // lax.axis_size("groups")
+    step = part // 16
+    kept, waits, fresh = len(carried), len(after), len(spans)
+    steps = max([(last - first) // step for first, last in spans], default=1)
 
     def kernel(group_ref, *refs):
         outs = refs[len(refs) - fresh :] if fresh else []
@@ -81,23 +86,25 @@
         if not fresh:
             refs[-1][...] = jnp.zeros_like(refs[-1])
 
-    specs = []
-    for k in places:
-        at_chunk = functools.partial(lambda k, i, g: (g[0] * per_group + k, i), k)
-        specs += [pl.BlockSpec((piece, tile), at_chunk)] * 2
+    in_specs, out_specs = [], [ANYWHERE] * kept
+    shapes = [jax.ShapeDtypeStruct(a.shape, a.dtype) for a in carried]
+    for first, last in spans:
+        at_rows = functools.partial(lambda f, i, g: (g[0] * (part // step) + f // step + i, 0), first)
+        in_specs += [pl.BlockSpec((step, width), at_rows)] * 2
+        out_specs.append(pl.BlockSpec((2, step, width), lambda i, g: (0, i, 0)))
+        shapes.append(jax.ShapeDtypeStruct((2, last - first, width), w_gate.dtype))
+    if not fresh:
+        out_specs.append(pl.BlockSpec((8, 128), lambda i, g: (0, 0)))
+        shapes.append(jax.ShapeDtypeStruct((8, 128), jnp.float32))
     results = pl.pallas_call(
         kernel,
         grid_spec=pltpu.PrefetchScalarGridSpec(
             num_scalar_prefetch=1,
-            grid=(width // tile if places else 1,),
-            in_specs=specs + [ANYWHERE] * (kept + waits),
-            out_specs=[ANYWHERE] * kept
-            + [pl.BlockSpec((2, piece, tile), lambda i, g: (0, 0, i))] * fresh
-            + [pl.BlockSpec((8, 128), lambda i, g: (0, 0))] * (not fresh),
+            grid=(steps,),
+            in_specs=in_specs + [ANYWHERE] * (kept + waits),
+            out_specs=out_specs,
         ),
-        out_shape=[jax.ShapeDtypeStruct(a.shape, a.dtype) for a in carried]
-        + [jax.ShapeDtypeStruct((2, piece, width), w_gate.dtype) for _ in places]
-        + [jax.ShapeDtypeStruct((8, 128), jnp.float32)] * (not fresh),
+        out_shape=shapes,
         input_output_aliases={1 + 2 * fresh + i: i for i in range(kept)},
         compiler_params=pltpu.CompilerParams(vmem_limit_bytes=VMEM_BYTES),
         cost_estimate=cost(2),
@@ -195,7 +202,7 @@
     def kernel(rank_ref, *refs):
         z = rank_ref[0]
         downs, arrived = refs[:slots], refs[slots : slots + len(sources)]
-        grad_ref, total, sem = refs[-3:]
+        grad_ref, sem = refs[-2:]
         rest = refs[slots + len(sources) :]
 
         def gather(wait):
@@ -213,19 +220,19 @@
             gather(False)
             gather(True)
 
-        if finish:
-            total[...] = rest[0][...]
+        wide = None
         for at in range(slots):
             term = jnp.dot(
                 downs[at][...],
                 grad_ref[at * features : (at + 1) * features, :],
                 preferred_element_type=jnp.float32,
             )
-            total[...] = total[...] + term if at or finish else term
+            wide = term if wide is None else wide + term
         if finish:
-            both_ref, out_ref = refs[-5:-3]
-            both_ref[0] = (total[...] * rest[1][0]).astype(jnp.bfloat16)
-            up_grad = (total[...] * rest[1][1]).astype(jnp.bfloat16)
+            both_ref, out_ref = refs[-4:-2]
+            wide = wide + rest[0][...]
+            both_ref[0] = (wide * rest[1][0]).astype(jnp.bfloat16)
+            up_grad = (wide * rest[1][1]).astype(jnp.bfloat16)
             both_ref[1] = up_grad
             part = jnp.dot(rest[2][...], up_grad, preferred_element_type=jnp.float32)
 
@@ -238,7 +245,7 @@
                 out_ref[...] += part
 
         else:
-            refs[-4][...] = total[...]
+            refs[-3][...] = wide
 
     operands = [w_down] * slots + [value for _, _, value in sources]
     specs = [pl.BlockSpec((tile, features), functools.partial(column, at)) for at in range(slots)]
@@ -271,7 +278,6 @@
             out_specs=out_specs,
             scratch_shapes=[
                 pltpu.VMEM((slots * features, count), jnp.bfloat16),
-                pltpu.VMEM((tile, count), jnp.float32),
                 pltpu.SemaphoreType.DMA((len(sources),)),
             ],
         ),
@@ -398,8 +404,7 @@
         n: (row, [([at_of(v) for v in pair], first) for pair, first in halves])
         for n, (row, halves) in far.items()
     }
-    chunks = 1 + max(n[0] for n in far)
-    piece = part // CHUNKS
+    edges = chunk_edges(part)
 
     def kernel(words_ref, *refs):
         outs = refs[-2:]
@@ -424,8 +429,9 @@
                     def _(s=s, g=g, h=h):
                         for j in range(tall):
                             shift = (h + j - g) % groups
-                            for k in range(CHUNKS):
-                                top = j * part + k * piece
+                            for k in range(len(CHUNKS)):
+                                top = j * part + edges[k]
+                                piece = edges[k + 1] - edges[k]
                                 for half in range(2):
                                     if (k, s, shift) in far_at:
                                         row, halves = far_at[k, s, shift]
@@ -455,7 +461,7 @@
     features, count = mine.shape
     groups = lax.axis_size("groups")
     tall = features // part
-    piece = part // CHUNKS
+    edges = chunk_edges(part)
 
     def kernel(words_ref, mine_ref, theirs_ref, late_mine_ref, late_theirs_ref, out_ref, rows_ref):
         away, group, inside = words_ref[0], words_ref[1], words_ref[2]
@@ -470,12 +476,12 @@
                         @pl.when((away > 0) & (group == g) & (inside == h * part))
                         def _(g=g, h=h):
                             for j in range(tall):
-                                for at, (k, r) in enumerate(late):
+                                row = 0
+                                for k, r in late:
+                                    top, piece = j * part + edges[k], edges[k + 1] - edges[k]
                                     if (h + j - g) % groups == r:
-                                        top = j * part + k * piece
-                                        rows_ref[top : top + piece] = extra[
-                                            at * piece : (at + 1) * piece
-                                        ]
+                                        rows_ref[top : top + piece] = extra[row : row + piece]
+                                    row += piece
 
         out_ref[...] = rows_ref[...].T
 
@@ -558,13 +564,15 @@
     count = layer_input.shape[0]
     features = out_grad.shape[1]
     part = rows // groups
-    piece = part // CHUNKS
+    edges = chunk_edges(part)
+    chunks = len(CHUNKS)
     split = max(1, ranks // blocks)
     group_word = jnp.full((1,), group, jnp.int32)
     rank_word = jnp.full((1,), rank, jnp.int32)
 
     below, above = spread_ranks(out_grad.T)
-    _, shares = share_rows(w_gate, w_up, group_word, [0, 1], piece, [], [])
+    spans = list(zip(edges, edges[1:]))
+    _, shares = share_rows(w_gate, w_up, group_word, spans[:2], [], [])
     slopes, in_down_part = prepare(gate_act, up_act, proj_h.T, [shares[0]])
     early_part = jnp.concatenate([project(proj_x, layer_input), in_down_part], axis=0)
     out_down_part = project(proj_g, out_grad)
@@ -576,16 +584,15 @@
             for r in range(1, groups):
                 fetched[k, s, r] = from_group(fetched[k, s, 0], r)
 
-    def forward(k, after, held=()):
-        waits = [fetched[n] for n in fetched if n[0] == k and n[2] == 0]
-        waits += [fetched[n] for n in fetched if n[0] == k - 1 and n[2] > 0]
-        waits = [w for w in waits if not any(w is h for h in held)]
-        places = [k + 2] if k + 2 < CHUNKS else []
+    def forward(k, waits, after, held=()):
+        names = [(k, 0)] + waits
+        arrived = [fetched[n] for n in fetched if (n[0], n[2]) in names]
+        arrived = [a for a in arrived if not any(a is h for h in held)]
         carried, fresh = share_rows(
-            w_gate, w_up, group_word, places, piece, list(held), waits + list(after)
+            w_gate, w_up, group_word, spans[k + 2 : k + 3], list(held), arrived + list(after)
         )
         ticks.append(fresh[0])
-        if places:
+        if k + 2 < chunks:
             shares.extend(fresh)
             fetch(k + 2)
         return carried
@@ -641,26 +648,32 @@
     fetch(0)
     fetch(1)
 
-    def hold_arrived(k, after, held=()):
+    def hold_arrived(k, waits, after, held=()):
         names = [(k, s, 0) for s in range(1, chips)]
-        values = forward(k, after, [fetched[n] for n in names] + list(held))
+        values = forward(k, waits, after, [fetched[n] for n in names] + list(held))
         for n, value in zip(names, values):
             fetched[n] = value
             for r in range(1, groups):
                 fetched[k, n[1], r] = from_group(value, r)
         return values[len(names) :]
 
+    def chunks_of(numbers, shifts):
+        return [(k, r) for r in shifts for k in numbers]
+
+    others = range(1, groups)
     bits = [1 << i for i in range(ranks.bit_length() - 1)]
-    hold_arrived(0, [slopes])
-    so_far = hidden_part(rank_word, below, above, w_down, None, None, None, [ticks[0]])
-    hold_arrived(1, [so_far])
-    forward(2, [below[2], above[1], early_part, out_down_part])
-    (early,) = forward(3, below[3:] + above[2:], [early_part])
+    hold_arrived(0, [], [slopes])
+    hold_arrived(1, chunks_of([0], others), [below[1], above[0]])
+    so_far = hidden_part(rank_word, below, above, w_down, None, None, None, [ticks[1]])
+    forward(
+        2, chunks_of([1], others), [so_far, below[2], above[1], early_part, out_down_part]
+    )
+    (early,) = forward(3, chunks_of([2], others), below[3:] + above[2:], [early_part])
     mine, up_out_part = hidden_part(
         rank_word, below, above, w_down, so_far, slopes, proj_u.T, [ticks[3]]
     )
     early = early + exchange(early, bits[0])
-    mine, early = forward(4, [], [mine, early])
+    mine, early = forward(4, chunks_of([3], others), [], [mine, early])
     theirs = swap_cores(mine)
 
     out_parts = jnp.stack([up_out_part, out_down_part]).reshape(2, ranks, -1, count)
@@ -677,21 +690,26 @@
     for bit in bits[1:-1]:
         early = early + exchange(early, bit)
 
-    first_names = [(k, 0) for k in range(5)] + [(k, 1) for k in range(4)]
-    first_mine = terms(first_names, [mine], [ticks[4]], 16, near=True)
-    (out_parts,) = forward(5, first_mine[0] + [early], [out_parts])
-    first_theirs = terms(first_names, [theirs], [ticks[5]], 16, near=True)
+    first_names = chunks_of(range(5), [0]) + chunks_of(range(4), others)
+    first_mine = terms(first_names, [mine], [ticks[4]], 32, near=True)
+    (out_parts,) = hold_arrived(5, chunks_of([4], others), first_mine[0] + [early], [out_parts])
+    first_theirs = terms(first_names, [theirs], [ticks[5]], 60, near=True)
     sums_mine, end_mine = carry_on(first_mine, first_theirs[0])
-    hold_arrived(6, first_theirs[0])
-    second_names = [(5, 0), (6, 0), (4, 1), (5, 1)]
-    second = terms(second_names, [mine, theirs], [ticks[6]] + sums_mine, 10)
-    sums_theirs, end_theirs = carry_on(first_theirs, second[0])
-    (out_parts,) = hold_arrived(7, second[0], [out_parts])
-    third_names = [(7, 0), (6, 1)]
-    received = [got for _, _, got in end_mine]
-    third = terms(third_names, [mine, theirs], [ticks[7]] + sums_theirs + received, 4)
-    sums_second, end_second = carry_on(second, third[0])
-
+    hold_arrived(6, [], first_theirs[0])
+    second_names = chunks_of([5, 6], [0]) + chunks_of([4, 5], others)
+    near_received = [got for names, _, got in end_mine if names is None]
+    far_received = [got for names, _, got in end_mine if names is not None]
+    second = terms(second_names, [mine, theirs], [ticks[6]] + far_received, 40)
+    sums_theirs, end_theirs = carry_on(first_theirs, second[0] + near_received)
+
+    last_names = chunks_of([6], others)
+    come = [fetched[n] for n in fetched if (n[0], n[2]) in last_names]
+    sums_second, end_second = carry_on(second, sums_theirs + come)
+    last = terms(last_names, [mine, theirs], sums_second, 60)
+    far_received = [got for names, _, got in end_theirs if names is not None]
+    sums_last, end_last = carry_on(last, far_received, 8)
+
+    (out_parts,), _ = share_rows(w_gate, w_up, group_word, [], [out_parts], sums_second)
     for bit in bits[-2::-1]:
         out_parts = halve(out_parts, bit)
     early = early.astype(jnp.bfloat16)
@@ -705,25 +723,23 @@
         [doc_outer(member, up_out, in_up), doc_outer(member, out_down, in_down)], axis=1
     )
 
-    sums_third, end_third = carry_on(third, [])
-    last_names = [(CHUNKS - 1, r) for r in range(1, groups)]
-    received = [got for _, _, got in end_theirs]
-    last = terms(last_names, [mine, theirs], sums_third + received, 20)
-    sums_last, end_last = carry_on(last, [], 40)
-
     first = rank * features
     away = (first // rows // CORES - chip) % chips
     owner = first // rows % CORES == core
     inside = first % rows
+    def tops(names):
+        sizes = [edges[n[0] + 1] - edges[n[0]] for n in names]
+        return [(sum(sizes[:i]), n) for i, n in enumerate(names)]
+
     near, far = [[], []], {}
     for (names, *m), (_, *t) in zip(end_mine, end_theirs):
         if names is None:
             near[0].append(m)
             near[1].append(t)
         else:
-            far.update((n, (i * piece, [(m, 0), (t, 0)])) for i, n in enumerate(names))
+            far.update((n, (row, [(m, 0), (t, 0)])) for row, n in tops(names))
     for names, *pair in end_second:
-        far.update((n, (i * piece, [(pair, 0), (pair, count)])) for i, n in enumerate(names))
+        far.update((n, (row, [(pair, 0), (pair, count)])) for row, n in tops(names))
     words = jnp.stack([away, group, inside, owner]).astype(jnp.int32)
     total_mine, total_theirs = assemble(
         words, count, features, part, near, far, chips, last[0]
@@ -737,9 +753,11 @@
         return value
 
     tail = {}
-    for names, value, got in end_third + end_last:
+    for names, value, got in end_last:
         value = (value.astype(jnp.float32) + got.astype(jnp.float32)).astype(jnp.bfloat16)
-        tail.update((n, value[i * piece : (i + 1) * piece]) for i, n in enumerate(names))
+        tail.update(
+            (n, value[row : row + edges[n[0] + 1] - edges[n[0]]]) for row, n in tops(names)
+        )
     late = sorted({(k, r) for k, _, r in tail})
     pieces = jnp.concatenate(
         [pick(away - 1, [tail[k, s, r] for s in range(1, chips)]) for k, r in late], axis=0

time: 287 us -> 295 us (1.028)
  starting transfers between devices: 79.7 us -> 90.5 us
  waiting for transfers between devices: 27.4 us -> 36.5 us
  Pallas kernels: 150 us -> 142 us
  local copies, waits for them, and re-layouts: 16.4 us -> 13.4 us
    ppermute x3, starting transfers between devices: 19.1 us -> 29.9 us  [swap_cores(): return lax.ppermute(value, 'dp', [(i, i ^ 1) for i in range(size)])]
    ppermute x8 -> x7, waiting for transfers between devices: 5.53 us -> 13.4 us  [from_chip(): lax.ppermute(value, 'dp', [((i + step) % size, i) for i in range(size)])]
    pallas_call x5 -> x4, Pallas kernels: 65.8 us -> 57.9 us  [weigh(): pl.pallas_call(kernel, grid=(steps,), out_shape=shapes, in_specs=specs +...]
    ppermute x12 -> x10, waiting for transfers between devices: 0.62 us -> 5.57 us  [send(): return lax.ppermute(value, ('groups', 'tensor', 'dp'), pairs)]
    ppermute x8 -> x7, waiting for transfers between devices: 19.4 us -> 15.4 us  [from_group(): lax.ppermute(value, 'groups', [((i + shift) % size, i) for i in range(siz...]
    ppermute x3, starting transfers between devices: 2.27 us -> 6.04 us  [exchange(): return lax.ppermute(value, 'tensor', [(i, i ^ bit) for i in range(ranks)])]
    ppermute x8 -> x7, starting transfers between devices: 8.99 us -> 5.68 us  [from_group(): lax.ppermute(value, 'groups', [((i + shift) % size, i) for i in range(siz...]
    pallas_call x5 -> x4, Pallas kernels: 12.4 us -> 10.9 us  [add(): pl.pallas_call(kernel, out_shape=[jax.ShapeDtypeStruct((h, count), jnp.bf...]
  transfers between devices with their start and end apart: 40 -> 36, of which waited for: 8 -> 12; matrix products, arithmetic and copies ran while one was open for 5% -> 5% of each run, Pallas kernels for 50% -> 46%
where the time goes in v7:
time: 295 us; the launch traced here: 294 us
  Pallas kernels  142 us (48%)
  starting transfers between devices  90.5 us (31%)
  waiting for transfers between devices  36.5 us (12%)
  local copies, waits for them, and re-layouts  13.4 us (5%)
  other arithmetic  7.37 us (2%)
  matrix products  3.1 us (1%)
    pallas_call x4, Pallas kernels, weigh(): pl.pallas_call(kernel, grid=(steps,), out_shape=shapes, in_specs=specs +...  57.9 us
    pallas_call x2, Pallas kernels, hidden_part(): pl.pallas_call(kernel, grid_spec=pltpu.PrefetchScalarGridSpec(num_scalar_...  35.4 us
    ppermute x3, starting transfers between devices, swap_cores(): return lax.ppermute(value, 'dp', [(i, i ^ 1) for i in range(size)])  29.9 us
    ppermute x10, starting transfers between devices, send(): return lax.ppermute(value, ('groups', 'tensor', 'dp'), pairs)  24.6 us
    pallas_call x9, Pallas kernels, share_rows(): pl.pallas_call(kernel, grid_spec=pltpu.PrefetchScalarGridSpec(num_scalar_...  17.6 us
    ppermute x7, waiting for transfers between devices, from_group(): lax.ppermute(value, 'groups', [((i + shift) % size, i) for i in range(siz...  15.4 us
    ppermute x3, starting transfers between devices, spread_ranks(): lax.ppermute(below[-1], 'tensor', [(i, i + 1) for i in range(ranks - 1)])  15.1 us
    ppermute x7, waiting for transfers between devices, from_chip(): lax.ppermute(value, 'dp', [((i + step) % size, i) for i in range(size)])  13.4 us
  transfers between devices with their start and end apart: 36, of which 12 were waited for; matrix products, arithmetic and copies ran while one was open for 5% of the time, Pallas kernels for 46%

profile of v7, /device:TPU:3, one launch (start us, length us, event | category | flops | bytes accessed | tf_op | source)
XLA Modules:
  0.0 293.9 jit_solution(9667045209335429403)
XLA Ops:
  6.0 5.1 %collective-permute-start.3 = (bf16[1024,512]{1,0:T(8,128)(2,1)}, bf16[1024,512]{1,0:T(8,128)(2,1)}, u32[]{:S(2)}, u32[]{:S(2)}) collective-permute-start(bf16[1024,512]{1,0:T(8,128)(2,1)} %bitcast.5.refs_2_), channel_id=1, source_target_pairs={{0,4},{4,8},{8,12},{1,5},{5,9},{9,13},{2,6},{6,10},{10,14},{3,7},{... | collective-permute-start | bytes 3145736 | tf_op jit(solution)/shard_map/ppermute | solution.py:120
  12.5 11.9 %prepare.1 = (f32[2,3584,512]{2,1,0:T(8,128)}, f32[64,512]{1,0:T(8,128)}) custom-call(bf16[512,3584]{1,0:T(8,128)(2,1)} %gate_ref.1, bf16[512,3584]{1,0:T(8,128)(2,1)} %up_ref.1, bf16[64,3584]{1,0:T(8,128)(2,1)} %bitcast.39, bf16[2,64,3584]{2,1,0:T(8,128)(2,1)} %get-tuple-element.29.refs_0_), custom_call_target="tpu_custom_call" | custom-call | flops 3240000000 | bytes 1 | tf_op jit(solution)/shard_map/prepare/pallas_call | solution.py:147
  32.3 5.0 %collective-permute-start.8 = (bf16[1024,512]{1,0:T(8,128)(2,1)}, bf16[1024,512]{1,0:T(8,128)(2,1)}, u32[]{:S(2)}, u32[]{:S(2)}) collective-permute-start(bf16[1024,512]{1,0:T(8,128)(2,1)} %collective-permute-done.3.refs_4_.refs_3_), channel_id=1, source_target_pairs={{0,4},{4,8},{8,12},{1,5},{5,9},{9,13},{2,6},{6,10},{10,14},{3,7},{... | collective-permute-start | bytes 3145736 | tf_op jit(solution)/shard_map/ppermute | solution.py:120
  38.4 6.2 %collective-permute-done.1.refs_2_ = bf16[2,64,3584]{2,1,0:T(8,128)(2,1)} collective-permute-done((bf16[2,64,3584]{2,1,0:T(8,128)(2,1)}, bf16[2,64,3584]{2,1,0:T(8,128)(2,1)}, u32[]{:S(2)}, u32[]{:S(2)}) %collective-permute-start.1) | collective-permute-done | bytes 917536 | tf_op jit(solution)/shard_map/ppermute | solution.py:54
  54.5 14.3 %hidden_part.2.refs_4_.refs_7_ = f32[3584,512]{1,0:T(8,128)} custom-call(s32[1]{0:T(128)} %bitcast.6.rank_ref, bf16[3584,4096]{1,0:T(8,128)(2,1)} %refs_1_.16, bf16[3584,4096]{1,0:T(8,128)(2,1)} %refs_1_.16, bf16[1024,512]{1,0:T(8,128)(2,1)} %bitcast.5.refs_2_, bf16[1024,512]{1,0:T(8,128)(2,1)} %collective-permute-done.3.refs_4_.refs_3_, ...), custom_call_target="tpu_custom_call" | custom-call | flops 3240000000 | bytes 1 | tf_op jit(solution)/shard_map/hidden_part/pallas_call | solution.py:272
  70.2 5.0 %collective-permute-start.13 = (bf16[1024,512]{1,0:T(8,128)(2,1)}, bf16[1024,512]{1,0:T(8,128)(2,1)}, u32[]{:S(2)}, u32[]{:S(2)}) collective-permute-start(bf16[1024,512]{1,0:T(8,128)(2,1)} %collective-permute-done.8.refs_5_.refs_2_), channel_id=1, source_target_pairs={{0,4},{4,8},{8,12},{1,5},{5,9},{9,13},{2,6},{6,10},{10,14},{3,7},{... | collective-permute-start | bytes 3145736 | tf_op jit(solution)/shard_map/ppermute | solution.py:120
  75.2 3.4 %share_rows.12 = bf16[2,96,3584]{2,1,0:T(8,128)(2,1)} custom-call(s32[1]{0:T(128)} %bitcast.1.group_ref, bf16[1024,3584]{1,0:T(8,128)(2,1)} %refs_0_.19, bf16[1024,3584]{1,0:T(8,128)(2,1)} %refs_1_.19, bf16[2,64,3584]{2,1,0:T(8,128)(2,1)} %collective-permute-done.7.refs_2_.refs_8_, bf16[2,64,3584]{2,1,0:T(8,128)(2,1)} %collective-permute-done.5.refs_3_.refs_4_, ...), custom_call_target="tpu_custom_call" | custom-call | flops 540000000 | bytes 1 | tf_op jit(solution)/shard_map/share_rows/pallas_call | solution.py:99
  80.0 3.9 %collective-permute-done.6.refs_4_.refs_5_ = bf16[2,64,3584]{2,1,0:T(8,128)(2,1)} collective-permute-done((bf16[2,64,3584]{2,1,0:T(8,128)(2,1)}, bf16[2,64,3584]{2,1,0:T(8,128)(2,1)}, u32[]{:S(2)}, u32[]{:S(2)}) %collective-permute-start.6) | collective-permute-done | bytes 917536 | tf_op jit(solution)/shard_map/ppermute | solution.py:54
  85.2 11.7 %collective-permute-done.11.refs_3_.refs_9_ = bf16[2,64,3584]{2,1,0:T(8,128)(2,1)S(1)} collective-permute-done((bf16[2,64,3584]{2,1,0:T(8,128)(2,1)}, bf16[2,64,3584]{2,1,0:T(8,128)(2,1)S(1)}, u32[]{:S(2)}, u32[]{:S(2)}) %collective-permute-start.11) | collective-permute-done | bytes 917536 | tf_op jit(solution)/shard_map/ppermute | solution.py:59
  102.9 21.1 %hidden_part.3 = (bf16[2,3584,512]{2,1,0:T(8,128)(2,1)}, f32[64,512]{1,0:T(8,128)}) custom-call(s32[1]{0:T(128)} %bitcast.6.rank_ref, bf16[3584,4096]{1,0:T(8,128)(2,1)} %refs_1_.16, bf16[3584,4096]{1,0:T(8,128)(2,1)} %refs_1_.16, bf16[1024,512]{1,0:T(8,128)(2,1)} %collective-permute-done.8.refs_5_.refs_2_, ...), custom_call_target="tpu_custom_call" | custom-call | flops 3240000000 | bytes 1 | tf_op jit(solution)/shard_map/hidden_part/pallas_call | solution.py:272
  128.1 11.4 %collective-permute-start.17 = (bf16[2,3584,512]{2,1,0:T(8,128)(2,1)}, bf16[2,3584,512]{2,1,0:T(8,128)(2,1)}, u32[]{:S(2)}, u32[]{:S(2)}) collective-permute-start(bf16[2,3584,512]{2,1,0:T(8,128)(2,1)} %get-tuple-element.40.refs_11_.refs_4_.refs_1_), channel_id=1, source_target_pairs={{0,1},{1,0},{2,3},{3,2},{4,5},{5,4},{6,7},{7,6},{8,9},{9,8},{10,11... | collective-permute-start | bytes 22020104 | tf_op jit(solution)/shard_map/ppermute | solution.py:48
  143.9 18.3 %weigh_rows.4.refs_3_.refs_0_ = bf16[1632,512]{1,0:T(8,128)(2,1)} custom-call(bf16[1024,3584]{1,0:T(8,128)(2,1)} %refs_0_.19, bf16[1024,3584]{1,0:T(8,128)(2,1)} %refs_1_.19, bf16[2,64,3584]{2,1,0:T(8,128)(2,1)} %get-tuple-element.31.refs_2_, bf16[2,64,3584]{2,1,0:T(8,128)(2,1)} %get-tuple-element.33.refs_3_, ...), custom_call_target="tpu_custom_call" | custom-call | flops 8640000000 | bytes 1 | tf_op jit(solution)/shard_map/weigh_rows/pallas_call | solution.py:349
  162.2 4.9 %collective-permute-start.16 = (bf16[1632,512]{1,0:T(8,128)(2,1)}, bf16[1632,512]{1,0:T(8,128)(2,1)}, u32[]{:S(2)}, u32[]{:S(2)}) collective-permute-start(bf16[1632,512]{1,0:T(8,128)(2,1)} %weigh_rows.4.refs_3_.refs_0_), channel_id=1, source_target_pairs={{4,0},{12,8},{1,5},{9,13},{6,2},{14,10},{3,7},{11,15},{20,16},{28,... | collective-permute-start | bytes 5013512 | tf_op jit(solution)/shard_map/ppermute | solution.py:526
  173.6 18.4 %weigh_rows.5.refs_2_.refs_1_.refs_0_ = bf16[1632,512]{1,0:T(8,128)(2,1)} custom-call(bf16[1024,3584]{1,0:T(8,128)(2,1)} %refs_0_.19, bf16[1024,3584]{1,0:T(8,128)(2,1)} %refs_1_.19, bf16[2,64,3584]{2,1,0:T(8,128)(2,1)} %get-tuple-element.31.refs_2_, bf16[2,64,3584]{2,1,0:T(8,128)(2,1)} %get-tuple-element.33.refs_3_, ...), custom_call_target="tpu_custom_call" | custom-call | flops 16200000512 | bytes 1 | tf_op jit(solution)/shard_map/weigh_rows/pallas_call | solution.py:349
  191.9 3.5 %add_terms.4 = (bf16[1024,512]{1,0:T(8,128)(2,1)}, bf16[608,512]{1,0:T(8,128)(2,1)}) custom-call(bf16[1632,512]{1,0:T(8,128)(2,1)} %weigh_rows.4.refs_3_.refs_0_, bf16[1632,512]{1,0:T(8,128)(2,1)} %collective-permute-done.16.refs_1_, bf16[1632,512]{1,0:T(8,128)(2,1)} %weigh_rows.5.refs_2_.refs_1_.refs_0_), custom_call_target="tpu_custom_call" | custom-call | flops 540000000 | bytes 1 | tf_op jit(solution)/shard_map/add_terms/pallas_call | solution.py:379
  196.1 4.7 %collective-permute-start.22 = (bf16[1632,512]{1,0:T(8,128)(2,1)S(1)}, bf16[1632,512]{1,0:T(8,128)(2,1)}, u32[]{:S(2)}, u32[]{:S(2)}) collective-permute-start(bf16[1632,512]{1,0:T(8,128)(2,1)S(1)} %copy-done.2), channel_id=1, source_target_pairs={{4,0},{12,8},{1,5},{9,13},{6,2},{14,10},{3,7},{11,15},{20,16},{28,... | collective-permute-start | bytes 5013512 | tf_op jit(solution)/shard_map/ppermute | solution.py:526
  205.1 12.1 %weigh_rows.6.refs_2_.refs_0_ = bf16[352,1024]{1,0:T(8,128)(2,1)} custom-call(bf16[2,96,3584]{2,1,0:T(8,128)(2,1)} %get-tuple-element.46.refs_0_, bf16[2,64,3584]{2,1,0:T(8,128)(2,1)} %get-tuple-element.47.refs_1_, bf16[2,96,3584]{2,1,0:T(8,128)(2,1)} %copy-done.15, bf16[2,96,3584]{2,1,0:T(8,128)(2,1)} %collective-permute-done.24.refs_3_, ...), custom_call_target="tpu_custom_call" | custom-call | flops 10800000000 | bytes 1 | tf_op jit(solution)/shard_map/weigh_rows/pallas_call | solution.py:349
  217.2 8.7 %collective-permute-start.28 = (bf16[352,1024]{1,0:T(8,128)(2,1)}, bf16[352,1024]{1,0:T(8,128)(2,1)S(1)}, u32[]{:S(2)}, u32[]{:S(2)}) collective-permute-start(bf16[352,1024]{1,0:T(8,128)(2,1)} %weigh_rows.6.refs_2_.refs_0_), channel_id=1, source_target_pairs={{4,0},{12,8},{1,5},{9,13},{6,2},{14,10},{3,7},{11,15},{20,16},{28,... | collective-permute-start | bytes 2162696 | tf_op jit(solution)/shard_map/ppermute | solution.py:526
  229.3 3.4 %add_terms.5 = (bf16[1024,512]{1,0:T(8,128)(2,1)}, bf16[608,512]{1,0:T(8,128)(2,1)}) custom-call(bf16[1632,512]{1,0:T(8,128)(2,1)} %weigh_rows.5.refs_2_.refs_1_.refs_0_, bf16[1632,512]{1,0:T(8,128)(2,1)} %collective-permute-done.22.refs_1_, bf16[352,1024]{1,0:T(8,128)(2,1)} %weigh_rows.6.refs_2_.refs_0_, bf16[1024,512]{1,0:T(8,128)(2,1)} %copy-done.10), custom_call_target="tpu_custom_call" | custom-call | flops 540000000 | bytes 1 | tf_op jit(solution)/shard_map/add_terms/pallas_call | solution.py:379
  242.6 4.6 %collective-permute-start.35 = (f32[32,512]{1,0:T(8,128)S(1)}, f32[32,512]{1,0:T(8,128)S(1)}, u32[]{:S(2)}, u32[]{:S(2)}) collective-permute-start(f32[32,512]{1,0:T(8,128)S(1)} %slice_select_fusion.2), channel_id=1, source_target_pairs={{0,4},{4,0},{8,12},{12,8},{1,5},{5,1},{9,13},{13,9},{2,6},{6,2},{1... | collective-permute-start | bytes 196616 | tf_op jit(solution)/shard_map/ppermute | solution.py:502
  247.1 9.2 %weigh_rows.7.refs_10_.refs_0_ = bf16[64,1024]{1,0:T(8,128)(2,1)} custom-call(bf16[2,64,3584]{2,1,0:T(8,128)(2,1)} %collective-permute-done.29.refs_4_.refs_0_, bf16[2,3584,512]{2,1,0:T(8,128)(2,1)} %get-tuple-element.40.refs_11_.refs_4_.refs_1_, bf16[2,3584,512]{2,1,0:T(8,128)(2,1)} %collective-permute-done.17.refs_11_.refs_5_.refs_2_, ...), custom_call_target="tpu_custom_call" | custom-call | flops 16200000512 | bytes 1 | tf_op jit(solution)/shard_map/weigh_rows/pallas_call | solution.py:349
  260.4 5.1 %assemble.1 = (bf16[1024,512]{1,0:T(8,128)(2,1)}, bf16[1024,512]{1,0:T(8,128)(2,1)}) custom-call(s32[4]{0:T(128)} %pad_add_fusion.words_ref, bf16[1024,512]{1,0:T(8,128)(2,1)} %get-tuple-element.45.refs_0_, bf16[1024,512]{1,0:T(8,128)(2,1)} %copy-done.10, bf16[1024,512]{1,0:T(8,128)(2,1)} %get-tuple-element.50.refs_2_, bf16[1024,512]{1,0:T(8,128)(2,1)} %copy-done.18, ...), custom_call_target="tpu_custom_call" | custom-call | flops 1350000000 | bytes 1 | tf_op jit(solution)/shard_map/assemble/pallas_call | solution.py:447
  265.5 11.4 %collective-permute-start.31 = (bf16[1024,512]{1,0:T(8,128)(2,1)}, bf16[1024,512]{1,0:T(8,128)(2,1)S(1)}, u32[]{:S(2)}, u32[]{:S(2)}) collective-permute-start(bf16[1024,512]{1,0:T(8,128)(2,1)} %get-tuple-element.53), channel_id=1, source_target_pairs={{0,1},{1,0},{2,3},{3,2},{4,5},{5,4},{6,7},{7,6},{8,9},{9,8},{10,11... | collective-permute-start | bytes 3145736 | tf_op jit(solution)/shard_map/ppermute | solution.py:48
  282.0 7.0 %collective-permute-start.34 = (bf16[64,512]{1,0:T(8,128)(2,1)S(1)}, bf16[64,512]{1,0:T(8,128)(2,1)S(1)}, u32[]{:S(2)}, u32[]{:S(2)}) collective-permute-start(bf16[64,512]{1,0:T(8,128)(2,1)S(1)} %get-tuple-element.62), channel_id=1, source_target_pairs={{0,1},{1,0},{2,3},{3,2},{4,5},{5,4},{6,7},{7,6},{8,9},{9,8},{10,11... | collective-permute-start | bytes 196616 | tf_op jit(solution)/shard_map/ppermute | solution.py:48
  (158 shorter events, 82.6 us)
Async XLA Ops:
  4.7 26.3 %collective-permute-start.4 = (bf16[1024,512]{1,0:T(8,128)(2,1)}, bf16[1024,512]{1,0:T(8,128)(2,1)S(1)}, u32[]{:S(2)}, u32[]{:S(2)}) collective-permute-start(bf16[1024,512]{1,0:T(8,128)(2,1)} %bitcast.5.refs_2_), channel_id=1, source_target_pairs={{4,0},{8,4},{12,8},{5,1},{9,5},{13,9},{6,2},{10,6},{14,10},{7,3},{... | collective-permute-start | bytes 3145736 | tf_op jit(solution)/shard_map/ppermute | solution.py:121
  6.0 26.3 %collective-permute-start.3 = (bf16[1024,512]{1,0:T(8,128)(2,1)}, bf16[1024,512]{1,0:T(8,128)(2,1)}, u32[]{:S(2)}, u32[]{:S(2)}) collective-permute-start(bf16[1024,512]{1,0:T(8,128)(2,1)} %bitcast.5.refs_2_), channel_id=1, source_target_pairs={{0,4},{4,8},{8,12},{1,5},{5,9},{9,13},{2,6},{6,10},{10,14},{3,7},{... | collective-permute-start | bytes 3145736 | tf_op jit(solution)/shard_map/ppermute | solution.py:120
  11.1 33.5 %collective-permute-start.1 = (bf16[2,64,3584]{2,1,0:T(8,128)(2,1)}, bf16[2,64,3584]{2,1,0:T(8,128)(2,1)}, u32[]{:S(2)}, u32[]{:S(2)}) collective-permute-start(bf16[2,64,3584]{2,1,0:T(8,128)(2,1)} %get-tuple-element.32), channel_id=1, source_target_pairs={{2,0},{3,1},{0,2},{1,3},{6,4},{7,5},{4,6},{5,7},{10,8},{11,9},{8,1... | collective-permute-start | bytes 2752520 | tf_op jit(solution)/shard_map/ppermute | solution.py:54
  31.0 37.8 %collective-permute-start.9 = (bf16[1024,512]{1,0:T(8,128)(2,1)S(1)}, bf16[1024,512]{1,0:T(8,128)(2,1)S(1)}, u32[]{:S(2)}, u32[]{:S(2)}) collective-permute-start(bf16[1024,512]{1,0:T(8,128)(2,1)S(1)} %collective-permute-done.4.refs_5_.refs_4_), channel_id=1, source_target_pairs={{4,0},{8,4},{12,8},{5,1},{9,5},{13,9},{6,2},{10,6},{14,10},{7,3},{... | collective-permute-start | bytes 3145736 | tf_op jit(solution)/shard_map/ppermute | solution.py:121
  32.3 37.8 %collective-permute-start.8 = (bf16[1024,512]{1,0:T(8,128)(2,1)}, bf16[1024,512]{1,0:T(8,128)(2,1)}, u32[]{:S(2)}, u32[]{:S(2)}) collective-permute-start(bf16[1024,512]{1,0:T(8,128)(2,1)} %collective-permute-done.3.refs_4_.refs_3_), channel_id=1, source_target_pairs={{0,4},{4,8},{8,12},{1,5},{5,9},{9,13},{2,6},{6,10},{10,14},{3,7},{... | collective-permute-start | bytes 3145736 | tf_op jit(solution)/shard_map/ppermute | solution.py:120
  37.3 37.9 %collective-permute-start.5 = (bf16[2,64,3584]{2,1,0:T(8,128)(2,1)}, bf16[2,64,3584]{2,1,0:T(8,128)(2,1)}, u32[]{:S(2)}, u32[]{:S(2)}) collective-permute-start(bf16[2,64,3584]{2,1,0:T(8,128)(2,1)} %get-tuple-element.34), channel_id=1, source_target_pairs={{2,0},{3,1},{0,2},{1,3},{6,4},{7,5},{4,6},{5,7},{10,8},{11,9},{8,1... | collective-permute-start | bytes 2752520 | tf_op jit(solution)/shard_map/ppermute | solution.py:54
  49.4 25.8 %collective-permute-start.7 = (bf16[2,64,3584]{2,1,0:T(8,128)(2,1)}, bf16[2,64,3584]{2,1,0:T(8,128)(2,1)}, u32[]{:S(2)}, u32[]{:S(2)}) collective-permute-start(bf16[2,64,3584]{2,1,0:T(8,128)(2,1)} %get-tuple-element.33.refs_3_), channel_id=1, source_target_pairs={{16,0},{0,16},{17,1},{1,17},{18,2},{2,18},{19,3},{3,19},{20,4},{4,... | collective-permute-start | bytes 2752520 | tf_op jit(solution)/shard_map/ppermute | solution.py:59
  53.4 30.5 %collective-permute-start.6 = (bf16[2,64,3584]{2,1,0:T(8,128)(2,1)}, bf16[2,64,3584]{2,1,0:T(8,128)(2,1)}, u32[]{:S(2)}, u32[]{:S(2)}) collective-permute-start(bf16[2,64,3584]{2,1,0:T(8,128)(2,1)} %get-tuple-element.35.refs_5_), channel_id=1, source_target_pairs={{2,0},{3,1},{0,2},{1,3},{6,4},{7,5},{4,6},{5,7},{10,8},{11,9},{8,1... | collective-permute-start | bytes 2752520 | tf_op jit(solution)/shard_map/ppermute | solution.py:54
  68.9 28.0 %collective-permute-start.14 = (bf16[1024,512]{1,0:T(8,128)(2,1)S(1)}, bf16[1024,512]{1,0:T(8,128)(2,1)S(1)}, u32[]{:S(2)}, u32[]{:S(2)}) collective-permute-start(bf16[1024,512]{1,0:T(8,128)(2,1)S(1)} %collective-permute-done.9.refs_6_.refs_5_), channel_id=1, source_target_pairs={{4,0},{8,4},{12,8},{5,1},{9,5},{13,9},{6,2},{10,6},{14,10},{7,3},{... | collective-permute-start | bytes 3145736 | tf_op jit(solution)/shard_map/ppermute | solution.py:121
  70.2 27.7 %collective-permute-start.13 = (bf16[1024,512]{1,0:T(8,128)(2,1)}, bf16[1024,512]{1,0:T(8,128)(2,1)}, u32[]{:S(2)}, u32[]{:S(2)}) collective-permute-start(bf16[1024,512]{1,0:T(8,128)(2,1)} %collective-permute-done.8.refs_5_.refs_2_), channel_id=1, source_target_pairs={{0,4},{4,8},{8,12},{1,5},{5,9},{9,13},{2,6},{6,10},{10,14},{3,7},{... | collective-permute-start | bytes 3145736 | tf_op jit(solution)/shard_map/ppermute | solution.py:120
  78.6 46.2 %collective-permute-start.10 = (bf16[2,96,3584]{2,1,0:T(8,128)(2,1)}, bf16[2,96,3584]{2,1,0:T(8,128)(2,1)S(1)}, u32[]{:S(2)}, u32[]{:S(2)}) collective-permute-start(bf16[2,96,3584]{2,1,0:T(8,128)(2,1)} %share_rows.12), channel_id=1, source_target_pairs={{2,0},{3,1},{0,2},{1,3},{6,4},{7,5},{4,6},{5,7},{10,8},{11,9},{8,1... | collective-permute-start | bytes 4128776 | tf_op jit(solution)/shard_map/ppermute | solution.py:54
  83.9 40.8 %collective-permute-start.12 = (bf16[2,64,3584]{2,1,0:T(8,128)(2,1)}, bf16[2,64,3584]{2,1,0:T(8,128)(2,1)}, u32[]{:S(2)}, u32[]{:S(2)}) collective-permute-start(bf16[2,64,3584]{2,1,0:T(8,128)(2,1)} %collective-permute-done.6.refs_4_.refs_5_), channel_id=1, source_target_pairs={{16,0},{0,16},{17,1},{1,17},{18,2},{2,18},{19,3},{3,19},{20,4},{4,... | collective-permute-start | bytes 2752520 | tf_op jit(solution)/shard_map/ppermute | solution.py:59
  128.1 45.5 %collective-permute-start.17 = (bf16[2,3584,512]{2,1,0:T(8,128)(2,1)}, bf16[2,3584,512]{2,1,0:T(8,128)(2,1)}, u32[]{:S(2)}, u32[]{:S(2)}) collective-permute-start(bf16[2,3584,512]{2,1,0:T(8,128)(2,1)} %get-tuple-element.40.refs_11_.refs_4_.refs_1_), channel_id=1, source_target_pairs={{0,1},{1,0},{2,3},{3,2},{4,5},{5,4},{6,7},{7,6},{8,9},{9,8},{10,11... | collective-permute-start | bytes 22020104 | tf_op jit(solution)/shard_map/ppermute | solution.py:48
  139.5 31.8 %collective-permute-start.18 = (bf16[2,96,3584]{2,1,0:T(8,128)(2,1)S(1)}, bf16[2,96,3584]{2,1,0:T(8,128)(2,1)}, u32[]{:S(2)}, u32[]{:S(2)}) collective-permute-start(bf16[2,96,3584]{2,1,0:T(8,128)(2,1)S(1)} %copy-done.14), channel_id=1, source_target_pairs={{2,0},{3,1},{0,2},{1,3},{6,4},{7,5},{4,6},{5,7},{10,8},{11,9},{8,1... | collective-permute-start | bytes 4128776 | tf_op jit(solution)/shard_map/ppermute | solution.py:54
  139.8 31.8 %collective-permute-start.20 = (bf16[2,96,3584]{2,1,0:T(8,128)(2,1)}, bf16[2,96,3584]{2,1,0:T(8,128)(2,1)S(1)}, u32[]{:S(2)}, u32[]{:S(2)}) collective-permute-start(bf16[2,96,3584]{2,1,0:T(8,128)(2,1)} %copy-done.4), channel_id=1, source_target_pairs={{16,0},{0,16},{17,1},{1,17},{18,2},{2,18},{19,3},{3,19},{20,4},{4,... | collective-permute-start | bytes 4128776 | tf_op jit(solution)/shard_map/ppermute | solution.py:59
  142.7 59.1 %collective-permute-start.23 = (bf16[2,64,3584]{2,1,0:T(8,128)(2,1)}, bf16[2,64,3584]{2,1,0:T(8,128)(2,1)}, u32[]{:S(2)}, u32[]{:S(2)}) collective-permute-start(bf16[2,64,3584]{2,1,0:T(8,128)(2,1)} %get-tuple-element.41.refs_12_), channel_id=1, source_target_pairs={{2,0},{3,1},{0,2},{1,3},{6,4},{7,5},{4,6},{5,7},{10,8},{11,9},{8,1... | collective-permute-start | bytes 2752520 | tf_op jit(solution)/shard_map/ppermute | solution.py:54
  162.2 29.7 %collective-permute-start.16 = (bf16[1632,512]{1,0:T(8,128)(2,1)}, bf16[1632,512]{1,0:T(8,128)(2,1)}, u32[]{:S(2)}, u32[]{:S(2)}) collective-permute-start(bf16[1632,512]{1,0:T(8,128)(2,1)} %weigh_rows.4.refs_3_.refs_0_), channel_id=1, source_target_pairs={{4,0},{12,8},{1,5},{9,13},{6,2},{14,10},{3,7},{11,15},{20,16},{28,... | collective-permute-start | bytes 5013512 | tf_op jit(solution)/shard_map/ppermute | solution.py:526
  173.3 30.9 %collective-permute-start.24 = (bf16[2,96,3584]{2,1,0:T(8,128)(2,1)}, bf16[2,96,3584]{2,1,0:T(8,128)(2,1)}, u32[]{:S(2)}, u32[]{:S(2)}) collective-permute-start(bf16[2,96,3584]{2,1,0:T(8,128)(2,1)} %get-tuple-element.46.refs_0_), channel_id=1, source_target_pairs={{16,0},{0,16},{17,1},{1,17},{18,2},{2,18},{19,3},{3,19},{20,4},{4,... | collective-permute-start | bytes 4128776 | tf_op jit(solution)/shard_map/ppermute | solution.py:59
  196.1 33.2 %collective-permute-start.22 = (bf16[1632,512]{1,0:T(8,128)(2,1)S(1)}, bf16[1632,512]{1,0:T(8,128)(2,1)}, u32[]{:S(2)}, u32[]{:S(2)}) collective-permute-start(bf16[1632,512]{1,0:T(8,128)(2,1)S(1)} %copy-done.2), channel_id=1, source_target_pairs={{4,0},{12,8},{1,5},{9,13},{6,2},{14,10},{3,7},{11,15},{20,16},{28,... | collective-permute-start | bytes 5013512 | tf_op jit(solution)/shard_map/ppermute | solution.py:526
  200.9 25.9 %collective-permute-start.21 = (bf16[1024,512]{1,0:T(8,128)(2,1)}, bf16[1024,512]{1,0:T(8,128)(2,1)S(1)}, u32[]{:S(2)}, u32[]{:S(2)}) collective-permute-start(bf16[1024,512]{1,0:T(8,128)(2,1)} %get-tuple-element.45.refs_0_), channel_id=1, source_target_pairs={{8,0},{13,5},{2,10},{7,15},{24,16},{29,21},{18,26},{23,31}} | collective-permute-start | bytes 3145736 | tf_op jit(solution)/shard_map/ppermute | solution.py:526
  202.4 31.8 %collective-permute-start.29 = (bf16[2,64,3584]{2,1,0:T(8,128)(2,1)}, bf16[2,64,3584]{2,1,0:T(8,128)(2,1)}, u32[]{:S(2)}, u32[]{:S(2)}) collective-permute-start(bf16[2,64,3584]{2,1,0:T(8,128)(2,1)} %get-tuple-element.47.refs_1_), channel_id=1, source_target_pairs={{16,0},{0,16},{17,1},{1,17},{18,2},{2,18},{19,3},{3,19},{20,4},{4,... | collective-permute-start | bytes 2752520 | tf_op jit(solution)/shard_map/ppermute | solution.py:59
  232.7 25.7 %collective-permute-start.27 = (bf16[608,512]{1,0:T(8,128)(2,1)}, bf16[608,512]{1,0:T(8,128)(2,1)S(1)}, u32[]{:S(2)}, u32[]{:S(2)}) collective-permute-start(bf16[608,512]{1,0:T(8,128)(2,1)} %get-tuple-element.51.refs_3_.refs_6_), channel_id=1, source_target_pairs={{0,8},{5,13},{10,2},{15,7},{16,24},{21,29},{26,18},{31,23}} | collective-permute-start | bytes 1867784 | tf_op jit(solution)/shard_map/ppermute | solution.py:526
  233.4 25.0 %collective-permute-start.26 = (bf16[1024,512]{1,0:T(8,128)(2,1)}, bf16[1024,512]{1,0:T(8,128)(2,1)S(1)}, u32[]{:S(2)}, u32[]{:S(2)}) collective-permute-start(bf16[1024,512]{1,0:T(8,128)(2,1)} %get-tuple-element.50.refs_2_), channel_id=1, source_target_pairs={{8,0},{13,5},{2,10},{7,15},{24,16},{29,21},{18,26},{23,31}} | collective-permute-start | bytes 3145736 | tf_op jit(solution)/shard_map/ppermute | solution.py:526
  265.5 24.4 %collective-permute-start.31 = (bf16[1024,512]{1,0:T(8,128)(2,1)}, bf16[1024,512]{1,0:T(8,128)(2,1)S(1)}, u32[]{:S(2)}, u32[]{:S(2)}) collective-permute-start(bf16[1024,512]{1,0:T(8,128)(2,1)} %get-tuple-element.53), channel_id=1, source_target_pairs={{0,1},{1,0},{2,3},{3,2},{4,5},{5,4},{6,7},{7,6},{8,9},{9,8},{10,11... | collective-permute-start | bytes 3145736 | tf_op jit(solution)/shard_map/ppermute | solution.py:48
  (43 other events, 469.2 us)

commit v8 on v7

--- a/solution.py
+++ b/solution.py
@@ -9,7 +9,7 @@
 from jax.sharding import PartitionSpec as P
 
 CORES = 2
-CHUNKS = (2, 2, 2, 2, 3, 3, 2)
+CHUNKS = (2,) * 8
 VMEM_BYTES = 60 * 1024 * 1024
 FLOPS_PER_US = 270_000_000
 ANYWHERE = pl.BlockSpec(memory_space=pl.ANY)
@@ -389,7 +389,7 @@
 
 def assemble(words, count, features, part, near, far, chips, after):
     groups = lax.axis_size("groups")
-    height = near[0][0][0].shape[0]
+    height = near[0][0].shape[0]
     tall = features // part
     arrays, index = [], {}
 
@@ -399,27 +399,23 @@
             arrays.append(value)
         return index[id(value)]
 
-    near_at = [[[at_of(v) for v in pair] for pair in half] for half in near]
-    far_at = {
-        n: (row, [([at_of(v) for v in pair], first) for pair, first in halves])
-        for n, (row, halves) in far.items()
-    }
+    near_at = [[at_of(v) for v in pair] for pair in near]
+    far_at = {n: (row, [at_of(v) for v in pair], first) for n, (row, pair, first) in far.items()}
     edges = chunk_edges(part)
 
     def kernel(words_ref, *refs):
-        outs = refs[-2:]
+        out = refs[-1]
         away, group, inside = words_ref[0], words_ref[1], words_ref[2]
 
         def total(pair, rows, cols):
             one, two = (refs[at][rows, cols].astype(jnp.float32) for at in pair)
             return (one + two).astype(jnp.bfloat16)
 
-        for j in range(len(near[0])):
+        for j in range(len(near)):
 
             @pl.when((away == 0) & (inside == j * height))
             def _(j=j):
-                for half in range(2):
-                    outs[half][...] = total(near_at[half][j], slice(0, height), slice(0, count))
+                out[...] = total(near_at[j], slice(0, height), slice(0, count))
 
         for s in range(1, chips):
             for g in range(groups):
@@ -432,25 +428,23 @@
                             for k in range(len(CHUNKS)):
                                 top = j * part + edges[k]
                                 piece = edges[k + 1] - edges[k]
-                                for half in range(2):
-                                    if (k, s, shift) in far_at:
-                                        row, halves = far_at[k, s, shift]
-                                        pair, first = halves[half]
-                                        value = total(
-                                            pair, slice(row, row + piece), slice(first, first + count)
-                                        )
-                                    else:
-                                        value = jnp.zeros((piece, count), jnp.bfloat16)
-                                    outs[half][top : top + piece] = value
+                                if (k, s, shift) in far_at:
+                                    row, pair, first = far_at[k, s, shift]
+                                    value = total(
+                                        pair, slice(row, row + piece), slice(first, first + count)
+                                    )
+                                else:
+                                    value = jnp.zeros((piece, count), jnp.bfloat16)
+                                out[top : top + piece] = value
 
     whole = pl.BlockSpec(memory_space=pltpu.VMEM)
     return pl.pallas_call(
         kernel,
-        out_shape=[jax.ShapeDtypeStruct((features, count), jnp.bfloat16)] * 2,
+        out_shape=jax.ShapeDtypeStruct((features, count), jnp.bfloat16),
         in_specs=[pl.BlockSpec(memory_space=pltpu.SMEM)]
         + [whole] * len(arrays)
         + [ANYWHERE] * len(after),
-        out_specs=[whole] * 2,
+        out_specs=whole,
         compiler_params=pltpu.CompilerParams(vmem_limit_bytes=VMEM_BYTES),
         cost_estimate=cost(5),
         name="assemble",
@@ -663,17 +657,15 @@
     others = range(1, groups)
     bits = [1 << i for i in range(ranks.bit_length() - 1)]
     hold_arrived(0, [], [slopes])
-    hold_arrived(1, chunks_of([0], others), [below[1], above[0]])
-    so_far = hidden_part(rank_word, below, above, w_down, None, None, None, [ticks[1]])
-    forward(
-        2, chunks_of([1], others), [so_far, below[2], above[1], early_part, out_down_part]
-    )
-    (early,) = forward(3, chunks_of([2], others), below[3:] + above[2:], [early_part])
+    so_far = hidden_part(rank_word, below, above, w_down, None, None, None, [ticks[0]])
+    hold_arrived(1, chunks_of([0], others), [so_far])
+    hold_arrived(2, chunks_of([1], others), [below[2], above[1], early_part, out_down_part])
+    (early,) = hold_arrived(3, chunks_of([2], others), below[3:] + above[2:], [early_part])
     mine, up_out_part = hidden_part(
         rank_word, below, above, w_down, so_far, slopes, proj_u.T, [ticks[3]]
     )
     early = early + exchange(early, bits[0])
-    mine, early = forward(4, chunks_of([3], others), [], [mine, early])
+    mine, early = forward(4, chunks_of([3], others) + [(5, 0)], [], [mine, early])
     theirs = swap_cores(mine)
 
     out_parts = jnp.stack([up_out_part, out_down_part]).reshape(2, ranks, -1, count)
@@ -692,17 +684,19 @@
 
     first_names = chunks_of(range(5), [0]) + chunks_of(range(4), others)
     first_mine = terms(first_names, [mine], [ticks[4]], 32, near=True)
-    (out_parts,) = hold_arrived(5, chunks_of([4], others), first_mine[0] + [early], [out_parts])
+    (out_parts,) = forward(
+        5, chunks_of([4], others) + [(6, 0)], first_mine[0] + [early], [out_parts]
+    )
     first_theirs = terms(first_names, [theirs], [ticks[5]], 60, near=True)
     sums_mine, end_mine = carry_on(first_mine, first_theirs[0])
-    hold_arrived(6, [], first_theirs[0])
-    second_names = chunks_of([5, 6], [0]) + chunks_of([4, 5], others)
+    forward(6, chunks_of([5], others) + [(7, 0)], first_theirs[0])
+    second_names = chunks_of([5, 6, 7], [0]) + chunks_of([4, 5, 6], others)
     near_received = [got for names, _, got in end_mine if names is None]
     far_received = [got for names, _, got in end_mine if names is not None]
     second = terms(second_names, [mine, theirs], [ticks[6]] + far_received, 40)
     sums_theirs, end_theirs = carry_on(first_theirs, second[0] + near_received)
 
-    last_names = chunks_of([6], others)
+    last_names = chunks_of([7], others)
     come = [fetched[n] for n in fetched if (n[0], n[2]) in last_names]
     sums_second, end_second = carry_on(second, sums_theirs + come)
     last = terms(last_names, [mine, theirs], sums_second, 60)
@@ -731,19 +725,21 @@
         sizes = [edges[n[0] + 1] - edges[n[0]] for n in names]
         return [(sum(sizes[:i]), n) for i, n in enumerate(names)]
 
-    near, far = [[], []], {}
-    for (names, *m), (_, *t) in zip(end_mine, end_theirs):
-        if names is None:
-            near[0].append(m)
-            near[1].append(t)
-        else:
-            far.update((n, (row, [(m, 0), (t, 0)])) for row, n in tops(names))
-    for names, *pair in end_second:
-        far.update((n, (row, [(pair, 0), (pair, count)])) for row, n in tops(names))
     words = jnp.stack([away, group, inside, owner]).astype(jnp.int32)
-    total_mine, total_theirs = assemble(
-        words, count, features, part, near, far, chips, last[0]
-    )
+
+    def assembled(end, first, after):
+        near = [pair for names, *pair in end if names is None]
+        far = {}
+        for names, *pair in end:
+            if names is not None:
+                far.update((n, (row, pair, 0)) for row, n in tops(names))
+        for names, *pair in end_second:
+            far.update((n, (row, pair, first)) for row, n in tops(names))
+        return assemble(words, count, features, part, near, far, chips, after)
+
+    received = [got for _, _, got in end_last]
+    total_theirs = assembled(end_theirs, count, received)
+    total_mine = assembled(end_mine, 0, [total_theirs])
     from_partner = swap_cores(total_theirs)
 
     def pick(index, options):

time: 295 us -> 289 us (0.980)
  starting transfers between devices: 90.5 us -> 77.3 us
  waiting for transfers between devices: 36.5 us -> 43.8 us
  local copies, waits for them, and re-layouts: 13.4 us -> 10.2 us
    ppermute x10, starting transfers between devices: 24.6 us -> 15.5 us  [send(): return lax.ppermute(value, ('groups', 'tensor', 'dp'), pairs)]
    ppermute x3, starting transfers between devices: 29.9 us -> 21.3 us  [swap_cores(): return lax.ppermute(value, 'dp', [(i, i ^ 1) for i in range(size)])]
    ppermute x7 -> x8, waiting for transfers between devices: 15.4 us -> 23.1 us  [from_group(): lax.ppermute(value, 'groups', [((i + shift) % size, i) for i in range(siz...]
    ppermute x10, waiting for transfers between devices: 5.57 us -> 10.3 us  [send(): return lax.ppermute(value, ('groups', 'tensor', 'dp'), pairs)]
    ppermute x7 -> x8, waiting for transfers between devices: 13.4 us -> 8.81 us  [from_chip(): lax.ppermute(value, 'dp', [((i + step) % size, i) for i in range(size)])]
    unnamed x64 -> x62, local copies, waits for them, and re-layouts: 12.6 us -> 9.41 us
    pallas_call x1 -> x2, Pallas kernels: 5.09 us -> 7.28 us  [assemble(): pl.pallas_call(kernel, out_shape=jax.ShapeDtypeStruct((features, count),...]
    ppermute x7 -> x8, starting transfers between devices: 5.43 us -> 7.6 us  [from_chip(): lax.ppermute(value, 'dp', [((i + step) % size, i) for i in range(size)])]
  transfers between devices with their start and end apart: 36 -> 38, of which waited for: 12 -> 10; matrix products, arithmetic and copies ran while one was open for 5% -> 5% of each run, Pallas kernels for 46% -> 46%
where the time goes in v8:
time: 289 us; the launch traced here: 288 us
  Pallas kernels  143 us (49%)
  starting transfers between devices  77.3 us (27%)
  waiting for transfers between devices  43.8 us (15%)
  local copies, waits for them, and re-layouts  10.2 us (4%)
  other arithmetic  7.61 us (3%)
  matrix products  4.92 us (2%)
    pallas_call x4, Pallas kernels, weigh(): pl.pallas_call(kernel, grid=(steps,), out_shape=shapes, in_specs=specs +...  57.9 us
    pallas_call x2, Pallas kernels, hidden_part(): pl.pallas_call(kernel, grid_spec=pltpu.PrefetchScalarGridSpec(num_scalar_...  35.4 us
    ppermute x8, waiting for transfers between devices, from_group(): lax.ppermute(value, 'groups', [((i + shift) % size, i) for i in range(siz...  23.1 us
    ppermute x3, starting transfers between devices, swap_cores(): return lax.ppermute(value, 'dp', [(i, i ^ 1) for i in range(size)])  21.3 us
    pallas_call x9, Pallas kernels, share_rows(): pl.pallas_call(kernel, grid_spec=pltpu.PrefetchScalarGridSpec(num_scalar_...  16.5 us
    ppermute x10, starting transfers between devices, send(): return lax.ppermute(value, ('groups', 'tensor', 'dp'), pairs)  15.5 us
    ppermute x3, starting transfers between devices, spread_ranks(): lax.ppermute(below[-1], 'tensor', [(i, i + 1) for i in range(ranks - 1)])  14.1 us
    pallas_call x1, Pallas kernels, prepare(): pl.pallas_call(kernel, grid=(hidden // tile,), out_shape=[jax.ShapeDtypeS...  11.9 us
  transfers between devices with their start and end apart: 38, of which 10 were waited for; matrix products, arithmetic and copies ran while one was open for 5% of the time, Pallas kernels for 46%

profile of v8, /device:TPU:3, one launch (start us, length us, event | category | flops | bytes accessed | tf_op | source)
XLA Modules:
  0.0 287.6 jit_solution(1931950614672126235)
XLA Ops:
  5.3 5.1 %collective-permute-start.3 = (bf16[1024,512]{1,0:T(8,128)(2,1)S(1)}, bf16[1024,512]{1,0:T(8,128)(2,1)}, u32[]{:S(2)}, u32[]{:S(2)}) collective-permute-start(bf16[1024,512]{1,0:T(8,128)(2,1)S(1)} %bitcast.33), channel_id=1, source_target_pairs={{0,4},{4,8},{8,12},{1,5},{5,9},{9,13},{2,6},{6,10},{10,14},{3,7},{... | collective-permute-start | bytes 3145736 | tf_op jit(solution)/shard_map/ppermute | solution.py:120
  11.7 11.9 %prepare.1 = (f32[2,3584,512]{2,1,0:T(8,128)}, f32[64,512]{1,0:T(8,128)}) custom-call(bf16[512,3584]{1,0:T(8,128)(2,1)} %gate_ref.1, bf16[512,3584]{1,0:T(8,128)(2,1)} %up_ref.1, bf16[64,3584]{1,0:T(8,128)(2,1)} %bitcast.42, bf16[2,64,3584]{2,1,0:T(8,128)(2,1)} %get-tuple-element.27.refs_0_), custom_call_target="tpu_custom_call" | custom-call | flops 3240000000 | bytes 1 | tf_op jit(solution)/shard_map/prepare/pallas_call | solution.py:147
  31.4 4.1 %collective-permute-start.7 = (bf16[1024,512]{1,0:T(8,128)(2,1)}, bf16[1024,512]{1,0:T(8,128)(2,1)S(1)}, u32[]{:S(2)}, u32[]{:S(2)}) collective-permute-start(bf16[1024,512]{1,0:T(8,128)(2,1)} %collective-permute-done.3.refs_3_), channel_id=1, source_target_pairs={{0,4},{4,8},{8,12},{1,5},{5,9},{9,13},{2,6},{6,10},{10,14},{3,7},{... | collective-permute-start | bytes 3145736 | tf_op jit(solution)/shard_map/ppermute | solution.py:120
  35.5 14.4 %hidden_part.2.refs_4_.refs_7_ = f32[3584,512]{1,0:T(8,128)} custom-call(s32[1]{0:T(128)} %bitcast.5.rank_ref, bf16[3584,4096]{1,0:T(8,128)(2,1)} %refs_1_.17, bf16[3584,4096]{1,0:T(8,128)(2,1)} %refs_1_.17, bf16[1024,512]{1,0:T(8,128)(2,1)} %bitcast.34, bf16[1024,512]{1,0:T(8,128)(2,1)} %collective-permute-done.3.refs_3_, ...), custom_call_target="tpu_custom_call" | custom-call | flops 3240000000 | bytes 1 | tf_op jit(solution)/shard_map/hidden_part/pallas_call | solution.py:272
  58.1 5.0 %collective-permute-start.11 = (bf16[1024,512]{1,0:T(8,128)(2,1)S(1)}, bf16[1024,512]{1,0:T(8,128)(2,1)}, u32[]{:S(2)}, u32[]{:S(2)}) collective-permute-start(bf16[1024,512]{1,0:T(8,128)(2,1)S(1)} %collective-permute-done.7.refs_4_.refs_2_), channel_id=1, source_target_pairs={{0,4},{4,8},{8,12},{1,5},{5,9},{9,13},{2,6},{6,10},{10,14},{3,7},{... | collective-permute-start | bytes 3145736 | tf_op jit(solution)/shard_map/ppermute | solution.py:120
  66.0 5.9 %collective-permute-done.6.refs_3_.refs_8_ = bf16[2,64,3584]{2,1,0:T(8,128)(2,1)S(1)} collective-permute-done((bf16[2,64,3584]{2,1,0:T(8,128)(2,1)}, bf16[2,64,3584]{2,1,0:T(8,128)(2,1)S(1)}, u32[]{:S(2)}, u32[]{:S(2)}) %collective-permute-start.6) | collective-permute-done | bytes 917536 | tf_op jit(solution)/shard_map/ppermute | solution.py:59
  77.0 6.6 %collective-permute-done.9.refs_2_ = bf16[2,64,3584]{2,1,0:T(8,128)(2,1)} collective-permute-done((bf16[2,64,3584]{2,1,0:T(8,128)(2,1)}, bf16[2,64,3584]{2,1,0:T(8,128)(2,1)}, u32[]{:S(2)}, u32[]{:S(2)}) %collective-permute-start.9) | collective-permute-done | bytes 917536 | tf_op jit(solution)/shard_map/ppermute | solution.py:54
  83.7 10.3 %collective-permute-done.10.refs_4_.refs_9_ = bf16[2,64,3584]{2,1,0:T(8,128)(2,1)S(1)} collective-permute-done((bf16[2,64,3584]{2,1,0:T(8,128)(2,1)}, bf16[2,64,3584]{2,1,0:T(8,128)(2,1)S(1)}, u32[]{:S(2)}, u32[]{:S(2)}) %collective-permute-start.10) | collective-permute-done | bytes 917536 | tf_op jit(solution)/shard_map/ppermute | solution.py:59
  100.2 21.0 %hidden_part.3 = (bf16[2,3584,512]{2,1,0:T(8,128)(2,1)}, f32[64,512]{1,0:T(8,128)}) custom-call(s32[1]{0:T(128)} %bitcast.5.rank_ref, bf16[3584,4096]{1,0:T(8,128)(2,1)} %refs_1_.17, bf16[3584,4096]{1,0:T(8,128)(2,1)} %refs_1_.17, bf16[1024,512]{1,0:T(8,128)(2,1)} %copy-done.3, bf16[1024,512]{1,0:T(8,128)(2,1)} %collective-permute-done.11.refs_5_.refs_3_, ...), custom_call_target="tpu_custom_call" | custom-call | flops 3240000000 | bytes 1 | tf_op jit(solution)/shard_map/hidden_part/pallas_call | solution.py:272
  125.9 4.3 %collective-permute-start.18 = (bf16[2,3584,512]{2,1,0:T(8,128)(2,1)}, bf16[2,3584,512]{2,1,0:T(8,128)(2,1)}, u32[]{:S(2)}, u32[]{:S(2)}) collective-permute-start(bf16[2,3584,512]{2,1,0:T(8,128)(2,1)} %get-tuple-element.41.refs_11_.refs_6_.refs_1_), channel_id=1, source_target_pairs={{0,1},{1,0},{2,3},{3,2},{4,5},{5,4},{6,7},{7,6},{8,9},{9,8},{10,11... | collective-permute-start | bytes 22020104 | tf_op jit(solution)/shard_map/ppermute | solution.py:48
  134.6 18.1 %weigh_rows.4.refs_6_.refs_0_ = bf16[1600,512]{1,0:T(8,128)(2,1)} custom-call(bf16[1024,3584]{1,0:T(8,128)(2,1)} %refs_0_.21, bf16[1024,3584]{1,0:T(8,128)(2,1)} %refs_1_.21, bf16[2,64,3584]{2,1,0:T(8,128)(2,1)} %get-tuple-element.29.refs_2_, bf16[2,64,3584]{2,1,0:T(8,128)(2,1)} %get-tuple-element.32.refs_3_, ...), custom_call_target="tpu_custom_call" | custom-call | flops 8640000000 | bytes 1 | tf_op jit(solution)/shard_map/weigh_rows/pallas_call | solution.py:349
  152.7 3.6 %collective-permute-start.17 = (bf16[1600,512]{1,0:T(8,128)(2,1)}, bf16[1600,512]{1,0:T(8,128)(2,1)}, u32[]{:S(2)}, u32[]{:S(2)}) collective-permute-start(bf16[1600,512]{1,0:T(8,128)(2,1)} %weigh_rows.4.refs_6_.refs_0_), channel_id=1, source_target_pairs={{4,0},{12,8},{1,5},{9,13},{6,2},{14,10},{3,7},{11,15},{20,16},{28,... | collective-permute-start | bytes 4915208 | tf_op jit(solution)/shard_map/ppermute | solution.py:520
  163.4 18.1 %weigh_rows.5.refs_2_.refs_3_.refs_0_ = bf16[1600,512]{1,0:T(8,128)(2,1)} custom-call(bf16[1024,3584]{1,0:T(8,128)(2,1)} %refs_0_.21, bf16[1024,3584]{1,0:T(8,128)(2,1)} %refs_1_.21, bf16[2,64,3584]{2,1,0:T(8,128)(2,1)} %get-tuple-element.29.refs_2_, bf16[2,64,3584]{2,1,0:T(8,128)(2,1)} %get-tuple-element.32.refs_3_, ...), custom_call_target="tpu_custom_call" | custom-call | flops 16200000512 | bytes 1 | tf_op jit(solution)/shard_map/weigh_rows/pallas_call | solution.py:349
  181.5 3.3 %add_terms.4 = (bf16[1024,512]{1,0:T(8,128)(2,1)}, bf16[576,512]{1,0:T(8,128)(2,1)}) custom-call(bf16[1600,512]{1,0:T(8,128)(2,1)} %weigh_rows.4.refs_6_.refs_0_, bf16[1600,512]{1,0:T(8,128)(2,1)} %collective-permute-done.17.refs_1_, bf16[1600,512]{1,0:T(8,128)(2,1)} %weigh_rows.5.refs_2_.refs_3_.refs_0_), custom_call_target="tpu_custom_call" | custom-call | flops 540000000 | bytes 1 | tf_op jit(solution)/shard_map/add_terms/pallas_call | solution.py:379
  191.5 6.9 %collective-permute-done.26.refs_5_ = bf16[2,64,3584]{2,1,0:T(8,128)(2,1)} collective-permute-done((bf16[2,64,3584]{2,1,0:T(8,128)(2,1)}, bf16[2,64,3584]{2,1,0:T(8,128)(2,1)}, u32[]{:S(2)}, u32[]{:S(2)}) %collective-permute-start.26) | collective-permute-done | bytes 917536 | tf_op jit(solution)/shard_map/ppermute | solution.py:59
  198.4 12.5 %weigh_rows.6.refs_2_.refs_0_ = bf16[384,1024]{1,0:T(8,128)(2,1)} custom-call(bf16[2,64,3584]{2,1,0:T(8,128)(2,1)} %copy-done.11, bf16[2,64,3584]{2,1,0:T(8,128)(2,1)} %copy-done.15, bf16[2,64,3584]{2,1,0:T(8,128)(2,1)} %collective-permute-done.24.refs_2_, bf16[2,64,3584]{2,1,0:T(8,128)(2,1)} %collective-permute-done.20.refs_3_, ...), custom_call_target="tpu_custom_call" | custom-call | flops 10800000000 | bytes 1 | tf_op jit(solution)/shard_map/weigh_rows/pallas_call | solution.py:349
  213.9 4.5 %collective-permute-done.28.refs_1_ = bf16[1600,512]{1,0:T(8,128)(2,1)} collective-permute-done((bf16[1600,512]{1,0:T(8,128)(2,1)}, bf16[1600,512]{1,0:T(8,128)(2,1)}, u32[]{:S(2)}, u32[]{:S(2)}) %collective-permute-start.28) | collective-permute-done | bytes 1638432 | tf_op jit(solution)/shard_map/ppermute | solution.py:520
  218.4 3.4 %add_terms.5 = (bf16[1024,512]{1,0:T(8,128)(2,1)}, bf16[576,512]{1,0:T(8,128)(2,1)}) custom-call(bf16[1600,512]{1,0:T(8,128)(2,1)} %weigh_rows.5.refs_2_.refs_3_.refs_0_, bf16[1600,512]{1,0:T(8,128)(2,1)} %collective-permute-done.28.refs_1_, bf16[384,1024]{1,0:T(8,128)(2,1)} %weigh_rows.6.refs_2_.refs_0_, bf16[1024,512]{1,0:T(8,128)(2,1)} %copy-done.8), custom_call_target="tpu_custom_call" | custom-call | flops 540000000 | bytes 1 | tf_op jit(solution)/shard_map/add_terms/pallas_call | solution.py:379
  223.2 3.6 %collective-permute-done.27.refs_1_ = bf16[384,1024]{1,0:T(8,128)(2,1)} collective-permute-done((bf16[384,1024]{1,0:T(8,128)(2,1)}, bf16[384,1024]{1,0:T(8,128)(2,1)}, u32[]{:S(2)}, u32[]{:S(2)}) %collective-permute-start.27) | collective-permute-done | bytes 786464 | tf_op jit(solution)/shard_map/ppermute | solution.py:520
  231.5 4.8 %collective-permute-start.37 = (f32[32,512]{1,0:T(8,128)S(1)}, f32[32,512]{1,0:T(8,128)S(1)}, u32[]{:S(2)}, u32[]{:S(2)}) collective-permute-start(f32[32,512]{1,0:T(8,128)S(1)} %slice_select_fusion.2), channel_id=1, source_target_pairs={{0,4},{4,0},{8,12},{12,8},{1,5},{5,1},{9,13},{13,9},{2,6},{6,2},{1... | collective-permute-start | bytes 196616 | tf_op jit(solution)/shard_map/ppermute | solution.py:496
  236.3 9.2 %weigh_rows.7.refs_0_ = bf16[64,1024]{1,0:T(8,128)(2,1)} custom-call(bf16[2,64,3584]{2,1,0:T(8,128)(2,1)} %copy-done.21, bf16[2,3584,512]{2,1,0:T(8,128)(2,1)} %get-tuple-element.41.refs_11_.refs_6_.refs_1_, bf16[2,3584,512]{2,1,0:T(8,128)(2,1)} %collective-permute-done.18.refs_11_.refs_7_.refs_2_, bf16[384,1024]{1,0:T(8,128)(2,1)} %add_terms.6.refs_3_.refs_4_.refs_1_), custom_call_target="tpu_custom_call" | custom-call | flops 16200000512 | bytes 1 | tf_op jit(solution)/shard_map/weigh_rows/pallas_call | solution.py:349
  255.7 3.7 %assemble.2.refs_6_ = bf16[1024,512]{1,0:T(8,128)(2,1)} custom-call(s32[4]{0:T(128)} %pad_add_fusion.words_ref, bf16[1024,512]{1,0:T(8,128)(2,1)} %get-tuple-element.48.refs_2_.refs_0_, bf16[1024,512]{1,0:T(8,128)(2,1)} %copy-done.20, bf16[576,512]{1,0:T(8,128)(2,1)} %get-tuple-element.49.refs_3_.refs_2_, bf16[576,512]{1,0:T(8,128)(2,1)} %copy-done.22, ...), custom_call_target="tpu_custom_call" | custom-call | flops 1350000000 | bytes 1 | tf_op jit(solution)/shard_map/assemble/pallas_call | solution.py:441
  259.4 17.0 %collective-permute-start.35 = (bf16[1024,512]{1,0:T(8,128)(2,1)}, bf16[1024,512]{1,0:T(8,128)(2,1)S(1)}, u32[]{:S(2)}, u32[]{:S(2)}) collective-permute-start(bf16[1024,512]{1,0:T(8,128)(2,1)} %assemble.2.refs_6_), channel_id=1, source_target_pairs={{0,1},{1,0},{2,3},{3,2},{4,5},{5,4},{6,7},{7,6},{8,9},{9,8},{10,11... | collective-permute-start | bytes 3145736 | tf_op jit(solution)/shard_map/ppermute | solution.py:48
  280.0 3.6 %assemble.3.mine_ref = bf16[1024,512]{1,0:T(8,128)(2,1)} custom-call(s32[4]{0:T(128)} %pad_add_fusion.words_ref, bf16[1024,512]{1,0:T(8,128)(2,1)} %get-tuple-element.46.refs_0_, bf16[1024,512]{1,0:T(8,128)(2,1)} %copy-done.8, bf16[576,512]{1,0:T(8,128)(2,1)} %get-tuple-element.47.refs_2_, bf16[576,512]{1,0:T(8,128)(2,1)} %collective-permute-done.23.refs_9_.refs_3_, ...), custom_call_target="tpu_custom_call" | custom-call | flops 1350000000 | bytes 1 | tf_op jit(solution)/shard_map/assemble/pallas_call | solution.py:441
  (161 shorter events, 85.7 us)
Async XLA Ops:
  4.0 26.1 %collective-permute-start.4 = (bf16[1024,512]{1,0:T(8,128)(2,1)S(1)}, bf16[1024,512]{1,0:T(8,128)(2,1)}, u32[]{:S(2)}, u32[]{:S(2)}) collective-permute-start(bf16[1024,512]{1,0:T(8,128)(2,1)S(1)} %bitcast.32), channel_id=1, source_target_pairs={{4,0},{8,4},{12,8},{5,1},{9,5},{13,9},{6,2},{10,6},{14,10},{7,3},{... | collective-permute-start | bytes 3145736 | tf_op jit(solution)/shard_map/ppermute | solution.py:121
  5.3 26.1 %collective-permute-start.3 = (bf16[1024,512]{1,0:T(8,128)(2,1)S(1)}, bf16[1024,512]{1,0:T(8,128)(2,1)}, u32[]{:S(2)}, u32[]{:S(2)}) collective-permute-start(bf16[1024,512]{1,0:T(8,128)(2,1)S(1)} %bitcast.33), channel_id=1, source_target_pairs={{0,4},{4,8},{8,12},{1,5},{5,9},{9,13},{2,6},{6,10},{10,14},{3,7},{... | collective-permute-start | bytes 3145736 | tf_op jit(solution)/shard_map/ppermute | solution.py:120
  10.4 39.5 %collective-permute-start.1 = (bf16[2,64,3584]{2,1,0:T(8,128)(2,1)}, bf16[2,64,3584]{2,1,0:T(8,128)(2,1)}, u32[]{:S(2)}, u32[]{:S(2)}) collective-permute-start(bf16[2,64,3584]{2,1,0:T(8,128)(2,1)} %get-tuple-element.30), channel_id=1, source_target_pairs={{2,0},{3,1},{0,2},{1,3},{6,4},{7,5},{4,6},{5,7},{10,8},{11,9},{8,1... | collective-permute-start | bytes 2752520 | tf_op jit(solution)/shard_map/ppermute | solution.py:54
  28.3 37.7 %collective-permute-start.5 = (bf16[2,64,3584]{2,1,0:T(8,128)(2,1)}, bf16[2,64,3584]{2,1,0:T(8,128)(2,1)}, u32[]{:S(2)}, u32[]{:S(2)}) collective-permute-start(bf16[2,64,3584]{2,1,0:T(8,128)(2,1)} %get-tuple-element.31.refs_5_), channel_id=1, source_target_pairs={{2,0},{3,1},{0,2},{1,3},{6,4},{7,5},{4,6},{5,7},{10,8},{11,9},{8,1... | collective-permute-start | bytes 2752520 | tf_op jit(solution)/shard_map/ppermute | solution.py:54
  30.1 26.7 %collective-permute-start.8 = (bf16[1024,512]{1,0:T(8,128)(2,1)}, bf16[1024,512]{1,0:T(8,128)(2,1)S(1)}, u32[]{:S(2)}, u32[]{:S(2)}) collective-permute-start(bf16[1024,512]{1,0:T(8,128)(2,1)} %collective-permute-done.4.refs_4_), channel_id=1, source_target_pairs={{4,0},{8,4},{12,8},{5,1},{9,5},{13,9},{6,2},{10,6},{14,10},{7,3},{... | collective-permute-start | bytes 3145736 | tf_op jit(solution)/shard_map/ppermute | solution.py:121
  31.4 26.7 %collective-permute-start.7 = (bf16[1024,512]{1,0:T(8,128)(2,1)}, bf16[1024,512]{1,0:T(8,128)(2,1)S(1)}, u32[]{:S(2)}, u32[]{:S(2)}) collective-permute-start(bf16[1024,512]{1,0:T(8,128)(2,1)} %collective-permute-done.3.refs_3_), channel_id=1, source_target_pairs={{0,4},{4,8},{8,12},{1,5},{5,9},{9,13},{2,6},{6,10},{10,14},{3,7},{... | collective-permute-start | bytes 3145736 | tf_op jit(solution)/shard_map/ppermute | solution.py:120
  56.8 26.9 %collective-permute-start.12 = (bf16[1024,512]{1,0:T(8,128)(2,1)S(1)}, bf16[1024,512]{1,0:T(8,128)(2,1)S(1)}, u32[]{:S(2)}, u32[]{:S(2)}) collective-permute-start(bf16[1024,512]{1,0:T(8,128)(2,1)S(1)} %collective-permute-done.8.refs_5_), channel_id=1, source_target_pairs={{4,0},{8,4},{12,8},{5,1},{9,5},{13,9},{6,2},{10,6},{14,10},{7,3},{... | collective-permute-start | bytes 3145736 | tf_op jit(solution)/shard_map/ppermute | solution.py:121
  58.1 25.5 %collective-permute-start.11 = (bf16[1024,512]{1,0:T(8,128)(2,1)S(1)}, bf16[1024,512]{1,0:T(8,128)(2,1)}, u32[]{:S(2)}, u32[]{:S(2)}) collective-permute-start(bf16[1024,512]{1,0:T(8,128)(2,1)S(1)} %collective-permute-done.7.refs_4_.refs_2_), channel_id=1, source_target_pairs={{0,4},{4,8},{8,12},{1,5},{5,9},{9,13},{2,6},{6,10},{10,14},{3,7},{... | collective-permute-start | bytes 3145736 | tf_op jit(solution)/shard_map/ppermute | solution.py:120
  75.8 46.2 %collective-permute-start.13 = (bf16[2,64,3584]{2,1,0:T(8,128)(2,1)}, bf16[2,64,3584]{2,1,0:T(8,128)(2,1)}, u32[]{:S(2)}, u32[]{:S(2)}) collective-permute-start(bf16[2,64,3584]{2,1,0:T(8,128)(2,1)} %get-tuple-element.37), channel_id=1, source_target_pairs={{2,0},{3,1},{0,2},{1,3},{6,4},{7,5},{4,6},{5,7},{10,8},{11,9},{8,1... | collective-permute-start | bytes 2752520 | tf_op jit(solution)/shard_map/ppermute | solution.py:54
  97.0 25.0 %collective-permute-start.14 = (bf16[2,64,3584]{2,1,0:T(8,128)(2,1)}, bf16[2,64,3584]{2,1,0:T(8,128)(2,1)S(1)}, u32[]{:S(2)}, u32[]{:S(2)}) collective-permute-start(bf16[2,64,3584]{2,1,0:T(8,128)(2,1)} %get-tuple-element.36.refs_5_), channel_id=1, source_target_pairs={{16,0},{0,16},{17,1},{1,17},{18,2},{2,18},{19,3},{3,19},{20,4},{4,... | collective-permute-start | bytes 2752520 | tf_op jit(solution)/shard_map/ppermute | solution.py:59
  97.7 25.1 %collective-permute-start.16 = (bf16[2,64,3584]{2,1,0:T(8,128)(2,1)}, bf16[2,64,3584]{2,1,0:T(8,128)(2,1)S(1)}, u32[]{:S(2)}, u32[]{:S(2)}) collective-permute-start(bf16[2,64,3584]{2,1,0:T(8,128)(2,1)} %get-tuple-element.38.refs_10_), channel_id=1, source_target_pairs={{2,0},{3,1},{0,2},{1,3},{6,4},{7,5},{4,6},{5,7},{10,8},{11,9},{8,1... | collective-permute-start | bytes 2752520 | tf_op jit(solution)/shard_map/ppermute | solution.py:54
  125.9 37.4 %collective-permute-start.18 = (bf16[2,3584,512]{2,1,0:T(8,128)(2,1)}, bf16[2,3584,512]{2,1,0:T(8,128)(2,1)}, u32[]{:S(2)}, u32[]{:S(2)}) collective-permute-start(bf16[2,3584,512]{2,1,0:T(8,128)(2,1)} %get-tuple-element.41.refs_11_.refs_6_.refs_1_), channel_id=1, source_target_pairs={{0,1},{1,0},{2,3},{3,2},{4,5},{5,4},{6,7},{7,6},{8,9},{9,8},{10,11... | collective-permute-start | bytes 22020104 | tf_op jit(solution)/shard_map/ppermute | solution.py:48
  130.3 28.7 %collective-permute-start.20 = (bf16[2,64,3584]{2,1,0:T(8,128)(2,1)}, bf16[2,64,3584]{2,1,0:T(8,128)(2,1)}, u32[]{:S(2)}, u32[]{:S(2)}) collective-permute-start(bf16[2,64,3584]{2,1,0:T(8,128)(2,1)} %collective-permute-done.13.refs_5_.refs_6_), channel_id=1, source_target_pairs={{16,0},{0,16},{17,1},{1,17},{18,2},{2,18},{19,3},{3,19},{20,4},{4,... | collective-permute-start | bytes 2752520 | tf_op jit(solution)/shard_map/ppermute | solution.py:59
  131.5 24.7 %collective-permute-start.19 = (f32[192,512]{1,0:T(8,128)S(1)}, f32[192,512]{1,0:T(8,128)S(1)}, u32[]{:S(2)}, u32[]{:S(2)}) collective-permute-start(f32[192,512]{1,0:T(8,128)S(1)} %pad_maximum_fusion), channel_id=1, source_target_pairs={{0,8},{4,12},{8,0},{12,4},{1,9},{5,13},{9,1},{13,5},{2,10},{6,14},... | collective-permute-start | bytes 1179656 | tf_op jit(solution)/shard_map/ppermute | solution.py:496
  133.4 25.6 %collective-permute-start.21 = (bf16[2,64,3584]{2,1,0:T(8,128)(2,1)}, bf16[2,64,3584]{2,1,0:T(8,128)(2,1)S(1)}, u32[]{:S(2)}, u32[]{:S(2)}) collective-permute-start(bf16[2,64,3584]{2,1,0:T(8,128)(2,1)} %get-tuple-element.42.refs_12_), channel_id=1, source_target_pairs={{2,0},{3,1},{0,2},{1,3},{6,4},{7,5},{4,6},{5,7},{10,8},{11,9},{8,1... | collective-permute-start | bytes 2752520 | tf_op jit(solution)/shard_map/ppermute | solution.py:54
  152.7 28.8 %collective-permute-start.17 = (bf16[1600,512]{1,0:T(8,128)(2,1)}, bf16[1600,512]{1,0:T(8,128)(2,1)}, u32[]{:S(2)}, u32[]{:S(2)}) collective-permute-start(bf16[1600,512]{1,0:T(8,128)(2,1)} %weigh_rows.4.refs_6_.refs_0_), channel_id=1, source_target_pairs={{4,0},{12,8},{1,5},{9,13},{6,2},{14,10},{3,7},{11,15},{20,16},{28,... | collective-permute-start | bytes 4915208 | tf_op jit(solution)/shard_map/ppermute | solution.py:520
  156.3 33.8 %collective-permute-start.25 = (bf16[2,64,3584]{2,1,0:T(8,128)(2,1)S(1)}, bf16[2,64,3584]{2,1,0:T(8,128)(2,1)}, u32[]{:S(2)}, u32[]{:S(2)}) collective-permute-start(bf16[2,64,3584]{2,1,0:T(8,128)(2,1)S(1)} %copy-done.12), channel_id=1, source_target_pairs={{16,0},{0,16},{17,1},{1,17},{18,2},{2,18},{19,3},{3,19},{20,4},{4,... | collective-permute-start | bytes 2752520 | tf_op jit(solution)/shard_map/ppermute | solution.py:59
  162.0 24.3 %collective-permute-start.24 = (bf16[2,64,3584]{2,1,0:T(8,128)(2,1)}, bf16[2,64,3584]{2,1,0:T(8,128)(2,1)}, u32[]{:S(2)}, u32[]{:S(2)}) collective-permute-start(bf16[2,64,3584]{2,1,0:T(8,128)(2,1)} %get-tuple-element.45.refs_12_), channel_id=1, source_target_pairs={{2,0},{3,1},{0,2},{1,3},{6,4},{7,5},{4,6},{5,7},{10,8},{11,9},{8,1... | collective-permute-start | bytes 2752520 | tf_op jit(solution)/shard_map/ppermute | solution.py:54
  163.1 35.2 %collective-permute-start.26 = (bf16[2,64,3584]{2,1,0:T(8,128)(2,1)}, bf16[2,64,3584]{2,1,0:T(8,128)(2,1)}, u32[]{:S(2)}, u32[]{:S(2)}) collective-permute-start(bf16[2,64,3584]{2,1,0:T(8,128)(2,1)} %copy-done.15), channel_id=1, source_target_pairs={{16,0},{0,16},{17,1},{1,17},{18,2},{2,18},{19,3},{3,19},{20,4},{4,... | collective-permute-start | bytes 2752520 | tf_op jit(solution)/shard_map/ppermute | solution.py:59
  186.3 36.9 %collective-permute-start.29 = (bf16[2,64,3584]{2,1,0:T(8,128)(2,1)}, bf16[2,64,3584]{2,1,0:T(8,128)(2,1)S(1)}, u32[]{:S(2)}, u32[]{:S(2)}) collective-permute-start(bf16[2,64,3584]{2,1,0:T(8,128)(2,1)} %collective-permute-done.24.refs_2_), channel_id=1, source_target_pairs={{16,0},{0,16},{17,1},{1,17},{18,2},{2,18},{19,3},{3,19},{20,4},{4,... | collective-permute-start | bytes 2752520 | tf_op jit(solution)/shard_map/ppermute | solution.py:59
  187.6 30.9 %collective-permute-start.28 = (bf16[1600,512]{1,0:T(8,128)(2,1)}, bf16[1600,512]{1,0:T(8,128)(2,1)}, u32[]{:S(2)}, u32[]{:S(2)}) collective-permute-start(bf16[1600,512]{1,0:T(8,128)(2,1)} %weigh_rows.5.refs_2_.refs_3_.refs_0_), channel_id=1, source_target_pairs={{4,0},{12,8},{1,5},{9,13},{6,2},{14,10},{3,7},{11,15},{20,16},{28,... | collective-permute-start | bytes 4915208 | tf_op jit(solution)/shard_map/ppermute | solution.py:520
  221.8 28.0 %collective-permute-start.32 = (bf16[576,512]{1,0:T(8,128)(2,1)}, bf16[576,512]{1,0:T(8,128)(2,1)S(1)}, u32[]{:S(2)}, u32[]{:S(2)}) collective-permute-start(bf16[576,512]{1,0:T(8,128)(2,1)} %get-tuple-element.49.refs_3_.refs_2_), channel_id=1, source_target_pairs={{0,8},{5,13},{10,2},{15,7},{16,24},{21,29},{26,18},{31,23}} | collective-permute-start | bytes 1769480 | tf_op jit(solution)/shard_map/ppermute | solution.py:520
  222.5 31.3 %collective-permute-start.31 = (bf16[1024,512]{1,0:T(8,128)(2,1)}, bf16[1024,512]{1,0:T(8,128)(2,1)S(1)}, u32[]{:S(2)}, u32[]{:S(2)}) collective-permute-start(bf16[1024,512]{1,0:T(8,128)(2,1)} %get-tuple-element.48.refs_2_.refs_0_), channel_id=1, source_target_pairs={{8,0},{13,5},{2,10},{7,15},{24,16},{29,21},{18,26},{23,31}} | collective-permute-start | bytes 3145736 | tf_op jit(solution)/shard_map/ppermute | solution.py:520
  229.3 24.5 %collective-permute-start.30 = (bf16[384,1024]{1,0:T(8,128)(2,1)}, bf16[384,1024]{1,0:T(8,128)(2,1)S(1)}, u32[]{:S(2)}, u32[]{:S(2)}) collective-permute-start(bf16[384,1024]{1,0:T(8,128)(2,1)} %add_terms.6.refs_3_.refs_4_.refs_1_), channel_id=1, source_target_pairs={{0,8},{5,13},{10,2},{15,7},{16,24},{21,29},{26,18},{31,23}} | collective-permute-start | bytes 2359304 | tf_op jit(solution)/shard_map/ppermute | solution.py:520
  (44 other events, 572.5 us)

commit v9 on v8

--- a/solution.py
+++ b/solution.py
@@ -522,6 +522,15 @@
 
 def later_steps(values, owners):
     ranks = lax.axis_size("tensor")
+    if ranks == 4 and len(values) == 2:
+        one, two = hops(owners[0], 2), hops(owners[1], 2)
+        if all(not {x[i] for x in one} & {x[i] for x in two} for i in range(2)):
+            rank, group, place = (lax.axis_index(a) for a in ("tensor", "groups", "dp"))
+            target = jnp.asarray(owners[0], jnp.int32)[group, place]
+            height = max(v.shape[0] for v in values)
+            high = [jnp.pad(v, ((0, height - v.shape[0]), (0, 0))) for v in values]
+            got = send(jnp.where((rank ^ target) & 2 != 0, *high), sorted(one + two))
+            return [(v, got) for v in values]
     ends = []
     for value, owner in zip(values, owners):
         bit, got = 2, None
@@ -631,8 +640,8 @@
         got = [send(out, hops(b[0][0], 1)) for out, b in zip(outs, bundles)]
         return outs, got, bundles
 
-    def carry_on(work, after, price=2):
-        outs, got, bundles = work
+    def carry_on(works, after, price=2):
+        outs, got, bundles = ([v for work in works for v in work[i]] for i in range(3))
         heights = [[sum(u[0].shape[-2] for u in units) for _, units, _ in b] for b in bundles]
         sums = list(add(outs, got, heights, after, price))
         routes = [route for b in bundles for route in b]
@@ -687,21 +696,21 @@
     (out_parts,) = forward(
         5, chunks_of([4], others) + [(6, 0)], first_mine[0] + [early], [out_parts]
     )
-    first_theirs = terms(first_names, [theirs], [ticks[5]], 60, near=True)
-    sums_mine, end_mine = carry_on(first_mine, first_theirs[0])
-    forward(6, chunks_of([5], others) + [(7, 0)], first_theirs[0])
+    near_theirs = terms([], [theirs], [ticks[5]], 44, near=True)
+    sums_mine, end_mine = carry_on([first_mine], near_theirs[0])
+    far_theirs = terms(first_names, [theirs], sums_mine, 40)
+    forward(6, chunks_of([5], others) + [(7, 0)], far_theirs[0])
+    come = [fetched[n] for n in fetched if n[0] == 6 and n[2] > 0]
+    sums_theirs, end_theirs = carry_on([near_theirs, far_theirs], [ticks[6]] + come)
     second_names = chunks_of([5, 6, 7], [0]) + chunks_of([4, 5, 6], others)
-    near_received = [got for names, _, got in end_mine if names is None]
-    far_received = [got for names, _, got in end_mine if names is not None]
-    second = terms(second_names, [mine, theirs], [ticks[6]] + far_received, 40)
-    sums_theirs, end_theirs = carry_on(first_theirs, second[0] + near_received)
-
     last_names = chunks_of([7], others)
+    received = [got for _, _, got in end_mine]
+    second = terms(second_names, [mine, theirs], [ticks[6]] + sums_theirs + received, 40)
     come = [fetched[n] for n in fetched if (n[0], n[2]) in last_names]
-    sums_second, end_second = carry_on(second, sums_theirs + come)
+    come += [got for _, _, got in end_theirs]
+    sums_second, end_second = carry_on([second], come)
     last = terms(last_names, [mine, theirs], sums_second, 60)
-    far_received = [got for names, _, got in end_theirs if names is not None]
-    sums_last, end_last = carry_on(last, far_received, 8)
+    sums_last, end_last = carry_on([last], [], 8)
 
     (out_parts,), _ = share_rows(w_gate, w_up, group_word, [], [out_parts], sums_second)
     for bit in bits[-2::-1]:

time: 289 us -> 311 us (1.076)
  Pallas kernels: 143 us -> 149 us
  other arithmetic: 7.61 us -> 12.6 us
  starting transfers between devices: 77.3 us -> 82.2 us
  local copies, waits for them, and re-layouts: 10.2 us -> 14.5 us
    ppermute x10 -> x9, waiting for transfers between devices: 10.3 us -> 18.9 us  [send(): return lax.ppermute(value, ('groups', 'tensor', 'dp'), pairs)]
    ppermute x8, waiting for transfers between devices: 23.1 us -> 16.3 us  [from_group(): lax.ppermute(value, 'groups', [((i + shift) % size, i) for i in range(siz...]
    pallas_call x4 -> x5, Pallas kernels: 57.9 us -> 64.5 us  [weigh(): pl.pallas_call(kernel, grid=(steps,), out_shape=shapes, in_specs=specs +...]
    ppermute x10 -> x9, starting transfers between devices: 15.5 us -> 19.9 us  [send(): return lax.ppermute(value, ('groups', 'tensor', 'dp'), pairs)]
    select_n x0 -> x2, other arithmetic: none -> 4.22 us  [later_steps(): got = send(jnp.where((rank ^ target) & 2 != 0, *high), sorted(one + two))]
    unnamed x62 -> x66, local copies, waits for them, and re-layouts: 9.41 us -> 13.1 us
  transfers between devices with their start and end apart: 38 -> 37, of which waited for: 10 -> 9; matrix products, arithmetic and copies ran while one was open for 5% -> 6% of each run, Pallas kernels for 46% -> 44%
where the time goes in v9:
time: 311 us; the launch traced here: 310 us
  Pallas kernels  149 us (48%)
  starting transfers between devices  82.2 us (26%)
  waiting for transfers between devices  45.5 us (15%)
  local copies, waits for them, and re-layouts  14.5 us (5%)
  other arithmetic  12.6 us (4%)
  matrix products  4.07 us (1%)
    pallas_call x5, Pallas kernels, weigh(): pl.pallas_call(kernel, grid=(steps,), out_shape=shapes, in_specs=specs +...  64.5 us
    pallas_call x2, Pallas kernels, hidden_part(): pl.pallas_call(kernel, grid_spec=pltpu.PrefetchScalarGridSpec(num_scalar_...  35.4 us
    ppermute x3, starting transfers between devices, swap_cores(): return lax.ppermute(value, 'dp', [(i, i ^ 1) for i in range(size)])  24.3 us
    ppermute x9, starting transfers between devices, send(): return lax.ppermute(value, ('groups', 'tensor', 'dp'), pairs)  19.9 us
    ppermute x9, waiting for transfers between devices, send(): return lax.ppermute(value, ('groups', 'tensor', 'dp'), pairs)  18.9 us
    pallas_call x9, Pallas kernels, share_rows(): pl.pallas_call(kernel, grid_spec=pltpu.PrefetchScalarGridSpec(num_scalar_...  16.5 us
    ppermute x8, waiting for transfers between devices, from_group(): lax.ppermute(value, 'groups', [((i + shift) % size, i) for i in range(siz...  16.3 us
    ppermute x3, starting transfers between devices, spread_ranks(): lax.ppermute(below[-1], 'tensor', [(i, i + 1) for i in range(ranks - 1)])  14.1 us
  transfers between devices with their start and end apart: 37, of which 9 were waited for; matrix products, arithmetic and copies ran while one was open for 6% of the time, Pallas kernels for 44%

profile of v9, /device:TPU:3, one launch (start us, length us, event | category | flops | bytes accessed | tf_op | source)
XLA Modules:
  0.0 309.9 jit_solution(15529984485364920061)
XLA Ops:
  5.3 5.1 %collective-permute-start.3 = (bf16[1024,512]{1,0:T(8,128)(2,1)S(1)}, bf16[1024,512]{1,0:T(8,128)(2,1)}, u32[]{:S(2)}, u32[]{:S(2)}) collective-permute-start(bf16[1024,512]{1,0:T(8,128)(2,1)S(1)} %bitcast.34), channel_id=1, source_target_pairs={{0,4},{4,8},{8,12},{1,5},{5,9},{9,13},{2,6},{6,10},{10,14},{3,7},{... | collective-permute-start | bytes 3145736 | tf_op jit(solution)/shard_map/ppermute | solution.py:120
  11.7 12.0 %prepare.1 = (f32[2,3584,512]{2,1,0:T(8,128)}, f32[64,512]{1,0:T(8,128)}) custom-call(bf16[512,3584]{1,0:T(8,128)(2,1)} %gate_ref.1, bf16[512,3584]{1,0:T(8,128)(2,1)} %up_ref.1, bf16[64,3584]{1,0:T(8,128)(2,1)} %bitcast.43, bf16[2,64,3584]{2,1,0:T(8,128)(2,1)} %get-tuple-element.27.refs_0_), custom_call_target="tpu_custom_call" | custom-call | flops 3240000000 | bytes 1 | tf_op jit(solution)/shard_map/prepare/pallas_call | solution.py:147
  31.4 4.1 %collective-permute-start.7 = (bf16[1024,512]{1,0:T(8,128)(2,1)}, bf16[1024,512]{1,0:T(8,128)(2,1)S(1)}, u32[]{:S(2)}, u32[]{:S(2)}) collective-permute-start(bf16[1024,512]{1,0:T(8,128)(2,1)} %collective-permute-done.3.refs_3_), channel_id=1, source_target_pairs={{0,4},{4,8},{8,12},{1,5},{5,9},{9,13},{2,6},{6,10},{10,14},{3,7},{... | collective-permute-start | bytes 3145736 | tf_op jit(solution)/shard_map/ppermute | solution.py:120
  35.5 14.3 %hidden_part.2.refs_4_.refs_7_ = f32[3584,512]{1,0:T(8,128)} custom-call(s32[1]{0:T(128)} %bitcast.5.rank_ref, bf16[3584,4096]{1,0:T(8,128)(2,1)} %refs_1_.17, bf16[3584,4096]{1,0:T(8,128)(2,1)} %refs_1_.17, bf16[1024,512]{1,0:T(8,128)(2,1)} %bitcast.35, bf16[1024,512]{1,0:T(8,128)(2,1)} %collective-permute-done.3.refs_3_, ...), custom_call_target="tpu_custom_call" | custom-call | flops 3240000000 | bytes 1 | tf_op jit(solution)/shard_map/hidden_part/pallas_call | solution.py:272
  58.1 5.0 %collective-permute-start.11 = (bf16[1024,512]{1,0:T(8,128)(2,1)S(1)}, bf16[1024,512]{1,0:T(8,128)(2,1)}, u32[]{:S(2)}, u32[]{:S(2)}) collective-permute-start(bf16[1024,512]{1,0:T(8,128)(2,1)S(1)} %collective-permute-done.7.refs_4_.refs_2_), channel_id=1, source_target_pairs={{0,4},{4,8},{8,12},{1,5},{5,9},{9,13},{2,6},{6,10},{10,14},{3,7},{... | collective-permute-start | bytes 3145736 | tf_op jit(solution)/shard_map/ppermute | solution.py:120
  65.9 5.9 %collective-permute-done.6.refs_3_.refs_8_.refs_6_ = bf16[2,64,3584]{2,1,0:T(8,128)(2,1)S(1)} collective-permute-done((bf16[2,64,3584]{2,1,0:T(8,128)(2,1)}, bf16[2,64,3584]{2,1,0:T(8,128)(2,1)S(1)}, u32[]{:S(2)}, u32[]{:S(2)}) %collective-permute-start.6) | collective-permute-done | bytes 917536 | tf_op jit(solution)/shard_map/ppermute | solution.py:59
  77.0 6.6 %collective-permute-done.9.refs_2_ = bf16[2,64,3584]{2,1,0:T(8,128)(2,1)} collective-permute-done((bf16[2,64,3584]{2,1,0:T(8,128)(2,1)}, bf16[2,64,3584]{2,1,0:T(8,128)(2,1)}, u32[]{:S(2)}, u32[]{:S(2)}) %collective-permute-start.9) | collective-permute-done | bytes 917536 | tf_op jit(solution)/shard_map/ppermute | solution.py:54
  83.6 10.4 %collective-permute-done.10.refs_4_.refs_9_.refs_7_ = bf16[2,64,3584]{2,1,0:T(8,128)(2,1)S(1)} collective-permute-done((bf16[2,64,3584]{2,1,0:T(8,128)(2,1)}, bf16[2,64,3584]{2,1,0:T(8,128)(2,1)S(1)}, u32[]{:S(2)}, u32[]{:S(2)}) %collective-permute-start.10) | collective-permute-done | bytes 917536 | tf_op jit(solution)/shard_map/ppermute | solution.py:59
  100.2 21.1 %hidden_part.3 = (bf16[2,3584,512]{2,1,0:T(8,128)(2,1)}, f32[64,512]{1,0:T(8,128)}) custom-call(s32[1]{0:T(128)} %bitcast.5.rank_ref, bf16[3584,4096]{1,0:T(8,128)(2,1)} %refs_1_.17, bf16[3584,4096]{1,0:T(8,128)(2,1)} %refs_1_.17, bf16[1024,512]{1,0:T(8,128)(2,1)} %copy-done.4, bf16[1024,512]{1,0:T(8,128)(2,1)} %collective-permute-done.11.refs_5_.refs_3_, ...), custom_call_target="tpu_custom_call" | custom-call | flops 3240000000 | bytes 1 | tf_op jit(solution)/shard_map/hidden_part/pallas_call | solution.py:272
  125.9 4.4 %collective-permute-start.18 = (bf16[2,3584,512]{2,1,0:T(8,128)(2,1)}, bf16[2,3584,512]{2,1,0:T(8,128)(2,1)}, u32[]{:S(2)}, u32[]{:S(2)}) collective-permute-start(bf16[2,3584,512]{2,1,0:T(8,128)(2,1)} %get-tuple-element.41.refs_11_.refs_6_.refs_1_), channel_id=1, source_target_pairs={{0,1},{1,0},{2,3},{3,2},{4,5},{5,4},{6,7},{7,6},{8,9},{9,8},{10,11... | collective-permute-start | bytes 22020104 | tf_op jit(solution)/shard_map/ppermute | solution.py:48
  136.6 18.3 %weigh_rows.5.refs_6_.refs_0_ = bf16[1600,512]{1,0:T(8,128)(2,1)} custom-call(bf16[1024,3584]{1,0:T(8,128)(2,1)} %refs_0_.21, bf16[1024,3584]{1,0:T(8,128)(2,1)} %refs_1_.21, bf16[2,64,3584]{2,1,0:T(8,128)(2,1)} %get-tuple-element.29.refs_2_.refs_0_, bf16[2,64,3584]{2,1,0:T(8,128)(2,1)} %get-tuple-element.32.refs_3_.refs_1_, ...), custom_call_target="tpu_custom_call" | custom-call | flops 8640000000 | bytes 1 | tf_op jit(solution)/shard_map/weigh_rows/pallas_call | solution.py:349
  154.9 3.5 %collective-permute-start.17 = (bf16[1600,512]{1,0:T(8,128)(2,1)}, bf16[1600,512]{1,0:T(8,128)(2,1)}, u32[]{:S(2)}, u32[]{:S(2)}) collective-permute-start(bf16[1600,512]{1,0:T(8,128)(2,1)} %weigh_rows.5.refs_6_.refs_0_), channel_id=1, source_target_pairs={{4,0},{12,8},{1,5},{9,13},{6,2},{14,10},{3,7},{11,15},{20,16},{28,... | collective-permute-start | bytes 4915208 | tf_op jit(solution)/shard_map/ppermute | solution.py:520
  165.7 13.8 %weigh_rows.6.refs_2_.refs_0_ = bf16[1024,512]{1,0:T(8,128)(2,1)} custom-call(bf16[1024,3584]{1,0:T(8,128)(2,1)} %refs_0_.21, bf16[1024,3584]{1,0:T(8,128)(2,1)} %refs_1_.21, bf16[2,3584,512]{2,1,0:T(8,128)(2,1)} %collective-permute-done.18.refs_2_.refs_9_.refs_7_, bf16[2,64,3584]{2,1,0:T(8,128)(2,1)} %get-tuple-element.45.refs_3_), custom_call_target="tpu_custom_call" | custom-call | flops 11880000512 | bytes 1 | tf_op jit(solution)/shard_map/weigh_rows/pallas_call | solution.py:349
  180.9 3.4 %add_terms.4 = (bf16[1024,512]{1,0:T(8,128)(2,1)}, bf16[576,512]{1,0:T(8,128)(2,1)}) custom-call(bf16[1600,512]{1,0:T(8,128)(2,1)} %weigh_rows.5.refs_6_.refs_0_, bf16[1600,512]{1,0:T(8,128)(2,1)} %collective-permute-done.17.refs_1_, bf16[1024,512]{1,0:T(8,128)(2,1)} %weigh_rows.6.refs_2_.refs_0_), custom_call_target="tpu_custom_call" | custom-call | flops 540000000 | bytes 1 | tf_op jit(solution)/shard_map/add_terms/pallas_call | solution.py:379
  187.7 10.8 %weigh_rows.7.refs_3_.refs_1_ = bf16[576,512]{1,0:T(8,128)(2,1)} custom-call(bf16[2,64,3584]{2,1,0:T(8,128)(2,1)} %get-tuple-element.29.refs_2_.refs_0_, bf16[2,64,3584]{2,1,0:T(8,128)(2,1)} %get-tuple-element.32.refs_3_.refs_1_, bf16[2,64,3584]{2,1,0:T(8,128)(2,1)} %get-tuple-element.34.refs_4_.refs_2_, ...), custom_call_target="tpu_custom_call" | custom-call | flops 10800000000 | bytes 1 | tf_op jit(solution)/shard_map/weigh_rows/pallas_call | solution.py:349
  201.9 8.6 %collective-permute-done.27.refs_3_ = bf16[576,512]{1,0:T(8,128)(2,1)S(1)} collective-permute-done((bf16[576,512]{1,0:T(8,128)(2,1)}, bf16[576,512]{1,0:T(8,128)(2,1)S(1)}, u32[]{:S(2)}, u32[]{:S(2)}) %collective-permute-start.27) | collective-permute-done | bytes 589856 | tf_op jit(solution)/shard_map/ppermute | solution.py:520
  212.2 3.4 %add_terms.5 = (bf16[1024,512]{1,0:T(8,128)(2,1)}, bf16[576,512]{1,0:T(8,128)(2,1)}) custom-call(bf16[1024,512]{1,0:T(8,128)(2,1)} %weigh_rows.6.refs_2_.refs_0_, bf16[576,512]{1,0:T(8,128)(2,1)} %weigh_rows.7.refs_3_.refs_1_, bf16[1024,512]{1,0:T(8,128)(2,1)} %copy-done.20, bf16[576,512]{1,0:T(8,128)(2,1)} %copy-done.25, ...), custom_call_target="tpu_custom_call" | custom-call | flops 540000000 | bytes 1 | tf_op jit(solution)/shard_map/add_terms/pallas_call | solution.py:379
  218.9 12.5 %weigh_rows.8.refs_0_ = bf16[384,1024]{1,0:T(8,128)(2,1)} custom-call(bf16[2,64,3584]{2,1,0:T(8,128)(2,1)} %copy-done.12, bf16[2,64,3584]{2,1,0:T(8,128)(2,1)} %copy-done.10, bf16[2,64,3584]{2,1,0:T(8,128)(2,1)} %collective-permute-done.23.refs_2_, bf16[2,64,3584]{2,1,0:T(8,128)(2,1)} %copy-done.23, ...), custom_call_target="tpu_custom_call" | custom-call | flops 10800000000 | bytes 1 | tf_op jit(solution)/shard_map/weigh_rows/pallas_call | solution.py:349
  231.4 8.7 %collective-permute-start.28 = (bf16[384,1024]{1,0:T(8,128)(2,1)}, bf16[384,1024]{1,0:T(8,128)(2,1)S(1)}, u32[]{:S(2)}, u32[]{:S(2)}) collective-permute-start(bf16[384,1024]{1,0:T(8,128)(2,1)} %weigh_rows.8.refs_0_), channel_id=1, source_target_pairs={{4,0},{12,8},{1,5},{9,13},{6,2},{14,10},{3,7},{11,15},{20,16},{28,... | collective-permute-start | bytes 2359304 | tf_op jit(solution)/shard_map/ppermute | solution.py:520
  241.2 8.2 %collective-permute-done.28.refs_1_ = bf16[384,1024]{1,0:T(8,128)(2,1)S(1)} collective-permute-done((bf16[384,1024]{1,0:T(8,128)(2,1)}, bf16[384,1024]{1,0:T(8,128)(2,1)S(1)}, u32[]{:S(2)}, u32[]{:S(2)}) %collective-permute-start.28) | collective-permute-done | bytes 786464 | tf_op jit(solution)/shard_map/ppermute | solution.py:520
  258.4 9.2 %weigh_rows.9.refs_0_ = bf16[64,1024]{1,0:T(8,128)(2,1)} custom-call(bf16[2,64,3584]{2,1,0:T(8,128)(2,1)} %collective-permute-done.29.refs_2_.refs_0_, bf16[2,3584,512]{2,1,0:T(8,128)(2,1)} %get-tuple-element.41.refs_11_.refs_6_.refs_1_, bf16[2,3584,512]{2,1,0:T(8,128)(2,1)} %collective-permute-done.18.refs_2_.refs_9_.refs_7_, ...), custom_call_target="tpu_custom_call" | custom-call | flops 16200000512 | bytes 1 | tf_op jit(solution)/shard_map/weigh_rows/pallas_call | solution.py:349
  276.3 3.4 %assemble.2.refs_5_ = bf16[1024,512]{1,0:T(8,128)(2,1)} custom-call(s32[4]{0:T(128)} %pad_add_fusion.words_ref, bf16[1024,512]{1,0:T(8,128)(2,1)} %get-tuple-element.48.refs_9_.refs_0_, bf16[1024,512]{1,0:T(8,128)(2,1)} %copy-done.2, bf16[576,512]{1,0:T(8,128)(2,1)} %get-tuple-element.49.refs_10_.refs_2_, bf16[384,1024]{1,0:T(8,128)(2,1)} %add_terms.6.refs_3_.refs_1_, ...), custom_call_target="tpu_custom_call" | custom-call | flops 1350000000 | bytes 1 | tf_op jit(solution)/shard_map/assemble/pallas_call | solution.py:441
  279.7 19.9 %collective-permute-start.34 = (bf16[1024,512]{1,0:T(8,128)(2,1)}, bf16[1024,512]{1,0:T(8,128)(2,1)S(1)}, u32[]{:S(2)}, u32[]{:S(2)}) collective-permute-start(bf16[1024,512]{1,0:T(8,128)(2,1)} %assemble.2.refs_5_), channel_id=1, source_target_pairs={{0,1},{1,0},{2,3},{3,2},{4,5},{5,4},{6,7},{7,6},{8,9},{9,8},{10,11... | collective-permute-start | bytes 3145736 | tf_op jit(solution)/shard_map/ppermute | solution.py:48
  302.5 3.4 %assemble.3.mine_ref = bf16[1024,512]{1,0:T(8,128)(2,1)} custom-call(s32[4]{0:T(128)} %pad_add_fusion.words_ref, bf16[1024,512]{1,0:T(8,128)(2,1)} %get-tuple-element.46.refs_10_.refs_0_, bf16[1024,512]{1,0:T(8,128)(2,1)} %copy-done.19, bf16[576,512]{1,0:T(8,128)(2,1)} %get-tuple-element.47.refs_11_.refs_2_, bf16[384,1024]{1,0:T(8,128)(2,1)} %add_terms.6.refs_3_.refs_1_, ...), custom_call_target="tpu_custom_call" | custom-call | flops 1350000000 | bytes 1 | tf_op jit(solution)/shard_map/assemble/pallas_call | solution.py:441
  (167 shorter events, 92.2 us)
Async XLA Ops:
  4.0 26.1 %collective-permute-start.4 = (bf16[1024,512]{1,0:T(8,128)(2,1)S(1)}, bf16[1024,512]{1,0:T(8,128)(2,1)}, u32[]{:S(2)}, u32[]{:S(2)}) collective-permute-start(bf16[1024,512]{1,0:T(8,128)(2,1)S(1)} %bitcast.33), channel_id=1, source_target_pairs={{4,0},{8,4},{12,8},{5,1},{9,5},{13,9},{6,2},{10,6},{14,10},{7,3},{... | collective-permute-start | bytes 3145736 | tf_op jit(solution)/shard_map/ppermute | solution.py:121
  5.3 26.1 %collective-permute-start.3 = (bf16[1024,512]{1,0:T(8,128)(2,1)S(1)}, bf16[1024,512]{1,0:T(8,128)(2,1)}, u32[]{:S(2)}, u32[]{:S(2)}) collective-permute-start(bf16[1024,512]{1,0:T(8,128)(2,1)S(1)} %bitcast.34), channel_id=1, source_target_pairs={{0,4},{4,8},{8,12},{1,5},{5,9},{9,13},{2,6},{6,10},{10,14},{3,7},{... | collective-permute-start | bytes 3145736 | tf_op jit(solution)/shard_map/ppermute | solution.py:120
  10.3 39.5 %collective-permute-start.1 = (bf16[2,64,3584]{2,1,0:T(8,128)(2,1)}, bf16[2,64,3584]{2,1,0:T(8,128)(2,1)}, u32[]{:S(2)}, u32[]{:S(2)}) collective-permute-start(bf16[2,64,3584]{2,1,0:T(8,128)(2,1)} %get-tuple-element.30), channel_id=1, source_target_pairs={{2,0},{3,1},{0,2},{1,3},{6,4},{7,5},{4,6},{5,7},{10,8},{11,9},{8,1... | collective-permute-start | bytes 2752520 | tf_op jit(solution)/shard_map/ppermute | solution.py:54
  28.3 37.7 %collective-permute-start.5 = (bf16[2,64,3584]{2,1,0:T(8,128)(2,1)}, bf16[2,64,3584]{2,1,0:T(8,128)(2,1)}, u32[]{:S(2)}, u32[]{:S(2)}) collective-permute-start(bf16[2,64,3584]{2,1,0:T(8,128)(2,1)} %get-tuple-element.31.refs_5_), channel_id=1, source_target_pairs={{2,0},{3,1},{0,2},{1,3},{6,4},{7,5},{4,6},{5,7},{10,8},{11,9},{8,1... | collective-permute-start | bytes 2752520 | tf_op jit(solution)/shard_map/ppermute | solution.py:54
  30.1 26.7 %collective-permute-start.8 = (bf16[1024,512]{1,0:T(8,128)(2,1)}, bf16[1024,512]{1,0:T(8,128)(2,1)S(1)}, u32[]{:S(2)}, u32[]{:S(2)}) collective-permute-start(bf16[1024,512]{1,0:T(8,128)(2,1)} %collective-permute-done.4.refs_4_), channel_id=1, source_target_pairs={{4,0},{8,4},{12,8},{5,1},{9,5},{13,9},{6,2},{10,6},{14,10},{7,3},{... | collective-permute-start | bytes 3145736 | tf_op jit(solution)/shard_map/ppermute | solution.py:121
  31.4 26.7 %collective-permute-start.7 = (bf16[1024,512]{1,0:T(8,128)(2,1)}, bf16[1024,512]{1,0:T(8,128)(2,1)S(1)}, u32[]{:S(2)}, u32[]{:S(2)}) collective-permute-start(bf16[1024,512]{1,0:T(8,128)(2,1)} %collective-permute-done.3.refs_3_), channel_id=1, source_target_pairs={{0,4},{4,8},{8,12},{1,5},{5,9},{9,13},{2,6},{6,10},{10,14},{3,7},{... | collective-permute-start | bytes 3145736 | tf_op jit(solution)/shard_map/ppermute | solution.py:120
  56.8 26.8 %collective-permute-start.12 = (bf16[1024,512]{1,0:T(8,128)(2,1)S(1)}, bf16[1024,512]{1,0:T(8,128)(2,1)S(1)}, u32[]{:S(2)}, u32[]{:S(2)}) collective-permute-start(bf16[1024,512]{1,0:T(8,128)(2,1)S(1)} %collective-permute-done.8.refs_5_), channel_id=1, source_target_pairs={{4,0},{8,4},{12,8},{5,1},{9,5},{13,9},{6,2},{10,6},{14,10},{7,3},{... | collective-permute-start | bytes 3145736 | tf_op jit(solution)/shard_map/ppermute | solution.py:121
  58.1 25.5 %collective-permute-start.11 = (bf16[1024,512]{1,0:T(8,128)(2,1)S(1)}, bf16[1024,512]{1,0:T(8,128)(2,1)}, u32[]{:S(2)}, u32[]{:S(2)}) collective-permute-start(bf16[1024,512]{1,0:T(8,128)(2,1)S(1)} %collective-permute-done.7.refs_4_.refs_2_), channel_id=1, source_target_pairs={{0,4},{4,8},{8,12},{1,5},{5,9},{9,13},{2,6},{6,10},{10,14},{3,7},{... | collective-permute-start | bytes 3145736 | tf_op jit(solution)/shard_map/ppermute | solution.py:120
  75.8 46.2 %collective-permute-start.13 = (bf16[2,64,3584]{2,1,0:T(8,128)(2,1)}, bf16[2,64,3584]{2,1,0:T(8,128)(2,1)}, u32[]{:S(2)}, u32[]{:S(2)}) collective-permute-start(bf16[2,64,3584]{2,1,0:T(8,128)(2,1)} %get-tuple-element.37), channel_id=1, source_target_pairs={{2,0},{3,1},{0,2},{1,3},{6,4},{7,5},{4,6},{5,7},{10,8},{11,9},{8,1... | collective-permute-start | bytes 2752520 | tf_op jit(solution)/shard_map/ppermute | solution.py:54
  97.0 25.0 %collective-permute-start.14 = (bf16[2,64,3584]{2,1,0:T(8,128)(2,1)}, bf16[2,64,3584]{2,1,0:T(8,128)(2,1)S(1)}, u32[]{:S(2)}, u32[]{:S(2)}) collective-permute-start(bf16[2,64,3584]{2,1,0:T(8,128)(2,1)} %get-tuple-element.36.refs_5_.refs_3_), channel_id=1, source_target_pairs={{16,0},{0,16},{17,1},{1,17},{18,2},{2,18},{19,3},{3,19},{20,4},{4,... | collective-permute-start | bytes 2752520 | tf_op jit(solution)/shard_map/ppermute | solution.py:59
  97.7 25.1 %collective-permute-start.16 = (bf16[2,64,3584]{2,1,0:T(8,128)(2,1)}, bf16[2,64,3584]{2,1,0:T(8,128)(2,1)S(1)}, u32[]{:S(2)}, u32[]{:S(2)}) collective-permute-start(bf16[2,64,3584]{2,1,0:T(8,128)(2,1)} %get-tuple-element.38.refs_10_), channel_id=1, source_target_pairs={{2,0},{3,1},{0,2},{1,3},{6,4},{7,5},{4,6},{5,7},{10,8},{11,9},{8,1... | collective-permute-start | bytes 2752520 | tf_op jit(solution)/shard_map/ppermute | solution.py:54
  125.9 39.8 %collective-permute-start.18 = (bf16[2,3584,512]{2,1,0:T(8,128)(2,1)}, bf16[2,3584,512]{2,1,0:T(8,128)(2,1)}, u32[]{:S(2)}, u32[]{:S(2)}) collective-permute-start(bf16[2,3584,512]{2,1,0:T(8,128)(2,1)} %get-tuple-element.41.refs_11_.refs_6_.refs_1_), channel_id=1, source_target_pairs={{0,1},{1,0},{2,3},{3,2},{4,5},{5,4},{6,7},{7,6},{8,9},{9,8},{10,11... | collective-permute-start | bytes 22020104 | tf_op jit(solution)/shard_map/ppermute | solution.py:48
  131.5 29.6 %collective-permute-start.20 = (bf16[2,64,3584]{2,1,0:T(8,128)(2,1)}, bf16[2,64,3584]{2,1,0:T(8,128)(2,1)S(1)}, u32[]{:S(2)}, u32[]{:S(2)}) collective-permute-start(bf16[2,64,3584]{2,1,0:T(8,128)(2,1)} %collective-permute-done.13.refs_5_.refs_6_.refs_4_), channel_id=1, source_target_pairs={{16,0},{0,16},{17,1},{1,17},{18,2},{2,18},{19,3},{3,19},{20,4},{4,... | collective-permute-start | bytes 2752520 | tf_op jit(solution)/shard_map/ppermute | solution.py:59
  133.6 24.8 %collective-permute-start.19 = (f32[192,512]{1,0:T(8,128)}, f32[192,512]{1,0:T(8,128)S(1)}, u32[]{:S(2)}, u32[]{:S(2)}) collective-permute-start(f32[192,512]{1,0:T(8,128)} %pad_maximum_fusion), channel_id=1, source_target_pairs={{0,8},{4,12},{8,0},{12,4},{1,9},{5,13},{9,1},{13,5},{2,10},{6,14},... | collective-permute-start | bytes 1179656 | tf_op jit(solution)/shard_map/ppermute | solution.py:496
  135.4 25.7 %collective-permute-start.21 = (bf16[2,64,3584]{2,1,0:T(8,128)(2,1)}, bf16[2,64,3584]{2,1,0:T(8,128)(2,1)S(1)}, u32[]{:S(2)}, u32[]{:S(2)}) collective-permute-start(bf16[2,64,3584]{2,1,0:T(8,128)(2,1)} %get-tuple-element.42.refs_12_), channel_id=1, source_target_pairs={{2,0},{3,1},{0,2},{1,3},{6,4},{7,5},{4,6},{5,7},{10,8},{11,9},{8,1... | collective-permute-start | bytes 2752520 | tf_op jit(solution)/shard_map/ppermute | solution.py:54
  154.9 26.0 %collective-permute-start.17 = (bf16[1600,512]{1,0:T(8,128)(2,1)}, bf16[1600,512]{1,0:T(8,128)(2,1)}, u32[]{:S(2)}, u32[]{:S(2)}) collective-permute-start(bf16[1600,512]{1,0:T(8,128)(2,1)} %weigh_rows.5.refs_6_.refs_0_), channel_id=1, source_target_pairs={{4,0},{12,8},{1,5},{9,13},{6,2},{14,10},{3,7},{11,15},{20,16},{28,... | collective-permute-start | bytes 4915208 | tf_op jit(solution)/shard_map/ppermute | solution.py:520
  158.4 40.0 %collective-permute-start.24 = (bf16[2,64,3584]{2,1,0:T(8,128)(2,1)S(1)}, bf16[2,64,3584]{2,1,0:T(8,128)(2,1)}, u32[]{:S(2)}, u32[]{:S(2)}) collective-permute-start(bf16[2,64,3584]{2,1,0:T(8,128)(2,1)S(1)} %copy-done.13), channel_id=1, source_target_pairs={{16,0},{0,16},{17,1},{1,17},{18,2},{2,18},{19,3},{3,19},{20,4},{4,... | collective-permute-start | bytes 2752520 | tf_op jit(solution)/shard_map/ppermute | solution.py:59
  164.4 35.6 %collective-permute-start.23 = (bf16[2,64,3584]{2,1,0:T(8,128)(2,1)}, bf16[2,64,3584]{2,1,0:T(8,128)(2,1)}, u32[]{:S(2)}, u32[]{:S(2)}) collective-permute-start(bf16[2,64,3584]{2,1,0:T(8,128)(2,1)} %get-tuple-element.45.refs_3_), channel_id=1, source_target_pairs={{2,0},{3,1},{0,2},{1,3},{6,4},{7,5},{4,6},{5,7},{10,8},{11,9},{8,1... | collective-permute-start | bytes 2752520 | tf_op jit(solution)/shard_map/ppermute | solution.py:54
  165.5 36.4 %collective-permute-start.25 = (bf16[2,64,3584]{2,1,0:T(8,128)(2,1)}, bf16[2,64,3584]{2,1,0:T(8,128)(2,1)S(1)}, u32[]{:S(2)}, u32[]{:S(2)}) collective-permute-start(bf16[2,64,3584]{2,1,0:T(8,128)(2,1)} %copy-done.10), channel_id=1, source_target_pairs={{16,0},{0,16},{17,1},{1,17},{18,2},{2,18},{19,3},{3,19},{20,4},{4,... | collective-permute-start | bytes 2752520 | tf_op jit(solution)/shard_map/ppermute | solution.py:59
  179.5 30.9 %collective-permute-start.26 = (bf16[1024,512]{1,0:T(8,128)(2,1)}, bf16[1024,512]{1,0:T(8,128)(2,1)S(1)}, u32[]{:S(2)}, u32[]{:S(2)}) collective-permute-start(bf16[1024,512]{1,0:T(8,128)(2,1)} %weigh_rows.6.refs_2_.refs_0_), channel_id=1, source_target_pairs={{4,0},{12,8},{1,5},{9,13},{6,2},{14,10},{3,7},{11,15},{20,16},{28,... | collective-permute-start | bytes 3145736 | tf_op jit(solution)/shard_map/ppermute | solution.py:520
  186.9 31.0 %collective-permute-start.22 = (bf16[1024,512]{1,0:T(8,128)(2,1)}, bf16[1024,512]{1,0:T(8,128)(2,1)S(1)}, u32[]{:S(2)}, u32[]{:S(2)}) collective-permute-start(bf16[1024,512]{1,0:T(8,128)(2,1)} %pad_select_fusion.1), channel_id=1, source_target_pairs={{0,8},{2,10},{5,13},{7,15},{8,0},{10,2},{13,5},{15,7},{16,24},{18,... | collective-permute-start | bytes 3145736 | tf_op jit(solution)/shard_map/ppermute | solution.py:520
  200.0 41.2 %collective-permute-start.29 = (bf16[2,64,3584]{2,1,0:T(8,128)(2,1)}, bf16[2,64,3584]{2,1,0:T(8,128)(2,1)}, u32[]{:S(2)}, u32[]{:S(2)}) collective-permute-start(bf16[2,64,3584]{2,1,0:T(8,128)(2,1)} %collective-permute-done.23.refs_2_), channel_id=1, source_target_pairs={{16,0},{0,16},{17,1},{1,17},{18,2},{2,18},{19,3},{3,19},{20,4},{4,... | collective-permute-start | bytes 2752520 | tf_op jit(solution)/shard_map/ppermute | solution.py:59
  217.2 32.1 %collective-permute-start.30 = (bf16[1024,512]{1,0:T(8,128)(2,1)S(1)}, bf16[1024,512]{1,0:T(8,128)(2,1)S(1)}, u32[]{:S(2)}, u32[]{:S(2)}) collective-permute-start(bf16[1024,512]{1,0:T(8,128)(2,1)S(1)} %pad_select_fusion), channel_id=1, source_target_pairs={{0,8},{2,10},{5,13},{7,15},{8,0},{10,2},{13,5},{15,7},{16,24},{18,... | collective-permute-start | bytes 3145736 | tf_op jit(solution)/shard_map/ppermute | solution.py:520
  279.7 26.2 %collective-permute-start.34 = (bf16[1024,512]{1,0:T(8,128)(2,1)}, bf16[1024,512]{1,0:T(8,128)(2,1)S(1)}, u32[]{:S(2)}, u32[]{:S(2)}) collective-permute-start(bf16[1024,512]{1,0:T(8,128)(2,1)} %assemble.2.refs_5_), channel_id=1, source_target_pairs={{0,1},{1,0},{2,3},{3,2},{4,5},{5,4},{6,7},{7,6},{8,9},{9,8},{10,11... | collective-permute-start | bytes 3145736 | tf_op jit(solution)/shard_map/ppermute | solution.py:48
  (45 other events, 503.6 us)

commit v10 on v9

--- a/solution.py
+++ b/solution.py
@@ -493,7 +493,8 @@
 
 def exchange(value, bit):
     ranks = lax.axis_size("tensor")
-    return lax.ppermute(value, "tensor", [(i, i ^ bit) for i in range(ranks)])
+    got = lax.ppermute(value.astype(jnp.bfloat16), "tensor", [(i, i ^ bit) for i in range(ranks)])
+    return got.astype(jnp.float32)
 
 
 def halve(value, bit):
@@ -520,9 +521,9 @@
     return lax.ppermute(value, ("groups", "tensor", "dp"), pairs)
 
 
-def later_steps(values, owners):
+def later_steps(values, owners, at_once):
     ranks = lax.axis_size("tensor")
-    if ranks == 4 and len(values) == 2:
+    if at_once and ranks == 4 and len(values) == 2:
         one, two = hops(owners[0], 2), hops(owners[1], 2)
         if all(not {x[i] for x in one} & {x[i] for x in two} for i in range(2)):
             rank, group, place = (lax.axis_index(a) for a in ("tensor", "groups", "dp"))
@@ -640,12 +641,12 @@
         got = [send(out, hops(b[0][0], 1)) for out, b in zip(outs, bundles)]
         return outs, got, bundles
 
-    def carry_on(works, after, price=2):
+    def carry_on(works, after, price=2, at_once=False):
         outs, got, bundles = ([v for work in works for v in work[i]] for i in range(3))
         heights = [[sum(u[0].shape[-2] for u in units) for _, units, _ in b] for b in bundles]
         sums = list(add(outs, got, heights, after, price))
         routes = [route for b in bundles for route in b]
-        ends = later_steps(sums, [table for table, _, _ in routes])
+        ends = later_steps(sums, [table for table, _, _ in routes], at_once)
         return sums, [(names, *end) for (_, _, names), end in zip(routes, ends)]
 
     fetch(0)
@@ -668,14 +669,18 @@
     hold_arrived(0, [], [slopes])
     so_far = hidden_part(rank_word, below, above, w_down, None, None, None, [ticks[0]])
     hold_arrived(1, chunks_of([0], others), [so_far])
-    hold_arrived(2, chunks_of([1], others), [below[2], above[1], early_part, out_down_part])
-    (early,) = hold_arrived(3, chunks_of([2], others), below[3:] + above[2:], [early_part])
+    hold_arrived(2, chunks_of([1], others), [below[2], above[1], out_down_part, early_part])
     mine, up_out_part = hidden_part(
-        rank_word, below, above, w_down, so_far, slopes, proj_u.T, [ticks[3]]
-    )
+        rank_word, below, above, w_down, so_far, slopes, proj_u.T, [ticks[2]]
+    )
+    mine, early = forward(3, chunks_of([2, 3], others) + [(4, 0)], [], [mine, early_part])
+    theirs = swap_cores(mine)
     early = early + exchange(early, bits[0])
-    mine, early = forward(4, chunks_of([3], others) + [(5, 0)], [], [mine, early])
-    theirs = swap_cores(mine)
+    first_names = chunks_of(range(5), [0]) + chunks_of(range(4), others)
+    near_mine = terms([], [mine], [ticks[3]], 24, near=True)
+    early, up_out_part = forward(
+        4, chunks_of([4], others) + [(5, 0)], near_mine[0], [early, up_out_part]
+    )
 
     out_parts = jnp.stack([up_out_part, out_down_part]).reshape(2, ranks, -1, count)
     out_parts = out_parts.transpose(1, 0, 2, 3).reshape(-1, count)
@@ -691,28 +696,30 @@
     for bit in bits[1:-1]:
         early = early + exchange(early, bit)
 
-    first_names = chunks_of(range(5), [0]) + chunks_of(range(4), others)
-    first_mine = terms(first_names, [mine], [ticks[4]], 32, near=True)
+    far_mine = terms(first_names, [mine], [ticks[4]], 6)
+    near_theirs = terms([], [theirs], far_mine[0] + [early], 11, near=True)
+    held = forward(
+        5, chunks_of([5], others), near_theirs[0], [fetched[6, s, 0] for s in range(1, chips)]
+    )
+    for s, value in enumerate(held, 1):
+        fetched[6, s, 0] = value
+        for r in range(1, groups):
+            fetched[6, s, r] = from_group(value, r)
+    sums_mine, end_mine = carry_on([near_mine, far_mine], near_theirs[0], at_once=True)
+    far_theirs = terms(first_names, [theirs], [ticks[5]] + sums_mine, 16)
     (out_parts,) = forward(
-        5, chunks_of([4], others) + [(6, 0)], first_mine[0] + [early], [out_parts]
-    )
-    near_theirs = terms([], [theirs], [ticks[5]], 44, near=True)
-    sums_mine, end_mine = carry_on([first_mine], near_theirs[0])
-    far_theirs = terms(first_names, [theirs], sums_mine, 40)
-    forward(6, chunks_of([5], others) + [(7, 0)], far_theirs[0])
-    come = [fetched[n] for n in fetched if n[0] == 6 and n[2] > 0]
-    sums_theirs, end_theirs = carry_on([near_theirs, far_theirs], [ticks[6]] + come)
-    second_names = chunks_of([5, 6, 7], [0]) + chunks_of([4, 5, 6], others)
-    last_names = chunks_of([7], others)
+        6, chunks_of([6], others) + [(7, 0)], far_theirs[0], [out_parts]
+    )
+    second_names = chunks_of([5, 6], [0]) + chunks_of([4, 5], others)
+    last_names = chunks_of([7], [0]) + chunks_of([6, 7], others)
+    second = terms(second_names, [mine, theirs], [ticks[6]], 9)
     received = [got for _, _, got in end_mine]
-    second = terms(second_names, [mine, theirs], [ticks[6]] + sums_theirs + received, 40)
-    come = [fetched[n] for n in fetched if (n[0], n[2]) in last_names]
-    come += [got for _, _, got in end_theirs]
-    sums_second, end_second = carry_on([second], come)
+    sums_theirs, end_theirs = carry_on([near_theirs, far_theirs], second[0] + received)
+    sums_second, end_second = carry_on([second], sums_theirs)
     last = terms(last_names, [mine, theirs], sums_second, 60)
-    sums_last, end_last = carry_on([last], [], 8)
-
-    (out_parts,), _ = share_rows(w_gate, w_up, group_word, [], [out_parts], sums_second)
+    received = [got for names, _, got in end_theirs + end_second if names is not None]
+    sums_last, end_last = carry_on([last], received, 2)
+
     for bit in bits[-2::-1]:
         out_parts = halve(out_parts, bit)
     early = early.astype(jnp.bfloat16)

time: 311 us -> 303 us (0.974)
  waiting for transfers between devices: 45.5 us -> 29.6 us
  Pallas kernels: 149 us -> 154 us
  starting transfers between devices: 82.2 us -> 86.8 us
    ppermute x9 -> x11, waiting for transfers between devices: 18.9 us -> 4.94 us  [send(): return lax.ppermute(value, ('groups', 'tensor', 'dp'), pairs)]
    ppermute x9 -> x11, starting transfers between devices: 19.9 us -> 28.9 us  [send(): return lax.ppermute(value, ('groups', 'tensor', 'dp'), pairs)]
    pallas_call x5 -> x6, Pallas kernels: 64.5 us -> 70.3 us  [weigh(): pl.pallas_call(kernel, grid=(steps,), out_shape=shapes, in_specs=specs +...]
    ppermute x8, waiting for transfers between devices: 8.72 us -> 4.54 us  [from_chip(): lax.ppermute(value, 'dp', [((i + step) % size, i) for i in range(size)])]
    select_n x2 -> x1, other arithmetic: 4.22 us -> 0.24 us  [later_steps(): got = send(jnp.where((rank ^ target) & 2 != 0, *high), sorted(one + two))]
    unnamed x66 -> x74, local copies, waits for them, and re-layouts: 13.1 us -> 14.4 us
    pallas_call x9 -> x8, Pallas kernels: 16.5 us -> 16 us  [share_rows(): pl.pallas_call(kernel, grid_spec=pltpu.PrefetchScalarGridSpec(num_scalar_...]
  transfers between devices with their start and end apart: 37 -> 39, of which waited for: 9 -> 6; matrix products, arithmetic and copies ran while one was open for 6% -> 6% of each run, Pallas kernels for 44% -> 47%
where the time goes in v10:
time: 303 us; the launch traced here: 302 us
  Pallas kernels  154 us (51%)
  starting transfers between devices  86.8 us (29%)
  waiting for transfers between devices  29.6 us (10%)
  local copies, waits for them, and re-layouts  15.9 us (5%)
  other arithmetic  10.1 us (3%)
  matrix products  3.1 us (1%)
    pallas_call x6, Pallas kernels, weigh(): pl.pallas_call(kernel, grid=(steps,), out_shape=shapes, in_specs=specs +...  70.3 us
    pallas_call x2, Pallas kernels, hidden_part(): pl.pallas_call(kernel, grid_spec=pltpu.PrefetchScalarGridSpec(num_scalar_...  35.4 us
    ppermute x11, starting transfers between devices, send(): return lax.ppermute(value, ('groups', 'tensor', 'dp'), pairs)  28.9 us
    ppermute x3, starting transfers between devices, swap_cores(): return lax.ppermute(value, 'dp', [(i, i ^ 1) for i in range(size)])  23 us
    ppermute x8, waiting for transfers between devices, from_group(): lax.ppermute(value, 'groups', [((i + shift) % size, i) for i in range(siz...  18.4 us
    pallas_call x8, Pallas kernels, share_rows(): pl.pallas_call(kernel, grid_spec=pltpu.PrefetchScalarGridSpec(num_scalar_...  16 us
    ppermute x3, starting transfers between devices, spread_ranks(): lax.ppermute(below[-1], 'tensor', [(i, i + 1) for i in range(ranks - 1)])  15 us
    unnamed x74, local copies, waits for them, and re-layouts  14.4 us
  transfers between devices with their start and end apart: 39, of which 6 were waited for; matrix products, arithmetic and copies ran while one was open for 6% of the time, Pallas kernels for 47%

profile of v10, /device:TPU:3, one launch (start us, length us, event | category | flops | bytes accessed | tf_op | source)
XLA Modules:
  0.0 301.6 jit_solution(13092272244230990914)
XLA Ops:
  6.1 5.0 %collective-permute-start = (bf16[1024,512]{1,0:T(8,128)(2,1)}, bf16[1024,512]{1,0:T(8,128)(2,1)}, u32[]{:S(2)}, u32[]{:S(2)}) collective-permute-start(bf16[1024,512]{1,0:T(8,128)(2,1)} %bitcast.34), channel_id=1, source_target_pairs={{0,4},{4,8},{8,12},{1,5},{5,9},{9,13},{2,6},{6,10},{10,14},{3,7},{... | collective-permute-start | bytes 3145736 | tf_op jit(solution)/shard_map/ppermute | solution.py:120
  12.5 12.1 %prepare.1 = (f32[2,3584,512]{2,1,0:T(8,128)}, f32[64,512]{1,0:T(8,128)}) custom-call(bf16[512,3584]{1,0:T(8,128)(2,1)} %gate_ref.1, bf16[512,3584]{1,0:T(8,128)(2,1)} %up_ref.1, bf16[64,3584]{1,0:T(8,128)(2,1)} %bitcast.43, bf16[2,64,3584]{2,1,0:T(8,128)(2,1)} %get-tuple-element.28.refs_0_), custom_call_target="tpu_custom_call" | custom-call | flops 3240000000 | bytes 1 | tf_op jit(solution)/shard_map/prepare/pallas_call | solution.py:147
  32.4 5.0 %collective-permute-start.1 = (bf16[1024,512]{1,0:T(8,128)(2,1)}, bf16[1024,512]{1,0:T(8,128)(2,1)}, u32[]{:S(2)}, u32[]{:S(2)}) collective-permute-start(bf16[1024,512]{1,0:T(8,128)(2,1)} %collective-permute-done.refs_3_), channel_id=1, source_target_pairs={{0,4},{4,8},{8,12},{1,5},{5,9},{9,13},{2,6},{6,10},{10,14},{3,7},{... | collective-permute-start | bytes 3145736 | tf_op jit(solution)/shard_map/ppermute | solution.py:120
  38.5 14.3 %hidden_part.2.refs_4_.refs_7_ = f32[3584,512]{1,0:T(8,128)} custom-call(s32[1]{0:T(128)} %bitcast.4.rank_ref, bf16[3584,4096]{1,0:T(8,128)(2,1)} %refs_1_.16, bf16[3584,4096]{1,0:T(8,128)(2,1)} %refs_1_.16, bf16[1024,512]{1,0:T(8,128)(2,1)} %bitcast.35, bf16[1024,512]{1,0:T(8,128)(2,1)} %collective-permute-done.refs_3_, ...), custom_call_target="tpu_custom_call" | custom-call | flops 3240000000 | bytes 1 | tf_op jit(solution)/shard_map/hidden_part/pallas_call | solution.py:272
  58.7 5.0 %collective-permute-start.2 = (bf16[1024,512]{1,0:T(8,128)(2,1)}, bf16[1024,512]{1,0:T(8,128)(2,1)}, u32[]{:S(2)}, u32[]{:S(2)}) collective-permute-start(bf16[1024,512]{1,0:T(8,128)(2,1)} %collective-permute-done.1.refs_4_.refs_2_), channel_id=1, source_target_pairs={{0,4},{4,8},{8,12},{1,5},{5,9},{9,13},{2,6},{6,10},{10,14},{3,7},{... | collective-permute-start | bytes 3145736 | tf_op jit(solution)/shard_map/ppermute | solution.py:120
  68.0 7.3 %collective-permute-done.10.refs_3_.refs_6_ = bf16[2,64,3584]{2,1,0:T(8,128)(2,1)S(1)} collective-permute-done((bf16[2,64,3584]{2,1,0:T(8,128)(2,1)}, bf16[2,64,3584]{2,1,0:T(8,128)(2,1)S(1)}, u32[]{:S(2)}, u32[]{:S(2)}) %collective-permute-start.10) | collective-permute-done | bytes 917536 | tf_op jit(solution)/shard_map/ppermute | solution.py:59
  79.9 4.1 %collective-permute-done.12.refs_5_.refs_3_ = bf16[2,64,3584]{2,1,0:T(8,128)(2,1)S(1)} collective-permute-done((bf16[2,64,3584]{2,1,0:T(8,128)(2,1)}, bf16[2,64,3584]{2,1,0:T(8,128)(2,1)S(1)}, u32[]{:S(2)}, u32[]{:S(2)}) %collective-permute-start.12) | collective-permute-done | bytes 917536 | tf_op jit(solution)/shard_map/ppermute | solution.py:54
  85.2 21.1 %hidden_part.3 = (bf16[2,3584,512]{2,1,0:T(8,128)(2,1)}, f32[64,512]{1,0:T(8,128)}) custom-call(s32[1]{0:T(128)} %bitcast.4.rank_ref, bf16[3584,4096]{1,0:T(8,128)(2,1)} %refs_1_.16, bf16[3584,4096]{1,0:T(8,128)(2,1)} %refs_1_.16, bf16[1024,512]{1,0:T(8,128)(2,1)} %collective-permute-done.1.refs_4_.refs_2_, ...), custom_call_target="tpu_custom_call" | custom-call | flops 3240000000 | bytes 1 | tf_op jit(solution)/shard_map/hidden_part/pallas_call | solution.py:272
  106.3 11.1 %collective-permute-done.13.refs_6_.refs_8_ = bf16[2,64,3584]{2,1,0:T(8,128)(2,1)S(1)} collective-permute-done((bf16[2,64,3584]{2,1,0:T(8,128)(2,1)S(1)}, bf16[2,64,3584]{2,1,0:T(8,128)(2,1)S(1)}, u32[]{:S(2)}, u32[]{:S(2)}) %collective-permute-start.13) | collective-permute-done | bytes 917536 | tf_op jit(solution)/shard_map/ppermute | solution.py:59
  120.4 4.4 %collective-permute-start.20 = (bf16[2,3584,512]{2,1,0:T(8,128)(2,1)}, bf16[2,3584,512]{2,1,0:T(8,128)(2,1)}, u32[]{:S(2)}, u32[]{:S(2)}) collective-permute-start(bf16[2,3584,512]{2,1,0:T(8,128)(2,1)} %get-tuple-element.39.refs_2_.refs_9_.refs_4_.refs_3_), channel_id=1, source_target_pairs={{0,1},{1,0},{2,3},{3,2},{4,5},{5,4},{6,7},{7,6},{8,9},{9,8},{10,11... | collective-permute-start | bytes 22020104 | tf_op jit(solution)/shard_map/ppermute | solution.py:48
  129.7 13.8 %weigh_rows.6.refs_7_.refs_0_ = bf16[1024,512]{1,0:T(8,128)(2,1)} custom-call(bf16[1024,3584]{1,0:T(8,128)(2,1)} %refs_0_.21, bf16[1024,3584]{1,0:T(8,128)(2,1)} %refs_1_.21, bf16[2,3584,512]{2,1,0:T(8,128)(2,1)} %get-tuple-element.39.refs_2_.refs_9_.refs_4_.refs_3_, bf16[2,64,3584]{2,1,0:T(8,128)(2,1)} %get-tuple-element.40.refs_3_), custom_call_target="tpu_custom_call" | custom-call | flops 6480000000 | bytes 1 | tf_op jit(solution)/shard_map/weigh_rows/pallas_call | solution.py:349
  143.5 4.0 %collective-permute-start.18 = (bf16[1024,512]{1,0:T(8,128)(2,1)}, bf16[1024,512]{1,0:T(8,128)(2,1)}, u32[]{:S(2)}, u32[]{:S(2)}) collective-permute-start(bf16[1024,512]{1,0:T(8,128)(2,1)} %weigh_rows.6.refs_7_.refs_0_), channel_id=1, source_target_pairs={{4,0},{12,8},{1,5},{9,13},{6,2},{14,10},{3,7},{11,15},{20,16},{28,... | collective-permute-start | bytes 3145736 | tf_op jit(solution)/shard_map/ppermute | solution.py:521
  157.0 10.8 %weigh_rows.7.refs_3_.refs_1_ = bf16[576,512]{1,0:T(8,128)(2,1)} custom-call(bf16[2,64,3584]{2,1,0:T(8,128)(2,1)} %get-tuple-element.32.refs_0_, bf16[2,64,3584]{2,1,0:T(8,128)(2,1)} %get-tuple-element.33.refs_1_, bf16[2,64,3584]{2,1,0:T(8,128)(2,1)} %get-tuple-element.37.refs_2_, bf16[2,64,3584]{2,1,0:T(8,128)(2,1)} %copy-done.8, ...), custom_call_target="tpu_custom_call" | custom-call | flops 1620000000 | bytes 1 | tf_op jit(solution)/shard_map/weigh_rows/pallas_call | solution.py:349
  170.3 13.8 %weigh_rows.8.refs_4_.refs_5_.refs_0_ = bf16[1024,512]{1,0:T(8,128)(2,1)} custom-call(bf16[1024,3584]{1,0:T(8,128)(2,1)} %refs_0_.21, bf16[1024,3584]{1,0:T(8,128)(2,1)} %refs_1_.21, bf16[2,3584,512]{2,1,0:T(8,128)(2,1)} %collective-permute-done.20.refs_2_.refs_9_.refs_5_.refs_4_, bf16[576,512]{1,0:T(8,128)(2,1)} %weigh_rows.7.refs_3_.refs_1_, ...), custom_call_target="tpu_custom_call" | custom-call | flops 2970000128 | bytes 1 | tf_op jit(solution)/shard_map/weigh_rows/pallas_call | solution.py:349
  193.5 3.3 %add_terms.4 = (bf16[1024,512]{1,0:T(8,128)(2,1)}, bf16[576,512]{1,0:T(8,128)(2,1)}) custom-call(bf16[1024,512]{1,0:T(8,128)(2,1)} %weigh_rows.6.refs_7_.refs_0_, bf16[576,512]{1,0:T(8,128)(2,1)} %weigh_rows.7.refs_3_.refs_1_, bf16[1024,512]{1,0:T(8,128)(2,1)} %collective-permute-done.18.refs_2_, bf16[576,512]{1,0:T(8,128)(2,1)} %copy-done.28, ...), custom_call_target="tpu_custom_call" | custom-call | flops 540000000 | bytes 1 | tf_op jit(solution)/shard_map/add_terms/pallas_call | solution.py:379
  196.9 10.9 %weigh_rows.9.refs_4_.refs_1_ = bf16[576,512]{1,0:T(8,128)(2,1)} custom-call(bf16[2,64,3584]{2,1,0:T(8,128)(2,1)} %get-tuple-element.32.refs_0_, bf16[2,64,3584]{2,1,0:T(8,128)(2,1)} %get-tuple-element.33.refs_1_, bf16[2,64,3584]{2,1,0:T(8,128)(2,1)} %get-tuple-element.37.refs_2_, bf16[2,64,3584]{2,1,0:T(8,128)(2,1)} %copy-done.8, ...), custom_call_target="tpu_custom_call" | custom-call | flops 4320000000 | bytes 1 | tf_op jit(solution)/shard_map/weigh_rows/pallas_call | solution.py:349
  213.3 10.9 %weigh_rows.10.refs_4_.refs_0_ = bf16[256,1024]{1,0:T(8,128)(2,1)} custom-call(bf16[2,64,3584]{2,1,0:T(8,128)(2,1)} %copy-done.14, bf16[2,64,3584]{2,1,0:T(8,128)(2,1)} %get-tuple-element.48.refs_1_, bf16[2,64,3584]{2,1,0:T(8,128)(2,1)} %copy-done.20, bf16[2,64,3584]{2,1,0:T(8,128)(2,1)} %copy-done.21, ...), custom_call_target="tpu_custom_call" | custom-call | flops 2430000128 | bytes 1 | tf_op jit(solution)/shard_map/weigh_rows/pallas_call | solution.py:349
  224.2 4.2 %collective-permute-start.27 = (bf16[256,1024]{1,0:T(8,128)(2,1)}, bf16[256,1024]{1,0:T(8,128)(2,1)}, u32[]{:S(2)}, u32[]{:S(2)}) collective-permute-start(bf16[256,1024]{1,0:T(8,128)(2,1)} %weigh_rows.10.refs_4_.refs_0_), channel_id=1, source_target_pairs={{4,0},{12,8},{1,5},{9,13},{6,2},{14,10},{3,7},{11,15},{20,16},{28,... | collective-permute-start | bytes 1572872 | tf_op jit(solution)/shard_map/ppermute | solution.py:521
  230.1 3.3 %add_terms.5 = (bf16[1024,512]{1,0:T(8,128)(2,1)}, bf16[576,512]{1,0:T(8,128)(2,1)}) custom-call(bf16[1024,512]{1,0:T(8,128)(2,1)} %weigh_rows.8.refs_4_.refs_5_.refs_0_, bf16[576,512]{1,0:T(8,128)(2,1)} %weigh_rows.9.refs_4_.refs_1_, bf16[1024,512]{1,0:T(8,128)(2,1)} %collective-permute-done.28.refs_2_, bf16[576,512]{1,0:T(8,128)(2,1)} %collective-permute-done.29.refs_3_, ...), custom_call_target="tpu_custom_call" | custom-call | flops 540000000 | bytes 1 | tf_op jit(solution)/shard_map/add_terms/pallas_call | solution.py:379
  237.8 10.2 %weigh_rows.11.refs_0_ = bf16[192,1024]{1,0:T(8,128)(2,1)} custom-call(bf16[2,64,3584]{2,1,0:T(8,128)(2,1)} %collective-permute-done.26.refs_3_.refs_0_, bf16[2,64,3584]{2,1,0:T(8,128)(2,1)} %collective-permute-done.25.refs_2_.refs_1_, bf16[2,64,3584]{2,1,0:T(8,128)(2,1)} %collective-permute-done.33.refs_2_, ...), custom_call_target="tpu_custom_call" | custom-call | flops 16200000512 | bytes 1 | tf_op jit(solution)/shard_map/weigh_rows/pallas_call | solution.py:349
  248.0 10.9 %collective-permute-start.34 = (bf16[192,1024]{1,0:T(8,128)(2,1)}, bf16[192,1024]{1,0:T(8,128)(2,1)S(1)}, u32[]{:S(2)}, u32[]{:S(2)}) collective-permute-start(bf16[192,1024]{1,0:T(8,128)(2,1)} %weigh_rows.11.refs_0_), channel_id=1, source_target_pairs={{4,0},{12,8},{1,5},{9,13},{6,2},{14,10},{3,7},{11,15},{20,16},{28,... | collective-permute-start | bytes 1179656 | tf_op jit(solution)/shard_map/ppermute | solution.py:521
  259.0 4.9 %collective-permute-done.34.refs_1_ = bf16[192,1024]{1,0:T(8,128)(2,1)S(1)} collective-permute-done((bf16[192,1024]{1,0:T(8,128)(2,1)}, bf16[192,1024]{1,0:T(8,128)(2,1)S(1)}, u32[]{:S(2)}, u32[]{:S(2)}) %collective-permute-start.34) | collective-permute-done | bytes 393248 | tf_op jit(solution)/shard_map/ppermute | solution.py:521
  269.6 3.5 %assemble.2.refs_5_ = bf16[1024,512]{1,0:T(8,128)(2,1)} custom-call(s32[4]{0:T(128)} %pad_add_fusion.words_ref, bf16[1024,512]{1,0:T(8,128)(2,1)} %get-tuple-element.51.refs_2_.refs_0_, bf16[1024,512]{1,0:T(8,128)(2,1)} %copy-done.26, bf16[576,512]{1,0:T(8,128)(2,1)} %get-tuple-element.52.refs_3_.refs_2_, bf16[576,512]{1,0:T(8,128)(2,1)} %copy-done.22, ...), custom_call_target="tpu_custom_call" | custom-call | flops 1350000000 | bytes 1 | tf_op jit(solution)/shard_map/assemble/pallas_call | solution.py:441
  273.1 18.5 %collective-permute-start.36 = (bf16[1024,512]{1,0:T(8,128)(2,1)}, bf16[1024,512]{1,0:T(8,128)(2,1)S(1)}, u32[]{:S(2)}, u32[]{:S(2)}) collective-permute-start(bf16[1024,512]{1,0:T(8,128)(2,1)} %assemble.2.refs_5_), channel_id=1, source_target_pairs={{0,1},{1,0},{2,3},{3,2},{4,5},{5,4},{6,7},{7,6},{8,9},{9,8},{10,11... | collective-permute-start | bytes 3145736 | tf_op jit(solution)/shard_map/ppermute | solution.py:48
  (184 shorter events, 87.4 us)
Async XLA Ops:
  4.8 26.3 %collective-permute-start.3 = (bf16[1024,512]{1,0:T(8,128)(2,1)}, bf16[1024,512]{1,0:T(8,128)(2,1)}, u32[]{:S(2)}, u32[]{:S(2)}) collective-permute-start(bf16[1024,512]{1,0:T(8,128)(2,1)} %bitcast.33), channel_id=1, source_target_pairs={{4,0},{8,4},{12,8},{5,1},{9,5},{13,9},{6,2},{10,6},{14,10},{7,3},{... | collective-permute-start | bytes 3145736 | tf_op jit(solution)/shard_map/ppermute | solution.py:121
  6.1 26.3 %collective-permute-start = (bf16[1024,512]{1,0:T(8,128)(2,1)}, bf16[1024,512]{1,0:T(8,128)(2,1)}, u32[]{:S(2)}, u32[]{:S(2)}) collective-permute-start(bf16[1024,512]{1,0:T(8,128)(2,1)} %bitcast.34), channel_id=1, source_target_pairs={{0,4},{4,8},{8,12},{1,5},{5,9},{9,13},{2,6},{6,10},{10,14},{3,7},{... | collective-permute-start | bytes 3145736 | tf_op jit(solution)/shard_map/ppermute | solution.py:120
  11.2 41.7 %collective-permute-start.8 = (bf16[2,64,3584]{2,1,0:T(8,128)(2,1)}, bf16[2,64,3584]{2,1,0:T(8,128)(2,1)}, u32[]{:S(2)}, u32[]{:S(2)}) collective-permute-start(bf16[2,64,3584]{2,1,0:T(8,128)(2,1)} %get-tuple-element.31), channel_id=1, source_target_pairs={{2,0},{3,1},{0,2},{1,3},{6,4},{7,5},{4,6},{5,7},{10,8},{11,9},{8,1... | collective-permute-start | bytes 2752520 | tf_op jit(solution)/shard_map/ppermute | solution.py:54
  28.2 24.7 %collective-permute-start.9 = (bf16[2,64,3584]{2,1,0:T(8,128)(2,1)}, bf16[2,64,3584]{2,1,0:T(8,128)(2,1)S(1)}, u32[]{:S(2)}, u32[]{:S(2)}) collective-permute-start(bf16[2,64,3584]{2,1,0:T(8,128)(2,1)} %get-tuple-element.32.refs_0_), channel_id=1, source_target_pairs={{16,0},{0,16},{17,1},{1,17},{18,2},{2,18},{19,3},{3,19},{20,4},{4,... | collective-permute-start | bytes 2752520 | tf_op jit(solution)/shard_map/ppermute | solution.py:59
  31.1 26.2 %collective-permute-start.4 = (bf16[1024,512]{1,0:T(8,128)(2,1)}, bf16[1024,512]{1,0:T(8,128)(2,1)}, u32[]{:S(2)}, u32[]{:S(2)}) collective-permute-start(bf16[1024,512]{1,0:T(8,128)(2,1)} %collective-permute-done.3.refs_4_), channel_id=1, source_target_pairs={{4,0},{8,4},{12,8},{5,1},{9,5},{13,9},{6,2},{10,6},{14,10},{7,3},{... | collective-permute-start | bytes 3145736 | tf_op jit(solution)/shard_map/ppermute | solution.py:121
  32.4 26.2 %collective-permute-start.1 = (bf16[1024,512]{1,0:T(8,128)(2,1)}, bf16[1024,512]{1,0:T(8,128)(2,1)}, u32[]{:S(2)}, u32[]{:S(2)}) collective-permute-start(bf16[1024,512]{1,0:T(8,128)(2,1)} %collective-permute-done.refs_3_), channel_id=1, source_target_pairs={{0,4},{4,8},{8,12},{1,5},{5,9},{9,13},{2,6},{6,10},{10,14},{3,7},{... | collective-permute-start | bytes 3145736 | tf_op jit(solution)/shard_map/ppermute | solution.py:120
  37.4 30.6 %collective-permute-start.7 = (bf16[2,64,3584]{2,1,0:T(8,128)(2,1)}, bf16[2,64,3584]{2,1,0:T(8,128)(2,1)S(1)}, u32[]{:S(2)}, u32[]{:S(2)}) collective-permute-start(bf16[2,64,3584]{2,1,0:T(8,128)(2,1)} %get-tuple-element.30.refs_5_), channel_id=1, source_target_pairs={{2,0},{3,1},{0,2},{1,3},{6,4},{7,5},{4,6},{5,7},{10,8},{11,9},{8,1... | collective-permute-start | bytes 2752520 | tf_op jit(solution)/shard_map/ppermute | solution.py:54
  57.1 26.9 %collective-permute-start.12 = (bf16[2,64,3584]{2,1,0:T(8,128)(2,1)}, bf16[2,64,3584]{2,1,0:T(8,128)(2,1)S(1)}, u32[]{:S(2)}, u32[]{:S(2)}) collective-permute-start(bf16[2,64,3584]{2,1,0:T(8,128)(2,1)} %get-tuple-element.38), channel_id=1, source_target_pairs={{2,0},{3,1},{0,2},{1,3},{6,4},{7,5},{4,6},{5,7},{10,8},{11,9},{8,1... | collective-permute-start | bytes 2752520 | tf_op jit(solution)/shard_map/ppermute | solution.py:54
  57.4 27.8 %collective-permute-start.5 = (bf16[1024,512]{1,0:T(8,128)(2,1)}, bf16[1024,512]{1,0:T(8,128)(2,1)}, u32[]{:S(2)}, u32[]{:S(2)}) collective-permute-start(bf16[1024,512]{1,0:T(8,128)(2,1)} %collective-permute-done.4.refs_5_), channel_id=1, source_target_pairs={{4,0},{8,4},{12,8},{5,1},{9,5},{13,9},{6,2},{10,6},{14,10},{7,3},{... | collective-permute-start | bytes 3145736 | tf_op jit(solution)/shard_map/ppermute | solution.py:121
  58.7 26.5 %collective-permute-start.2 = (bf16[1024,512]{1,0:T(8,128)(2,1)}, bf16[1024,512]{1,0:T(8,128)(2,1)}, u32[]{:S(2)}, u32[]{:S(2)}) collective-permute-start(bf16[1024,512]{1,0:T(8,128)(2,1)} %collective-permute-done.1.refs_4_.refs_2_), channel_id=1, source_target_pairs={{0,4},{4,8},{8,12},{1,5},{5,9},{9,13},{2,6},{6,10},{10,14},{3,7},{... | collective-permute-start | bytes 3145736 | tf_op jit(solution)/shard_map/ppermute | solution.py:120
  78.4 27.8 %collective-permute-start.14 = (bf16[2,64,3584]{2,1,0:T(8,128)(2,1)}, bf16[2,64,3584]{2,1,0:T(8,128)(2,1)S(1)}, u32[]{:S(2)}, u32[]{:S(2)}) collective-permute-start(bf16[2,64,3584]{2,1,0:T(8,128)(2,1)} %get-tuple-element.35.refs_10_), channel_id=1, source_target_pairs={{2,0},{3,1},{0,2},{1,3},{6,4},{7,5},{4,6},{5,7},{10,8},{11,9},{8,1... | collective-permute-start | bytes 2752520 | tf_op jit(solution)/shard_map/ppermute | solution.py:54
  79.1 27.1 %collective-permute-start.11 = (bf16[2,64,3584]{2,1,0:T(8,128)(2,1)}, bf16[2,64,3584]{2,1,0:T(8,128)(2,1)S(1)}, u32[]{:S(2)}, u32[]{:S(2)}) collective-permute-start(bf16[2,64,3584]{2,1,0:T(8,128)(2,1)} %get-tuple-element.37.refs_2_), channel_id=1, source_target_pairs={{16,0},{0,16},{17,1},{1,17},{18,2},{2,18},{19,3},{3,19},{20,4},{4,... | collective-permute-start | bytes 2752520 | tf_op jit(solution)/shard_map/ppermute | solution.py:59
  84.0 33.3 %collective-permute-start.13 = (bf16[2,64,3584]{2,1,0:T(8,128)(2,1)S(1)}, bf16[2,64,3584]{2,1,0:T(8,128)(2,1)S(1)}, u32[]{:S(2)}, u32[]{:S(2)}) collective-permute-start(bf16[2,64,3584]{2,1,0:T(8,128)(2,1)S(1)} %collective-permute-done.12.refs_5_.refs_3_), channel_id=1, source_target_pairs={{16,0},{0,16},{17,1},{1,17},{18,2},{2,18},{19,3},{3,19},{20,4},{4,... | collective-permute-start | bytes 2752520 | tf_op jit(solution)/shard_map/ppermute | solution.py:59
  120.4 49.9 %collective-permute-start.20 = (bf16[2,3584,512]{2,1,0:T(8,128)(2,1)}, bf16[2,3584,512]{2,1,0:T(8,128)(2,1)}, u32[]{:S(2)}, u32[]{:S(2)}) collective-permute-start(bf16[2,3584,512]{2,1,0:T(8,128)(2,1)} %get-tuple-element.39.refs_2_.refs_9_.refs_4_.refs_3_), channel_id=1, source_target_pairs={{0,1},{1,0},{2,3},{3,2},{4,5},{5,4},{6,7},{7,6},{8,9},{9,8},{10,11... | collective-permute-start | bytes 22020104 | tf_op jit(solution)/shard_map/ppermute | solution.py:48
  143.5 49.2 %collective-permute-start.18 = (bf16[1024,512]{1,0:T(8,128)(2,1)}, bf16[1024,512]{1,0:T(8,128)(2,1)}, u32[]{:S(2)}, u32[]{:S(2)}) collective-permute-start(bf16[1024,512]{1,0:T(8,128)(2,1)} %weigh_rows.6.refs_7_.refs_0_), channel_id=1, source_target_pairs={{4,0},{12,8},{1,5},{9,13},{6,2},{14,10},{3,7},{11,15},{20,16},{28,... | collective-permute-start | bytes 3145736 | tf_op jit(solution)/shard_map/ppermute | solution.py:521
  152.6 31.5 %collective-permute-start.23 = (bf16[2,64,3584]{2,1,0:T(8,128)(2,1)}, bf16[2,64,3584]{2,1,0:T(8,128)(2,1)S(1)}, u32[]{:S(2)}, u32[]{:S(2)}) collective-permute-start(bf16[2,64,3584]{2,1,0:T(8,128)(2,1)} %get-tuple-element.43.refs_10_), channel_id=1, source_target_pairs={{2,0},{3,1},{0,2},{1,3},{6,4},{7,5},{4,6},{5,7},{10,8},{11,9},{8,1... | collective-permute-start | bytes 2752520 | tf_op jit(solution)/shard_map/ppermute | solution.py:54
  152.9 31.2 %collective-permute-start.24 = (bf16[2,64,3584]{2,1,0:T(8,128)(2,1)}, bf16[2,64,3584]{2,1,0:T(8,128)(2,1)S(1)}, u32[]{:S(2)}, u32[]{:S(2)}) collective-permute-start(bf16[2,64,3584]{2,1,0:T(8,128)(2,1)} %copy-done.14), channel_id=1, source_target_pairs={{16,0},{0,16},{17,1},{1,17},{18,2},{2,18},{19,3},{3,19},{20,4},{4,... | collective-permute-start | bytes 2752520 | tf_op jit(solution)/shard_map/ppermute | solution.py:59
  167.8 24.9 %collective-permute-start.19 = (bf16[576,512]{1,0:T(8,128)(2,1)}, bf16[576,512]{1,0:T(8,128)(2,1)S(1)}, u32[]{:S(2)}, u32[]{:S(2)}) collective-permute-start(bf16[576,512]{1,0:T(8,128)(2,1)} %weigh_rows.7.refs_3_.refs_1_), channel_id=1, source_target_pairs={{4,0},{12,8},{1,5},{9,13},{6,2},{14,10},{3,7},{11,15},{20,16},{28,... | collective-permute-start | bytes 1769480 | tf_op jit(solution)/shard_map/ppermute | solution.py:521
  188.1 23.7 %collective-permute-start.25 = (bf16[2,64,3584]{2,1,0:T(8,128)(2,1)}, bf16[2,64,3584]{2,1,0:T(8,128)(2,1)}, u32[]{:S(2)}, u32[]{:S(2)}) collective-permute-start(bf16[2,64,3584]{2,1,0:T(8,128)(2,1)} %get-tuple-element.48.refs_1_), channel_id=1, source_target_pairs={{16,0},{0,16},{17,1},{1,17},{18,2},{2,18},{19,3},{3,19},{20,4},{4,... | collective-permute-start | bytes 2752520 | tf_op jit(solution)/shard_map/ppermute | solution.py:59
  190.4 38.7 %collective-permute-start.28 = (bf16[1024,512]{1,0:T(8,128)(2,1)S(1)}, bf16[1024,512]{1,0:T(8,128)(2,1)}, u32[]{:S(2)}, u32[]{:S(2)}) collective-permute-start(bf16[1024,512]{1,0:T(8,128)(2,1)S(1)} %copy-done.2), channel_id=1, source_target_pairs={{4,0},{12,8},{1,5},{9,13},{6,2},{14,10},{3,7},{11,15},{20,16},{28,... | collective-permute-start | bytes 3145736 | tf_op jit(solution)/shard_map/ppermute | solution.py:521
  211.0 26.8 %collective-permute-start.33 = (bf16[2,64,3584]{2,1,0:T(8,128)(2,1)}, bf16[2,64,3584]{2,1,0:T(8,128)(2,1)}, u32[]{:S(2)}, u32[]{:S(2)}) collective-permute-start(bf16[2,64,3584]{2,1,0:T(8,128)(2,1)} %collective-permute-done.26.refs_3_.refs_0_), channel_id=1, source_target_pairs={{16,0},{0,16},{17,1},{1,17},{18,2},{2,18},{19,3},{3,19},{20,4},{4,... | collective-permute-start | bytes 2752520 | tf_op jit(solution)/shard_map/ppermute | solution.py:59
  233.4 25.5 %collective-permute-start.32 = (bf16[576,512]{1,0:T(8,128)(2,1)}, bf16[576,512]{1,0:T(8,128)(2,1)S(1)}, u32[]{:S(2)}, u32[]{:S(2)}) collective-permute-start(bf16[576,512]{1,0:T(8,128)(2,1)} %get-tuple-element.52.refs_3_.refs_2_), channel_id=1, source_target_pairs={{0,8},{5,13},{10,2},{15,7},{16,24},{21,29},{26,18},{31,23}} | collective-permute-start | bytes 1769480 | tf_op jit(solution)/shard_map/ppermute | solution.py:521
  234.1 33.7 %collective-permute-start.31 = (bf16[1024,512]{1,0:T(8,128)(2,1)}, bf16[1024,512]{1,0:T(8,128)(2,1)S(1)}, u32[]{:S(2)}, u32[]{:S(2)}) collective-permute-start(bf16[1024,512]{1,0:T(8,128)(2,1)} %get-tuple-element.51.refs_2_.refs_0_), channel_id=1, source_target_pairs={{8,0},{13,5},{2,10},{7,15},{24,16},{29,21},{18,26},{23,31}} | collective-permute-start | bytes 3145736 | tf_op jit(solution)/shard_map/ppermute | solution.py:521
  273.1 24.5 %collective-permute-start.36 = (bf16[1024,512]{1,0:T(8,128)(2,1)}, bf16[1024,512]{1,0:T(8,128)(2,1)S(1)}, u32[]{:S(2)}, u32[]{:S(2)}) collective-permute-start(bf16[1024,512]{1,0:T(8,128)(2,1)} %assemble.2.refs_5_), channel_id=1, source_target_pairs={{0,1},{1,0},{2,3},{3,2},{4,5},{5,4},{6,7},{7,6},{8,9},{9,8},{10,11... | collective-permute-start | bytes 3145736 | tf_op jit(solution)/shard_map/ppermute | solution.py:48
  (51 other events, 573.8 us)

commit v11 on v10

--- a/solution.py
+++ b/solution.py
@@ -493,8 +493,7 @@
 
 def exchange(value, bit):
     ranks = lax.axis_size("tensor")
-    got = lax.ppermute(value.astype(jnp.bfloat16), "tensor", [(i, i ^ bit) for i in range(ranks)])
-    return got.astype(jnp.float32)
+    return lax.ppermute(value.astype(jnp.bfloat16), "tensor", [(i, i ^ bit) for i in range(ranks)])
 
 
 def halve(value, bit):
@@ -502,7 +501,7 @@
     high = lax.axis_index("tensor") & bit != 0
     low_rows, high_rows = value[:half], value[half:]
     got = exchange(jnp.where(high, low_rows, high_rows), bit)
-    return jnp.where(high, high_rows, low_rows) + got
+    return jnp.where(high, high_rows, low_rows), got
 
 
 def hops(owner, bit):
@@ -673,14 +672,15 @@
     mine, up_out_part = hidden_part(
         rank_word, below, above, w_down, so_far, slopes, proj_u.T, [ticks[2]]
     )
-    mine, early = forward(3, chunks_of([2, 3], others) + [(4, 0)], [], [mine, early_part])
+    mine, early = forward(3, chunks_of([2], others) + [(4, 0)], [], [mine, early_part])
     theirs = swap_cores(mine)
-    early = early + exchange(early, bits[0])
-    first_names = chunks_of(range(5), [0]) + chunks_of(range(4), others)
-    near_mine = terms([], [mine], [ticks[3]], 24, near=True)
-    early, up_out_part = forward(
-        4, chunks_of([4], others) + [(5, 0)], near_mine[0], [early, up_out_part]
-    )
+    got = exchange(early, bits[0])
+    first_names = chunks_of(range(5), [0]) + chunks_of(range(3), others)
+    first_mine = terms(first_names, [mine], [ticks[3]], 24, near=True)
+    early, got, up_out_part = forward(
+        4, chunks_of([3], others) + [(5, 0)], first_mine[0], [early, got, up_out_part]
+    )
+    early = early + got
 
     out_parts = jnp.stack([up_out_part, out_down_part]).reshape(2, ranks, -1, count)
     out_parts = out_parts.transpose(1, 0, 2, 3).reshape(-1, count)
@@ -691,37 +691,35 @@
         jnp.concatenate([early, jnp.where(high, out_parts[:half], out_parts[half:])], axis=0),
         bits[-1],
     )
+    first_theirs = terms(first_names, [theirs], [ticks[4]], 24, near=True)
+    (got,) = forward(5, chunks_of([4], others) + [(6, 0)], first_theirs[0], [got])
     early = early + got[:width]
     out_parts = jnp.where(high, out_parts[half:], out_parts[:half]) + got[width:]
     for bit in bits[1:-1]:
         early = early + exchange(early, bit)
-
-    far_mine = terms(first_names, [mine], [ticks[4]], 6)
-    near_theirs = terms([], [theirs], far_mine[0] + [early], 11, near=True)
-    held = forward(
-        5, chunks_of([5], others), near_theirs[0], [fetched[6, s, 0] for s in range(1, chips)]
-    )
+    for bit in bits[-2:0:-1]:
+        out_parts, got = halve(out_parts, bit)
+        out_parts = out_parts + got
+    out_parts, got = halve(out_parts, bits[0])
+    sums_mine, end_mine = carry_on([first_mine], first_theirs[0], at_once=True)
+    second_names = chunks_of([5, 6], [0]) + chunks_of([3, 4, 5], others)
+    last_names = chunks_of([7], [0]) + chunks_of([6, 7], others)
+    second = terms(second_names, [mine, theirs], [ticks[5]] + sums_mine, 16)
+    held = [fetched[7, s, 0] for s in range(1, chips)]
+    got, *held = forward(6, chunks_of([5], others), second[0], [got] + held)
     for s, value in enumerate(held, 1):
-        fetched[6, s, 0] = value
+        fetched[7, s, 0] = value
         for r in range(1, groups):
-            fetched[6, s, r] = from_group(value, r)
-    sums_mine, end_mine = carry_on([near_mine, far_mine], near_theirs[0], at_once=True)
-    far_theirs = terms(first_names, [theirs], [ticks[5]] + sums_mine, 16)
-    (out_parts,) = forward(
-        6, chunks_of([6], others) + [(7, 0)], far_theirs[0], [out_parts]
-    )
-    second_names = chunks_of([5, 6], [0]) + chunks_of([4, 5], others)
-    last_names = chunks_of([7], [0]) + chunks_of([6, 7], others)
-    second = terms(second_names, [mine, theirs], [ticks[6]], 9)
+            fetched[7, s, r] = from_group(value, r)
+    out_parts = out_parts + got
     received = [got for _, _, got in end_mine]
-    sums_theirs, end_theirs = carry_on([near_theirs, far_theirs], second[0] + received)
+    received += [fetched[n] for n in fetched if n[0] == 6 and n[2] > 0]
+    sums_theirs, end_theirs = carry_on([first_theirs], [ticks[6]] + received)
     sums_second, end_second = carry_on([second], sums_theirs)
     last = terms(last_names, [mine, theirs], sums_second, 60)
     received = [got for names, _, got in end_theirs + end_second if names is not None]
     sums_last, end_last = carry_on([last], received, 2)
 
-    for bit in bits[-2::-1]:
-        out_parts = halve(out_parts, bit)
     early = early.astype(jnp.bfloat16)
     width = in_down_part.shape[0]
     in_up, in_down = early[:width], early[width:]

time: 303 us -> 298 us (0.983)
  Pallas kernels: 154 us -> 141 us
  waiting for transfers between devices: 29.6 us -> 36.1 us
    ppermute x8, waiting for transfers between devices: 4.54 us -> 18.4 us  [from_chip(): lax.ppermute(value, 'dp', [((i + step) % size, i) for i in range(size)])]
    pallas_call x6 -> x4, Pallas kernels: 70.3 us -> 57.2 us  [weigh(): pl.pallas_call(kernel, grid=(steps,), out_shape=shapes, in_specs=specs +...]
    ppermute x8, waiting for transfers between devices: 18.4 us -> 8.22 us  [from_group(): lax.ppermute(value, 'groups', [((i + shift) % size, i) for i in range(siz...]
    unnamed x74 -> x68, local copies, waits for them, and re-layouts: 14.4 us -> 13.2 us
    ppermute x11 -> x9, starting transfers between devices: 28.9 us -> 29.4 us  [send(): return lax.ppermute(value, ('groups', 'tensor', 'dp'), pairs)]
  transfers between devices with their start and end apart: 39 -> 37, of which waited for: 6 -> 8; matrix products, arithmetic and copies ran while one was open for 6% -> 6% of each run, Pallas kernels for 47% -> 44%
where the time goes in v11:
time: 298 us; the launch traced here: 295 us
  Pallas kernels  141 us (47%)
  starting transfers between devices  87.7 us (29%)
  waiting for transfers between devices  36.1 us (12%)
  local copies, waits for them, and re-layouts  14.7 us (5%)
  other arithmetic  11.1 us (4%)
  matrix products  3.08 us (1%)
    pallas_call x4, Pallas kernels, weigh(): pl.pallas_call(kernel, grid=(steps,), out_shape=shapes, in_specs=specs +...  57.2 us
    pallas_call x2, Pallas kernels, hidden_part(): pl.pallas_call(kernel, grid_spec=pltpu.PrefetchScalarGridSpec(num_scalar_...  35.4 us
    ppermute x9, starting transfers between devices, send(): return lax.ppermute(value, ('groups', 'tensor', 'dp'), pairs)  29.4 us
    ppermute x3, starting transfers between devices, swap_cores(): return lax.ppermute(value, 'dp', [(i, i ^ 1) for i in range(size)])  23 us
    ppermute x8, waiting for transfers between devices, from_chip(): lax.ppermute(value, 'dp', [((i + step) % size, i) for i in range(size)])  18.4 us
    pallas_call x8, Pallas kernels, share_rows(): pl.pallas_call(kernel, grid_spec=pltpu.PrefetchScalarGridSpec(num_scalar_...  15.8 us
    ppermute x3, starting transfers between devices, spread_ranks(): lax.ppermute(below[-1], 'tensor', [(i, i + 1) for i in range(ranks - 1)])  15 us
    unnamed x68, local copies, waits for them, and re-layouts  13.2 us
  transfers between devices with their start and end apart: 37, of which 8 were waited for; matrix products, arithmetic and copies ran while one was open for 6% of the time, Pallas kernels for 44%

profile of v11, /device:TPU:3, one launch (start us, length us, event | category | flops | bytes accessed | tf_op | source)
XLA Modules:
  0.0 295.4 jit_solution(10093832305697412413)
XLA Ops:
  0.7 2.7 share_rows.8
  6.9 5.1 %collective-permute-start.3 = (bf16[1024,512]{1,0:T(8,128)(2,1)}, bf16[1024,512]{1,0:T(8,128)(2,1)}, u32[]{:S(2)}, u32[]{:S(2)}) collective-permute-start(bf16[1024,512]{1,0:T(8,128)(2,1)} %bitcast.34), channel_id=1, source_target_pairs={{0,4},{4,8},{8,12},{1,5},{5,9},{9,13},{2,6},{6,10},{10,14},{3,7},{... | collective-permute-start | bytes 3145736 | tf_op jit(solution)/shard_map/ppermute | solution.py:120
  13.4 11.9 %prepare.1 = (f32[2,3584,512]{2,1,0:T(8,128)}, f32[64,512]{1,0:T(8,128)}) custom-call(bf16[512,3584]{1,0:T(8,128)(2,1)} %gate_ref.1, bf16[512,3584]{1,0:T(8,128)(2,1)} %up_ref.1, bf16[64,3584]{1,0:T(8,128)(2,1)} %bitcast.43, bf16[2,64,3584]{2,1,0:T(8,128)(2,1)} %get-tuple-element.30.refs_0_), custom_call_target="tpu_custom_call" | custom-call | flops 3240000000 | bytes 1 | tf_op jit(solution)/shard_map/prepare/pallas_call | solution.py:147
  33.2 5.0 %collective-permute-start.7 = (bf16[1024,512]{1,0:T(8,128)(2,1)}, bf16[1024,512]{1,0:T(8,128)(2,1)}, u32[]{:S(2)}, u32[]{:S(2)}) collective-permute-start(bf16[1024,512]{1,0:T(8,128)(2,1)} %collective-permute-done.3.refs_3_), channel_id=1, source_target_pairs={{0,4},{4,8},{8,12},{1,5},{5,9},{9,13},{2,6},{6,10},{10,14},{3,7},{... | collective-permute-start | bytes 3145736 | tf_op jit(solution)/shard_map/ppermute | solution.py:120
  39.3 14.3 %hidden_part.2.refs_4_.refs_7_ = f32[3584,512]{1,0:T(8,128)} custom-call(s32[1]{0:T(128)} %bitcast.5.rank_ref, bf16[3584,4096]{1,0:T(8,128)(2,1)} %refs_1_.16, bf16[3584,4096]{1,0:T(8,128)(2,1)} %refs_1_.16, bf16[1024,512]{1,0:T(8,128)(2,1)} %bitcast.35, bf16[1024,512]{1,0:T(8,128)(2,1)} %collective-permute-done.3.refs_3_, ...), custom_call_target="tpu_custom_call" | custom-call | flops 3240000000 | bytes 1 | tf_op jit(solution)/shard_map/hidden_part/pallas_call | solution.py:272
  59.2 5.0 %collective-permute-start.12 = (bf16[1024,512]{1,0:T(8,128)(2,1)}, bf16[1024,512]{1,0:T(8,128)(2,1)}, u32[]{:S(2)}, u32[]{:S(2)}) collective-permute-start(bf16[1024,512]{1,0:T(8,128)(2,1)} %collective-permute-done.7.refs_4_.refs_2_), channel_id=1, source_target_pairs={{0,4},{4,8},{8,12},{1,5},{5,9},{9,13},{2,6},{6,10},{10,14},{3,7},{... | collective-permute-start | bytes 3145736 | tf_op jit(solution)/shard_map/ppermute | solution.py:120
  67.9 8.2 %collective-permute-done.6.refs_3_.refs_8_ = bf16[2,64,3584]{2,1,0:T(8,128)(2,1)S(1)} collective-permute-done((bf16[2,64,3584]{2,1,0:T(8,128)(2,1)}, bf16[2,64,3584]{2,1,0:T(8,128)(2,1)S(1)}, u32[]{:S(2)}, u32[]{:S(2)}) %collective-permute-start.6) | collective-permute-done | bytes 917536 | tf_op jit(solution)/shard_map/ppermute | solution.py:59
  82.7 21.0 %hidden_part.3 = (bf16[2,3584,512]{2,1,0:T(8,128)(2,1)}, f32[64,512]{1,0:T(8,128)}) custom-call(s32[1]{0:T(128)} %bitcast.5.rank_ref, bf16[3584,4096]{1,0:T(8,128)(2,1)} %refs_1_.16, bf16[3584,4096]{1,0:T(8,128)(2,1)} %refs_1_.16, bf16[1024,512]{1,0:T(8,128)(2,1)} %collective-permute-done.7.refs_4_.refs_2_, ...), custom_call_target="tpu_custom_call" | custom-call | flops 3240000000 | bytes 1 | tf_op jit(solution)/shard_map/hidden_part/pallas_call | solution.py:272
  109.2 4.5 %collective-permute-start.15 = (bf16[2,3584,512]{2,1,0:T(8,128)(2,1)}, bf16[2,3584,512]{2,1,0:T(8,128)(2,1)}, u32[]{:S(2)}, u32[]{:S(2)}) collective-permute-start(bf16[2,3584,512]{2,1,0:T(8,128)(2,1)} %get-tuple-element.41.refs_10_.refs_5_.refs_3_), channel_id=1, source_target_pairs={{0,1},{1,0},{2,3},{3,2},{4,5},{5,4},{6,7},{7,6},{8,9},{9,8},{10,11... | collective-permute-start | bytes 22020104 | tf_op jit(solution)/shard_map/ppermute | solution.py:48
  117.8 17.7 %weigh_rows.4.refs_8_.refs_0_ = bf16[1536,512]{1,0:T(8,128)(2,1)} custom-call(bf16[1024,3584]{1,0:T(8,128)(2,1)} %refs_0_.21, bf16[1024,3584]{1,0:T(8,128)(2,1)} %refs_1_.21, bf16[2,64,3584]{2,1,0:T(8,128)(2,1)} %get-tuple-element.32.refs_2_, bf16[2,64,3584]{2,1,0:T(8,128)(2,1)} %get-tuple-element.35.refs_3_, ...), custom_call_target="tpu_custom_call" | custom-call | flops 6480000000 | bytes 1 | tf_op jit(solution)/shard_map/weigh_rows/pallas_call | solution.py:349
  135.5 4.2 %collective-permute-start.14 = (bf16[1536,512]{1,0:T(8,128)(2,1)}, bf16[1536,512]{1,0:T(8,128)(2,1)}, u32[]{:S(2)}, u32[]{:S(2)}) collective-permute-start(bf16[1536,512]{1,0:T(8,128)(2,1)} %weigh_rows.4.refs_8_.refs_0_), channel_id=1, source_target_pairs={{4,0},{12,8},{1,5},{9,13},{6,2},{14,10},{3,7},{11,15},{20,16},{28,... | collective-permute-start | bytes 4718600 | tf_op jit(solution)/shard_map/ppermute | solution.py:520
  148.8 15.3 %collective-permute-done.20.refs_5_.refs_1_.refs_3_ = bf16[2,64,3584]{2,1,0:T(8,128)(2,1)S(1)} collective-permute-done((bf16[2,64,3584]{2,1,0:T(8,128)(2,1)}, bf16[2,64,3584]{2,1,0:T(8,128)(2,1)S(1)}, u32[]{:S(2)}, u32[]{:S(2)}) %collective-permute-start.20) | collective-permute-done | bytes 917536 | tf_op jit(solution)/shard_map/ppermute | solution.py:54
  165.6 17.7 %weigh_rows.5.refs_2_.refs_6_.refs_0_ = bf16[1536,512]{1,0:T(8,128)(2,1)} custom-call(bf16[1024,3584]{1,0:T(8,128)(2,1)} %refs_0_.21, bf16[1024,3584]{1,0:T(8,128)(2,1)} %refs_1_.21, bf16[2,64,3584]{2,1,0:T(8,128)(2,1)} %get-tuple-element.32.refs_2_, bf16[2,64,3584]{2,1,0:T(8,128)(2,1)} %get-tuple-element.35.refs_3_, ...), custom_call_target="tpu_custom_call" | custom-call | flops 6480000000 | bytes 1 | tf_op jit(solution)/shard_map/weigh_rows/pallas_call | solution.py:349
  190.7 3.3 %add_terms.4 = (bf16[1024,512]{1,0:T(8,128)(2,1)}, bf16[512,512]{1,0:T(8,128)(2,1)}) custom-call(bf16[1536,512]{1,0:T(8,128)(2,1)} %weigh_rows.4.refs_8_.refs_0_, bf16[1536,512]{1,0:T(8,128)(2,1)} %collective-permute-done.14.refs_1_, bf16[1536,512]{1,0:T(8,128)(2,1)} %weigh_rows.5.refs_2_.refs_6_.refs_0_), custom_call_target="tpu_custom_call" | custom-call | flops 540000000 | bytes 1 | tf_op jit(solution)/shard_map/add_terms/pallas_call | solution.py:379
  197.7 11.7 %weigh_rows.6.refs_4_.refs_0_ = bf16[320,1024]{1,0:T(8,128)(2,1)} custom-call(bf16[2,64,3584]{2,1,0:T(8,128)(2,1)} %copy-done.10, bf16[2,64,3584]{2,1,0:T(8,128)(2,1)} %copy-done.6, bf16[2,64,3584]{2,1,0:T(8,128)(2,1)} %copy-done.16, bf16[2,64,3584]{2,1,0:T(8,128)(2,1)} %collective-permute-done.21.refs_3_, bf16[2,64,3584]{2,1,0:T(8,128)(2,1)} %copy-done.15, ...), custom_call_target="tpu_custom_call" | custom-call | flops 4320000000 | bytes 1 | tf_op jit(solution)/shard_map/weigh_rows/pallas_call | solution.py:349
  212.2 6.9 %collective-permute-start.24 = (bf16[320,1024]{1,0:T(8,128)(2,1)}, bf16[320,1024]{1,0:T(8,128)(2,1)}, u32[]{:S(2)}, u32[]{:S(2)}) collective-permute-start(bf16[320,1024]{1,0:T(8,128)(2,1)} %weigh_rows.6.refs_4_.refs_0_), channel_id=1, source_target_pairs={{4,0},{12,8},{1,5},{9,13},{6,2},{14,10},{3,7},{11,15},{20,16},{28,... | collective-permute-start | bytes 1966088 | tf_op jit(solution)/shard_map/ppermute | solution.py:520
  222.6 3.3 %add_terms.5 = (bf16[1024,512]{1,0:T(8,128)(2,1)}, bf16[512,512]{1,0:T(8,128)(2,1)}) custom-call(bf16[1536,512]{1,0:T(8,128)(2,1)} %weigh_rows.5.refs_2_.refs_6_.refs_0_, bf16[1536,512]{1,0:T(8,128)(2,1)} %collective-permute-done.25.refs_1_, f32[8,128]{1,0:T(8,128)} %get-tuple-element.53.refs_2_, bf16[1024,512]{1,0:T(8,128)(2,1)} %copy-done.5, ...), custom_call_target="tpu_custom_call" | custom-call | flops 540000000 | bytes 1 | tf_op jit(solution)/shard_map/add_terms/pallas_call | solution.py:379
  230.3 10.1 %weigh_rows.7.refs_0_ = bf16[192,1024]{1,0:T(8,128)(2,1)} custom-call(bf16[2,64,3584]{2,1,0:T(8,128)(2,1)} %get-tuple-element.56.refs_0_, bf16[2,64,3584]{2,1,0:T(8,128)(2,1)} %collective-permute-done.28.refs_5_.refs_1_, bf16[2,64,3584]{2,1,0:T(8,128)(2,1)} %collective-permute-done.32.refs_2_, ...), custom_call_target="tpu_custom_call" | custom-call | flops 16200000512 | bytes 1 | tf_op jit(solution)/shard_map/weigh_rows/pallas_call | solution.py:349
  240.4 12.1 %collective-permute-start.33 = (bf16[192,1024]{1,0:T(8,128)(2,1)}, bf16[192,1024]{1,0:T(8,128)(2,1)S(1)}, u32[]{:S(2)}, u32[]{:S(2)}) collective-permute-start(bf16[192,1024]{1,0:T(8,128)(2,1)} %weigh_rows.7.refs_0_), channel_id=1, source_target_pairs={{4,0},{12,8},{1,5},{9,13},{6,2},{14,10},{3,7},{11,15},{20,16},{28,... | collective-permute-start | bytes 1179656 | tf_op jit(solution)/shard_map/ppermute | solution.py:520
  252.7 4.9 %collective-permute-done.33.refs_1_ = bf16[192,1024]{1,0:T(8,128)(2,1)S(1)} collective-permute-done((bf16[192,1024]{1,0:T(8,128)(2,1)}, bf16[192,1024]{1,0:T(8,128)(2,1)S(1)}, u32[]{:S(2)}, u32[]{:S(2)}) %collective-permute-start.33) | collective-permute-done | bytes 393248 | tf_op jit(solution)/shard_map/ppermute | solution.py:520
  263.2 3.5 %assemble.2.refs_5_ = bf16[1024,512]{1,0:T(8,128)(2,1)} custom-call(s32[4]{0:T(128)} %pad_add_fusion.words_ref, bf16[1024,512]{1,0:T(8,128)(2,1)} %get-tuple-element.54.refs_2_.refs_0_, bf16[1024,512]{1,0:T(8,128)(2,1)} %copy-done.22, bf16[512,512]{1,0:T(8,128)(2,1)} %get-tuple-element.55.refs_3_.refs_2_, bf16[512,512]{1,0:T(8,128)(2,1)} %copy-done.17, ...), custom_call_target="tpu_custom_call" | custom-call | flops 1350000000 | bytes 1 | tf_op jit(solution)/shard_map/assemble/pallas_call | solution.py:441
  266.8 18.5 %collective-permute-start.35 = (bf16[1024,512]{1,0:T(8,128)(2,1)}, bf16[1024,512]{1,0:T(8,128)(2,1)S(1)}, u32[]{:S(2)}, u32[]{:S(2)}) collective-permute-start(bf16[1024,512]{1,0:T(8,128)(2,1)} %assemble.2.refs_5_), channel_id=1, source_target_pairs={{0,1},{1,0},{2,3},{3,2},{4,5},{5,4},{6,7},{7,6},{8,9},{9,8},{10,11... | collective-permute-start | bytes 3145736 | tf_op jit(solution)/shard_map/ppermute | solution.py:48
  288.0 3.3 %assemble.3.mine_ref = bf16[1024,512]{1,0:T(8,128)(2,1)} custom-call(s32[4]{0:T(128)} %pad_add_fusion.words_ref, bf16[1024,512]{1,0:T(8,128)(2,1)} %get-tuple-element.46.refs_8_.refs_0_, bf16[1024,512]{1,0:T(8,128)(2,1)} %copy-done.5, bf16[512,512]{1,0:T(8,128)(2,1)} %get-tuple-element.47.refs_9_.refs_2_, ...), custom_call_target="tpu_custom_call" | custom-call | flops 1350000000 | bytes 1 | tf_op jit(solution)/shard_map/assemble/pallas_call | solution.py:441
  292.4 3.0 %finish.1 = bf16[512,1024]{1,0:T(8,128)(2,1)} custom-call(s32[4]{0:T(128)} %pad_add_fusion.words_ref, bf16[1024,512]{1,0:T(8,128)(2,1)} %assemble.3.mine_ref, bf16[1024,512]{1,0:T(8,128)(2,1)} %copy-done.23, bf16[192,512]{1,0:T(8,128)(2,1)} %get-tuple-element.61.late_mine_ref, bf16[192,512]{1,0:T(8,128)(2,1)} %copy-done.26), custom_call_target="tpu_custom_call" | custom-call | flops 810000000 | bytes 1 | tf_op jit(solution)/shard_map/finish/pallas_call | solution.py:482
  (170 shorter events, 80.3 us)
Async XLA Ops:
  5.6 26.3 %collective-permute-start.4 = (bf16[1024,512]{1,0:T(8,128)(2,1)}, bf16[1024,512]{1,0:T(8,128)(2,1)}, u32[]{:S(2)}, u32[]{:S(2)}) collective-permute-start(bf16[1024,512]{1,0:T(8,128)(2,1)} %bitcast.33), channel_id=1, source_target_pairs={{4,0},{8,4},{12,8},{5,1},{9,5},{13,9},{6,2},{10,6},{14,10},{7,3},{... | collective-permute-start | bytes 3145736 | tf_op jit(solution)/shard_map/ppermute | solution.py:121
  6.9 26.3 %collective-permute-start.3 = (bf16[1024,512]{1,0:T(8,128)(2,1)}, bf16[1024,512]{1,0:T(8,128)(2,1)}, u32[]{:S(2)}, u32[]{:S(2)}) collective-permute-start(bf16[1024,512]{1,0:T(8,128)(2,1)} %bitcast.34), channel_id=1, source_target_pairs={{0,4},{4,8},{8,12},{1,5},{5,9},{9,13},{2,6},{6,10},{10,14},{3,7},{... | collective-permute-start | bytes 3145736 | tf_op jit(solution)/shard_map/ppermute | solution.py:120
  12.0 41.7 %collective-permute-start.1 = (bf16[2,64,3584]{2,1,0:T(8,128)(2,1)}, bf16[2,64,3584]{2,1,0:T(8,128)(2,1)}, u32[]{:S(2)}, u32[]{:S(2)}) collective-permute-start(bf16[2,64,3584]{2,1,0:T(8,128)(2,1)} %get-tuple-element.33), channel_id=1, source_target_pairs={{2,0},{3,1},{0,2},{1,3},{6,4},{7,5},{4,6},{5,7},{10,8},{11,9},{8,1... | collective-permute-start | bytes 2752520 | tf_op jit(solution)/shard_map/ppermute | solution.py:54
  28.3 25.4 %collective-permute-start.2 = (bf16[2,64,3584]{2,1,0:T(8,128)(2,1)}, bf16[2,64,3584]{2,1,0:T(8,128)(2,1)S(1)}, u32[]{:S(2)}, u32[]{:S(2)}) collective-permute-start(bf16[2,64,3584]{2,1,0:T(8,128)(2,1)} %get-tuple-element.32.refs_2_), channel_id=1, source_target_pairs={{16,0},{0,16},{17,1},{1,17},{18,2},{2,18},{19,3},{3,19},{20,4},{4,... | collective-permute-start | bytes 2752520 | tf_op jit(solution)/shard_map/ppermute | solution.py:59
  31.9 26.0 %collective-permute-start.8 = (bf16[1024,512]{1,0:T(8,128)(2,1)}, bf16[1024,512]{1,0:T(8,128)(2,1)}, u32[]{:S(2)}, u32[]{:S(2)}) collective-permute-start(bf16[1024,512]{1,0:T(8,128)(2,1)} %collective-permute-done.4.refs_4_), channel_id=1, source_target_pairs={{4,0},{8,4},{12,8},{5,1},{9,5},{13,9},{6,2},{10,6},{14,10},{7,3},{... | collective-permute-start | bytes 3145736 | tf_op jit(solution)/shard_map/ppermute | solution.py:121
  33.2 26.0 %collective-permute-start.7 = (bf16[1024,512]{1,0:T(8,128)(2,1)}, bf16[1024,512]{1,0:T(8,128)(2,1)}, u32[]{:S(2)}, u32[]{:S(2)}) collective-permute-start(bf16[1024,512]{1,0:T(8,128)(2,1)} %collective-permute-done.3.refs_3_), channel_id=1, source_target_pairs={{0,4},{4,8},{8,12},{1,5},{5,9},{9,13},{2,6},{6,10},{10,14},{3,7},{... | collective-permute-start | bytes 3145736 | tf_op jit(solution)/shard_map/ppermute | solution.py:120
  38.2 29.7 %collective-permute-start.5 = (bf16[2,64,3584]{2,1,0:T(8,128)(2,1)}, bf16[2,64,3584]{2,1,0:T(8,128)(2,1)S(1)}, u32[]{:S(2)}, u32[]{:S(2)}) collective-permute-start(bf16[2,64,3584]{2,1,0:T(8,128)(2,1)} %get-tuple-element.34.refs_5_), channel_id=1, source_target_pairs={{2,0},{3,1},{0,2},{1,3},{6,4},{7,5},{4,6},{5,7},{10,8},{11,9},{8,1... | collective-permute-start | bytes 2752520 | tf_op jit(solution)/shard_map/ppermute | solution.py:54
  57.9 23.9 %collective-permute-start.13 = (bf16[1024,512]{1,0:T(8,128)(2,1)}, bf16[1024,512]{1,0:T(8,128)(2,1)}, u32[]{:S(2)}, u32[]{:S(2)}) collective-permute-start(bf16[1024,512]{1,0:T(8,128)(2,1)} %collective-permute-done.8.refs_5_), channel_id=1, source_target_pairs={{4,0},{8,4},{12,8},{5,1},{9,5},{13,9},{6,2},{10,6},{14,10},{7,3},{... | collective-permute-start | bytes 3145736 | tf_op jit(solution)/shard_map/ppermute | solution.py:121
  67.7 36.1 %collective-permute-start.9 = (bf16[2,64,3584]{2,1,0:T(8,128)(2,1)}, bf16[2,64,3584]{2,1,0:T(8,128)(2,1)S(1)}, u32[]{:S(2)}, u32[]{:S(2)}) collective-permute-start(bf16[2,64,3584]{2,1,0:T(8,128)(2,1)} %get-tuple-element.38), channel_id=1, source_target_pairs={{2,0},{3,1},{0,2},{1,3},{6,4},{7,5},{4,6},{5,7},{10,8},{11,9},{8,1... | collective-permute-start | bytes 2752520 | tf_op jit(solution)/shard_map/ppermute | solution.py:54
  79.1 26.7 %collective-permute-start.10 = (bf16[2,64,3584]{2,1,0:T(8,128)(2,1)}, bf16[2,64,3584]{2,1,0:T(8,128)(2,1)S(1)}, u32[]{:S(2)}, u32[]{:S(2)}) collective-permute-start(bf16[2,64,3584]{2,1,0:T(8,128)(2,1)} %get-tuple-element.39.refs_10_), channel_id=1, source_target_pairs={{2,0},{3,1},{0,2},{1,3},{6,4},{7,5},{4,6},{5,7},{10,8},{11,9},{8,1... | collective-permute-start | bytes 2752520 | tf_op jit(solution)/shard_map/ppermute | solution.py:54
  79.9 26.0 %collective-permute-start.11 = (bf16[2,64,3584]{2,1,0:T(8,128)(2,1)}, bf16[2,64,3584]{2,1,0:T(8,128)(2,1)S(1)}, u32[]{:S(2)}, u32[]{:S(2)}) collective-permute-start(bf16[2,64,3584]{2,1,0:T(8,128)(2,1)} %get-tuple-element.37.refs_4_), channel_id=1, source_target_pairs={{16,0},{0,16},{17,1},{1,17},{18,2},{2,18},{19,3},{3,19},{20,4},{4,... | collective-permute-start | bytes 2752520 | tf_op jit(solution)/shard_map/ppermute | solution.py:59
  109.2 56.1 %collective-permute-start.15 = (bf16[2,3584,512]{2,1,0:T(8,128)(2,1)}, bf16[2,3584,512]{2,1,0:T(8,128)(2,1)}, u32[]{:S(2)}, u32[]{:S(2)}) collective-permute-start(bf16[2,3584,512]{2,1,0:T(8,128)(2,1)} %get-tuple-element.41.refs_10_.refs_5_.refs_3_), channel_id=1, source_target_pairs={{0,1},{1,0},{2,3},{3,2},{4,5},{5,4},{6,7},{7,6},{8,9},{9,8},{10,11... | collective-permute-start | bytes 22020104 | tf_op jit(solution)/shard_map/ppermute | solution.py:48
  113.7 26.0 %collective-permute-start.17 = (bf16[2,64,3584]{2,1,0:T(8,128)(2,1)}, bf16[2,64,3584]{2,1,0:T(8,128)(2,1)S(1)}, u32[]{:S(2)}, u32[]{:S(2)}) collective-permute-start(bf16[2,64,3584]{2,1,0:T(8,128)(2,1)} %copy-done.9), channel_id=1, source_target_pairs={{16,0},{0,16},{17,1},{1,17},{18,2},{2,18},{19,3},{3,19},{20,4},{4,... | collective-permute-start | bytes 2752520 | tf_op jit(solution)/shard_map/ppermute | solution.py:59
  113.9 26.2 %collective-permute-start.18 = (bf16[2,64,3584]{2,1,0:T(8,128)(2,1)}, bf16[2,64,3584]{2,1,0:T(8,128)(2,1)S(1)}, u32[]{:S(2)}, u32[]{:S(2)}) collective-permute-start(bf16[2,64,3584]{2,1,0:T(8,128)(2,1)} %get-tuple-element.42.refs_11_), channel_id=1, source_target_pairs={{2,0},{3,1},{0,2},{1,3},{6,4},{7,5},{4,6},{5,7},{10,8},{11,9},{8,1... | collective-permute-start | bytes 2752520 | tf_op jit(solution)/shard_map/ppermute | solution.py:54
  135.5 55.2 %collective-permute-start.14 = (bf16[1536,512]{1,0:T(8,128)(2,1)}, bf16[1536,512]{1,0:T(8,128)(2,1)}, u32[]{:S(2)}, u32[]{:S(2)}) collective-permute-start(bf16[1536,512]{1,0:T(8,128)(2,1)} %weigh_rows.4.refs_8_.refs_0_), channel_id=1, source_target_pairs={{4,0},{12,8},{1,5},{9,13},{6,2},{14,10},{3,7},{11,15},{20,16},{28,... | collective-permute-start | bytes 4718600 | tf_op jit(solution)/shard_map/ppermute | solution.py:520
  139.6 43.7 %collective-permute-start.21 = (bf16[2,64,3584]{2,1,0:T(8,128)(2,1)S(1)}, bf16[2,64,3584]{2,1,0:T(8,128)(2,1)}, u32[]{:S(2)}, u32[]{:S(2)}) collective-permute-start(bf16[2,64,3584]{2,1,0:T(8,128)(2,1)S(1)} %copy-done.3), channel_id=1, source_target_pairs={{16,0},{0,16},{17,1},{1,17},{18,2},{2,18},{19,3},{3,19},{20,4},{4,... | collective-permute-start | bytes 2752520 | tf_op jit(solution)/shard_map/ppermute | solution.py:59
  146.4 39.4 %collective-permute-start.23 = (bf16[192,512]{1,0:T(8,128)(2,1)S(1)}, bf16[192,512]{1,0:T(8,128)(2,1)S(1)}, u32[]{:S(2)}, u32[]{:S(2)}) collective-permute-start(bf16[192,512]{1,0:T(8,128)(2,1)S(1)} %pad_maximum_fusion.2), channel_id=1, source_target_pairs={{0,8},{4,12},{8,0},{12,4},{1,9},{5,13},{9,1},{13,5},{2,10},{6,14},... | collective-permute-start | bytes 589832 | tf_op jit(solution)/shard_map/ppermute | solution.py:496
  164.2 32.4 %collective-permute-start.22 = (bf16[2,64,3584]{2,1,0:T(8,128)(2,1)}, bf16[2,64,3584]{2,1,0:T(8,128)(2,1)S(1)}, u32[]{:S(2)}, u32[]{:S(2)}) collective-permute-start(bf16[2,64,3584]{2,1,0:T(8,128)(2,1)} %copy-done.10), channel_id=1, source_target_pairs={{16,0},{0,16},{17,1},{1,17},{18,2},{2,18},{19,3},{3,19},{20,4},{4,... | collective-permute-start | bytes 2752520 | tf_op jit(solution)/shard_map/ppermute | solution.py:59
  165.3 56.2 %collective-permute-start.28 = (bf16[2,64,3584]{2,1,0:T(8,128)(2,1)S(1)}, bf16[2,64,3584]{2,1,0:T(8,128)(2,1)}, u32[]{:S(2)}, u32[]{:S(2)}) collective-permute-start(bf16[2,64,3584]{2,1,0:T(8,128)(2,1)S(1)} %collective-permute-done.20.refs_5_.refs_1_.refs_3_), channel_id=1, source_target_pairs={{16,0},{0,16},{17,1},{1,17},{18,2},{2,18},{19,3},{3,19},{20,4},{4,... | collective-permute-start | bytes 2752520 | tf_op jit(solution)/shard_map/ppermute | solution.py:59
  183.3 38.2 %collective-permute-start.25 = (bf16[1536,512]{1,0:T(8,128)(2,1)}, bf16[1536,512]{1,0:T(8,128)(2,1)}, u32[]{:S(2)}, u32[]{:S(2)}) collective-permute-start(bf16[1536,512]{1,0:T(8,128)(2,1)} %weigh_rows.5.refs_2_.refs_6_.refs_0_), channel_id=1, source_target_pairs={{4,0},{12,8},{1,5},{9,13},{6,2},{14,10},{3,7},{11,15},{20,16},{28,... | collective-permute-start | bytes 4718600 | tf_op jit(solution)/shard_map/ppermute | solution.py:520
  196.6 24.9 %collective-permute-start.19 = (bf16[1024,512]{1,0:T(8,128)(2,1)}, bf16[1024,512]{1,0:T(8,128)(2,1)S(1)}, u32[]{:S(2)}, u32[]{:S(2)}) collective-permute-start(bf16[1024,512]{1,0:T(8,128)(2,1)} %pad_select_fusion), channel_id=1, source_target_pairs={{0,8},{2,10},{5,13},{7,15},{8,0},{10,2},{13,5},{15,7},{16,24},{18,... | collective-permute-start | bytes 3145736 | tf_op jit(solution)/shard_map/ppermute | solution.py:520
  225.8 26.8 %collective-permute-start.31 = (bf16[512,512]{1,0:T(8,128)(2,1)}, bf16[512,512]{1,0:T(8,128)(2,1)S(1)}, u32[]{:S(2)}, u32[]{:S(2)}) collective-permute-start(bf16[512,512]{1,0:T(8,128)(2,1)} %get-tuple-element.55.refs_3_.refs_2_), channel_id=1, source_target_pairs={{0,8},{5,13},{10,2},{15,7},{16,24},{21,29},{26,18},{31,23}} | collective-permute-start | bytes 1572872 | tf_op jit(solution)/shard_map/ppermute | solution.py:520
  226.5 35.0 %collective-permute-start.30 = (bf16[1024,512]{1,0:T(8,128)(2,1)}, bf16[1024,512]{1,0:T(8,128)(2,1)S(1)}, u32[]{:S(2)}, u32[]{:S(2)}) collective-permute-start(bf16[1024,512]{1,0:T(8,128)(2,1)} %get-tuple-element.54.refs_2_.refs_0_), channel_id=1, source_target_pairs={{8,0},{13,5},{2,10},{7,15},{24,16},{29,21},{18,26},{23,31}} | collective-permute-start | bytes 3145736 | tf_op jit(solution)/shard_map/ppermute | solution.py:520
  266.8 24.5 %collective-permute-start.35 = (bf16[1024,512]{1,0:T(8,128)(2,1)}, bf16[1024,512]{1,0:T(8,128)(2,1)S(1)}, u32[]{:S(2)}, u32[]{:S(2)}) collective-permute-start(bf16[1024,512]{1,0:T(8,128)(2,1)} %assemble.2.refs_5_), channel_id=1, source_target_pairs={{0,1},{1,0},{2,3},{3,2},{4,5},{5,4},{6,7},{7,6},{8,9},{9,8},{10,11... | collective-permute-start | bytes 3145736 | tf_op jit(solution)/shard_map/ppermute | solution.py:48
  (46 other events, 500.8 us)

commit v12 on v11

--- a/solution.py
+++ b/solution.py
@@ -359,32 +359,46 @@
     )(*flat, *grads, *extras, *after)
 
 
-def add(values, others, heights, after, price=2):
+def add(values, others, heights, after, price=2, first=None):
     pairs = len(values)
     flat = [h for hs in heights for h in hs]
+    words = [] if first is None else [first]
 
     def kernel(*refs):
-        outs = list(refs[len(refs) - len(flat) :])
+        ins = refs[len(words) :]
+        outs = refs[len(refs) - len(flat) - len(words) :]
+        at_out = 0
         for at in range(pairs):
             top = 0
             for height in heights[at]:
                 rows = slice(top, top + height)
-                outs.pop(0)[...] = (
-                    refs[at][rows].astype(jnp.float32) + refs[pairs + at][rows].astype(jnp.float32)
+                outs[at_out][...] = (
+                    ins[at][rows].astype(jnp.float32) + ins[pairs + at][rows].astype(jnp.float32)
                 ).astype(jnp.bfloat16)
                 top += height
+                at_out += 1
+        for at in range(2 * len(words)):
+
+            @pl.when(refs[0][0] == 1 - at)
+            def _(at=at):
+                outs[-1][: flat[at]] = outs[at][...]
+                if flat[at] < max(flat):
+                    outs[-1][flat[at] :] = jnp.zeros((max(flat) - flat[at], count), jnp.bfloat16)
 
     count = values[0].shape[1]
     whole = pl.BlockSpec(memory_space=pltpu.VMEM)
+    shapes = [jax.ShapeDtypeStruct((h, count), jnp.bfloat16) for h in flat + [max(flat)] * len(words)]
     return pl.pallas_call(
         kernel,
-        out_shape=[jax.ShapeDtypeStruct((h, count), jnp.bfloat16) for h in flat],
-        in_specs=[whole] * (2 * pairs) + [ANYWHERE] * len(after),
-        out_specs=[whole] * len(flat),
+        out_shape=shapes,
+        in_specs=[pl.BlockSpec(memory_space=pltpu.SMEM)] * len(words)
+        + [whole] * (2 * pairs)
+        + [ANYWHERE] * len(after),
+        out_specs=[whole] * len(shapes),
         compiler_params=pltpu.CompilerParams(vmem_limit_bytes=VMEM_BYTES),
         cost_estimate=cost(price),
         name="add_terms",
-    )(*values, *others, *after)
+    )(*words, *values, *others, *after)
 
 
 def assemble(words, count, features, part, near, far, chips, after):
@@ -520,17 +534,15 @@
     return lax.ppermute(value, ("groups", "tensor", "dp"), pairs)
 
 
-def later_steps(values, owners, at_once):
+def exchangeable(owners):
+    if lax.axis_size("tensor") != 4 or len(owners) != 2:
+        return False
+    one, two = hops(owners[0], 2), hops(owners[1], 2)
+    return all(not {x[i] for x in one} & {x[i] for x in two} for i in range(2))
+
+
+def later_steps(values, owners):
     ranks = lax.axis_size("tensor")
-    if at_once and ranks == 4 and len(values) == 2:
-        one, two = hops(owners[0], 2), hops(owners[1], 2)
-        if all(not {x[i] for x in one} & {x[i] for x in two} for i in range(2)):
-            rank, group, place = (lax.axis_index(a) for a in ("tensor", "groups", "dp"))
-            target = jnp.asarray(owners[0], jnp.int32)[group, place]
-            height = max(v.shape[0] for v in values)
-            high = [jnp.pad(v, ((0, height - v.shape[0]), (0, 0))) for v in values]
-            got = send(jnp.where((rank ^ target) & 2 != 0, *high), sorted(one + two))
-            return [(v, got) for v in values]
     ends = []
     for value, owner in zip(values, owners):
         bit, got = 2, None
@@ -643,9 +655,17 @@
     def carry_on(works, after, price=2, at_once=False):
         outs, got, bundles = ([v for work in works for v in work[i]] for i in range(3))
         heights = [[sum(u[0].shape[-2] for u in units) for _, units, _ in b] for b in bundles]
-        sums = list(add(outs, got, heights, after, price))
         routes = [route for b in bundles for route in b]
-        ends = later_steps(sums, [table for table, _, _ in routes], at_once)
+        owners = [table for table, _, _ in routes]
+        if at_once and exchangeable(owners):
+            target = place * rows // features
+            first = ((rank ^ target) & 2 != 0).astype(jnp.int32).reshape(1)
+            *sums, sent = add(outs, got, heights, after, price, first)
+            came = send(sent, sorted(hops(owners[0], 2) + hops(owners[1], 2)))
+            ends = [(v, came) for v in sums]
+        else:
+            sums = list(add(outs, got, heights, after, price))
+            ends = later_steps(sums, owners)
         return sums, [(names, *end) for (_, _, names), end in zip(routes, ends)]
 
     fetch(0)
@@ -692,7 +712,13 @@
         bits[-1],
     )
     first_theirs = terms(first_names, [theirs], [ticks[4]], 24, near=True)
-    (got,) = forward(5, chunks_of([4], others) + [(6, 0)], first_theirs[0], [got])
+    got, *held = forward(
+        5, chunks_of([4], others), first_theirs[0], [got] + [fetched[6, s, 0] for s in range(1, chips)]
+    )
+    for s, value in enumerate(held, 1):
+        fetched[6, s, 0] = value
+        for r in range(1, groups):
+            fetched[6, s, r] = from_group(value, r)
     early = early + got[:width]
     out_parts = jnp.where(high, out_parts[half:], out_parts[:half]) + got[width:]
     for bit in bits[1:-1]:

time: 298 us -> 277 us (0.930)
  waiting for transfers between devices: 36.1 us -> 25.5 us
  starting transfers between devices: 87.7 us -> 79.8 us
    ppermute x8, waiting for transfers between devices: 18.4 us -> 2.11 us  [from_chip(): lax.ppermute(value, 'dp', [((i + step) % size, i) for i in range(size)])]
    ppermute x9, starting transfers between devices: 29.4 us -> 23.6 us  [send(): return lax.ppermute(value, ('groups', 'tensor', 'dp'), pairs)]
  transfers between devices with their start and end apart: 37 -> 37, of which waited for: 8 -> 10; matrix products, arithmetic and copies ran while one was open for 6% -> 5% of each run, Pallas kernels for 44% -> 47%
where the time goes in v12:
time: 277 us; the launch traced here: 275 us
  Pallas kernels  141 us (51%)
  starting transfers between devices  79.8 us (29%)
  waiting for transfers between devices  25.5 us (9%)
  local copies, waits for them, and re-layouts  15.6 us (6%)
  other arithmetic  8.18 us (3%)
  matrix products  3.08 us (1%)
    pallas_call x4, Pallas kernels, weigh(): pl.pallas_call(kernel, grid=(steps,), out_shape=shapes, in_specs=specs +...  57.2 us
    pallas_call x2, Pallas kernels, hidden_part(): pl.pallas_call(kernel, grid_spec=pltpu.PrefetchScalarGridSpec(num_scalar_...  35.4 us
    ppermute x9, starting transfers between devices, send(): return lax.ppermute(value, ('groups', 'tensor', 'dp'), pairs)  23.6 us
    ppermute x3, starting transfers between devices, swap_cores(): return lax.ppermute(value, 'dp', [(i, i ^ 1) for i in range(size)])  23.2 us
    pallas_call x8, Pallas kernels, share_rows(): pl.pallas_call(kernel, grid_spec=pltpu.PrefetchScalarGridSpec(num_scalar_...  15.8 us
    ppermute x3, starting transfers between devices, spread_ranks(): lax.ppermute(below[-1], 'tensor', [(i, i + 1) for i in range(ranks - 1)])  15 us
    unnamed x68, local copies, waits for them, and re-layouts  14.7 us
    pallas_call x1, Pallas kernels, prepare(): pl.pallas_call(kernel, grid=(hidden // tile,), out_shape=[jax.ShapeDtypeS...  11.9 us
  transfers between devices with their start and end apart: 37, of which 10 were waited for; matrix products, arithmetic and copies ran while one was open for 5% of the time, Pallas kernels for 47%

profile of v12, /device:TPU:3, one launch (start us, length us, event | category | flops | bytes accessed | tf_op | source)
XLA Modules:
  0.0 274.8 jit_solution(5278778532682486465)
XLA Ops:
  0.7 2.7 share_rows.8
  6.9 5.1 %collective-permute-start.3 = (bf16[1024,512]{1,0:T(8,128)(2,1)}, bf16[1024,512]{1,0:T(8,128)(2,1)}, u32[]{:S(2)}, u32[]{:S(2)}) collective-permute-start(bf16[1024,512]{1,0:T(8,128)(2,1)} %bitcast.34), channel_id=1, source_target_pairs={{0,4},{4,8},{8,12},{1,5},{5,9},{9,13},{2,6},{6,10},{10,14},{3,7},{... | collective-permute-start | bytes 3145736 | tf_op jit(solution)/shard_map/ppermute | solution.py:120
  13.4 11.9 %prepare.1 = (f32[2,3584,512]{2,1,0:T(8,128)}, f32[64,512]{1,0:T(8,128)}) custom-call(bf16[512,3584]{1,0:T(8,128)(2,1)} %gate_ref.1, bf16[512,3584]{1,0:T(8,128)(2,1)} %up_ref.1, bf16[64,3584]{1,0:T(8,128)(2,1)} %bitcast.43, bf16[2,64,3584]{2,1,0:T(8,128)(2,1)} %get-tuple-element.32.refs_0_), custom_call_target="tpu_custom_call" | custom-call | flops 3240000000 | bytes 1 | tf_op jit(solution)/shard_map/prepare/pallas_call | solution.py:147
  33.2 5.0 %collective-permute-start.7 = (bf16[1024,512]{1,0:T(8,128)(2,1)}, bf16[1024,512]{1,0:T(8,128)(2,1)}, u32[]{:S(2)}, u32[]{:S(2)}) collective-permute-start(bf16[1024,512]{1,0:T(8,128)(2,1)} %collective-permute-done.3.refs_3_), channel_id=1, source_target_pairs={{0,4},{4,8},{8,12},{1,5},{5,9},{9,13},{2,6},{6,10},{10,14},{3,7},{... | collective-permute-start | bytes 3145736 | tf_op jit(solution)/shard_map/ppermute | solution.py:120
  39.3 14.3 %hidden_part.2.refs_4_.refs_7_ = f32[3584,512]{1,0:T(8,128)} custom-call(s32[1]{0:T(128)} %bitcast.6.rank_ref, bf16[3584,4096]{1,0:T(8,128)(2,1)} %refs_1_.16, bf16[3584,4096]{1,0:T(8,128)(2,1)} %refs_1_.16, bf16[1024,512]{1,0:T(8,128)(2,1)} %bitcast.35, bf16[1024,512]{1,0:T(8,128)(2,1)} %collective-permute-done.3.refs_3_, ...), custom_call_target="tpu_custom_call" | custom-call | flops 3240000000 | bytes 1 | tf_op jit(solution)/shard_map/hidden_part/pallas_call | solution.py:272
  59.2 5.0 %collective-permute-start.12 = (bf16[1024,512]{1,0:T(8,128)(2,1)}, bf16[1024,512]{1,0:T(8,128)(2,1)}, u32[]{:S(2)}, u32[]{:S(2)}) collective-permute-start(bf16[1024,512]{1,0:T(8,128)(2,1)} %collective-permute-done.7.refs_4_.refs_2_), channel_id=1, source_target_pairs={{0,4},{4,8},{8,12},{1,5},{5,9},{9,13},{2,6},{6,10},{10,14},{3,7},{... | collective-permute-start | bytes 3145736 | tf_op jit(solution)/shard_map/ppermute | solution.py:120
  67.9 8.2 %collective-permute-done.6.refs_3_.refs_8_ = bf16[2,64,3584]{2,1,0:T(8,128)(2,1)S(1)} collective-permute-done((bf16[2,64,3584]{2,1,0:T(8,128)(2,1)}, bf16[2,64,3584]{2,1,0:T(8,128)(2,1)S(1)}, u32[]{:S(2)}, u32[]{:S(2)}) %collective-permute-start.6) | collective-permute-done | bytes 917536 | tf_op jit(solution)/shard_map/ppermute | solution.py:59
  82.7 21.0 %hidden_part.3 = (bf16[2,3584,512]{2,1,0:T(8,128)(2,1)}, f32[64,512]{1,0:T(8,128)}) custom-call(s32[1]{0:T(128)} %bitcast.6.rank_ref, bf16[3584,4096]{1,0:T(8,128)(2,1)} %refs_1_.16, bf16[3584,4096]{1,0:T(8,128)(2,1)} %refs_1_.16, bf16[1024,512]{1,0:T(8,128)(2,1)} %collective-permute-done.7.refs_4_.refs_2_, ...), custom_call_target="tpu_custom_call" | custom-call | flops 3240000000 | bytes 1 | tf_op jit(solution)/shard_map/hidden_part/pallas_call | solution.py:272
  109.2 4.5 %collective-permute-start.15 = (bf16[2,3584,512]{2,1,0:T(8,128)(2,1)}, bf16[2,3584,512]{2,1,0:T(8,128)(2,1)}, u32[]{:S(2)}, u32[]{:S(2)}) collective-permute-start(bf16[2,3584,512]{2,1,0:T(8,128)(2,1)} %get-tuple-element.43.refs_10_.refs_5_.refs_3_), channel_id=1, source_target_pairs={{0,1},{1,0},{2,3},{3,2},{4,5},{5,4},{6,7},{7,6},{8,9},{9,8},{10,11... | collective-permute-start | bytes 22020104 | tf_op jit(solution)/shard_map/ppermute | solution.py:48
  116.5 17.6 %weigh_rows.4.refs_8_.refs_1_ = bf16[1536,512]{1,0:T(8,128)(2,1)} custom-call(bf16[1024,3584]{1,0:T(8,128)(2,1)} %refs_0_.21, bf16[1024,3584]{1,0:T(8,128)(2,1)} %refs_1_.21, bf16[2,64,3584]{2,1,0:T(8,128)(2,1)} %get-tuple-element.34.refs_2_, bf16[2,64,3584]{2,1,0:T(8,128)(2,1)} %get-tuple-element.37.refs_3_, ...), custom_call_target="tpu_custom_call" | custom-call | flops 6480000000 | bytes 1 | tf_op jit(solution)/shard_map/weigh_rows/pallas_call | solution.py:349
  134.1 4.3 %collective-permute-start.14 = (bf16[1536,512]{1,0:T(8,128)(2,1)}, bf16[1536,512]{1,0:T(8,128)(2,1)}, u32[]{:S(2)}, u32[]{:S(2)}) collective-permute-start(bf16[1536,512]{1,0:T(8,128)(2,1)} %weigh_rows.4.refs_8_.refs_1_), channel_id=1, source_target_pairs={{4,0},{12,8},{1,5},{9,13},{6,2},{14,10},{3,7},{11,15},{20,16},{28,... | collective-permute-start | bytes 4718600 | tf_op jit(solution)/shard_map/ppermute | solution.py:534
  148.5 17.7 %weigh_rows.5.refs_3_.refs_6_.refs_0_ = bf16[1536,512]{1,0:T(8,128)(2,1)} custom-call(bf16[1024,3584]{1,0:T(8,128)(2,1)} %refs_0_.21, bf16[1024,3584]{1,0:T(8,128)(2,1)} %refs_1_.21, bf16[2,64,3584]{2,1,0:T(8,128)(2,1)} %get-tuple-element.34.refs_2_, bf16[2,64,3584]{2,1,0:T(8,128)(2,1)} %get-tuple-element.37.refs_3_, ...), custom_call_target="tpu_custom_call" | custom-call | flops 6480000000 | bytes 1 | tf_op jit(solution)/shard_map/weigh_rows/pallas_call | solution.py:349
  170.9 2.4 collective-permute-start.25
  174.8 3.8 %add_terms.4 = (bf16[1024,512]{1,0:T(8,128)(2,1)}, bf16[512,512]{1,0:T(8,128)(2,1)}, bf16[1024,512]{1,0:T(8,128)(2,1)}) custom-call(s32[1]{0:T(128)} %bitcast.4.refs_0_, bf16[1536,512]{1,0:T(8,128)(2,1)} %weigh_rows.4.refs_8_.refs_1_, bf16[1536,512]{1,0:T(8,128)(2,1)} %collective-permute-done.14.refs_2_, bf16[1536,512]{1,0:T(8,128)(2,1)} %weigh_rows.5.refs_3_.refs_6_.refs_0_), custom_call_target="tpu_custom_call" | custom-call | flops 540000000 | bytes 1 | tf_op jit(solution)/shard_map/add_terms/pallas_call | solution.py:391
  180.8 11.8 %weigh_rows.6.refs_4_.refs_0_ = bf16[320,1024]{1,0:T(8,128)(2,1)} custom-call(bf16[2,64,3584]{2,1,0:T(8,128)(2,1)} %copy-done.10, bf16[2,64,3584]{2,1,0:T(8,128)(2,1)} %get-tuple-element.54.refs_1_.refs_3_, bf16[2,64,3584]{2,1,0:T(8,128)(2,1)} %copy-done.15, bf16[2,64,3584]{2,1,0:T(8,128)(2,1)} %collective-permute-done.22.refs_4_.refs_3_, ...), custom_call_target="tpu_custom_call" | custom-call | flops 4320000000 | bytes 1 | tf_op jit(solution)/shard_map/weigh_rows/pallas_call | solution.py:349
  197.0 5.1 %collective-permute-start.24 = (bf16[320,1024]{1,0:T(8,128)(2,1)}, bf16[320,1024]{1,0:T(8,128)(2,1)}, u32[]{:S(2)}, u32[]{:S(2)}) collective-permute-start(bf16[320,1024]{1,0:T(8,128)(2,1)} %weigh_rows.6.refs_4_.refs_0_), channel_id=1, source_target_pairs={{4,0},{12,8},{1,5},{9,13},{6,2},{14,10},{3,7},{11,15},{20,16},{28,... | collective-permute-start | bytes 1966088 | tf_op jit(solution)/shard_map/ppermute | solution.py:534
  203.6 3.3 %add_terms.5 = (bf16[1024,512]{1,0:T(8,128)(2,1)}, bf16[512,512]{1,0:T(8,128)(2,1)}) custom-call(bf16[1536,512]{1,0:T(8,128)(2,1)} %weigh_rows.5.refs_3_.refs_6_.refs_0_, bf16[1536,512]{1,0:T(8,128)(2,1)} %collective-permute-done.25.refs_1_, f32[8,128]{1,0:T(8,128)} %get-tuple-element.57.refs_2_, ...), custom_call_target="tpu_custom_call" | custom-call | flops 540000000 | bytes 1 | tf_op jit(solution)/shard_map/add_terms/pallas_call | solution.py:391
  213.5 10.2 %weigh_rows.7.refs_0_ = bf16[192,1024]{1,0:T(8,128)(2,1)} custom-call(bf16[2,64,3584]{2,1,0:T(8,128)(2,1)} %get-tuple-element.60.refs_0_, bf16[2,64,3584]{2,1,0:T(8,128)(2,1)} %collective-permute-done.28.refs_5_.refs_1_, bf16[2,64,3584]{2,1,0:T(8,128)(2,1)} %collective-permute-done.32.refs_2_, ...), custom_call_target="tpu_custom_call" | custom-call | flops 16200000512 | bytes 1 | tf_op jit(solution)/shard_map/weigh_rows/pallas_call | solution.py:349
  223.7 7.4 %collective-permute-start.33 = (bf16[192,1024]{1,0:T(8,128)(2,1)}, bf16[192,1024]{1,0:T(8,128)(2,1)S(1)}, u32[]{:S(2)}, u32[]{:S(2)}) collective-permute-start(bf16[192,1024]{1,0:T(8,128)(2,1)} %weigh_rows.7.refs_0_), channel_id=1, source_target_pairs={{4,0},{12,8},{1,5},{9,13},{6,2},{14,10},{3,7},{11,15},{20,16},{28,... | collective-permute-start | bytes 1179656 | tf_op jit(solution)/shard_map/ppermute | solution.py:534
  231.2 5.6 %collective-permute-done.33.refs_1_ = bf16[192,1024]{1,0:T(8,128)(2,1)S(1)} collective-permute-done((bf16[192,1024]{1,0:T(8,128)(2,1)}, bf16[192,1024]{1,0:T(8,128)(2,1)S(1)}, u32[]{:S(2)}, u32[]{:S(2)}) %collective-permute-start.33) | collective-permute-done | bytes 393248 | tf_op jit(solution)/shard_map/ppermute | solution.py:534
  242.5 3.5 %assemble.2.refs_5_ = bf16[1024,512]{1,0:T(8,128)(2,1)} custom-call(s32[4]{0:T(128)} %pad_add_fusion.words_ref, bf16[1024,512]{1,0:T(8,128)(2,1)} %get-tuple-element.58.refs_2_.refs_0_, bf16[1024,512]{1,0:T(8,128)(2,1)} %copy-done.21, bf16[512,512]{1,0:T(8,128)(2,1)} %get-tuple-element.59.refs_3_.refs_2_, bf16[512,512]{1,0:T(8,128)(2,1)} %copy-done.16, ...), custom_call_target="tpu_custom_call" | custom-call | flops 1350000000 | bytes 1 | tf_op jit(solution)/shard_map/assemble/pallas_call | solution.py:455
  246.0 18.7 %collective-permute-start.35 = (bf16[1024,512]{1,0:T(8,128)(2,1)}, bf16[1024,512]{1,0:T(8,128)(2,1)S(1)}, u32[]{:S(2)}, u32[]{:S(2)}) collective-permute-start(bf16[1024,512]{1,0:T(8,128)(2,1)} %assemble.2.refs_5_), channel_id=1, source_target_pairs={{0,1},{1,0},{2,3},{3,2},{4,5},{5,4},{6,7},{7,6},{8,9},{9,8},{10,11... | collective-permute-start | bytes 3145736 | tf_op jit(solution)/shard_map/ppermute | solution.py:48
  267.4 3.3 %assemble.3.mine_ref = bf16[1024,512]{1,0:T(8,128)(2,1)} custom-call(s32[4]{0:T(128)} %pad_add_fusion.words_ref, bf16[1024,512]{1,0:T(8,128)(2,1)} %get-tuple-element.48.refs_8_.refs_0_, bf16[1024,512]{1,0:T(8,128)(2,1)} %collective-permute-done.19.refs_3_.refs_4_.refs_1_, bf16[512,512]{1,0:T(8,128)(2,1)} %get-tuple-element.50.refs_9_.refs_2_, ...), custom_call_target="tpu_custom_call" | custom-call | flops 1350000000 | bytes 1 | tf_op jit(solution)/shard_map/assemble/pallas_call | solution.py:455
  271.8 3.0 %finish.1 = bf16[512,1024]{1,0:T(8,128)(2,1)} custom-call(s32[4]{0:T(128)} %pad_add_fusion.words_ref, bf16[1024,512]{1,0:T(8,128)(2,1)} %assemble.3.mine_ref, bf16[1024,512]{1,0:T(8,128)(2,1)} %copy-done.22, bf16[192,512]{1,0:T(8,128)(2,1)} %get-tuple-element.65.late_mine_ref, bf16[192,512]{1,0:T(8,128)(2,1)} %copy-done.27), custom_call_target="tpu_custom_call" | custom-call | flops 810000000 | bytes 1 | tf_op jit(solution)/shard_map/finish/pallas_call | solution.py:496
  (168 shorter events, 78.4 us)
Async XLA Ops:
  5.6 26.3 %collective-permute-start.4 = (bf16[1024,512]{1,0:T(8,128)(2,1)}, bf16[1024,512]{1,0:T(8,128)(2,1)}, u32[]{:S(2)}, u32[]{:S(2)}) collective-permute-start(bf16[1024,512]{1,0:T(8,128)(2,1)} %bitcast.33), channel_id=1, source_target_pairs={{4,0},{8,4},{12,8},{5,1},{9,5},{13,9},{6,2},{10,6},{14,10},{7,3},{... | collective-permute-start | bytes 3145736 | tf_op jit(solution)/shard_map/ppermute | solution.py:121
  6.9 26.3 %collective-permute-start.3 = (bf16[1024,512]{1,0:T(8,128)(2,1)}, bf16[1024,512]{1,0:T(8,128)(2,1)}, u32[]{:S(2)}, u32[]{:S(2)}) collective-permute-start(bf16[1024,512]{1,0:T(8,128)(2,1)} %bitcast.34), channel_id=1, source_target_pairs={{0,4},{4,8},{8,12},{1,5},{5,9},{9,13},{2,6},{6,10},{10,14},{3,7},{... | collective-permute-start | bytes 3145736 | tf_op jit(solution)/shard_map/ppermute | solution.py:120
  12.0 41.7 %collective-permute-start.1 = (bf16[2,64,3584]{2,1,0:T(8,128)(2,1)}, bf16[2,64,3584]{2,1,0:T(8,128)(2,1)}, u32[]{:S(2)}, u32[]{:S(2)}) collective-permute-start(bf16[2,64,3584]{2,1,0:T(8,128)(2,1)} %get-tuple-element.35), channel_id=1, source_target_pairs={{2,0},{3,1},{0,2},{1,3},{6,4},{7,5},{4,6},{5,7},{10,8},{11,9},{8,1... | collective-permute-start | bytes 2752520 | tf_op jit(solution)/shard_map/ppermute | solution.py:54
  28.3 25.4 %collective-permute-start.2 = (bf16[2,64,3584]{2,1,0:T(8,128)(2,1)}, bf16[2,64,3584]{2,1,0:T(8,128)(2,1)S(1)}, u32[]{:S(2)}, u32[]{:S(2)}) collective-permute-start(bf16[2,64,3584]{2,1,0:T(8,128)(2,1)} %get-tuple-element.34.refs_2_), channel_id=1, source_target_pairs={{16,0},{0,16},{17,1},{1,17},{18,2},{2,18},{19,3},{3,19},{20,4},{4,... | collective-permute-start | bytes 2752520 | tf_op jit(solution)/shard_map/ppermute | solution.py:59
  31.9 26.0 %collective-permute-start.8 = (bf16[1024,512]{1,0:T(8,128)(2,1)}, bf16[1024,512]{1,0:T(8,128)(2,1)}, u32[]{:S(2)}, u32[]{:S(2)}) collective-permute-start(bf16[1024,512]{1,0:T(8,128)(2,1)} %collective-permute-done.4.refs_4_), channel_id=1, source_target_pairs={{4,0},{8,4},{12,8},{5,1},{9,5},{13,9},{6,2},{10,6},{14,10},{7,3},{... | collective-permute-start | bytes 3145736 | tf_op jit(solution)/shard_map/ppermute | solution.py:121
  33.2 26.0 %collective-permute-start.7 = (bf16[1024,512]{1,0:T(8,128)(2,1)}, bf16[1024,512]{1,0:T(8,128)(2,1)}, u32[]{:S(2)}, u32[]{:S(2)}) collective-permute-start(bf16[1024,512]{1,0:T(8,128)(2,1)} %collective-permute-done.3.refs_3_), channel_id=1, source_target_pairs={{0,4},{4,8},{8,12},{1,5},{5,9},{9,13},{2,6},{6,10},{10,14},{3,7},{... | collective-permute-start | bytes 3145736 | tf_op jit(solution)/shard_map/ppermute | solution.py:120
  38.2 29.7 %collective-permute-start.5 = (bf16[2,64,3584]{2,1,0:T(8,128)(2,1)}, bf16[2,64,3584]{2,1,0:T(8,128)(2,1)S(1)}, u32[]{:S(2)}, u32[]{:S(2)}) collective-permute-start(bf16[2,64,3584]{2,1,0:T(8,128)(2,1)} %get-tuple-element.36.refs_5_), channel_id=1, source_target_pairs={{2,0},{3,1},{0,2},{1,3},{6,4},{7,5},{4,6},{5,7},{10,8},{11,9},{8,1... | collective-permute-start | bytes 2752520 | tf_op jit(solution)/shard_map/ppermute | solution.py:54
  67.7 36.1 %collective-permute-start.9 = (bf16[2,64,3584]{2,1,0:T(8,128)(2,1)}, bf16[2,64,3584]{2,1,0:T(8,128)(2,1)S(1)}, u32[]{:S(2)}, u32[]{:S(2)}) collective-permute-start(bf16[2,64,3584]{2,1,0:T(8,128)(2,1)} %get-tuple-element.40), channel_id=1, source_target_pairs={{2,0},{3,1},{0,2},{1,3},{6,4},{7,5},{4,6},{5,7},{10,8},{11,9},{8,1... | collective-permute-start | bytes 2752520 | tf_op jit(solution)/shard_map/ppermute | solution.py:54
  79.1 26.7 %collective-permute-start.10 = (bf16[2,64,3584]{2,1,0:T(8,128)(2,1)}, bf16[2,64,3584]{2,1,0:T(8,128)(2,1)S(1)}, u32[]{:S(2)}, u32[]{:S(2)}) collective-permute-start(bf16[2,64,3584]{2,1,0:T(8,128)(2,1)} %get-tuple-element.41.refs_10_), channel_id=1, source_target_pairs={{2,0},{3,1},{0,2},{1,3},{6,4},{7,5},{4,6},{5,7},{10,8},{11,9},{8,1... | collective-permute-start | bytes 2752520 | tf_op jit(solution)/shard_map/ppermute | solution.py:54
  79.9 26.0 %collective-permute-start.11 = (bf16[2,64,3584]{2,1,0:T(8,128)(2,1)}, bf16[2,64,3584]{2,1,0:T(8,128)(2,1)S(1)}, u32[]{:S(2)}, u32[]{:S(2)}) collective-permute-start(bf16[2,64,3584]{2,1,0:T(8,128)(2,1)} %get-tuple-element.39.refs_4_), channel_id=1, source_target_pairs={{16,0},{0,16},{17,1},{1,17},{18,2},{2,18},{19,3},{3,19},{20,4},{4,... | collective-permute-start | bytes 2752520 | tf_op jit(solution)/shard_map/ppermute | solution.py:59
  109.2 39.0 %collective-permute-start.15 = (bf16[2,3584,512]{2,1,0:T(8,128)(2,1)}, bf16[2,3584,512]{2,1,0:T(8,128)(2,1)}, u32[]{:S(2)}, u32[]{:S(2)}) collective-permute-start(bf16[2,3584,512]{2,1,0:T(8,128)(2,1)} %get-tuple-element.43.refs_10_.refs_5_.refs_3_), channel_id=1, source_target_pairs={{0,1},{1,0},{2,3},{3,2},{4,5},{5,4},{6,7},{7,6},{8,9},{9,8},{10,11... | collective-permute-start | bytes 22020104 | tf_op jit(solution)/shard_map/ppermute | solution.py:48
  113.6 24.8 %collective-permute-start.17 = (bf16[2,64,3584]{2,1,0:T(8,128)(2,1)}, bf16[2,64,3584]{2,1,0:T(8,128)(2,1)S(1)}, u32[]{:S(2)}, u32[]{:S(2)}) collective-permute-start(bf16[2,64,3584]{2,1,0:T(8,128)(2,1)} %copy-done.9), channel_id=1, source_target_pairs={{16,0},{0,16},{17,1},{1,17},{18,2},{2,18},{19,3},{3,19},{20,4},{4,... | collective-permute-start | bytes 2752520 | tf_op jit(solution)/shard_map/ppermute | solution.py:59
  113.9 24.9 %collective-permute-start.18 = (bf16[2,64,3584]{2,1,0:T(8,128)(2,1)}, bf16[2,64,3584]{2,1,0:T(8,128)(2,1)S(1)}, u32[]{:S(2)}, u32[]{:S(2)}) collective-permute-start(bf16[2,64,3584]{2,1,0:T(8,128)(2,1)} %get-tuple-element.44.refs_11_), channel_id=1, source_target_pairs={{2,0},{3,1},{0,2},{1,3},{6,4},{7,5},{4,6},{5,7},{10,8},{11,9},{8,1... | collective-permute-start | bytes 2752520 | tf_op jit(solution)/shard_map/ppermute | solution.py:54
  134.1 40.1 %collective-permute-start.14 = (bf16[1536,512]{1,0:T(8,128)(2,1)}, bf16[1536,512]{1,0:T(8,128)(2,1)}, u32[]{:S(2)}, u32[]{:S(2)}) collective-permute-start(bf16[1536,512]{1,0:T(8,128)(2,1)} %weigh_rows.4.refs_8_.refs_1_), channel_id=1, source_target_pairs={{4,0},{12,8},{1,5},{9,13},{6,2},{14,10},{3,7},{11,15},{20,16},{28,... | collective-permute-start | bytes 4718600 | tf_op jit(solution)/shard_map/ppermute | solution.py:534
  138.4 27.8 %collective-permute-start.22 = (bf16[2,64,3584]{2,1,0:T(8,128)(2,1)S(1)}, bf16[2,64,3584]{2,1,0:T(8,128)(2,1)}, u32[]{:S(2)}, u32[]{:S(2)}) collective-permute-start(bf16[2,64,3584]{2,1,0:T(8,128)(2,1)S(1)} %copy-done.4), channel_id=1, source_target_pairs={{16,0},{0,16},{17,1},{1,17},{18,2},{2,18},{19,3},{3,19},{20,4},{4,... | collective-permute-start | bytes 2752520 | tf_op jit(solution)/shard_map/ppermute | solution.py:59
  142.0 24.2 %collective-permute-start.21 = (bf16[2,64,3584]{2,1,0:T(8,128)(2,1)}, bf16[2,64,3584]{2,1,0:T(8,128)(2,1)S(1)}, u32[]{:S(2)}, u32[]{:S(2)}) collective-permute-start(bf16[2,64,3584]{2,1,0:T(8,128)(2,1)} %get-tuple-element.47.refs_11_), channel_id=1, source_target_pairs={{2,0},{3,1},{0,2},{1,3},{6,4},{7,5},{4,6},{5,7},{10,8},{11,9},{8,1... | collective-permute-start | bytes 2752520 | tf_op jit(solution)/shard_map/ppermute | solution.py:54
  148.2 31.0 %collective-permute-start.23 = (bf16[2,64,3584]{2,1,0:T(8,128)(2,1)}, bf16[2,64,3584]{2,1,0:T(8,128)(2,1)}, u32[]{:S(2)}, u32[]{:S(2)}) collective-permute-start(bf16[2,64,3584]{2,1,0:T(8,128)(2,1)} %copy-done.10), channel_id=1, source_target_pairs={{16,0},{0,16},{17,1},{1,17},{18,2},{2,18},{19,3},{3,19},{20,4},{4,... | collective-permute-start | bytes 2752520 | tf_op jit(solution)/shard_map/ppermute | solution.py:59
  169.9 25.0 %collective-permute-start.27 = (bf16[2,64,3584]{2,1,0:T(8,128)(2,1)}, bf16[2,64,3584]{2,1,0:T(8,128)(2,1)S(1)}, u32[]{:S(2)}, u32[]{:S(2)}) collective-permute-start(bf16[2,64,3584]{2,1,0:T(8,128)(2,1)} %get-tuple-element.55.refs_7_), channel_id=1, source_target_pairs={{2,0},{3,1},{0,2},{1,3},{6,4},{7,5},{4,6},{5,7},{10,8},{11,9},{8,1... | collective-permute-start | bytes 2752520 | tf_op jit(solution)/shard_map/ppermute | solution.py:54
  170.9 32.7 %collective-permute-start.25 = (bf16[1536,512]{1,0:T(8,128)(2,1)S(1)}, bf16[1536,512]{1,0:T(8,128)(2,1)}, u32[]{:S(2)}, u32[]{:S(2)}) collective-permute-start(bf16[1536,512]{1,0:T(8,128)(2,1)S(1)} %copy-done.2), channel_id=1, source_target_pairs={{4,0},{12,8},{1,5},{9,13},{6,2},{14,10},{3,7},{11,15},{20,16},{28,... | collective-permute-start | bytes 4718600 | tf_op jit(solution)/shard_map/ppermute | solution.py:534
  174.3 29.3 %collective-permute-start.28 = (bf16[2,64,3584]{2,1,0:T(8,128)(2,1)}, bf16[2,64,3584]{2,1,0:T(8,128)(2,1)}, u32[]{:S(2)}, u32[]{:S(2)}) collective-permute-start(bf16[2,64,3584]{2,1,0:T(8,128)(2,1)} %get-tuple-element.54.refs_1_.refs_3_), channel_id=1, source_target_pairs={{16,0},{0,16},{17,1},{1,17},{18,2},{2,18},{19,3},{3,19},{20,4},{4,... | collective-permute-start | bytes 2752520 | tf_op jit(solution)/shard_map/ppermute | solution.py:59
  179.2 24.4 %collective-permute-start.19 = (bf16[1024,512]{1,0:T(8,128)(2,1)}, bf16[1024,512]{1,0:T(8,128)(2,1)}, u32[]{:S(2)}, u32[]{:S(2)}) collective-permute-start(bf16[1024,512]{1,0:T(8,128)(2,1)} %get-tuple-element.49), channel_id=1, source_target_pairs={{0,8},{2,10},{5,13},{7,15},{8,0},{10,2},{13,5},{15,7},{16,24},{18,... | collective-permute-start | bytes 3145736 | tf_op jit(solution)/shard_map/ppermute | solution.py:534
  206.9 24.2 %collective-permute-start.31 = (bf16[512,512]{1,0:T(8,128)(2,1)}, bf16[512,512]{1,0:T(8,128)(2,1)S(1)}, u32[]{:S(2)}, u32[]{:S(2)}) collective-permute-start(bf16[512,512]{1,0:T(8,128)(2,1)} %get-tuple-element.59.refs_3_.refs_2_), channel_id=1, source_target_pairs={{0,8},{5,13},{10,2},{15,7},{16,24},{21,29},{26,18},{31,23}} | collective-permute-start | bytes 1572872 | tf_op jit(solution)/shard_map/ppermute | solution.py:534
  207.6 33.1 %collective-permute-start.30 = (bf16[1024,512]{1,0:T(8,128)(2,1)}, bf16[1024,512]{1,0:T(8,128)(2,1)S(1)}, u32[]{:S(2)}, u32[]{:S(2)}) collective-permute-start(bf16[1024,512]{1,0:T(8,128)(2,1)} %get-tuple-element.58.refs_2_.refs_0_), channel_id=1, source_target_pairs={{8,0},{13,5},{2,10},{7,15},{24,16},{29,21},{18,26},{23,31}} | collective-permute-start | bytes 3145736 | tf_op jit(solution)/shard_map/ppermute | solution.py:534
  246.0 24.7 %collective-permute-start.35 = (bf16[1024,512]{1,0:T(8,128)(2,1)}, bf16[1024,512]{1,0:T(8,128)(2,1)S(1)}, u32[]{:S(2)}, u32[]{:S(2)}) collective-permute-start(bf16[1024,512]{1,0:T(8,128)(2,1)} %assemble.2.refs_5_), channel_id=1, source_target_pairs={{0,1},{1,0},{2,3},{3,2},{4,5},{5,4},{6,7},{7,6},{8,9},{9,8},{10,11... | collective-permute-start | bytes 3145736 | tf_op jit(solution)/shard_map/ppermute | solution.py:48
  (46 other events, 488.8 us)

commit v13 on v12

--- a/solution.py
+++ b/solution.py
@@ -401,7 +401,7 @@
     )(*words, *values, *others, *after)
 
 
-def assemble(words, count, features, part, near, far, chips, after):
+def assemble(words, count, features, part, near, far, chips, after, cuts):
     groups = lax.axis_size("groups")
     height = near[0][0].shape[0]
     tall = features // part
@@ -416,9 +416,10 @@
     near_at = [[at_of(v) for v in pair] for pair in near]
     far_at = {n: (row, [at_of(v) for v in pair], first) for n, (row, pair, first) in far.items()}
     edges = chunk_edges(part)
+    height_out = features // cuts
 
     def kernel(words_ref, *refs):
-        out = refs[-1]
+        outs = refs[-cuts:]
         away, group, inside = words_ref[0], words_ref[1], words_ref[2]
 
         def total(pair, rows, cols):
@@ -429,7 +430,10 @@
 
             @pl.when((away == 0) & (inside == j * height))
             def _(j=j):
-                out[...] = total(near_at[j], slice(0, height), slice(0, count))
+                for at, out in enumerate(outs):
+                    out[...] = total(
+                        near_at[j], slice(at * height_out, (at + 1) * height_out), slice(0, count)
+                    )
 
         for s in range(1, chips):
             for g in range(groups):
@@ -449,35 +453,45 @@
                                     )
                                 else:
                                     value = jnp.zeros((piece, count), jnp.bfloat16)
-                                out[top : top + piece] = value
+                                at = top % height_out
+                                outs[top // height_out][at : at + piece] = value
 
     whole = pl.BlockSpec(memory_space=pltpu.VMEM)
     return pl.pallas_call(
         kernel,
-        out_shape=jax.ShapeDtypeStruct((features, count), jnp.bfloat16),
+        out_shape=[jax.ShapeDtypeStruct((height_out, count), jnp.bfloat16)] * cuts,
         in_specs=[pl.BlockSpec(memory_space=pltpu.SMEM)]
         + [whole] * len(arrays)
         + [ANYWHERE] * len(after),
-        out_specs=whole,
+        out_specs=[whole] * cuts,
         compiler_params=pltpu.CompilerParams(vmem_limit_bytes=VMEM_BYTES),
-        cost_estimate=cost(5),
+        cost_estimate=cost(1),
         name="assemble",
     )(words, *arrays, *after)
 
 
 def finish(words, part, mine, theirs, late_mine, late_theirs, late, chips):
-    features, count = mine.shape
+    count = mine[0].shape[1]
+    features = sum(m.shape[0] for m in mine)
     groups = lax.axis_size("groups")
     tall = features // part
     edges = chunk_edges(part)
 
-    def kernel(words_ref, mine_ref, theirs_ref, late_mine_ref, late_theirs_ref, out_ref, rows_ref):
+    def kernel(words_ref, *refs):
+        mine_refs, theirs_refs = refs[: len(mine)], refs[len(mine) : len(mine) + len(theirs)]
+        late_mine_ref, late_theirs_ref, out_ref, rows_ref = refs[-4:]
         away, group, inside = words_ref[0], words_ref[1], words_ref[2]
-        for own, base, extra in ((1, mine_ref, late_mine_ref), (0, theirs_ref, late_theirs_ref)):
+        for own, bases, extra in (
+            (1, mine_refs, late_mine_ref),
+            (0, theirs_refs, late_theirs_ref),
+        ):
 
             @pl.when(words_ref[3] == own)
-            def _(base=base, extra=extra):
-                rows_ref[...] = base[...]
+            def _(bases=bases, extra=extra):
+                first = 0
+                for base in bases:
+                    rows_ref[first : first + base.shape[0]] = base[...]
+                    first += base.shape[0]
                 for g in range(groups):
                     for h in range(0, groups, tall):
 
@@ -493,16 +507,17 @@
 
         out_ref[...] = rows_ref[...].T
 
+    whole = pl.BlockSpec(memory_space=pltpu.VMEM)
     return pl.pallas_call(
         kernel,
-        out_shape=jax.ShapeDtypeStruct((count, features), mine.dtype),
-        in_specs=[pl.BlockSpec(memory_space=pltpu.SMEM)] + [pl.BlockSpec(memory_space=pltpu.VMEM)] * 4,
-        out_specs=pl.BlockSpec(memory_space=pltpu.VMEM),
-        scratch_shapes=[pltpu.VMEM((features, count), mine.dtype)],
+        out_shape=jax.ShapeDtypeStruct((count, features), jnp.bfloat16),
+        in_specs=[pl.BlockSpec(memory_space=pltpu.SMEM)] + [whole] * (len(mine) + len(theirs) + 2),
+        out_specs=whole,
+        scratch_shapes=[pltpu.VMEM((features, count), jnp.bfloat16)],
         compiler_params=pltpu.CompilerParams(vmem_limit_bytes=VMEM_BYTES),
         cost_estimate=cost(3),
         name="finish",
-    )(words, mine, theirs, late_mine, late_theirs)
+    )(words, *mine, *theirs, late_mine, late_theirs)
 
 
 def exchange(value, bit):
@@ -767,7 +782,7 @@
 
     words = jnp.stack([away, group, inside, owner]).astype(jnp.int32)
 
-    def assembled(end, first, after):
+    def assembled(end, first, after, cuts):
         near = [pair for names, *pair in end if names is None]
         far = {}
         for names, *pair in end:
@@ -775,12 +790,11 @@
                 far.update((n, (row, pair, 0)) for row, n in tops(names))
         for names, *pair in end_second:
             far.update((n, (row, pair, first)) for row, n in tops(names))
-        return assemble(words, count, features, part, near, far, chips, after)
-
-    received = [got for _, _, got in end_last]
-    total_theirs = assembled(end_theirs, count, received)
-    total_mine = assembled(end_mine, 0, [total_theirs])
-    from_partner = swap_cores(total_theirs)
+        return assemble(words, count, features, part, near, far, chips, after, cuts)
+
+    total_theirs = assembled(end_theirs, count, sums_last, 2)
+    total_mine = assembled(end_mine, 0, total_theirs, 1)
+    from_partner = [swap_cores(v) for v in total_theirs]
 
     def pick(index, options):
         value = options[0]
@@ -789,8 +803,13 @@
         return value
 
     tail = {}
-    for names, value, got in end_last:
-        value = (value.astype(jnp.float32) + got.astype(jnp.float32)).astype(jnp.bfloat16)
+    settled = add(
+        [v for _, v, _ in end_last],
+        [got for _, _, got in end_last],
+        [[v.shape[0]] for _, v, _ in end_last],
+        total_mine,
+    )
+    for (names, _, _), value in zip(end_last, settled):
         tail.update(
             (n, value[row : row + edges[n[0] + 1] - edges[n[0]]]) for row, n in tops(names)
         )

time: 277 us -> 271 us (0.978)
  starting transfers between devices: 79.8 us -> 73.4 us
    ppermute x3 -> x4, starting transfers between devices: 23.2 us -> 16.6 us  [swap_cores(): return lax.ppermute(value, 'dp', [(i, i ^ 1) for i in range(size)])]
    pallas_call x4 -> x5, Pallas kernels: 11.3 us -> 13.3 us  [add(): pl.pallas_call(kernel, out_shape=shapes, in_specs=[pl.BlockSpec(memory_sp...]
    unnamed x68 -> x74, local copies, waits for them, and re-layouts: 14.7 us -> 15.5 us
  transfers between devices with their start and end apart: 37 -> 38, of which waited for: 10 -> 10; matrix products, arithmetic and copies ran while one was open for 5% -> 5% of each run, Pallas kernels for 47% -> 50%
where the time goes in v13:
time: 271 us; the launch traced here: 270 us
  Pallas kernels  143 us (53%)
  starting transfers between devices  73.4 us (27%)
  waiting for transfers between devices  24.9 us (9%)
  local copies, waits for them, and re-layouts  17.4 us (6%)
  other arithmetic  6.24 us (2%)
  matrix products  3.09 us (1%)
    pallas_call x4, Pallas kernels, weigh(): pl.pallas_call(kernel, grid=(steps,), out_shape=shapes, in_specs=specs +...  57.2 us
    pallas_call x2, Pallas kernels, hidden_part(): pl.pallas_call(kernel, grid_spec=pltpu.PrefetchScalarGridSpec(num_scalar_...  35.3 us
    ppermute x9, starting transfers between devices, send(): return lax.ppermute(value, ('groups', 'tensor', 'dp'), pairs)  23.7 us
    ppermute x4, starting transfers between devices, swap_cores(): return lax.ppermute(value, 'dp', [(i, i ^ 1) for i in range(size)])  16.6 us
    pallas_call x8, Pallas kernels, share_rows(): pl.pallas_call(kernel, grid_spec=pltpu.PrefetchScalarGridSpec(num_scalar_...  15.9 us
    unnamed x74, local copies, waits for them, and re-layouts  15.5 us
    ppermute x3, starting transfers between devices, spread_ranks(): lax.ppermute(below[-1], 'tensor', [(i, i + 1) for i in range(ranks - 1)])  15 us
    pallas_call x5, Pallas kernels, add(): pl.pallas_call(kernel, out_shape=shapes, in_specs=[pl.BlockSpec(memory_sp...  13.3 us
  transfers between devices with their start and end apart: 38, of which 10 were waited for; matrix products, arithmetic and copies ran while one was open for 5% of the time, Pallas kernels for 50%

profile of v13, /device:TPU:3, one launch (start us, length us, event | category | flops | bytes accessed | tf_op | source)
XLA Modules:
  0.0 269.8 jit_solution(7441958754090149385)
XLA Ops:
  0.7 2.7 share_rows.8
  6.9 5.1 %collective-permute-start.3 = (bf16[1024,512]{1,0:T(8,128)(2,1)}, bf16[1024,512]{1,0:T(8,128)(2,1)}, u32[]{:S(2)}, u32[]{:S(2)}) collective-permute-start(bf16[1024,512]{1,0:T(8,128)(2,1)} %bitcast.34), channel_id=1, source_target_pairs={{0,4},{4,8},{8,12},{1,5},{5,9},{9,13},{2,6},{6,10},{10,14},{3,7},{... | collective-permute-start | bytes 3145736 | tf_op jit(solution)/shard_map/ppermute | solution.py:120
  13.3 12.0 %prepare.1 = (f32[2,3584,512]{2,1,0:T(8,128)}, f32[64,512]{1,0:T(8,128)}) custom-call(bf16[512,3584]{1,0:T(8,128)(2,1)} %gate_ref.1, bf16[512,3584]{1,0:T(8,128)(2,1)} %up_ref.1, bf16[64,3584]{1,0:T(8,128)(2,1)} %bitcast.43, bf16[2,64,3584]{2,1,0:T(8,128)(2,1)} %get-tuple-element.34.refs_0_), custom_call_target="tpu_custom_call" | custom-call | flops 3240000000 | bytes 1 | tf_op jit(solution)/shard_map/prepare/pallas_call | solution.py:147
  33.2 5.0 %collective-permute-start.7 = (bf16[1024,512]{1,0:T(8,128)(2,1)}, bf16[1024,512]{1,0:T(8,128)(2,1)}, u32[]{:S(2)}, u32[]{:S(2)}) collective-permute-start(bf16[1024,512]{1,0:T(8,128)(2,1)} %collective-permute-done.3.refs_3_), channel_id=1, source_target_pairs={{0,4},{4,8},{8,12},{1,5},{5,9},{9,13},{2,6},{6,10},{10,14},{3,7},{... | collective-permute-start | bytes 3145736 | tf_op jit(solution)/shard_map/ppermute | solution.py:120
  39.3 14.3 %hidden_part.2.refs_4_.refs_7_ = f32[3584,512]{1,0:T(8,128)} custom-call(s32[1]{0:T(128)} %bitcast.6.rank_ref, bf16[3584,4096]{1,0:T(8,128)(2,1)} %refs_1_.16, bf16[3584,4096]{1,0:T(8,128)(2,1)} %refs_1_.16, bf16[1024,512]{1,0:T(8,128)(2,1)} %bitcast.35, bf16[1024,512]{1,0:T(8,128)(2,1)} %collective-permute-done.3.refs_3_, ...), custom_call_target="tpu_custom_call" | custom-call | flops 3240000000 | bytes 1 | tf_op jit(solution)/shard_map/hidden_part/pallas_call | solution.py:272
  59.2 5.0 %collective-permute-start.12 = (bf16[1024,512]{1,0:T(8,128)(2,1)}, bf16[1024,512]{1,0:T(8,128)(2,1)}, u32[]{:S(2)}, u32[]{:S(2)}) collective-permute-start(bf16[1024,512]{1,0:T(8,128)(2,1)} %collective-permute-done.7.refs_4_.refs_2_), channel_id=1, source_target_pairs={{0,4},{4,8},{8,12},{1,5},{5,9},{9,13},{2,6},{6,10},{10,14},{3,7},{... | collective-permute-start | bytes 3145736 | tf_op jit(solution)/shard_map/ppermute | solution.py:120
  68.0 8.2 %collective-permute-done.6.refs_3_.refs_8_ = bf16[2,64,3584]{2,1,0:T(8,128)(2,1)S(1)} collective-permute-done((bf16[2,64,3584]{2,1,0:T(8,128)(2,1)}, bf16[2,64,3584]{2,1,0:T(8,128)(2,1)S(1)}, u32[]{:S(2)}, u32[]{:S(2)}) %collective-permute-start.6) | collective-permute-done | bytes 917536 | tf_op jit(solution)/shard_map/ppermute | solution.py:59
  82.7 21.0 %hidden_part.3 = (bf16[2,3584,512]{2,1,0:T(8,128)(2,1)}, f32[64,512]{1,0:T(8,128)}) custom-call(s32[1]{0:T(128)} %bitcast.6.rank_ref, bf16[3584,4096]{1,0:T(8,128)(2,1)} %refs_1_.16, bf16[3584,4096]{1,0:T(8,128)(2,1)} %refs_1_.16, bf16[1024,512]{1,0:T(8,128)(2,1)} %collective-permute-done.7.refs_4_.refs_2_, ...), custom_call_target="tpu_custom_call" | custom-call | flops 3240000000 | bytes 1 | tf_op jit(solution)/shard_map/hidden_part/pallas_call | solution.py:272
  109.2 4.5 %collective-permute-start.15 = (bf16[2,3584,512]{2,1,0:T(8,128)(2,1)}, bf16[2,3584,512]{2,1,0:T(8,128)(2,1)}, u32[]{:S(2)}, u32[]{:S(2)}) collective-permute-start(bf16[2,3584,512]{2,1,0:T(8,128)(2,1)} %get-tuple-element.45.refs_10_.refs_5_.refs_3_), channel_id=1, source_target_pairs={{0,1},{1,0},{2,3},{3,2},{4,5},{5,4},{6,7},{7,6},{8,9},{9,8},{10,11... | collective-permute-start | bytes 22020104 | tf_op jit(solution)/shard_map/ppermute | solution.py:48
  116.3 17.6 %weigh_rows.4.refs_8_.refs_1_ = bf16[1536,512]{1,0:T(8,128)(2,1)} custom-call(bf16[1024,3584]{1,0:T(8,128)(2,1)} %refs_0_.21, bf16[1024,3584]{1,0:T(8,128)(2,1)} %refs_1_.21, bf16[2,64,3584]{2,1,0:T(8,128)(2,1)} %get-tuple-element.36.refs_2_, bf16[2,64,3584]{2,1,0:T(8,128)(2,1)} %get-tuple-element.39.refs_3_, ...), custom_call_target="tpu_custom_call" | custom-call | flops 6480000000 | bytes 1 | tf_op jit(solution)/shard_map/weigh_rows/pallas_call | solution.py:349
  133.9 4.3 %collective-permute-start.14 = (bf16[1536,512]{1,0:T(8,128)(2,1)}, bf16[1536,512]{1,0:T(8,128)(2,1)}, u32[]{:S(2)}, u32[]{:S(2)}) collective-permute-start(bf16[1536,512]{1,0:T(8,128)(2,1)} %weigh_rows.4.refs_8_.refs_1_), channel_id=1, source_target_pairs={{4,0},{12,8},{1,5},{9,13},{6,2},{14,10},{3,7},{11,15},{20,16},{28,... | collective-permute-start | bytes 4718600 | tf_op jit(solution)/shard_map/ppermute | solution.py:549
  148.3 17.6 %weigh_rows.5.refs_3_.refs_6_.refs_0_ = bf16[1536,512]{1,0:T(8,128)(2,1)} custom-call(bf16[1024,3584]{1,0:T(8,128)(2,1)} %refs_0_.21, bf16[1024,3584]{1,0:T(8,128)(2,1)} %refs_1_.21, bf16[2,64,3584]{2,1,0:T(8,128)(2,1)} %get-tuple-element.36.refs_2_, bf16[2,64,3584]{2,1,0:T(8,128)(2,1)} %get-tuple-element.39.refs_3_, ...), custom_call_target="tpu_custom_call" | custom-call | flops 6480000000 | bytes 1 | tf_op jit(solution)/shard_map/weigh_rows/pallas_call | solution.py:349
  170.6 2.4 collective-permute-start.25
  174.6 3.8 %add_terms.5 = (bf16[1024,512]{1,0:T(8,128)(2,1)}, bf16[512,512]{1,0:T(8,128)(2,1)}, bf16[1024,512]{1,0:T(8,128)(2,1)}) custom-call(s32[1]{0:T(128)} %bitcast.4.refs_0_, bf16[1536,512]{1,0:T(8,128)(2,1)} %weigh_rows.4.refs_8_.refs_1_, bf16[1536,512]{1,0:T(8,128)(2,1)} %collective-permute-done.14.refs_2_, bf16[1536,512]{1,0:T(8,128)(2,1)} %weigh_rows.5.refs_3_.refs_6_.refs_0_), custom_call_target="tpu_custom_call" | custom-call | flops 540000000 | bytes 1 | tf_op jit(solution)/shard_map/add_terms/pallas_call | solution.py:391
  180.9 11.8 %weigh_rows.6.refs_4_.refs_0_ = bf16[320,1024]{1,0:T(8,128)(2,1)} custom-call(bf16[2,64,3584]{2,1,0:T(8,128)(2,1)} %copy-done.10, bf16[2,64,3584]{2,1,0:T(8,128)(2,1)} %get-tuple-element.56.refs_1_.refs_3_, bf16[2,64,3584]{2,1,0:T(8,128)(2,1)} %copy-done.15, bf16[2,64,3584]{2,1,0:T(8,128)(2,1)} %collective-permute-done.22.refs_4_.refs_3_, ...), custom_call_target="tpu_custom_call" | custom-call | flops 4320000000 | bytes 1 | tf_op jit(solution)/shard_map/weigh_rows/pallas_call | solution.py:349
  197.0 4.2 %collective-permute-start.24 = (bf16[320,1024]{1,0:T(8,128)(2,1)}, bf16[320,1024]{1,0:T(8,128)(2,1)S(1)}, u32[]{:S(2)}, u32[]{:S(2)}) collective-permute-start(bf16[320,1024]{1,0:T(8,128)(2,1)} %weigh_rows.6.refs_4_.refs_0_), channel_id=1, source_target_pairs={{4,0},{12,8},{1,5},{9,13},{6,2},{14,10},{3,7},{11,15},{20,16},{28,... | collective-permute-start | bytes 1966088 | tf_op jit(solution)/shard_map/ppermute | solution.py:549
  202.1 3.2 %add_terms.6 = (bf16[1024,512]{1,0:T(8,128)(2,1)}, bf16[512,512]{1,0:T(8,128)(2,1)}) custom-call(bf16[1536,512]{1,0:T(8,128)(2,1)} %weigh_rows.5.refs_3_.refs_6_.refs_0_, bf16[1536,512]{1,0:T(8,128)(2,1)} %collective-permute-done.25.refs_1_, f32[8,128]{1,0:T(8,128)} %get-tuple-element.59.refs_2_, ...), custom_call_target="tpu_custom_call" | custom-call | flops 540000000 | bytes 1 | tf_op jit(solution)/shard_map/add_terms/pallas_call | solution.py:391
  213.2 10.1 %weigh_rows.7.refs_0_ = bf16[192,1024]{1,0:T(8,128)(2,1)} custom-call(bf16[2,64,3584]{2,1,0:T(8,128)(2,1)} %get-tuple-element.62.refs_0_, bf16[2,64,3584]{2,1,0:T(8,128)(2,1)} %collective-permute-done.28.refs_5_.refs_1_, bf16[2,64,3584]{2,1,0:T(8,128)(2,1)} %collective-permute-done.32.refs_2_, ...), custom_call_target="tpu_custom_call" | custom-call | flops 16200000512 | bytes 1 | tf_op jit(solution)/shard_map/weigh_rows/pallas_call | solution.py:349
  223.4 8.2 %collective-permute-start.33 = (bf16[192,1024]{1,0:T(8,128)(2,1)}, bf16[192,1024]{1,0:T(8,128)(2,1)S(1)}, u32[]{:S(2)}, u32[]{:S(2)}) collective-permute-start(bf16[192,1024]{1,0:T(8,128)(2,1)} %weigh_rows.7.refs_0_), channel_id=1, source_target_pairs={{4,0},{12,8},{1,5},{9,13},{6,2},{14,10},{3,7},{11,15},{20,16},{28,... | collective-permute-start | bytes 1179656 | tf_op jit(solution)/shard_map/ppermute | solution.py:549
  231.7 4.9 %collective-permute-done.33.refs_1_ = bf16[192,1024]{1,0:T(8,128)(2,1)S(1)} collective-permute-done((bf16[192,1024]{1,0:T(8,128)(2,1)}, bf16[192,1024]{1,0:T(8,128)(2,1)S(1)}, u32[]{:S(2)}, u32[]{:S(2)}) %collective-permute-start.33) | collective-permute-done | bytes 393248 | tf_op jit(solution)/shard_map/ppermute | solution.py:549
  241.2 3.4 %assemble.2 = (bf16[512,512]{1,0:T(8,128)(2,1)}, bf16[512,512]{1,0:T(8,128)(2,1)}) custom-call(s32[4]{0:T(128)} %pad_add_fusion.words_ref, bf16[1024,512]{1,0:T(8,128)(2,1)} %get-tuple-element.60.refs_2_.refs_0_, bf16[1024,512]{1,0:T(8,128)(2,1)} %copy-done.20, bf16[512,512]{1,0:T(8,128)(2,1)} %get-tuple-element.61.refs_3_.refs_2_, ...), custom_call_target="tpu_custom_call" | custom-call | flops 270000000 | bytes 1 | tf_op jit(solution)/shard_map/assemble/pallas_call | solution.py:460
  244.6 10.6 %collective-permute-start.34 = (bf16[512,512]{1,0:T(8,128)(2,1)}, bf16[512,512]{1,0:T(8,128)(2,1)S(1)}, u32[]{:S(2)}, u32[]{:S(2)}) collective-permute-start(bf16[512,512]{1,0:T(8,128)(2,1)} %get-tuple-element.63.refs_5_), channel_id=1, source_target_pairs={{0,1},{1,0},{2,3},{3,2},{4,5},{5,4},{6,7},{7,6},{8,9},{9,8},{10,11... | collective-permute-start | bytes 1572872 | tf_op jit(solution)/shard_map/ppermute | solution.py:48
  255.4 3.3 %assemble.3.refs_2_.refs_0_ = bf16[1024,512]{1,0:T(8,128)(2,1)} custom-call(s32[4]{0:T(128)} %pad_add_fusion.words_ref, bf16[1024,512]{1,0:T(8,128)(2,1)} %get-tuple-element.50.refs_8_.refs_0_, bf16[1024,512]{1,0:T(8,128)(2,1)} %collective-permute-done.19.refs_3_.refs_4_.refs_1_, bf16[512,512]{1,0:T(8,128)(2,1)} %get-tuple-element.52.refs_9_.refs_2_, ...), custom_call_target="tpu_custom_call" | custom-call | flops 270000000 | bytes 1 | tf_op jit(solution)/shard_map/assemble/pallas_call | solution.py:460
  266.8 3.0 %finish.1 = bf16[512,1024]{1,0:T(8,128)(2,1)} custom-call(s32[4]{0:T(128)} %pad_add_fusion.words_ref, bf16[1024,512]{1,0:T(8,128)(2,1)} %assemble.3.refs_2_.refs_0_, bf16[512,512]{1,0:T(8,128)(2,1)} %copy-done.25, bf16[512,512]{1,0:T(8,128)(2,1)} %copy-done.26, bf16[192,512]{1,0:T(8,128)(2,1)} %get-tuple-element.69.refs_3_, bf16[192,512]{1,0:T(8,128)(2,1)} %copy-done.29), custom_call_target="tpu_custom_call" | custom-call | flops 810000000 | bytes 1 | tf_op jit(solution)/shard_map/finish/pallas_call | solution.py:511
  (176 shorter events, 82.1 us)
Async XLA Ops:
  5.6 26.3 %collective-permute-start.4 = (bf16[1024,512]{1,0:T(8,128)(2,1)}, bf16[1024,512]{1,0:T(8,128)(2,1)}, u32[]{:S(2)}, u32[]{:S(2)}) collective-permute-start(bf16[1024,512]{1,0:T(8,128)(2,1)} %bitcast.33), channel_id=1, source_target_pairs={{4,0},{8,4},{12,8},{5,1},{9,5},{13,9},{6,2},{10,6},{14,10},{7,3},{... | collective-permute-start | bytes 3145736 | tf_op jit(solution)/shard_map/ppermute | solution.py:121
  6.9 26.3 %collective-permute-start.3 = (bf16[1024,512]{1,0:T(8,128)(2,1)}, bf16[1024,512]{1,0:T(8,128)(2,1)}, u32[]{:S(2)}, u32[]{:S(2)}) collective-permute-start(bf16[1024,512]{1,0:T(8,128)(2,1)} %bitcast.34), channel_id=1, source_target_pairs={{0,4},{4,8},{8,12},{1,5},{5,9},{9,13},{2,6},{6,10},{10,14},{3,7},{... | collective-permute-start | bytes 3145736 | tf_op jit(solution)/shard_map/ppermute | solution.py:120
  12.0 41.7 %collective-permute-start.1 = (bf16[2,64,3584]{2,1,0:T(8,128)(2,1)}, bf16[2,64,3584]{2,1,0:T(8,128)(2,1)}, u32[]{:S(2)}, u32[]{:S(2)}) collective-permute-start(bf16[2,64,3584]{2,1,0:T(8,128)(2,1)} %get-tuple-element.37), channel_id=1, source_target_pairs={{2,0},{3,1},{0,2},{1,3},{6,4},{7,5},{4,6},{5,7},{10,8},{11,9},{8,1... | collective-permute-start | bytes 2752520 | tf_op jit(solution)/shard_map/ppermute | solution.py:54
  28.3 25.3 %collective-permute-start.2 = (bf16[2,64,3584]{2,1,0:T(8,128)(2,1)}, bf16[2,64,3584]{2,1,0:T(8,128)(2,1)S(1)}, u32[]{:S(2)}, u32[]{:S(2)}) collective-permute-start(bf16[2,64,3584]{2,1,0:T(8,128)(2,1)} %get-tuple-element.36.refs_2_), channel_id=1, source_target_pairs={{16,0},{0,16},{17,1},{1,17},{18,2},{2,18},{19,3},{3,19},{20,4},{4,... | collective-permute-start | bytes 2752520 | tf_op jit(solution)/shard_map/ppermute | solution.py:59
  31.9 26.0 %collective-permute-start.8 = (bf16[1024,512]{1,0:T(8,128)(2,1)}, bf16[1024,512]{1,0:T(8,128)(2,1)}, u32[]{:S(2)}, u32[]{:S(2)}) collective-permute-start(bf16[1024,512]{1,0:T(8,128)(2,1)} %collective-permute-done.4.refs_4_), channel_id=1, source_target_pairs={{4,0},{8,4},{12,8},{5,1},{9,5},{13,9},{6,2},{10,6},{14,10},{7,3},{... | collective-permute-start | bytes 3145736 | tf_op jit(solution)/shard_map/ppermute | solution.py:121
  33.2 26.0 %collective-permute-start.7 = (bf16[1024,512]{1,0:T(8,128)(2,1)}, bf16[1024,512]{1,0:T(8,128)(2,1)}, u32[]{:S(2)}, u32[]{:S(2)}) collective-permute-start(bf16[1024,512]{1,0:T(8,128)(2,1)} %collective-permute-done.3.refs_3_), channel_id=1, source_target_pairs={{0,4},{4,8},{8,12},{1,5},{5,9},{9,13},{2,6},{6,10},{10,14},{3,7},{... | collective-permute-start | bytes 3145736 | tf_op jit(solution)/shard_map/ppermute | solution.py:120
  38.2 29.7 %collective-permute-start.5 = (bf16[2,64,3584]{2,1,0:T(8,128)(2,1)}, bf16[2,64,3584]{2,1,0:T(8,128)(2,1)S(1)}, u32[]{:S(2)}, u32[]{:S(2)}) collective-permute-start(bf16[2,64,3584]{2,1,0:T(8,128)(2,1)} %get-tuple-element.38.refs_5_), channel_id=1, source_target_pairs={{2,0},{3,1},{0,2},{1,3},{6,4},{7,5},{4,6},{5,7},{10,8},{11,9},{8,1... | collective-permute-start | bytes 2752520 | tf_op jit(solution)/shard_map/ppermute | solution.py:54
  57.9 23.9 %collective-permute-start.13 = (bf16[1024,512]{1,0:T(8,128)(2,1)}, bf16[1024,512]{1,0:T(8,128)(2,1)}, u32[]{:S(2)}, u32[]{:S(2)}) collective-permute-start(bf16[1024,512]{1,0:T(8,128)(2,1)} %collective-permute-done.8.refs_5_), channel_id=1, source_target_pairs={{4,0},{8,4},{12,8},{5,1},{9,5},{13,9},{6,2},{10,6},{14,10},{7,3},{... | collective-permute-start | bytes 3145736 | tf_op jit(solution)/shard_map/ppermute | solution.py:121
  59.2 23.5 %collective-permute-start.12 = (bf16[1024,512]{1,0:T(8,128)(2,1)}, bf16[1024,512]{1,0:T(8,128)(2,1)}, u32[]{:S(2)}, u32[]{:S(2)}) collective-permute-start(bf16[1024,512]{1,0:T(8,128)(2,1)} %collective-permute-done.7.refs_4_.refs_2_), channel_id=1, source_target_pairs={{0,4},{4,8},{8,12},{1,5},{5,9},{9,13},{2,6},{6,10},{10,14},{3,7},{... | collective-permute-start | bytes 3145736 | tf_op jit(solution)/shard_map/ppermute | solution.py:120
  67.7 36.1 %collective-permute-start.9 = (bf16[2,64,3584]{2,1,0:T(8,128)(2,1)}, bf16[2,64,3584]{2,1,0:T(8,128)(2,1)S(1)}, u32[]{:S(2)}, u32[]{:S(2)}) collective-permute-start(bf16[2,64,3584]{2,1,0:T(8,128)(2,1)} %get-tuple-element.42), channel_id=1, source_target_pairs={{2,0},{3,1},{0,2},{1,3},{6,4},{7,5},{4,6},{5,7},{10,8},{11,9},{8,1... | collective-permute-start | bytes 2752520 | tf_op jit(solution)/shard_map/ppermute | solution.py:54
  79.2 26.7 %collective-permute-start.10 = (bf16[2,64,3584]{2,1,0:T(8,128)(2,1)}, bf16[2,64,3584]{2,1,0:T(8,128)(2,1)S(1)}, u32[]{:S(2)}, u32[]{:S(2)}) collective-permute-start(bf16[2,64,3584]{2,1,0:T(8,128)(2,1)} %get-tuple-element.43.refs_10_), channel_id=1, source_target_pairs={{2,0},{3,1},{0,2},{1,3},{6,4},{7,5},{4,6},{5,7},{10,8},{11,9},{8,1... | collective-permute-start | bytes 2752520 | tf_op jit(solution)/shard_map/ppermute | solution.py:54
  79.9 26.0 %collective-permute-start.11 = (bf16[2,64,3584]{2,1,0:T(8,128)(2,1)}, bf16[2,64,3584]{2,1,0:T(8,128)(2,1)S(1)}, u32[]{:S(2)}, u32[]{:S(2)}) collective-permute-start(bf16[2,64,3584]{2,1,0:T(8,128)(2,1)} %get-tuple-element.41.refs_4_), channel_id=1, source_target_pairs={{16,0},{0,16},{17,1},{1,17},{18,2},{2,18},{19,3},{3,19},{20,4},{4,... | collective-permute-start | bytes 2752520 | tf_op jit(solution)/shard_map/ppermute | solution.py:59
  109.2 38.8 %collective-permute-start.15 = (bf16[2,3584,512]{2,1,0:T(8,128)(2,1)}, bf16[2,3584,512]{2,1,0:T(8,128)(2,1)}, u32[]{:S(2)}, u32[]{:S(2)}) collective-permute-start(bf16[2,3584,512]{2,1,0:T(8,128)(2,1)} %get-tuple-element.45.refs_10_.refs_5_.refs_3_), channel_id=1, source_target_pairs={{0,1},{1,0},{2,3},{3,2},{4,5},{5,4},{6,7},{7,6},{8,9},{9,8},{10,11... | collective-permute-start | bytes 22020104 | tf_op jit(solution)/shard_map/ppermute | solution.py:48
  113.7 24.5 %collective-permute-start.17 = (bf16[2,64,3584]{2,1,0:T(8,128)(2,1)}, bf16[2,64,3584]{2,1,0:T(8,128)(2,1)S(1)}, u32[]{:S(2)}, u32[]{:S(2)}) collective-permute-start(bf16[2,64,3584]{2,1,0:T(8,128)(2,1)} %copy-done.9), channel_id=1, source_target_pairs={{16,0},{0,16},{17,1},{1,17},{18,2},{2,18},{19,3},{3,19},{20,4},{4,... | collective-permute-start | bytes 2752520 | tf_op jit(solution)/shard_map/ppermute | solution.py:59
  113.9 24.8 %collective-permute-start.18 = (bf16[2,64,3584]{2,1,0:T(8,128)(2,1)}, bf16[2,64,3584]{2,1,0:T(8,128)(2,1)S(1)}, u32[]{:S(2)}, u32[]{:S(2)}) collective-permute-start(bf16[2,64,3584]{2,1,0:T(8,128)(2,1)} %get-tuple-element.46.refs_11_), channel_id=1, source_target_pairs={{2,0},{3,1},{0,2},{1,3},{6,4},{7,5},{4,6},{5,7},{10,8},{11,9},{8,1... | collective-permute-start | bytes 2752520 | tf_op jit(solution)/shard_map/ppermute | solution.py:54
  133.9 40.1 %collective-permute-start.14 = (bf16[1536,512]{1,0:T(8,128)(2,1)}, bf16[1536,512]{1,0:T(8,128)(2,1)}, u32[]{:S(2)}, u32[]{:S(2)}) collective-permute-start(bf16[1536,512]{1,0:T(8,128)(2,1)} %weigh_rows.4.refs_8_.refs_1_), channel_id=1, source_target_pairs={{4,0},{12,8},{1,5},{9,13},{6,2},{14,10},{3,7},{11,15},{20,16},{28,... | collective-permute-start | bytes 4718600 | tf_op jit(solution)/shard_map/ppermute | solution.py:549
  138.2 27.7 %collective-permute-start.22 = (bf16[2,64,3584]{2,1,0:T(8,128)(2,1)S(1)}, bf16[2,64,3584]{2,1,0:T(8,128)(2,1)}, u32[]{:S(2)}, u32[]{:S(2)}) collective-permute-start(bf16[2,64,3584]{2,1,0:T(8,128)(2,1)S(1)} %copy-done.4), channel_id=1, source_target_pairs={{16,0},{0,16},{17,1},{1,17},{18,2},{2,18},{19,3},{3,19},{20,4},{4,... | collective-permute-start | bytes 2752520 | tf_op jit(solution)/shard_map/ppermute | solution.py:59
  141.8 24.2 %collective-permute-start.21 = (bf16[2,64,3584]{2,1,0:T(8,128)(2,1)}, bf16[2,64,3584]{2,1,0:T(8,128)(2,1)S(1)}, u32[]{:S(2)}, u32[]{:S(2)}) collective-permute-start(bf16[2,64,3584]{2,1,0:T(8,128)(2,1)} %get-tuple-element.49.refs_11_), channel_id=1, source_target_pairs={{2,0},{3,1},{0,2},{1,3},{6,4},{7,5},{4,6},{5,7},{10,8},{11,9},{8,1... | collective-permute-start | bytes 2752520 | tf_op jit(solution)/shard_map/ppermute | solution.py:54
  148.0 31.2 %collective-permute-start.23 = (bf16[2,64,3584]{2,1,0:T(8,128)(2,1)}, bf16[2,64,3584]{2,1,0:T(8,128)(2,1)}, u32[]{:S(2)}, u32[]{:S(2)}) collective-permute-start(bf16[2,64,3584]{2,1,0:T(8,128)(2,1)} %copy-done.10), channel_id=1, source_target_pairs={{16,0},{0,16},{17,1},{1,17},{18,2},{2,18},{19,3},{3,19},{20,4},{4,... | collective-permute-start | bytes 2752520 | tf_op jit(solution)/shard_map/ppermute | solution.py:59
  169.6 25.0 %collective-permute-start.27 = (bf16[2,64,3584]{2,1,0:T(8,128)(2,1)}, bf16[2,64,3584]{2,1,0:T(8,128)(2,1)S(1)}, u32[]{:S(2)}, u32[]{:S(2)}) collective-permute-start(bf16[2,64,3584]{2,1,0:T(8,128)(2,1)} %get-tuple-element.57.refs_7_), channel_id=1, source_target_pairs={{2,0},{3,1},{0,2},{1,3},{6,4},{7,5},{4,6},{5,7},{10,8},{11,9},{8,1... | collective-permute-start | bytes 2752520 | tf_op jit(solution)/shard_map/ppermute | solution.py:54
  170.6 31.5 %collective-permute-start.25 = (bf16[1536,512]{1,0:T(8,128)(2,1)S(1)}, bf16[1536,512]{1,0:T(8,128)(2,1)}, u32[]{:S(2)}, u32[]{:S(2)}) collective-permute-start(bf16[1536,512]{1,0:T(8,128)(2,1)S(1)} %copy-done.2), channel_id=1, source_target_pairs={{4,0},{12,8},{1,5},{9,13},{6,2},{14,10},{3,7},{11,15},{20,16},{28,... | collective-permute-start | bytes 4718600 | tf_op jit(solution)/shard_map/ppermute | solution.py:549
  174.1 28.0 %collective-permute-start.28 = (bf16[2,64,3584]{2,1,0:T(8,128)(2,1)}, bf16[2,64,3584]{2,1,0:T(8,128)(2,1)}, u32[]{:S(2)}, u32[]{:S(2)}) collective-permute-start(bf16[2,64,3584]{2,1,0:T(8,128)(2,1)} %get-tuple-element.56.refs_1_.refs_3_), channel_id=1, source_target_pairs={{16,0},{0,16},{17,1},{1,17},{18,2},{2,18},{19,3},{3,19},{20,4},{4,... | collective-permute-start | bytes 2752520 | tf_op jit(solution)/shard_map/ppermute | solution.py:59
  205.4 26.3 %collective-permute-start.31 = (bf16[512,512]{1,0:T(8,128)(2,1)}, bf16[512,512]{1,0:T(8,128)(2,1)S(1)}, u32[]{:S(2)}, u32[]{:S(2)}) collective-permute-start(bf16[512,512]{1,0:T(8,128)(2,1)} %get-tuple-element.61.refs_3_.refs_2_), channel_id=1, source_target_pairs={{0,8},{5,13},{10,2},{15,7},{16,24},{21,29},{26,18},{31,23}} | collective-permute-start | bytes 1572872 | tf_op jit(solution)/shard_map/ppermute | solution.py:549
  206.1 34.2 %collective-permute-start.30 = (bf16[1024,512]{1,0:T(8,128)(2,1)}, bf16[1024,512]{1,0:T(8,128)(2,1)S(1)}, u32[]{:S(2)}, u32[]{:S(2)}) collective-permute-start(bf16[1024,512]{1,0:T(8,128)(2,1)} %get-tuple-element.60.refs_2_.refs_0_), channel_id=1, source_target_pairs={{8,0},{13,5},{2,10},{7,15},{24,16},{29,21},{18,26},{23,31}} | collective-permute-start | bytes 3145736 | tf_op jit(solution)/shard_map/ppermute | solution.py:549
  (50 other events, 520.0 us)

commit v14 on v13

--- a/solution.py
+++ b/solution.py
@@ -734,14 +734,6 @@
         fetched[6, s, 0] = value
         for r in range(1, groups):
             fetched[6, s, r] = from_group(value, r)
-    early = early + got[:width]
-    out_parts = jnp.where(high, out_parts[half:], out_parts[:half]) + got[width:]
-    for bit in bits[1:-1]:
-        early = early + exchange(early, bit)
-    for bit in bits[-2:0:-1]:
-        out_parts, got = halve(out_parts, bit)
-        out_parts = out_parts + got
-    out_parts, got = halve(out_parts, bits[0])
     sums_mine, end_mine = carry_on([first_mine], first_theirs[0], at_once=True)
     second_names = chunks_of([5, 6], [0]) + chunks_of([3, 4, 5], others)
     last_names = chunks_of([7], [0]) + chunks_of([6, 7], others)
@@ -752,7 +744,13 @@
         fetched[7, s, 0] = value
         for r in range(1, groups):
             fetched[7, s, r] = from_group(value, r)
-    out_parts = out_parts + got
+    early = early + got[:width]
+    out_parts = jnp.where(high, out_parts[half:], out_parts[:half]) + got[width:]
+    for bit in bits[1:-1]:
+        early = early + exchange(early, bit)
+    for bit in bits[-2::-1]:
+        out_parts, got = halve(out_parts, bit)
+        out_parts = out_parts + got
     received = [got for _, _, got in end_mine]
     received += [fetched[n] for n in fetched if n[0] == 6 and n[2] > 0]
     sums_theirs, end_theirs = carry_on([first_theirs], [ticks[6]] + received)

time: 271 us -> 270 us (level)
  starting transfers between devices: 73.4 us -> 61.7 us
  waiting for transfers between devices: 24.9 us -> 31.3 us
  other arithmetic: 6.24 us -> 9.41 us
    ppermute x9, starting transfers between devices: 23.7 us -> 13.4 us  [send(): return lax.ppermute(value, ('groups', 'tensor', 'dp'), pairs)]
    ppermute x8, waiting for transfers between devices: 9.21 us -> 17.5 us  [from_group(): lax.ppermute(value, 'groups', [((i + shift) % size, i) for i in range(siz...]
    unnamed x74 -> x72, local copies, waits for them, and re-layouts: 15.5 us -> 16.4 us
  transfers between devices with their start and end apart: 38 -> 38, of which waited for: 10 -> 10; matrix products, arithmetic and copies ran while one was open for 5% -> 6% of each run, Pallas kernels for 50% -> 51%
where the time goes in v14:
time: 270 us; the launch traced here: 269 us
  Pallas kernels  144 us (53%)
  starting transfers between devices  61.7 us (23%)
  waiting for transfers between devices  31.3 us (12%)
  local copies, waits for them, and re-layouts  18.3 us (7%)
  other arithmetic  9.41 us (3%)
  matrix products  3.15 us (1%)
    pallas_call x4, Pallas kernels, weigh(): pl.pallas_call(kernel, grid=(steps,), out_shape=shapes, in_specs=specs +...  57.3 us
    pallas_call x2, Pallas kernels, hidden_part(): pl.pallas_call(kernel, grid_spec=pltpu.PrefetchScalarGridSpec(num_scalar_...  35.3 us
    ppermute x8, waiting for transfers between devices, from_group(): lax.ppermute(value, 'groups', [((i + shift) % size, i) for i in range(siz...  17.5 us
    unnamed x72, local copies, waits for them, and re-layouts  16.4 us
    pallas_call x8, Pallas kernels, share_rows(): pl.pallas_call(kernel, grid_spec=pltpu.PrefetchScalarGridSpec(num_scalar_...  15.9 us
    ppermute x4, starting transfers between devices, swap_cores(): return lax.ppermute(value, 'dp', [(i, i ^ 1) for i in range(size)])  15.3 us
    ppermute x3, starting transfers between devices, spread_ranks(): lax.ppermute(below[-1], 'tensor', [(i, i + 1) for i in range(ranks - 1)])  15.1 us
    ppermute x9, starting transfers between devices, send(): return lax.ppermute(value, ('groups', 'tensor', 'dp'), pairs)  13.4 us
  transfers between devices with their start and end apart: 38, of which 10 were waited for; matrix products, arithmetic and copies ran while one was open for 6% of the time, Pallas kernels for 51%

profile of v14, /device:TPU:3, one launch (start us, length us, event | category | flops | bytes accessed | tf_op | source)
XLA Modules:
  0.0 268.7 jit_solution(4656084006689988313)
XLA Ops:
  0.7 2.7 %share_rows.8 = (bf16[2,64,3584]{2,1,0:T(8,128)(2,1)}, bf16[2,64,3584]{2,1,0:T(8,128)(2,1)}) custom-call(s32[1]{0:T(128)} %bitcast.1.group_ref, bf16[1024,3584]{1,0:T(8,128)(2,1)} %refs_0_.21, bf16[1024,3584]{1,0:T(8,128)(2,1)} %refs_1_.21, bf16[1024,3584]{1,0:T(8,128)(2,1)} %refs_0_.21, bf16[1024,3584]{1,0:T(8,128)(2,1)} %refs_1_.21), custom_call_target="tpu_custom_call" | custom-call | flops 540000000 | bytes 1 | tf_op jit(solution)/shard_map/share_rows/pallas_call | solution.py:99
  6.9 5.1 %collective-permute-start.3 = (bf16[1024,512]{1,0:T(8,128)(2,1)}, bf16[1024,512]{1,0:T(8,128)(2,1)}, u32[]{:S(2)}, u32[]{:S(2)}) collective-permute-start(bf16[1024,512]{1,0:T(8,128)(2,1)} %bitcast.34), channel_id=1, source_target_pairs={{0,4},{4,8},{8,12},{1,5},{5,9},{9,13},{2,6},{6,10},{10,14},{3,7},{... | collective-permute-start | bytes 3145736 | tf_op jit(solution)/shard_map/ppermute | solution.py:120
  13.4 12.0 %prepare.1 = (f32[2,3584,512]{2,1,0:T(8,128)}, f32[64,512]{1,0:T(8,128)}) custom-call(bf16[512,3584]{1,0:T(8,128)(2,1)} %gate_ref.1, bf16[512,3584]{1,0:T(8,128)(2,1)} %up_ref.1, bf16[64,3584]{1,0:T(8,128)(2,1)} %bitcast.43, bf16[2,64,3584]{2,1,0:T(8,128)(2,1)} %get-tuple-element.34.refs_0_), custom_call_target="tpu_custom_call" | custom-call | flops 3240000000 | bytes 1 | tf_op jit(solution)/shard_map/prepare/pallas_call | solution.py:147
  33.3 5.0 %collective-permute-start.7 = (bf16[1024,512]{1,0:T(8,128)(2,1)}, bf16[1024,512]{1,0:T(8,128)(2,1)}, u32[]{:S(2)}, u32[]{:S(2)}) collective-permute-start(bf16[1024,512]{1,0:T(8,128)(2,1)} %collective-permute-done.3.refs_3_), channel_id=1, source_target_pairs={{0,4},{4,8},{8,12},{1,5},{5,9},{9,13},{2,6},{6,10},{10,14},{3,7},{... | collective-permute-start | bytes 3145736 | tf_op jit(solution)/shard_map/ppermute | solution.py:120
  39.3 14.3 %hidden_part.2.refs_4_.refs_7_ = f32[3584,512]{1,0:T(8,128)} custom-call(s32[1]{0:T(128)} %bitcast.6.rank_ref, bf16[3584,4096]{1,0:T(8,128)(2,1)} %refs_1_.16, bf16[3584,4096]{1,0:T(8,128)(2,1)} %refs_1_.16, bf16[1024,512]{1,0:T(8,128)(2,1)} %bitcast.35, bf16[1024,512]{1,0:T(8,128)(2,1)} %collective-permute-done.3.refs_3_, ...), custom_call_target="tpu_custom_call" | custom-call | flops 3240000000 | bytes 1 | tf_op jit(solution)/shard_map/hidden_part/pallas_call | solution.py:272
  60.2 5.0 %collective-permute-start.12 = (bf16[1024,512]{1,0:T(8,128)(2,1)}, bf16[1024,512]{1,0:T(8,128)(2,1)}, u32[]{:S(2)}, u32[]{:S(2)}) collective-permute-start(bf16[1024,512]{1,0:T(8,128)(2,1)} %collective-permute-done.7.refs_4_.refs_2_), channel_id=1, source_target_pairs={{0,4},{4,8},{8,12},{1,5},{5,9},{9,13},{2,6},{6,10},{10,14},{3,7},{... | collective-permute-start | bytes 3145736 | tf_op jit(solution)/shard_map/ppermute | solution.py:120
  69.9 7.1 %collective-permute-done.6.refs_3_.refs_8_ = bf16[2,64,3584]{2,1,0:T(8,128)(2,1)S(1)} collective-permute-done((bf16[2,64,3584]{2,1,0:T(8,128)(2,1)}, bf16[2,64,3584]{2,1,0:T(8,128)(2,1)S(1)}, u32[]{:S(2)}, u32[]{:S(2)}) %collective-permute-start.6) | collective-permute-done | bytes 917536 | tf_op jit(solution)/shard_map/ppermute | solution.py:59
  83.7 21.0 %hidden_part.3 = (bf16[2,3584,512]{2,1,0:T(8,128)(2,1)}, f32[64,512]{1,0:T(8,128)}) custom-call(s32[1]{0:T(128)} %bitcast.6.rank_ref, bf16[3584,4096]{1,0:T(8,128)(2,1)} %refs_1_.16, bf16[3584,4096]{1,0:T(8,128)(2,1)} %refs_1_.16, bf16[1024,512]{1,0:T(8,128)(2,1)} %collective-permute-done.7.refs_4_.refs_2_, ...), custom_call_target="tpu_custom_call" | custom-call | flops 3240000000 | bytes 1 | tf_op jit(solution)/shard_map/hidden_part/pallas_call | solution.py:272
  104.7 3.1 %collective-permute-done.10.refs_6_ = bf16[2,64,3584]{2,1,0:T(8,128)(2,1)S(1)} collective-permute-done((bf16[2,64,3584]{2,1,0:T(8,128)(2,1)}, bf16[2,64,3584]{2,1,0:T(8,128)(2,1)S(1)}, u32[]{:S(2)}, u32[]{:S(2)}) %collective-permute-start.10) | collective-permute-done | bytes 917536 | tf_op jit(solution)/shard_map/ppermute | solution.py:54
  111.1 4.5 %collective-permute-start.15 = (bf16[2,3584,512]{2,1,0:T(8,128)(2,1)}, bf16[2,3584,512]{2,1,0:T(8,128)(2,1)}, u32[]{:S(2)}, u32[]{:S(2)}) collective-permute-start(bf16[2,3584,512]{2,1,0:T(8,128)(2,1)} %get-tuple-element.45.refs_10_.refs_5_.refs_3_), channel_id=1, source_target_pairs={{0,1},{1,0},{2,3},{3,2},{4,5},{5,4},{6,7},{7,6},{8,9},{9,8},{10,11... | collective-permute-start | bytes 22020104 | tf_op jit(solution)/shard_map/ppermute | solution.py:48
  117.5 17.7 %weigh_rows.4.refs_8_.refs_1_ = bf16[1536,512]{1,0:T(8,128)(2,1)} custom-call(bf16[1024,3584]{1,0:T(8,128)(2,1)} %refs_0_.21, bf16[1024,3584]{1,0:T(8,128)(2,1)} %refs_1_.21, bf16[2,64,3584]{2,1,0:T(8,128)(2,1)} %get-tuple-element.36.refs_2_, bf16[2,64,3584]{2,1,0:T(8,128)(2,1)} %get-tuple-element.39.refs_3_, ...), custom_call_target="tpu_custom_call" | custom-call | flops 6480000000 | bytes 1 | tf_op jit(solution)/shard_map/weigh_rows/pallas_call | solution.py:349
  135.2 4.5 %collective-permute-start.14 = (bf16[1536,512]{1,0:T(8,128)(2,1)}, bf16[1536,512]{1,0:T(8,128)(2,1)}, u32[]{:S(2)}, u32[]{:S(2)}) collective-permute-start(bf16[1536,512]{1,0:T(8,128)(2,1)} %weigh_rows.4.refs_8_.refs_1_), channel_id=1, source_target_pairs={{4,0},{12,8},{1,5},{9,13},{6,2},{14,10},{3,7},{11,15},{20,16},{28,... | collective-permute-start | bytes 4718600 | tf_op jit(solution)/shard_map/ppermute | solution.py:549
  149.6 17.7 %weigh_rows.5.refs_3_.refs_6_.refs_0_ = bf16[1536,512]{1,0:T(8,128)(2,1)} custom-call(bf16[1024,3584]{1,0:T(8,128)(2,1)} %refs_0_.21, bf16[1024,3584]{1,0:T(8,128)(2,1)} %refs_1_.21, bf16[2,64,3584]{2,1,0:T(8,128)(2,1)} %get-tuple-element.36.refs_2_, bf16[2,64,3584]{2,1,0:T(8,128)(2,1)} %get-tuple-element.39.refs_3_, ...), custom_call_target="tpu_custom_call" | custom-call | flops 6480000000 | bytes 1 | tf_op jit(solution)/shard_map/weigh_rows/pallas_call | solution.py:349
  175.7 3.8 %add_terms.5 = (bf16[1024,512]{1,0:T(8,128)(2,1)}, bf16[512,512]{1,0:T(8,128)(2,1)}, bf16[1024,512]{1,0:T(8,128)(2,1)}) custom-call(s32[1]{0:T(128)} %bitcast.4.refs_0_, bf16[1536,512]{1,0:T(8,128)(2,1)} %weigh_rows.4.refs_8_.refs_1_, bf16[1536,512]{1,0:T(8,128)(2,1)} %collective-permute-done.14.refs_2_, bf16[1536,512]{1,0:T(8,128)(2,1)} %weigh_rows.5.refs_3_.refs_6_.refs_0_), custom_call_target="tpu_custom_call" | custom-call | flops 540000000 | bytes 1 | tf_op jit(solution)/shard_map/add_terms/pallas_call | solution.py:391
  181.8 11.8 %weigh_rows.6.refs_4_.refs_0_ = bf16[320,1024]{1,0:T(8,128)(2,1)} custom-call(bf16[2,64,3584]{2,1,0:T(8,128)(2,1)} %copy-done.7, bf16[2,64,3584]{2,1,0:T(8,128)(2,1)} %get-tuple-element.56.refs_1_.refs_3_, bf16[2,64,3584]{2,1,0:T(8,128)(2,1)} %copy-done.16, bf16[2,64,3584]{2,1,0:T(8,128)(2,1)} %collective-permute-done.22.refs_4_.refs_3_, ...), custom_call_target="tpu_custom_call" | custom-call | flops 4320000000 | bytes 1 | tf_op jit(solution)/shard_map/weigh_rows/pallas_call | solution.py:349
  202.5 3.2 %add_terms.6 = (bf16[1024,512]{1,0:T(8,128)(2,1)}, bf16[512,512]{1,0:T(8,128)(2,1)}) custom-call(bf16[1536,512]{1,0:T(8,128)(2,1)} %weigh_rows.5.refs_3_.refs_6_.refs_0_, bf16[1536,512]{1,0:T(8,128)(2,1)} %collective-permute-done.25.refs_1_, f32[8,128]{1,0:T(8,128)} %get-tuple-element.59.refs_2_, bf16[1024,512]{1,0:T(8,128)(2,1)} %copy-done.6, ...), custom_call_target="tpu_custom_call" | custom-call | flops 540000000 | bytes 1 | tf_op jit(solution)/shard_map/add_terms/pallas_call | solution.py:391
  213.1 7.3 %collective-permute-done.31.refs_2_ = bf16[2,64,3584]{2,1,0:T(8,128)(2,1)} collective-permute-done((bf16[2,64,3584]{2,1,0:T(8,128)(2,1)}, bf16[2,64,3584]{2,1,0:T(8,128)(2,1)}, u32[]{:S(2)}, u32[]{:S(2)}) %collective-permute-start.31) | collective-permute-done | bytes 917536 | tf_op jit(solution)/shard_map/ppermute | solution.py:59
  220.4 10.1 %weigh_rows.7.refs_0_ = bf16[192,1024]{1,0:T(8,128)(2,1)} custom-call(bf16[2,64,3584]{2,1,0:T(8,128)(2,1)} %get-tuple-element.62.refs_0_, bf16[2,64,3584]{2,1,0:T(8,128)(2,1)} %collective-permute-done.27.refs_5_.refs_1_, bf16[2,64,3584]{2,1,0:T(8,128)(2,1)} %collective-permute-done.31.refs_2_, ...), custom_call_target="tpu_custom_call" | custom-call | flops 16200000512 | bytes 1 | tf_op jit(solution)/shard_map/weigh_rows/pallas_call | solution.py:349
  232.7 4.2 %collective-permute-done.32.refs_1_ = bf16[192,1024]{1,0:T(8,128)(2,1)S(1)} collective-permute-done((bf16[192,1024]{1,0:T(8,128)(2,1)}, bf16[192,1024]{1,0:T(8,128)(2,1)S(1)}, u32[]{:S(2)}, u32[]{:S(2)}) %collective-permute-start.32) | collective-permute-done | bytes 393248 | tf_op jit(solution)/shard_map/ppermute | solution.py:549
  241.4 3.5 %assemble.2 = (bf16[512,512]{1,0:T(8,128)(2,1)}, bf16[512,512]{1,0:T(8,128)(2,1)}) custom-call(s32[4]{0:T(128)} %pad_add_fusion.words_ref, bf16[1024,512]{1,0:T(8,128)(2,1)} %get-tuple-element.60.refs_2_.refs_0_, bf16[1024,512]{1,0:T(8,128)(2,1)} %copy-done.25, bf16[512,512]{1,0:T(8,128)(2,1)} %get-tuple-element.61.refs_3_.refs_2_, ...), custom_call_target="tpu_custom_call" | custom-call | flops 270000000 | bytes 1 | tf_op jit(solution)/shard_map/assemble/pallas_call | solution.py:460
  244.9 7.8 %collective-permute-start.33 = (bf16[512,512]{1,0:T(8,128)(2,1)}, bf16[512,512]{1,0:T(8,128)(2,1)S(1)}, u32[]{:S(2)}, u32[]{:S(2)}) collective-permute-start(bf16[512,512]{1,0:T(8,128)(2,1)} %get-tuple-element.63.refs_5_), channel_id=1, source_target_pairs={{0,1},{1,0},{2,3},{3,2},{4,5},{5,4},{6,7},{7,6},{8,9},{9,8},{10,11... | collective-permute-start | bytes 1572872 | tf_op jit(solution)/shard_map/ppermute | solution.py:48
  252.8 3.3 %assemble.3.refs_2_.refs_0_ = bf16[1024,512]{1,0:T(8,128)(2,1)} custom-call(s32[4]{0:T(128)} %pad_add_fusion.words_ref, bf16[1024,512]{1,0:T(8,128)(2,1)} %get-tuple-element.50.refs_8_.refs_0_, bf16[1024,512]{1,0:T(8,128)(2,1)} %copy-done.6, bf16[512,512]{1,0:T(8,128)(2,1)} %get-tuple-element.52.refs_9_.refs_2_, ...), custom_call_target="tpu_custom_call" | custom-call | flops 270000000 | bytes 1 | tf_op jit(solution)/shard_map/assemble/pallas_call | solution.py:460
  260.6 3.0 %collective-permute-start.36 = (bf16[192,512]{1,0:T(8,128)(2,1)S(1)}, bf16[192,512]{1,0:T(8,128)(2,1)S(1)}, u32[]{:S(2)}, u32[]{:S(2)}) collective-permute-start(bf16[192,512]{1,0:T(8,128)(2,1)S(1)} %get-tuple-element.68), channel_id=1, source_target_pairs={{0,1},{1,0},{2,3},{3,2},{4,5},{5,4},{6,7},{7,6},{8,9},{9,8},{10,11... | collective-permute-start | bytes 589832 | tf_op jit(solution)/shard_map/ppermute | solution.py:48
  265.7 3.0 %finish.1 = bf16[512,1024]{1,0:T(8,128)(2,1)} custom-call(s32[4]{0:T(128)} %pad_add_fusion.words_ref, bf16[1024,512]{1,0:T(8,128)(2,1)} %assemble.3.refs_2_.refs_0_, bf16[512,512]{1,0:T(8,128)(2,1)} %copy-done.28, bf16[512,512]{1,0:T(8,128)(2,1)} %copy-done.29, bf16[192,512]{1,0:T(8,128)(2,1)} %get-tuple-element.69.refs_3_, bf16[192,512]{1,0:T(8,128)(2,1)} %copy-done.32), custom_call_target="tpu_custom_call" | custom-call | flops 810000000 | bytes 1 | tf_op jit(solution)/shard_map/finish/pallas_call | solution.py:511
  (174 shorter events, 87.0 us)
Async XLA Ops:
  5.6 26.3 %collective-permute-start.4 = (bf16[1024,512]{1,0:T(8,128)(2,1)}, bf16[1024,512]{1,0:T(8,128)(2,1)}, u32[]{:S(2)}, u32[]{:S(2)}) collective-permute-start(bf16[1024,512]{1,0:T(8,128)(2,1)} %bitcast.33), channel_id=1, source_target_pairs={{4,0},{8,4},{12,8},{5,1},{9,5},{13,9},{6,2},{10,6},{14,10},{7,3},{... | collective-permute-start | bytes 3145736 | tf_op jit(solution)/shard_map/ppermute | solution.py:121
  6.9 26.3 %collective-permute-start.3 = (bf16[1024,512]{1,0:T(8,128)(2,1)}, bf16[1024,512]{1,0:T(8,128)(2,1)}, u32[]{:S(2)}, u32[]{:S(2)}) collective-permute-start(bf16[1024,512]{1,0:T(8,128)(2,1)} %bitcast.34), channel_id=1, source_target_pairs={{0,4},{4,8},{8,12},{1,5},{5,9},{9,13},{2,6},{6,10},{10,14},{3,7},{... | collective-permute-start | bytes 3145736 | tf_op jit(solution)/shard_map/ppermute | solution.py:120
  12.0 41.6 %collective-permute-start.1 = (bf16[2,64,3584]{2,1,0:T(8,128)(2,1)}, bf16[2,64,3584]{2,1,0:T(8,128)(2,1)S(1)}, u32[]{:S(2)}, u32[]{:S(2)}) collective-permute-start(bf16[2,64,3584]{2,1,0:T(8,128)(2,1)} %get-tuple-element.37), channel_id=1, source_target_pairs={{2,0},{3,1},{0,2},{1,3},{6,4},{7,5},{4,6},{5,7},{10,8},{11,9},{8,1... | collective-permute-start | bytes 2752520 | tf_op jit(solution)/shard_map/ppermute | solution.py:54
  28.4 25.3 %collective-permute-start.2 = (bf16[2,64,3584]{2,1,0:T(8,128)(2,1)}, bf16[2,64,3584]{2,1,0:T(8,128)(2,1)S(1)}, u32[]{:S(2)}, u32[]{:S(2)}) collective-permute-start(bf16[2,64,3584]{2,1,0:T(8,128)(2,1)} %get-tuple-element.36.refs_2_), channel_id=1, source_target_pairs={{16,0},{0,16},{17,1},{1,17},{18,2},{2,18},{19,3},{3,19},{20,4},{4,... | collective-permute-start | bytes 2752520 | tf_op jit(solution)/shard_map/ppermute | solution.py:59
  32.0 26.9 %collective-permute-start.8 = (bf16[1024,512]{1,0:T(8,128)(2,1)}, bf16[1024,512]{1,0:T(8,128)(2,1)}, u32[]{:S(2)}, u32[]{:S(2)}) collective-permute-start(bf16[1024,512]{1,0:T(8,128)(2,1)} %collective-permute-done.4.refs_4_), channel_id=1, source_target_pairs={{4,0},{8,4},{12,8},{5,1},{9,5},{13,9},{6,2},{10,6},{14,10},{7,3},{... | collective-permute-start | bytes 3145736 | tf_op jit(solution)/shard_map/ppermute | solution.py:121
  33.3 26.9 %collective-permute-start.7 = (bf16[1024,512]{1,0:T(8,128)(2,1)}, bf16[1024,512]{1,0:T(8,128)(2,1)}, u32[]{:S(2)}, u32[]{:S(2)}) collective-permute-start(bf16[1024,512]{1,0:T(8,128)(2,1)} %collective-permute-done.3.refs_3_), channel_id=1, source_target_pairs={{0,4},{4,8},{8,12},{1,5},{5,9},{9,13},{2,6},{6,10},{10,14},{3,7},{... | collective-permute-start | bytes 3145736 | tf_op jit(solution)/shard_map/ppermute | solution.py:120
  38.3 31.6 %collective-permute-start.5 = (bf16[2,64,3584]{2,1,0:T(8,128)(2,1)}, bf16[2,64,3584]{2,1,0:T(8,128)(2,1)}, u32[]{:S(2)}, u32[]{:S(2)}) collective-permute-start(bf16[2,64,3584]{2,1,0:T(8,128)(2,1)} %get-tuple-element.38.refs_5_), channel_id=1, source_target_pairs={{2,0},{3,1},{0,2},{1,3},{6,4},{7,5},{4,6},{5,7},{10,8},{11,9},{8,1... | collective-permute-start | bytes 2752520 | tf_op jit(solution)/shard_map/ppermute | solution.py:54
  58.9 23.8 %collective-permute-start.13 = (bf16[1024,512]{1,0:T(8,128)(2,1)}, bf16[1024,512]{1,0:T(8,128)(2,1)S(1)}, u32[]{:S(2)}, u32[]{:S(2)}) collective-permute-start(bf16[1024,512]{1,0:T(8,128)(2,1)} %collective-permute-done.8.refs_5_), channel_id=1, source_target_pairs={{4,0},{8,4},{12,8},{5,1},{9,5},{13,9},{6,2},{10,6},{14,10},{7,3},{... | collective-permute-start | bytes 3145736 | tf_op jit(solution)/shard_map/ppermute | solution.py:121
  60.2 23.5 %collective-permute-start.12 = (bf16[1024,512]{1,0:T(8,128)(2,1)}, bf16[1024,512]{1,0:T(8,128)(2,1)}, u32[]{:S(2)}, u32[]{:S(2)}) collective-permute-start(bf16[1024,512]{1,0:T(8,128)(2,1)} %collective-permute-done.7.refs_4_.refs_2_), channel_id=1, source_target_pairs={{0,4},{4,8},{8,12},{1,5},{5,9},{9,13},{2,6},{6,10},{10,14},{3,7},{... | collective-permute-start | bytes 3145736 | tf_op jit(solution)/shard_map/ppermute | solution.py:120
  69.6 35.0 %collective-permute-start.9 = (bf16[2,64,3584]{2,1,0:T(8,128)(2,1)}, bf16[2,64,3584]{2,1,0:T(8,128)(2,1)S(1)}, u32[]{:S(2)}, u32[]{:S(2)}) collective-permute-start(bf16[2,64,3584]{2,1,0:T(8,128)(2,1)} %get-tuple-element.42), channel_id=1, source_target_pairs={{2,0},{3,1},{0,2},{1,3},{6,4},{7,5},{4,6},{5,7},{10,8},{11,9},{8,1... | collective-permute-start | bytes 2752520 | tf_op jit(solution)/shard_map/ppermute | solution.py:54
  80.0 27.8 %collective-permute-start.10 = (bf16[2,64,3584]{2,1,0:T(8,128)(2,1)}, bf16[2,64,3584]{2,1,0:T(8,128)(2,1)S(1)}, u32[]{:S(2)}, u32[]{:S(2)}) collective-permute-start(bf16[2,64,3584]{2,1,0:T(8,128)(2,1)} %get-tuple-element.43.refs_10_), channel_id=1, source_target_pairs={{2,0},{3,1},{0,2},{1,3},{6,4},{7,5},{4,6},{5,7},{10,8},{11,9},{8,1... | collective-permute-start | bytes 2752520 | tf_op jit(solution)/shard_map/ppermute | solution.py:54
  80.7 27.1 %collective-permute-start.11 = (bf16[2,64,3584]{2,1,0:T(8,128)(2,1)}, bf16[2,64,3584]{2,1,0:T(8,128)(2,1)S(1)}, u32[]{:S(2)}, u32[]{:S(2)}) collective-permute-start(bf16[2,64,3584]{2,1,0:T(8,128)(2,1)} %get-tuple-element.41.refs_4_), channel_id=1, source_target_pairs={{16,0},{0,16},{17,1},{1,17},{18,2},{2,18},{19,3},{3,19},{20,4},{4,... | collective-permute-start | bytes 2752520 | tf_op jit(solution)/shard_map/ppermute | solution.py:59
  111.1 38.2 %collective-permute-start.15 = (bf16[2,3584,512]{2,1,0:T(8,128)(2,1)}, bf16[2,3584,512]{2,1,0:T(8,128)(2,1)}, u32[]{:S(2)}, u32[]{:S(2)}) collective-permute-start(bf16[2,3584,512]{2,1,0:T(8,128)(2,1)} %get-tuple-element.45.refs_10_.refs_5_.refs_3_), channel_id=1, source_target_pairs={{0,1},{1,0},{2,3},{3,2},{4,5},{5,4},{6,7},{7,6},{8,9},{9,8},{10,11... | collective-permute-start | bytes 22020104 | tf_op jit(solution)/shard_map/ppermute | solution.py:48
  115.6 24.1 %collective-permute-start.17 = (bf16[2,64,3584]{2,1,0:T(8,128)(2,1)}, bf16[2,64,3584]{2,1,0:T(8,128)(2,1)S(1)}, u32[]{:S(2)}, u32[]{:S(2)}) collective-permute-start(bf16[2,64,3584]{2,1,0:T(8,128)(2,1)} %copy-done.10), channel_id=1, source_target_pairs={{16,0},{0,16},{17,1},{1,17},{18,2},{2,18},{19,3},{3,19},{20,4},{4,... | collective-permute-start | bytes 2752520 | tf_op jit(solution)/shard_map/ppermute | solution.py:59
  115.8 25.0 %collective-permute-start.18 = (bf16[2,64,3584]{2,1,0:T(8,128)(2,1)}, bf16[2,64,3584]{2,1,0:T(8,128)(2,1)S(1)}, u32[]{:S(2)}, u32[]{:S(2)}) collective-permute-start(bf16[2,64,3584]{2,1,0:T(8,128)(2,1)} %get-tuple-element.46.refs_11_), channel_id=1, source_target_pairs={{2,0},{3,1},{0,2},{1,3},{6,4},{7,5},{4,6},{5,7},{10,8},{11,9},{8,1... | collective-permute-start | bytes 2752520 | tf_op jit(solution)/shard_map/ppermute | solution.py:54
  135.2 40.5 %collective-permute-start.14 = (bf16[1536,512]{1,0:T(8,128)(2,1)}, bf16[1536,512]{1,0:T(8,128)(2,1)}, u32[]{:S(2)}, u32[]{:S(2)}) collective-permute-start(bf16[1536,512]{1,0:T(8,128)(2,1)} %weigh_rows.4.refs_8_.refs_1_), channel_id=1, source_target_pairs={{4,0},{12,8},{1,5},{9,13},{6,2},{14,10},{3,7},{11,15},{20,16},{28,... | collective-permute-start | bytes 4718600 | tf_op jit(solution)/shard_map/ppermute | solution.py:549
  139.7 27.6 %collective-permute-start.22 = (bf16[2,64,3584]{2,1,0:T(8,128)(2,1)S(1)}, bf16[2,64,3584]{2,1,0:T(8,128)(2,1)}, u32[]{:S(2)}, u32[]{:S(2)}) collective-permute-start(bf16[2,64,3584]{2,1,0:T(8,128)(2,1)S(1)} %copy-done.4), channel_id=1, source_target_pairs={{16,0},{0,16},{17,1},{1,17},{18,2},{2,18},{19,3},{3,19},{20,4},{4,... | collective-permute-start | bytes 2752520 | tf_op jit(solution)/shard_map/ppermute | solution.py:59
  149.4 32.5 %collective-permute-start.23 = (bf16[2,64,3584]{2,1,0:T(8,128)(2,1)}, bf16[2,64,3584]{2,1,0:T(8,128)(2,1)}, u32[]{:S(2)}, u32[]{:S(2)}) collective-permute-start(bf16[2,64,3584]{2,1,0:T(8,128)(2,1)} %copy-done.7), channel_id=1, source_target_pairs={{16,0},{0,16},{17,1},{1,17},{18,2},{2,18},{19,3},{3,19},{20,4},{4,... | collective-permute-start | bytes 2752520 | tf_op jit(solution)/shard_map/ppermute | solution.py:59
  171.7 29.8 %collective-permute-start.25 = (bf16[1536,512]{1,0:T(8,128)(2,1)S(1)}, bf16[1536,512]{1,0:T(8,128)(2,1)}, u32[]{:S(2)}, u32[]{:S(2)}) collective-permute-start(bf16[1536,512]{1,0:T(8,128)(2,1)S(1)} %copy-done.2), channel_id=1, source_target_pairs={{4,0},{12,8},{1,5},{9,13},{6,2},{14,10},{3,7},{11,15},{20,16},{28,... | collective-permute-start | bytes 4718600 | tf_op jit(solution)/shard_map/ppermute | solution.py:549
  174.9 26.6 %collective-permute-start.27 = (bf16[2,64,3584]{2,1,0:T(8,128)(2,1)}, bf16[2,64,3584]{2,1,0:T(8,128)(2,1)}, u32[]{:S(2)}, u32[]{:S(2)}) collective-permute-start(bf16[2,64,3584]{2,1,0:T(8,128)(2,1)} %get-tuple-element.56.refs_1_.refs_3_), channel_id=1, source_target_pairs={{16,0},{0,16},{17,1},{1,17},{18,2},{2,18},{19,3},{3,19},{20,4},{4,... | collective-permute-start | bytes 2752520 | tf_op jit(solution)/shard_map/ppermute | solution.py:59
  194.2 26.2 %collective-permute-start.31 = (bf16[2,64,3584]{2,1,0:T(8,128)(2,1)}, bf16[2,64,3584]{2,1,0:T(8,128)(2,1)}, u32[]{:S(2)}, u32[]{:S(2)}) collective-permute-start(bf16[2,64,3584]{2,1,0:T(8,128)(2,1)} %get-tuple-element.62.refs_0_), channel_id=1, source_target_pairs={{16,0},{0,16},{17,1},{1,17},{18,2},{2,18},{19,3},{3,19},{20,4},{4,... | collective-permute-start | bytes 2752520 | tf_op jit(solution)/shard_map/ppermute | solution.py:59
  201.5 30.4 %collective-permute-start.37 = (bf16[32,512]{1,0:T(8,128)(2,1)}, bf16[32,512]{1,0:T(8,128)(2,1)}, u32[]{:S(2)}, u32[]{:S(2)}) collective-permute-start(bf16[32,512]{1,0:T(8,128)(2,1)} %select_convert_fusion.1), channel_id=1, source_target_pairs={{0,4},{4,0},{8,12},{12,8},{1,5},{5,1},{9,13},{13,9},{2,6},{6,2},{1... | collective-permute-start | bytes 98312 | tf_op jit(solution)/shard_map/ppermute | solution.py:525
  205.7 27.0 %collective-permute-start.30 = (bf16[512,512]{1,0:T(8,128)(2,1)}, bf16[512,512]{1,0:T(8,128)(2,1)S(1)}, u32[]{:S(2)}, u32[]{:S(2)}) collective-permute-start(bf16[512,512]{1,0:T(8,128)(2,1)} %get-tuple-element.61.refs_3_.refs_2_), channel_id=1, source_target_pairs={{0,8},{5,13},{10,2},{15,7},{16,24},{21,29},{26,18},{31,23}} | collective-permute-start | bytes 1572872 | tf_op jit(solution)/shard_map/ppermute | solution.py:549
  206.4 34.1 %collective-permute-start.29 = (bf16[1024,512]{1,0:T(8,128)(2,1)}, bf16[1024,512]{1,0:T(8,128)(2,1)S(1)}, u32[]{:S(2)}, u32[]{:S(2)}) collective-permute-start(bf16[1024,512]{1,0:T(8,128)(2,1)} %get-tuple-element.60.refs_2_.refs_0_), channel_id=1, source_target_pairs={{8,0},{13,5},{2,10},{7,15},{24,16},{29,21},{18,26},{23,31}} | collective-permute-start | bytes 3145736 | tf_op jit(solution)/shard_map/ppermute | solution.py:549
  (49 other events, 479.9 us)

commit v15 on v14

--- a/solution.py
+++ b/solution.py
@@ -709,23 +709,30 @@
     )
     mine, early = forward(3, chunks_of([2], others) + [(4, 0)], [], [mine, early_part])
     theirs = swap_cores(mine)
-    got = exchange(early, bits[0])
+
+    halvings = [bits[0], bits[-1]] + bits[1:-1]
+    order = sorted(range(ranks), key=lambda r: [bool(r & b) for b in halvings])
+    out_parts = jnp.stack([up_out_part, out_down_part]).reshape(2, ranks, -1, count)
+    out_parts = jnp.concatenate([out_parts[:, r] for r in order], axis=0).reshape(-1, count)
+    width = early.shape[0]
+
+    def exchange_with(early, parts, bit):
+        half = parts.shape[0] // 2
+        high = rank & bit != 0
+        got = exchange(
+            jnp.concatenate([early, jnp.where(high, parts[:half], parts[half:])], axis=0), bit
+        )
+        return jnp.where(high, parts[half:], parts[:half]), got
+
+    out_parts, got = exchange_with(early, out_parts, bits[0])
     first_names = chunks_of(range(5), [0]) + chunks_of(range(3), others)
     first_mine = terms(first_names, [mine], [ticks[3]], 24, near=True)
-    early, got, up_out_part = forward(
-        4, chunks_of([3], others) + [(5, 0)], first_mine[0], [early, got, up_out_part]
-    )
-    early = early + got
-
-    out_parts = jnp.stack([up_out_part, out_down_part]).reshape(2, ranks, -1, count)
-    out_parts = out_parts.transpose(1, 0, 2, 3).reshape(-1, count)
-    half = out_parts.shape[0] // 2
-    high = rank & bits[-1] != 0
-    width = early.shape[0]
-    got = exchange(
-        jnp.concatenate([early, jnp.where(high, out_parts[:half], out_parts[half:])], axis=0),
-        bits[-1],
-    )
+    early, out_parts, got = forward(
+        4, chunks_of([3], others) + [(5, 0)], first_mine[0], [early, out_parts, got]
+    )
+
+    early, out_parts = early + got[:width], out_parts + got[width:]
+    out_parts, got = exchange_with(early, out_parts, bits[-1])
     first_theirs = terms(first_names, [theirs], [ticks[4]], 24, near=True)
     got, *held = forward(
         5, chunks_of([4], others), first_theirs[0], [got] + [fetched[6, s, 0] for s in range(1, chips)]
@@ -744,11 +751,9 @@
         fetched[7, s, 0] = value
         for r in range(1, groups):
             fetched[7, s, r] = from_group(value, r)
-    early = early + got[:width]
-    out_parts = jnp.where(high, out_parts[half:], out_parts[:half]) + got[width:]
+    early, out_parts = early + got[:width], out_parts + got[width:]
     for bit in bits[1:-1]:
         early = early + exchange(early, bit)
-    for bit in bits[-2::-1]:
         out_parts, got = halve(out_parts, bit)
         out_parts = out_parts + got
     received = [got for _, _, got in end_mine]

time: 270 us -> 269 us (level)
    unnamed x72 -> x74, local copies, waits for them, and re-layouts: 16.4 us -> 14.8 us
  transfers between devices with their start and end apart: 38 -> 37, of which waited for: 10 -> 11; matrix products, arithmetic and copies ran while one was open for 6% -> 6% of each run, Pallas kernels for 51% -> 51%
where the time goes in v15:
time: 269 us; the launch traced here: 268 us
  Pallas kernels  144 us (54%)
  starting transfers between devices  61.8 us (23%)
  waiting for transfers between devices  34 us (13%)
  local copies, waits for them, and re-layouts  16.7 us (6%)
  other arithmetic  7.73 us (3%)
  matrix products  3.16 us (1%)
    pallas_call x4, Pallas kernels, weigh(): pl.pallas_call(kernel, grid=(steps,), out_shape=shapes, in_specs=specs +...  57.2 us
    pallas_call x2, Pallas kernels, hidden_part(): pl.pallas_call(kernel, grid_spec=pltpu.PrefetchScalarGridSpec(num_scalar_...  35.3 us
    ppermute x8, waiting for transfers between devices, from_group(): lax.ppermute(value, 'groups', [((i + shift) % size, i) for i in range(siz...  20 us
    pallas_call x8, Pallas kernels, share_rows(): pl.pallas_call(kernel, grid_spec=pltpu.PrefetchScalarGridSpec(num_scalar_...  15.9 us
    ppermute x3, starting transfers between devices, spread_ranks(): lax.ppermute(below[-1], 'tensor', [(i, i + 1) for i in range(ranks - 1)])  15 us
    unnamed x74, local copies, waits for them, and re-layouts  14.8 us
    ppermute x4, starting transfers between devices, swap_cores(): return lax.ppermute(value, 'dp', [(i, i ^ 1) for i in range(size)])  14.5 us
    ppermute x9, starting transfers between devices, send(): return lax.ppermute(value, ('groups', 'tensor', 'dp'), pairs)  14.2 us
  transfers between devices with their start and end apart: 37, of which 11 were waited for; matrix products, arithmetic and copies ran while one was open for 6% of the time, Pallas kernels for 51%

profile of v15, /device:TPU:3, one launch (start us, length us, event | category | flops | bytes accessed | tf_op | source)
XLA Modules:
  0.0 268.0 jit_solution(9786094424281933794)
XLA Ops:
  6.9 5.1 %collective-permute-start.3 = (bf16[1024,512]{1,0:T(8,128)(2,1)}, bf16[1024,512]{1,0:T(8,128)(2,1)}, u32[]{:S(2)}, u32[]{:S(2)}) collective-permute-start(bf16[1024,512]{1,0:T(8,128)(2,1)} %bitcast.39), channel_id=1, source_target_pairs={{0,4},{4,8},{8,12},{1,5},{5,9},{9,13},{2,6},{6,10},{10,14},{3,7},{... | collective-permute-start | bytes 3145736 | tf_op jit(solution)/shard_map/ppermute | solution.py:120
  13.3 12.0 %prepare.1 = (f32[2,3584,512]{2,1,0:T(8,128)}, f32[64,512]{1,0:T(8,128)}) custom-call(bf16[512,3584]{1,0:T(8,128)(2,1)} %gate_ref.1, bf16[512,3584]{1,0:T(8,128)(2,1)} %up_ref.1, bf16[64,3584]{1,0:T(8,128)(2,1)} %bitcast.49, bf16[2,64,3584]{2,1,0:T(8,128)(2,1)} %get-tuple-element.34.refs_0_), custom_call_target="tpu_custom_call" | custom-call | flops 3240000000 | bytes 1 | tf_op jit(solution)/shard_map/prepare/pallas_call | solution.py:147
  33.2 5.0 %collective-permute-start.7 = (bf16[1024,512]{1,0:T(8,128)(2,1)}, bf16[1024,512]{1,0:T(8,128)(2,1)}, u32[]{:S(2)}, u32[]{:S(2)}) collective-permute-start(bf16[1024,512]{1,0:T(8,128)(2,1)} %collective-permute-done.3.refs_3_), channel_id=1, source_target_pairs={{0,4},{4,8},{8,12},{1,5},{5,9},{9,13},{2,6},{6,10},{10,14},{3,7},{... | collective-permute-start | bytes 3145736 | tf_op jit(solution)/shard_map/ppermute | solution.py:120
  39.3 14.3 %hidden_part.2.refs_4_.refs_7_ = f32[3584,512]{1,0:T(8,128)} custom-call(s32[1]{0:T(128)} %bitcast.6.rank_ref, bf16[3584,4096]{1,0:T(8,128)(2,1)} %refs_1_.16, bf16[3584,4096]{1,0:T(8,128)(2,1)} %refs_1_.16, bf16[1024,512]{1,0:T(8,128)(2,1)} %bitcast.40, bf16[1024,512]{1,0:T(8,128)(2,1)} %collective-permute-done.3.refs_3_, ...), custom_call_target="tpu_custom_call" | custom-call | flops 3240000000 | bytes 1 | tf_op jit(solution)/shard_map/hidden_part/pallas_call | solution.py:272
  60.1 5.0 %collective-permute-start.12 = (bf16[1024,512]{1,0:T(8,128)(2,1)}, bf16[1024,512]{1,0:T(8,128)(2,1)}, u32[]{:S(2)}, u32[]{:S(2)}) collective-permute-start(bf16[1024,512]{1,0:T(8,128)(2,1)} %collective-permute-done.7.refs_4_.refs_2_), channel_id=1, source_target_pairs={{0,4},{4,8},{8,12},{1,5},{5,9},{9,13},{2,6},{6,10},{10,14},{3,7},{... | collective-permute-start | bytes 3145736 | tf_op jit(solution)/shard_map/ppermute | solution.py:120
  69.8 7.1 %collective-permute-done.6.refs_3_.refs_8_ = bf16[2,64,3584]{2,1,0:T(8,128)(2,1)S(1)} collective-permute-done((bf16[2,64,3584]{2,1,0:T(8,128)(2,1)}, bf16[2,64,3584]{2,1,0:T(8,128)(2,1)S(1)}, u32[]{:S(2)}, u32[]{:S(2)}) %collective-permute-start.6) | collective-permute-done | bytes 917536 | tf_op jit(solution)/shard_map/ppermute | solution.py:59
  83.6 21.0 %hidden_part.3 = (bf16[2,3584,512]{2,1,0:T(8,128)(2,1)}, f32[64,512]{1,0:T(8,128)}) custom-call(s32[1]{0:T(128)} %bitcast.6.rank_ref, bf16[3584,4096]{1,0:T(8,128)(2,1)} %refs_1_.16, bf16[3584,4096]{1,0:T(8,128)(2,1)} %refs_1_.16, bf16[1024,512]{1,0:T(8,128)(2,1)} %collective-permute-done.7.refs_4_.refs_2_, ...), custom_call_target="tpu_custom_call" | custom-call | flops 3240000000 | bytes 1 | tf_op jit(solution)/shard_map/hidden_part/pallas_call | solution.py:272
  104.6 3.1 %collective-permute-done.10.refs_6_ = bf16[2,64,3584]{2,1,0:T(8,128)(2,1)S(1)} collective-permute-done((bf16[2,64,3584]{2,1,0:T(8,128)(2,1)}, bf16[2,64,3584]{2,1,0:T(8,128)(2,1)S(1)}, u32[]{:S(2)}, u32[]{:S(2)}) %collective-permute-start.10) | collective-permute-done | bytes 917536 | tf_op jit(solution)/shard_map/ppermute | solution.py:54
  111.1 4.5 %collective-permute-start.15 = (bf16[2,3584,512]{2,1,0:T(8,128)(2,1)}, bf16[2,3584,512]{2,1,0:T(8,128)(2,1)}, u32[]{:S(2)}, u32[]{:S(2)}) collective-permute-start(bf16[2,3584,512]{2,1,0:T(8,128)(2,1)} %get-tuple-element.45.refs_10_.refs_5_.refs_3_), channel_id=1, source_target_pairs={{0,1},{1,0},{2,3},{3,2},{4,5},{5,4},{6,7},{7,6},{8,9},{9,8},{10,11... | collective-permute-start | bytes 22020104 | tf_op jit(solution)/shard_map/ppermute | solution.py:48
  118.2 17.7 %weigh_rows.4.refs_8_.refs_1_ = bf16[1536,512]{1,0:T(8,128)(2,1)} custom-call(bf16[1024,3584]{1,0:T(8,128)(2,1)} %refs_0_.21, bf16[1024,3584]{1,0:T(8,128)(2,1)} %refs_1_.21, bf16[2,64,3584]{2,1,0:T(8,128)(2,1)} %get-tuple-element.36.refs_2_, bf16[2,64,3584]{2,1,0:T(8,128)(2,1)} %get-tuple-element.39.refs_3_, ...), custom_call_target="tpu_custom_call" | custom-call | flops 6480000000 | bytes 1 | tf_op jit(solution)/shard_map/weigh_rows/pallas_call | solution.py:349
  135.8 4.5 %collective-permute-start.14 = (bf16[1536,512]{1,0:T(8,128)(2,1)}, bf16[1536,512]{1,0:T(8,128)(2,1)}, u32[]{:S(2)}, u32[]{:S(2)}) collective-permute-start(bf16[1536,512]{1,0:T(8,128)(2,1)} %weigh_rows.4.refs_8_.refs_1_), channel_id=1, source_target_pairs={{4,0},{12,8},{1,5},{9,13},{6,2},{14,10},{3,7},{11,15},{20,16},{28,... | collective-permute-start | bytes 4718600 | tf_op jit(solution)/shard_map/ppermute | solution.py:549
  149.5 17.6 %weigh_rows.5.refs_3_.refs_6_.refs_0_ = bf16[1536,512]{1,0:T(8,128)(2,1)} custom-call(bf16[1024,3584]{1,0:T(8,128)(2,1)} %refs_0_.21, bf16[1024,3584]{1,0:T(8,128)(2,1)} %refs_1_.21, bf16[2,64,3584]{2,1,0:T(8,128)(2,1)} %get-tuple-element.36.refs_2_, bf16[2,64,3584]{2,1,0:T(8,128)(2,1)} %get-tuple-element.39.refs_3_, ...), custom_call_target="tpu_custom_call" | custom-call | flops 6480000000 | bytes 1 | tf_op jit(solution)/shard_map/weigh_rows/pallas_call | solution.py:349
  174.8 3.8 %add_terms.5 = (bf16[1024,512]{1,0:T(8,128)(2,1)}, bf16[512,512]{1,0:T(8,128)(2,1)}, bf16[1024,512]{1,0:T(8,128)(2,1)}) custom-call(s32[1]{0:T(128)} %bitcast.4.refs_0_, bf16[1536,512]{1,0:T(8,128)(2,1)} %weigh_rows.4.refs_8_.refs_1_, bf16[1536,512]{1,0:T(8,128)(2,1)} %collective-permute-done.14.refs_2_, bf16[1536,512]{1,0:T(8,128)(2,1)} %weigh_rows.5.refs_3_.refs_6_.refs_0_), custom_call_target="tpu_custom_call" | custom-call | flops 540000000 | bytes 1 | tf_op jit(solution)/shard_map/add_terms/pallas_call | solution.py:391
  179.5 3.0 %collective-permute-done.23.refs_4_.refs_2_ = bf16[2,64,3584]{2,1,0:T(8,128)(2,1)} collective-permute-done((bf16[2,64,3584]{2,1,0:T(8,128)(2,1)}, bf16[2,64,3584]{2,1,0:T(8,128)(2,1)}, u32[]{:S(2)}, u32[]{:S(2)}) %collective-permute-start.23) | collective-permute-done | bytes 917536 | tf_op jit(solution)/shard_map/ppermute | solution.py:59
  182.5 11.7 %weigh_rows.6.refs_4_.refs_0_ = bf16[320,1024]{1,0:T(8,128)(2,1)} custom-call(bf16[2,64,3584]{2,1,0:T(8,128)(2,1)} %copy-done.9, bf16[2,64,3584]{2,1,0:T(8,128)(2,1)} %get-tuple-element.56.refs_1_.refs_3_, bf16[2,64,3584]{2,1,0:T(8,128)(2,1)} %copy-done.16, bf16[2,64,3584]{2,1,0:T(8,128)(2,1)} %collective-permute-done.22.refs_4_.refs_3_, ...), custom_call_target="tpu_custom_call" | custom-call | flops 4320000000 | bytes 1 | tf_op jit(solution)/shard_map/weigh_rows/pallas_call | solution.py:349
  203.4 3.2 %add_terms.6 = (bf16[1024,512]{1,0:T(8,128)(2,1)}, bf16[512,512]{1,0:T(8,128)(2,1)}) custom-call(bf16[1536,512]{1,0:T(8,128)(2,1)} %weigh_rows.5.refs_3_.refs_6_.refs_0_, bf16[1536,512]{1,0:T(8,128)(2,1)} %collective-permute-done.25.refs_1_, f32[8,128]{1,0:T(8,128)} %get-tuple-element.59.refs_2_, bf16[1024,512]{1,0:T(8,128)(2,1)} %copy-done.6, ...), custom_call_target="tpu_custom_call" | custom-call | flops 540000000 | bytes 1 | tf_op jit(solution)/shard_map/add_terms/pallas_call | solution.py:391
  212.2 8.2 %collective-permute-done.31.refs_2_ = bf16[2,64,3584]{2,1,0:T(8,128)(2,1)} collective-permute-done((bf16[2,64,3584]{2,1,0:T(8,128)(2,1)}, bf16[2,64,3584]{2,1,0:T(8,128)(2,1)}, u32[]{:S(2)}, u32[]{:S(2)}) %collective-permute-start.31) | collective-permute-done | bytes 917536 | tf_op jit(solution)/shard_map/ppermute | solution.py:59
  220.4 10.1 %weigh_rows.7.refs_0_ = bf16[192,1024]{1,0:T(8,128)(2,1)} custom-call(bf16[2,64,3584]{2,1,0:T(8,128)(2,1)} %get-tuple-element.62.refs_0_, bf16[2,64,3584]{2,1,0:T(8,128)(2,1)} %copy-done.25, bf16[2,64,3584]{2,1,0:T(8,128)(2,1)} %collective-permute-done.31.refs_2_, bf16[2,3584,512]{2,1,0:T(8,128)(2,1)} %get-tuple-element.45.refs_10_.refs_5_.refs_3_, ...), custom_call_target="tpu_custom_call" | custom-call | flops 16200000512 | bytes 1 | tf_op jit(solution)/shard_map/weigh_rows/pallas_call | solution.py:349
  232.0 4.8 %collective-permute-done.32.refs_1_ = bf16[192,1024]{1,0:T(8,128)(2,1)S(1)} collective-permute-done((bf16[192,1024]{1,0:T(8,128)(2,1)}, bf16[192,1024]{1,0:T(8,128)(2,1)S(1)}, u32[]{:S(2)}, u32[]{:S(2)}) %collective-permute-start.32) | collective-permute-done | bytes 393248 | tf_op jit(solution)/shard_map/ppermute | solution.py:549
  241.4 3.5 %assemble.2 = (bf16[512,512]{1,0:T(8,128)(2,1)}, bf16[512,512]{1,0:T(8,128)(2,1)}) custom-call(s32[4]{0:T(128)} %pad_add_fusion.words_ref, bf16[1024,512]{1,0:T(8,128)(2,1)} %get-tuple-element.60.refs_2_.refs_0_, bf16[1024,512]{1,0:T(8,128)(2,1)} %copy-done.24, bf16[512,512]{1,0:T(8,128)(2,1)} %get-tuple-element.61.refs_3_.refs_2_, ...), custom_call_target="tpu_custom_call" | custom-call | flops 270000000 | bytes 1 | tf_op jit(solution)/shard_map/assemble/pallas_call | solution.py:460
  244.9 7.0 %collective-permute-start.33 = (bf16[512,512]{1,0:T(8,128)(2,1)}, bf16[512,512]{1,0:T(8,128)(2,1)S(1)}, u32[]{:S(2)}, u32[]{:S(2)}) collective-permute-start(bf16[512,512]{1,0:T(8,128)(2,1)} %get-tuple-element.63.refs_5_), channel_id=1, source_target_pairs={{0,1},{1,0},{2,3},{3,2},{4,5},{5,4},{6,7},{7,6},{8,9},{9,8},{10,11... | collective-permute-start | bytes 1572872 | tf_op jit(solution)/shard_map/ppermute | solution.py:48
  252.0 3.3 %assemble.3.refs_2_.refs_0_ = bf16[1024,512]{1,0:T(8,128)(2,1)} custom-call(s32[4]{0:T(128)} %pad_add_fusion.words_ref, bf16[1024,512]{1,0:T(8,128)(2,1)} %get-tuple-element.50.refs_8_.refs_0_, bf16[1024,512]{1,0:T(8,128)(2,1)} %copy-done.6, bf16[512,512]{1,0:T(8,128)(2,1)} %get-tuple-element.52.refs_9_.refs_2_, ...), custom_call_target="tpu_custom_call" | custom-call | flops 270000000 | bytes 1 | tf_op jit(solution)/shard_map/assemble/pallas_call | solution.py:460
  259.8 3.0 %collective-permute-start.36 = (bf16[192,512]{1,0:T(8,128)(2,1)S(1)}, bf16[192,512]{1,0:T(8,128)(2,1)S(1)}, u32[]{:S(2)}, u32[]{:S(2)}) collective-permute-start(bf16[192,512]{1,0:T(8,128)(2,1)S(1)} %get-tuple-element.68), channel_id=1, source_target_pairs={{0,1},{1,0},{2,3},{3,2},{4,5},{5,4},{6,7},{7,6},{8,9},{9,8},{10,11... | collective-permute-start | bytes 589832 | tf_op jit(solution)/shard_map/ppermute | solution.py:48
  264.9 3.0 %finish.1 = bf16[512,1024]{1,0:T(8,128)(2,1)} custom-call(s32[4]{0:T(128)} %pad_add_fusion.words_ref, bf16[1024,512]{1,0:T(8,128)(2,1)} %assemble.3.refs_2_.refs_0_, bf16[512,512]{1,0:T(8,128)(2,1)} %copy-done.27, bf16[512,512]{1,0:T(8,128)(2,1)} %copy-done.28, bf16[192,512]{1,0:T(8,128)(2,1)} %get-tuple-element.69.refs_3_, bf16[192,512]{1,0:T(8,128)(2,1)} %copy-done.31), custom_call_target="tpu_custom_call" | custom-call | flops 810000000 | bytes 1 | tf_op jit(solution)/shard_map/finish/pallas_call | solution.py:511
  (175 shorter events, 85.3 us)
Async XLA Ops:
  5.6 26.3 %collective-permute-start.4 = (bf16[1024,512]{1,0:T(8,128)(2,1)}, bf16[1024,512]{1,0:T(8,128)(2,1)}, u32[]{:S(2)}, u32[]{:S(2)}) collective-permute-start(bf16[1024,512]{1,0:T(8,128)(2,1)} %bitcast.38), channel_id=1, source_target_pairs={{4,0},{8,4},{12,8},{5,1},{9,5},{13,9},{6,2},{10,6},{14,10},{7,3},{... | collective-permute-start | bytes 3145736 | tf_op jit(solution)/shard_map/ppermute | solution.py:121
  6.9 26.3 %collective-permute-start.3 = (bf16[1024,512]{1,0:T(8,128)(2,1)}, bf16[1024,512]{1,0:T(8,128)(2,1)}, u32[]{:S(2)}, u32[]{:S(2)}) collective-permute-start(bf16[1024,512]{1,0:T(8,128)(2,1)} %bitcast.39), channel_id=1, source_target_pairs={{0,4},{4,8},{8,12},{1,5},{5,9},{9,13},{2,6},{6,10},{10,14},{3,7},{... | collective-permute-start | bytes 3145736 | tf_op jit(solution)/shard_map/ppermute | solution.py:120
  12.0 41.6 %collective-permute-start.1 = (bf16[2,64,3584]{2,1,0:T(8,128)(2,1)}, bf16[2,64,3584]{2,1,0:T(8,128)(2,1)S(1)}, u32[]{:S(2)}, u32[]{:S(2)}) collective-permute-start(bf16[2,64,3584]{2,1,0:T(8,128)(2,1)} %get-tuple-element.37), channel_id=1, source_target_pairs={{2,0},{3,1},{0,2},{1,3},{6,4},{7,5},{4,6},{5,7},{10,8},{11,9},{8,1... | collective-permute-start | bytes 2752520 | tf_op jit(solution)/shard_map/ppermute | solution.py:54
  28.3 25.3 %collective-permute-start.2 = (bf16[2,64,3584]{2,1,0:T(8,128)(2,1)}, bf16[2,64,3584]{2,1,0:T(8,128)(2,1)S(1)}, u32[]{:S(2)}, u32[]{:S(2)}) collective-permute-start(bf16[2,64,3584]{2,1,0:T(8,128)(2,1)} %get-tuple-element.36.refs_2_), channel_id=1, source_target_pairs={{16,0},{0,16},{17,1},{1,17},{18,2},{2,18},{19,3},{3,19},{20,4},{4,... | collective-permute-start | bytes 2752520 | tf_op jit(solution)/shard_map/ppermute | solution.py:59
  31.9 26.9 %collective-permute-start.8 = (bf16[1024,512]{1,0:T(8,128)(2,1)}, bf16[1024,512]{1,0:T(8,128)(2,1)}, u32[]{:S(2)}, u32[]{:S(2)}) collective-permute-start(bf16[1024,512]{1,0:T(8,128)(2,1)} %collective-permute-done.4.refs_4_), channel_id=1, source_target_pairs={{4,0},{8,4},{12,8},{5,1},{9,5},{13,9},{6,2},{10,6},{14,10},{7,3},{... | collective-permute-start | bytes 3145736 | tf_op jit(solution)/shard_map/ppermute | solution.py:121
  33.2 26.9 %collective-permute-start.7 = (bf16[1024,512]{1,0:T(8,128)(2,1)}, bf16[1024,512]{1,0:T(8,128)(2,1)}, u32[]{:S(2)}, u32[]{:S(2)}) collective-permute-start(bf16[1024,512]{1,0:T(8,128)(2,1)} %collective-permute-done.3.refs_3_), channel_id=1, source_target_pairs={{0,4},{4,8},{8,12},{1,5},{5,9},{9,13},{2,6},{6,10},{10,14},{3,7},{... | collective-permute-start | bytes 3145736 | tf_op jit(solution)/shard_map/ppermute | solution.py:120
  38.2 31.6 %collective-permute-start.5 = (bf16[2,64,3584]{2,1,0:T(8,128)(2,1)}, bf16[2,64,3584]{2,1,0:T(8,128)(2,1)}, u32[]{:S(2)}, u32[]{:S(2)}) collective-permute-start(bf16[2,64,3584]{2,1,0:T(8,128)(2,1)} %get-tuple-element.38.refs_5_), channel_id=1, source_target_pairs={{2,0},{3,1},{0,2},{1,3},{6,4},{7,5},{4,6},{5,7},{10,8},{11,9},{8,1... | collective-permute-start | bytes 2752520 | tf_op jit(solution)/shard_map/ppermute | solution.py:54
  58.8 23.8 %collective-permute-start.13 = (bf16[1024,512]{1,0:T(8,128)(2,1)}, bf16[1024,512]{1,0:T(8,128)(2,1)S(1)}, u32[]{:S(2)}, u32[]{:S(2)}) collective-permute-start(bf16[1024,512]{1,0:T(8,128)(2,1)} %collective-permute-done.8.refs_5_), channel_id=1, source_target_pairs={{4,0},{8,4},{12,8},{5,1},{9,5},{13,9},{6,2},{10,6},{14,10},{7,3},{... | collective-permute-start | bytes 3145736 | tf_op jit(solution)/shard_map/ppermute | solution.py:121
  60.1 23.5 %collective-permute-start.12 = (bf16[1024,512]{1,0:T(8,128)(2,1)}, bf16[1024,512]{1,0:T(8,128)(2,1)}, u32[]{:S(2)}, u32[]{:S(2)}) collective-permute-start(bf16[1024,512]{1,0:T(8,128)(2,1)} %collective-permute-done.7.refs_4_.refs_2_), channel_id=1, source_target_pairs={{0,4},{4,8},{8,12},{1,5},{5,9},{9,13},{2,6},{6,10},{10,14},{3,7},{... | collective-permute-start | bytes 3145736 | tf_op jit(solution)/shard_map/ppermute | solution.py:120
  69.6 35.0 %collective-permute-start.9 = (bf16[2,64,3584]{2,1,0:T(8,128)(2,1)}, bf16[2,64,3584]{2,1,0:T(8,128)(2,1)S(1)}, u32[]{:S(2)}, u32[]{:S(2)}) collective-permute-start(bf16[2,64,3584]{2,1,0:T(8,128)(2,1)} %get-tuple-element.42), channel_id=1, source_target_pairs={{2,0},{3,1},{0,2},{1,3},{6,4},{7,5},{4,6},{5,7},{10,8},{11,9},{8,1... | collective-permute-start | bytes 2752520 | tf_op jit(solution)/shard_map/ppermute | solution.py:54
  79.9 27.8 %collective-permute-start.10 = (bf16[2,64,3584]{2,1,0:T(8,128)(2,1)}, bf16[2,64,3584]{2,1,0:T(8,128)(2,1)S(1)}, u32[]{:S(2)}, u32[]{:S(2)}) collective-permute-start(bf16[2,64,3584]{2,1,0:T(8,128)(2,1)} %get-tuple-element.43.refs_10_), channel_id=1, source_target_pairs={{2,0},{3,1},{0,2},{1,3},{6,4},{7,5},{4,6},{5,7},{10,8},{11,9},{8,1... | collective-permute-start | bytes 2752520 | tf_op jit(solution)/shard_map/ppermute | solution.py:54
  80.7 27.1 %collective-permute-start.11 = (bf16[2,64,3584]{2,1,0:T(8,128)(2,1)}, bf16[2,64,3584]{2,1,0:T(8,128)(2,1)S(1)}, u32[]{:S(2)}, u32[]{:S(2)}) collective-permute-start(bf16[2,64,3584]{2,1,0:T(8,128)(2,1)} %get-tuple-element.41.refs_4_), channel_id=1, source_target_pairs={{16,0},{0,16},{17,1},{1,17},{18,2},{2,18},{19,3},{3,19},{20,4},{4,... | collective-permute-start | bytes 2752520 | tf_op jit(solution)/shard_map/ppermute | solution.py:59
  111.1 38.1 %collective-permute-start.15 = (bf16[2,3584,512]{2,1,0:T(8,128)(2,1)}, bf16[2,3584,512]{2,1,0:T(8,128)(2,1)}, u32[]{:S(2)}, u32[]{:S(2)}) collective-permute-start(bf16[2,3584,512]{2,1,0:T(8,128)(2,1)} %get-tuple-element.45.refs_10_.refs_5_.refs_3_), channel_id=1, source_target_pairs={{0,1},{1,0},{2,3},{3,2},{4,5},{5,4},{6,7},{7,6},{8,9},{9,8},{10,11... | collective-permute-start | bytes 22020104 | tf_op jit(solution)/shard_map/ppermute | solution.py:48
  115.6 24.7 %collective-permute-start.17 = (bf16[2,64,3584]{2,1,0:T(8,128)(2,1)}, bf16[2,64,3584]{2,1,0:T(8,128)(2,1)S(1)}, u32[]{:S(2)}, u32[]{:S(2)}) collective-permute-start(bf16[2,64,3584]{2,1,0:T(8,128)(2,1)} %copy-done.10), channel_id=1, source_target_pairs={{16,0},{0,16},{17,1},{1,17},{18,2},{2,18},{19,3},{3,19},{20,4},{4,... | collective-permute-start | bytes 2752520 | tf_op jit(solution)/shard_map/ppermute | solution.py:59
  115.8 25.5 %collective-permute-start.18 = (bf16[2,64,3584]{2,1,0:T(8,128)(2,1)}, bf16[2,64,3584]{2,1,0:T(8,128)(2,1)S(1)}, u32[]{:S(2)}, u32[]{:S(2)}) collective-permute-start(bf16[2,64,3584]{2,1,0:T(8,128)(2,1)} %get-tuple-element.46.refs_11_), channel_id=1, source_target_pairs={{2,0},{3,1},{0,2},{1,3},{6,4},{7,5},{4,6},{5,7},{10,8},{11,9},{8,1... | collective-permute-start | bytes 2752520 | tf_op jit(solution)/shard_map/ppermute | solution.py:54
  135.8 39.0 %collective-permute-start.14 = (bf16[1536,512]{1,0:T(8,128)(2,1)}, bf16[1536,512]{1,0:T(8,128)(2,1)}, u32[]{:S(2)}, u32[]{:S(2)}) collective-permute-start(bf16[1536,512]{1,0:T(8,128)(2,1)} %weigh_rows.4.refs_8_.refs_1_), channel_id=1, source_target_pairs={{4,0},{12,8},{1,5},{9,13},{6,2},{14,10},{3,7},{11,15},{20,16},{28,... | collective-permute-start | bytes 4718600 | tf_op jit(solution)/shard_map/ppermute | solution.py:549
  140.3 26.9 %collective-permute-start.22 = (bf16[2,64,3584]{2,1,0:T(8,128)(2,1)S(1)}, bf16[2,64,3584]{2,1,0:T(8,128)(2,1)}, u32[]{:S(2)}, u32[]{:S(2)}) collective-permute-start(bf16[2,64,3584]{2,1,0:T(8,128)(2,1)S(1)} %copy-done.4), channel_id=1, source_target_pairs={{16,0},{0,16},{17,1},{1,17},{18,2},{2,18},{19,3},{3,19},{20,4},{4,... | collective-permute-start | bytes 2752520 | tf_op jit(solution)/shard_map/ppermute | solution.py:59
  149.2 33.2 %collective-permute-start.23 = (bf16[2,64,3584]{2,1,0:T(8,128)(2,1)}, bf16[2,64,3584]{2,1,0:T(8,128)(2,1)}, u32[]{:S(2)}, u32[]{:S(2)}) collective-permute-start(bf16[2,64,3584]{2,1,0:T(8,128)(2,1)} %copy-done.9), channel_id=1, source_target_pairs={{16,0},{0,16},{17,1},{1,17},{18,2},{2,18},{19,3},{3,19},{20,4},{4,... | collective-permute-start | bytes 2752520 | tf_op jit(solution)/shard_map/ppermute | solution.py:59
  172.0 30.2 %collective-permute-start.25 = (bf16[1536,512]{1,0:T(8,128)(2,1)S(1)}, bf16[1536,512]{1,0:T(8,128)(2,1)}, u32[]{:S(2)}, u32[]{:S(2)}) collective-permute-start(bf16[1536,512]{1,0:T(8,128)(2,1)S(1)} %copy-done.2), channel_id=1, source_target_pairs={{4,0},{12,8},{1,5},{9,13},{6,2},{14,10},{3,7},{11,15},{20,16},{28,... | collective-permute-start | bytes 4718600 | tf_op jit(solution)/shard_map/ppermute | solution.py:549
  174.4 27.7 %collective-permute-start.27 = (bf16[2,64,3584]{2,1,0:T(8,128)(2,1)}, bf16[2,64,3584]{2,1,0:T(8,128)(2,1)S(1)}, u32[]{:S(2)}, u32[]{:S(2)}) collective-permute-start(bf16[2,64,3584]{2,1,0:T(8,128)(2,1)} %get-tuple-element.56.refs_1_.refs_3_), channel_id=1, source_target_pairs={{16,0},{0,16},{17,1},{1,17},{18,2},{2,18},{19,3},{3,19},{20,4},{4,... | collective-permute-start | bytes 2752520 | tf_op jit(solution)/shard_map/ppermute | solution.py:59
  178.6 23.5 %collective-permute-start.19 = (bf16[1024,512]{1,0:T(8,128)(2,1)}, bf16[1024,512]{1,0:T(8,128)(2,1)S(1)}, u32[]{:S(2)}, u32[]{:S(2)}) collective-permute-start(bf16[1024,512]{1,0:T(8,128)(2,1)} %get-tuple-element.51), channel_id=1, source_target_pairs={{0,8},{2,10},{5,13},{7,15},{8,0},{10,2},{13,5},{15,7},{16,24},{18,... | collective-permute-start | bytes 3145736 | tf_op jit(solution)/shard_map/ppermute | solution.py:549
  194.8 25.6 %collective-permute-start.31 = (bf16[2,64,3584]{2,1,0:T(8,128)(2,1)}, bf16[2,64,3584]{2,1,0:T(8,128)(2,1)}, u32[]{:S(2)}, u32[]{:S(2)}) collective-permute-start(bf16[2,64,3584]{2,1,0:T(8,128)(2,1)} %get-tuple-element.62.refs_0_), channel_id=1, source_target_pairs={{16,0},{0,16},{17,1},{1,17},{18,2},{2,18},{19,3},{3,19},{20,4},{4,... | collective-permute-start | bytes 2752520 | tf_op jit(solution)/shard_map/ppermute | solution.py:59
  206.7 25.3 %collective-permute-start.30 = (bf16[512,512]{1,0:T(8,128)(2,1)}, bf16[512,512]{1,0:T(8,128)(2,1)S(1)}, u32[]{:S(2)}, u32[]{:S(2)}) collective-permute-start(bf16[512,512]{1,0:T(8,128)(2,1)} %get-tuple-element.61.refs_3_.refs_2_), channel_id=1, source_target_pairs={{0,8},{5,13},{10,2},{15,7},{16,24},{21,29},{26,18},{31,23}} | collective-permute-start | bytes 1572872 | tf_op jit(solution)/shard_map/ppermute | solution.py:549
  207.4 33.1 %collective-permute-start.29 = (bf16[1024,512]{1,0:T(8,128)(2,1)}, bf16[1024,512]{1,0:T(8,128)(2,1)S(1)}, u32[]{:S(2)}, u32[]{:S(2)}) collective-permute-start(bf16[1024,512]{1,0:T(8,128)(2,1)} %get-tuple-element.60.refs_2_.refs_0_), channel_id=1, source_target_pairs={{8,0},{13,5},{2,10},{7,15},{24,16},{29,21},{18,26},{23,31}} | collective-permute-start | bytes 3145736 | tf_op jit(solution)/shard_map/ppermute | solution.py:549
  (49 other events, 499.9 us)
